TPU v7x, 128 devices: a whole 4x4x4 slice. The times are simulated.
128 devices in a mesh: aux: 8 (over x, core), orb: 16 (over y, z).
Axes of the slice: x: 4, y: 4, z: 4, core: 2. Of those that a mesh axis runs over, the one named last changes fastest.
Arguments:
- three_center: bfloat16 [1280, 16, 3, 4096], P(('aux', 'orb')), may hold values from -1.25 to 1.25
- atom_size: int32 [16], replicated, may hold values from 32 to 64
- tensor_pattern: int32 [80, 16, 3], P('aux', 'orb'), may hold values 0 or 1
- green_occ: bfloat16 [16, 3, 4096], P('orb'), may hold values from -0.5 to 0.5
- green_virt: bfloat16 [16, 3, 4096], P('orb'), may hold values from -0.5 to 0.5
- green_pattern: int32 [16, 3], P('orb'), may hold values 0 or 1
Outputs:
- chi: float32 [1280, 1280], P(('aux', 'orb'))
Inputs may be any that keep to these rules, and one draw needn't show every extreme that they name: `atom_size`: functions in use per block.
All inputs are finite; a program needn't handle non-finite values. No bound on the sum of `tensor_pattern` or of `green_pattern` on one device may be relied on, other than what follows from the above.
Results may differ from a plain program's by a relative error of at most 0.0041.
Values may be sent and summed in bfloat16 or wider, within the bound.
No kernel may reach another device: no remote copies, remote signals or barrier semaphores. Data moves between devices by JAX's collectives and lax.ppermute only.
A program may use at most 128 MiB of HBM per device.

v0:
```python
import jax
import jax.numpy as jnp
from jax import lax
from jax.sharding import PartitionSpec as P

BS = 64
R = 1
W = 3
ABS = 16


def padded(block, sides, width):
    for axis, dim in sides:
        count = lax.axis_size(axis)
        forward = [(i, i + 1) for i in range(count - 1)]
        backward = [(target, source) for source, target in forward]
        low = lax.ppermute(
            lax.slice_in_dim(block, block.shape[dim] - width, None, axis=dim), axis, forward
        )
        high = lax.ppermute(lax.slice_in_dim(block, 0, width, axis=dim), axis, backward)
        block = jnp.concatenate([low, block, high], axis=dim)
    return block


def block_masks(atom_size, first_block, local_blocks):
    total_blocks = atom_size.shape[0]
    owned = first_block + jnp.arange(local_blocks, dtype=jnp.int32)
    offsets = jnp.arange(W, dtype=jnp.int32)
    partner = owned[:, None] + offsets[None, :] - R
    inside = (partner >= 0) & (partner < total_blocks)
    catalog = jnp.arange(total_blocks, dtype=jnp.int32)
    size_partner = jnp.sum(jnp.where(partner[:, :, None] == catalog, atom_size, 0), axis=2)
    size_owned = jnp.sum(jnp.where(owned[:, None] == catalog, atom_size, 0), axis=1)
    funcs = jnp.arange(BS, dtype=jnp.int32)
    rows_ok = (funcs[None, None, :] < size_partner[:, :, None]) & inside[:, :, None]
    cols_ok = funcs[None, :] < size_owned[:, None]
    pair_ok = rows_ok[:, :, :, None] & cols_ok[:, None, None, :]
    return (inside, pair_ok.reshape(local_blocks, W, BS * BS))


def first_products(padded_occ, tensor):
    rows = tensor.shape[0]
    local_blocks = tensor.shape[1]
    results = []
    for target in range(W):
        total = jnp.zeros((rows, local_blocks, BS, BS), jnp.float32)
        for source in range(W):
            if abs(target - source) <= R:
                green = padded_occ[source : source + local_blocks, target - source + R].reshape(
                    local_blocks, BS, BS
                )
                block = tensor[:, :, source].reshape(rows, local_blocks, BS, BS)
                total = total + jnp.einsum(
                    "nlm,pnmv->pnlv", green, block, preferred_element_type=jnp.float32
                )
        results.append(total.astype(jnp.bfloat16).reshape(rows, local_blocks, BS * BS))
    return jnp.concatenate(results, axis=2).reshape(rows, local_blocks * W * BS * BS)


def second_products(padded_tensor, virt):
    rows = padded_tensor.shape[0]
    local_blocks = virt.shape[0]
    results = []
    for target in range(W):
        total = jnp.zeros((rows, local_blocks, BS, BS), jnp.float32)
        for source in range(W):
            if abs(target - source) <= R:
                block = padded_tensor[
                    :, source : source + local_blocks, target - source + R
                ].reshape(rows, local_blocks, BS, BS)
                green = virt[:, source].reshape(local_blocks, BS, BS)
                total = total + jnp.einsum(
                    "pnls,nsv->pnlv", block, green, preferred_element_type=jnp.float32
                )
        results.append(total.astype(jnp.bfloat16).reshape(rows, local_blocks, BS * BS))
    return jnp.concatenate(results, axis=2).reshape(rows, local_blocks * W * BS * BS)


def body(three_center, atom_size, tensor_pattern, green_occ, green_virt, green_pattern):
    regrouped = lax.all_to_all(three_center, "orb", split_axis=1, concat_axis=0, tiled=True)
    local_blocks = regrouped.shape[1]
    first_block = lax.axis_index("orb") * local_blocks
    inside, pair_ok = block_masks(atom_size, first_block, local_blocks)
    pattern_rows = jnp.repeat(tensor_pattern, ABS, axis=0)
    keep = (pattern_rows[..., None] > 0) & pair_ok[None]
    tensor = jnp.where(keep, regrouped, jnp.zeros((), regrouped.dtype))
    diagonal = jnp.arange(W, dtype=jnp.int32) == R
    green_keep = ((green_pattern > 0) | diagonal[None, :]) & inside
    green_mask = green_keep[..., None] & pair_ok
    occ = jnp.where(green_mask, green_occ, jnp.zeros((), green_occ.dtype))
    virt = jnp.where(green_mask, green_virt, jnp.zeros((), green_virt.dtype))
    padded_occ = padded(occ, (("orb", 0),), R)
    padded_tensor = padded(tensor, (("orb", 1),), R)
    first = first_products(padded_occ, tensor)
    second = second_products(padded_tensor, virt)
    left_all, right_all = (
        lax.all_to_all(first, "aux", split_axis=1, concat_axis=0, tiled=True),
        lax.all_to_all(second, "aux", split_axis=1, concat_axis=0, tiled=True),
    )
    return lax.psum_scatter(
        lax.dot_general(
            left_all, right_all, (((1,), (1,)), ((), ())), preferred_element_type=jnp.float32
        ),
        ("aux", "orb"),
        scatter_dimension=0,
        tiled=True,
    )


def solution(mesh):
    return jax.shard_map(
        body,
        mesh=mesh,
        in_specs=(
            P(("aux", "orb"), None, None, None),
            P(),
            P("aux", "orb", None),
            P("orb", None, None),
            P("orb", None, None),
            P("orb", None),
        ),
        out_specs=P(("aux", "orb"), None),
        check_vma=False,
    )
```

profile of v0, /device:TPU:0, one launch (start us, length us, event | category | flops | bytes accessed | tf_op | source)
XLA Modules:
  0.0 537.0 jit_solution(3487629076170227426)
XLA Ops:
  6.5 7.2 %copy.128 = bf16[10,16,3,4096]{3,0,2,1:T(8,128)(2,1)} copy(bf16[10,16,3,4096]{3,1,2,0:T(8,128)(2,1)} %param.6) | data formatting | bytes 7864320 | tf_op args[0]
  13.7 8.3 %all-to-all-start = ((bf16[10,16,3,4096]{3,0,2,1:T(8,128)(2,1)}), bf16[10,16,3,4096]{3,0,2,1:T(8,128)(2,1)}, u32[]{:S(2)}, u32[]{:S(2)}) async-start(bf16[10,16,3,4096]{3,0,2,1:T(8,128)(2,1)} %copy.128), calls=%async_computation | async-start | bytes 12582912 | tf_op jit(solution)/shard_map/all_to_all | solution.py:80
  24.2 3.8 collective-permute-start
  30.4 45.1 %collective-permute-done = bf16[1,3,4096]{2,1,0:T(4,128)(2,1)S(1)} collective-permute-done((bf16[1,3,4096]{2,1,0:T(4,128)(2,1)S(1)}, bf16[1,3,4096]{2,1,0:T(4,128)(2,1)S(1)}, u32[]{:S(2)}, u32[]{:S(2)}) %collective-permute-start) | collective-permute-done | bytes 24608 | tf_op jit(solution)/shard_map/ppermute | solution.py:17
  79.6 44.7 %all-to-all-done = bf16[10,16,3,4096]{3,0,2,1:T(8,128)(2,1)} async-done(((bf16[10,16,3,4096]{3,0,2,1:T(8,128)(2,1)}), bf16[10,16,3,4096]{3,0,2,1:T(8,128)(2,1)}, u32[]{:S(2)}, u32[]{:S(2)}) %all-to-all-start) | async-done | bytes 3932192 | tf_op jit(solution)/shard_map/all_to_all | solution.py:80
  124.3 6.2 %copy.129 = bf16[16,10,1,3,4096]{4,1,0,3,2:T(8,128)(2,1)} copy(bf16[16,10,1,3,4096]{4,1,3,0,2:T(8,128)(2,1)} %bitcast.1) | data formatting | bytes 7864320 | tf_op jit(solution)/shard_map/all_to_all | solution.py:80
  130.6 6.6 %all_to_all.44 = bf16[160,1,3,4096]{3,0,2,1:T(8,128)(2,1)} reshape(bf16[16,10,1,3,4096]{4,1,0,3,2:T(8,128)(2,1)} %copy.129) | data formatting | bytes 7864320 | tf_op jit(solution)/shard_map/all_to_all | solution.py:80
  137.2 5.5 %and_select_fusion = bf16[160,1,3,4096]{3,0,2,1:T(8,128)(2,1)} fusion(bf16[160,1,3,4096]{3,0,2,1:T(8,128)(2,1)} %all_to_all.44, pred[3,4096]{1,0:T(4,128)(4,1)S(1)} %broadcast_and_fusion, pred[160,3]{0,1:T(4,128)(4,1)S(1)} %gt.24), kind=kLoop, calls=%fused_computation | loop fusion | flops 3932160 | bytes 7877088 | tf_op jit(solution)/shard_map/jit(_where)/select_n | solution.py:86
  150.9 4.8 reshape.442
  155.7 3.9 reshape.440
  159.6 3.9 reshape.447
  163.5 5.6 %copy.131 = bf16[160,64,64]{0,1,2:T(8,128)(2,1)S(1)} copy(bf16[160,64,64]{2,1,0:T(8,128)(2,1)} %reshape.442) | data formatting | bytes 2621440 | tf_op jit(solution)/shard_map/reshape.26
  169.1 6.6 %copy.130 = bf16[160,64,64]{0,1,2:T(8,128)(2,1)} copy(bf16[160,64,64]{2,1,0:T(8,128)(2,1)} %reshape.440) | data formatting | bytes 2621440 | tf_op jit(solution)/shard_map/reshape.23
  175.7 6.6 %copy.135 = bf16[160,64,64]{0,1,2:T(8,128)(2,1)} copy(bf16[160,64,64]{2,1,0:T(8,128)(2,1)} %reshape.447) | data formatting | bytes 2621440 | tf_op jit(solution)/shard_map/reshape.35
  190.3 6.2 %copy.136 = bf16[160,1,64,64]{3,2,0,1:T(8,128)(2,1)} copy(bf16[160,1,64,64]{0,2,3,1:T(8,128)(2,1)} %fusion.6) | data formatting | bytes 2621440 | tf_op jit(solution)/shard_map/convert_element_type | solution.py:56
  196.5 4.7 reshape.449
  201.2 4.9 fusion.7
  206.1 6.4 %copy.132 = bf16[160,1,64,64]{3,2,0,1:T(8,128)(2,1)} copy(bf16[160,1,64,64]{0,2,3,1:T(8,128)(2,1)} %fusion.7) | data formatting | bytes 2621440 | tf_op jit(solution)/shard_map/convert_element_type | solution.py:56
  212.5 4.6 reshape.444
  220.8 5.3 copy.139
  235.9 4.8 all-to-all-start.1
  241.2 4.8 fusion.2
  246.0 4.8 fusion.4
  250.9 4.8 fusion
  265.4 3.7 copy.149
  278.6 4.3 add_convert_fusion.2
  282.8 3.8 copy.155
  288.5 4.3 add_convert_fusion
  292.8 4.0 copy.157
  302.8 52.1 %all_to_all.56 = bf16[160,8,1536]{2,0,1:T(8,128)(2,1)S(1)} all-to-all(bf16[160,8,1536]{2,0,1:T(8,128)(2,1)} %copy.158), channel_id=1, replica_groups=mesh['aux'=8,'orb'=16] {'aux'}, dimensions={1} | all-to-all | bytes 7864320 | tf_op jit(solution)/shard_map/all_to_all | solution.py:98
  354.9 8.7 %fusion.26 = f32[1280,1280]{1,0:T(8,128)} fusion(bf16[1280,1536]{1,0:T(8,128)(2,1)} %bitcast.10, bf16[1280,1536]{1,0:T(8,128)(2,1)S(1)} %bitcast.135), kind=kOutput, calls=%fused_computation.57 | convolution fusion | flops 5033164800 | bytes 14417920 | tf_op jit(solution)/shard_map/dot_general | solution.py:101
  363.7 164.7 %all-reduce.3.cloned.1.call-done = f32[1280,1280]{1,0:T(8,128)} async-done(((f32[1280,1280]{1,0:T(8,128)}), f32[1280,1280]{1,0:T(8,128)}) %all-reduce.3.cloned.1.call-update) | async-done | bytes 6553616
  (93 shorter events, 67.2 us)
Async XLA Ops:
  13.7 8.4 %copy-start.13 = (s32[16]{0:T(128)S(1)}, s32[16]{0:T(128)}, u32[]{:S(2)}) copy-start(s32[16]{0:T(128)} %param.7) | copy-start | bytes 196
  13.7 10.3 %copy-start.14 = (s32[1,3]{1,0:T(1,128)S(1)}, s32[1,3]{1,0:T(1,128)}, u32[]{:S(2)}) copy-start(s32[1,3]{1,0:T(1,128)} %param.11) | copy-start | bytes 40
  13.7 10.3 %copy-start.10 = (bf16[1,3,4096]{2,1,0:T(4,128)(2,1)S(1)}, bf16[1,3,4096]{2,1,0:T(4,128)(2,1)}, u32[]{:S(2)}) copy-start(bf16[1,3,4096]{2,1,0:T(4,128)(2,1)} %param.10) | copy-start | bytes 73732
  13.7 10.3 %copy-start.11 = (bf16[1,3,4096]{2,1,0:T(4,128)(2,1)S(1)}, bf16[1,3,4096]{2,1,0:T(4,128)(2,1)}, u32[]{:S(2)}) copy-start(bf16[1,3,4096]{2,1,0:T(4,128)(2,1)} %param.9) | copy-start | bytes 73732
  13.7 15.6 %copy-start.12 = (s32[10,1,3]{0,1,2:T(1,128)S(1)}, s32[10,1,3]{0,1,2:T(1,128)}, u32[]{:S(2)}) copy-start(s32[10,1,3]{0,1,2:T(1,128)} %param.8) | copy-start | bytes 364
  13.7 110.6 %all-to-all-start = ((bf16[10,16,3,4096]{3,0,2,1:T(8,128)(2,1)}), bf16[10,16,3,4096]{3,0,2,1:T(8,128)(2,1)}, u32[]{:S(2)}, u32[]{:S(2)}) async-start(bf16[10,16,3,4096]{3,0,2,1:T(8,128)(2,1)} %copy.128), calls=%async_computation | async-start | bytes 12582912 | tf_op jit(solution)/shard_map/all_to_all | solution.py:80
  24.2 51.3 %collective-permute-start = (bf16[1,3,4096]{2,1,0:T(4,128)(2,1)S(1)}, bf16[1,3,4096]{2,1,0:T(4,128)(2,1)S(1)}, u32[]{:S(2)}, u32[]{:S(2)}) collective-permute-start(bf16[1,3,4096]{2,1,0:T(4,128)(2,1)S(1)} %get-tuple-element.23), channel_id=1, source_target_pairs={{0,1},{1,2},{2,3},{3,4},{4,5},{5,6},{6,7},{7,8},{8,9},{9,10},{10,1... | collective-permute-start | bytes 73736 | tf_op jit(solution)/shard_map/ppermute | solution.py:17
  27.9 51.3 %collective-permute-start.1 = (bf16[1,3,4096]{2,1,0:T(4,128)(2,1)S(1)}, bf16[1,3,4096]{2,1,0:T(4,128)(2,1)S(1)}, u32[]{:S(2)}, u32[]{:S(2)}) collective-permute-start(bf16[1,3,4096]{2,1,0:T(4,128)(2,1)S(1)} %get-tuple-element.23), channel_id=1, source_target_pairs={{1,0},{2,1},{3,2},{4,3},{5,4},{6,5},{7,6},{8,7},{9,8},{10,9},{11,1... | collective-permute-start | bytes 73736 | tf_op jit(solution)/shard_map/ppermute | solution.py:20
  146.2 109.5 %collective-permute-start.2 = (bf16[160,1,3,4096]{3,0,2,1:T(8,128)(2,1)}, bf16[160,1,3,4096]{3,0,2,1:T(8,128)(2,1)}, u32[]{:S(2)}, u32[]{:S(2)}) collective-permute-start(bf16[160,1,3,4096]{3,0,2,1:T(8,128)(2,1)} %and_select_fusion), channel_id=1, source_target_pairs={{0,1},{1,2},{2,3},{3,4},{4,5},{5,6},{6,7},{7,8},{8,9},{9,10},{10,1... | collective-permute-start | bytes 11796488 | tf_op jit(solution)/shard_map/ppermute | solution.py:17
  149.5 109.7 %collective-permute-start.3 = (bf16[160,1,3,4096]{3,0,2,1:T(8,128)(2,1)}, bf16[160,1,3,4096]{3,0,2,1:T(8,128)(2,1)}, u32[]{:S(2)}, u32[]{:S(2)}) collective-permute-start(bf16[160,1,3,4096]{3,0,2,1:T(8,128)(2,1)} %and_select_fusion), channel_id=1, source_target_pairs={{1,0},{2,1},{3,2},{4,3},{5,4},{6,5},{7,6},{8,7},{9,8},{10,9},{11,1... | collective-permute-start | bytes 11796488 | tf_op jit(solution)/shard_map/ppermute | solution.py:20
  182.3 1.6 copy-start.3
  183.9 1.6 copy-start.4
  217.1 1.6 copy-start.5
  235.9 5.3 copy-start
  235.9 66.9 %all-to-all-start.1 = ((bf16[160,8,1536]{2,0,1:T(8,128)(2,1)}), bf16[160,8,1536]{2,0,1:T(8,128)(2,1)}, u32[]{:S(2)}, u32[]{:S(2)}) async-start(bf16[160,8,1536]{2,0,1:T(8,128)(2,1)} %copy.140), calls=%async_computation.1 | async-start | bytes 7864320 | tf_op jit(solution)/shard_map/all_to_all | solution.py:97
  240.7 287.7 %all-reduce.3.cloned.1.call-start = ((), (), s32[]{:S(2)}) async-start(), calls=%async_computation.3 | async-start | bytes 13107200
  241.2 4.9 copy-start.1
  246.0 4.8 copy-start.2
  269.2 2.2 copy-start.6
  269.2 2.9 copy-start.7
  292.8 4.0 copy-start.8
  292.8 4.0 copy-start.9
Sparse Core Ops, SparseCore 0:
  363.8 164.5 all-reduce.2
where the time goes:
time: 545 us; the launch traced here: 537 us
  waiting for transfers between devices  258 us (47%)
  local copies, waits for them, and re-layouts  131 us (24%)
  blocking collectives  52.1 us (10%)
  matrix products  47.1 us (9%)
  starting transfers between devices  23.4 us (4%)
  between operations  13.9 us (3%)
  other arithmetic  10.9 us (2%)
    unnamed x2, waiting for transfers between devices  165 us
    all_to_all x1, blocking collectives, body(): lax.all_to_all(second, 'aux', split_axis=1, concat_axis=0, tiled=True)  52.1 us
    ppermute x2, waiting for transfers between devices, padded(): lax.ppermute(lax.slice_in_dim(block, block.shape[dim] - width, None, axis...  45.1 us
    all_to_all x1, waiting for transfers between devices, body(): lax.all_to_all(three_center, 'orb', split_axis=1, concat_axis=0, tiled=True)  44.7 us
    another operation x16, local copies, waits for them, and re-layouts  32.2 us
    dot_general x7, matrix products, second_products(): jnp.einsum('pnls,nsv->pnlv', block, green, preferred_element_type=jnp.flo...  24.5 us
    slice x6, local copies, waits for them, and re-layouts, second_products(): padded_tensor[:, source:source + local_blocks, target - source + R]  18.4 us
    convert_element_type x3, local copies, waits for them, and re-layouts, first_products(): total.astype(jnp.bfloat16).reshape(rows, local_blocks, BS * BS)  17.9 us
  transfers between devices with their start and end apart: 7, of which 4 were waited for; matrix products, arithmetic and copies ran while one was open for 27% of the time, Pallas kernels for 0%

commit v1 on v0

v1 whole, which is shorter than its diff:
```python
import functools

import jax
import jax.numpy as jnp
import numpy as np
from jax import lax
from jax.experimental import pallas as pl
from jax.experimental.pallas import tpu as pltpu
from jax.sharding import PartitionSpec as P

BS = 64
R = 1
W = 3
ABS = 16
NOB = 16
NPD = 10
NG = 10
BF = jnp.bfloat16
F32 = jnp.float32
VLIM = 56 * 1024 * 1024

STEPS = [(k // 2, k % 2) for k in range(8)]


def pairs_of(k):
    dx, dc = STEPS[k]
    return [(i, ((i // 2 + dx) % 4) * 2 + ((i % 2) ^ dc)) for i in range(8)]


def dest_of(a, k):
    dx, dc = STEPS[k]
    return lax.rem(a // 2 + dx, 4) * 2 + (lax.rem(a, 2) if dc == 0 else 1 - lax.rem(a, 2))


def src_of(a, k):
    dx, dc = STEPS[k]
    return lax.rem(a // 2 + 4 - dx, 4) * 2 + (lax.rem(a, 2) if dc == 0 else 1 - lax.rem(a, 2))


def swap16():
    r = np.arange(256)
    m = np.zeros((256, 256), np.float32)
    m[r, (r % 16) * 16 + r // 16] = 1.0
    return jnp.asarray(m, BF)


def vspec():
    return pl.BlockSpec(memory_space=pltpu.VMEM)


def sspec():
    return pl.BlockSpec(memory_space=pltpu.SMEM)


def spread_kernel(pos, perm, x_ref, ta_ref, *rest):
    tb, s = rest[:8], rest[8]
    a = pos[0]
    for d in range(W):
        x = x_ref[0, d]
        for o in range(16):
            ta_ref[o, d] = x[:, 256 * o : 256 * o + 256]
        halves = [
            jnp.concatenate([x[:, 128 * (16 * h + c) : 128 * (16 * h + c) + 128] for c in range(16)], axis=0)
            for h in range(2)
        ]
        y = jnp.dot(perm[...], jnp.concatenate(halves, axis=1), preferred_element_type=F32).astype(BF)
        for n in range(NOB):
            for h in range(2):
                s[n, d, 16 * h : 16 * h + 16] = y[16 * n : 16 * n + 16, 128 * h : 128 * h + 128]
    for k in range(8):
        t = dest_of(a, k)
        for i in range(2):
            tb[k][i, :, 0] = s[2 * t + i]


def spread(pos, perm, x):
    return pl.pallas_call(
        spread_kernel,
        grid=(NPD,),
        in_specs=[
            sspec(),
            pl.BlockSpec((256, 256), lambda i: (0, 0)),
            pl.BlockSpec((1, W, NOB, 4096), lambda i: (i, 0, 0, 0)),
        ],
        out_specs=[pl.BlockSpec((16, W, NOB, 256), lambda i: (0, i, 0, 0))]
        + [pl.BlockSpec((2, W, 1, 32, 128), lambda i: (0, 0, i, 0, 0))] * 8,
        out_shape=[jax.ShapeDtypeStruct((16, NPD * W, NOB, 256), BF)]
        + [jax.ShapeDtypeStruct((2, W, NPD, 32, 128), BF)] * 8,
        scratch_shapes=[pltpu.VMEM((NOB, W, 32, 128), BF)],
        compiler_params=pltpu.CompilerParams(vmem_limit_bytes=VLIM),
        cost_estimate=pl.CostEstimate(flops=10**9, bytes_accessed=12 * 10**6, transcendentals=0),
        name="spread",
    )(pos, perm, x)


def greens_kernel(pos, g_ref, k4_ref, w_ref):
    a = pos[0]
    lane = lax.broadcasted_iota(jnp.int32, (64, 128), 1)
    zero = jnp.zeros((64, 128), BF)

    def one(n, carry):
        for d in range(W):
            v = g_ref[n, 64 * d : 64 * d + 64, 0:64]
            vv = jnp.concatenate([v, v], axis=1)
            lo = jnp.where(lane < 64, vv, zero)
            hi = jnp.where(lane < 64, zero, vv)
            for r in range(4):
                for t in range(2):
                    part = zero if r // 2 != t else (lo if r % 2 == 0 else hi)
                    k4_ref[n, d, 64 * r : 64 * r + 64, 128 * t : 128 * t + 128] = part
        return carry

    lax.fori_loop(0, NOB, one, 0)
    z = jnp.zeros((32, 64), BF)
    for i in range(2):
        for g in range(2):
            for e in range(W):
                cols = []
                for d in range(W):
                    f = e - d + 1
                    if f < 0 or f >= W:
                        cols.append(z)
                        continue
                    m = 2 * a + i + d - 1
                    ok = (m >= 0) & (m < NOB)
                    mc = jnp.clip(m, 0, NOB - 1)
                    row = (f * 2 + g) * 32
                    v = g_ref[mc, row : row + 32, :][:, 64:128]
                    cols.append(jnp.where(ok, v, z))
                row = (g * W + e) * 32
                w_ref[i, row : row + 32, :] = jnp.concatenate(cols, axis=1)


def greens(pos, g):
    return pl.pallas_call(
        greens_kernel,
        in_specs=[sspec(), vspec()],
        out_specs=[vspec(), vspec()],
        out_shape=[
            jax.ShapeDtypeStruct((NOB, W, 256, 256), BF),
            jax.ShapeDtypeStruct((2, 192, 192), BF),
        ],
        compiler_params=pltpu.CompilerParams(vmem_limit_bytes=VLIM),
        cost_estimate=pl.CostEstimate(flops=10**6, bytes_accessed=8 * 10**6, transcendentals=0),
        name="greens",
    )(pos, g)


def second_kernel(pos, pat, perm, ta_ref, k4_ref, *rest):
    outs, s = rest[:8], rest[8]
    a = pos[0]
    s[0] = jnp.zeros(s.shape[1:], BF)
    s[NOB + 1] = jnp.zeros(s.shape[1:], BF)

    def regroup(g, carry):
        for d in range(W):
            x = ta_ref[pl.ds(16 * g, 16), d].reshape(256, 256)
            y = jnp.dot(perm[...], x, preferred_element_type=F32)
            for n in range(NOB):
                keep = pat[((a * NOB + n) * NG + g) * W + d] > 0
                part = y[16 * n : 16 * n + 16]
                s[n + 1, d, pl.ds(pl.multiple_of(16 * g, 16), 16)] = jnp.where(
                    keep, part, jnp.zeros_like(part)
                ).astype(BF)
        return carry

    lax.fori_loop(0, NG, regroup, 0)
    for k in range(8):
        t = dest_of(a, k)

        def one(i, carry, k=k, t=t):
            n = 2 * t + i
            for e in range(W):
                acc = None
                for d in range(W):
                    f = e - d + 1
                    if 0 <= f < W:
                        p = jnp.dot(s[n + d, f], k4_ref[n, d], preferred_element_type=F32)
                        acc = p if acc is None else acc + p
                outs[k][i * W + e] = acc.astype(BF)
            return carry

        lax.fori_loop(0, 2, one, 0)


def second_products(pos, pat, perm, ta, k4):
    return pl.pallas_call(
        second_kernel,
        in_specs=[sspec(), sspec(), vspec(), vspec(), vspec()],
        out_specs=[vspec()] * 8,
        out_shape=[jax.ShapeDtypeStruct((2 * W, 160, 256), BF)] * 8,
        scratch_shapes=[pltpu.VMEM((NOB + 2, W, 160, 256), BF)],
        compiler_params=pltpu.CompilerParams(vmem_limit_bytes=VLIM),
        cost_estimate=pl.CostEstimate(flops=4 * 10**9, bytes_accessed=15 * 10**6, transcendentals=0),
        name="second",
    )(pos, pat, perm, ta, k4)


def first_kernel(pos, pat, perm, w_ref, *rest):
    tb, out, s = rest[:8], rest[8], rest[9]
    a, o = pos[0], pos[1]
    lane = lax.broadcasted_iota(jnp.int32, (96, NPD * 128), 1)
    low = lax.rem(lane, 128) < 64
    for k in range(8):
        src = src_of(a, k)
        base = lax.rem(src, 2) * 40 + (src // 2) * 10

        def one(i, carry, k=k, src=src, base=base):
            n = 2 * a + i
            columns = []
            for p in range(NPD):
                rows = []
                for d in range(W):
                    keep = pat[((src * NOB + n) * NG + lax.div(o * NPD + p, ABS)) * W + d] > 0
                    x = tb[k][i, d, p]
                    x = jnp.where(keep, x, jnp.zeros_like(x))
                    rows.append(x)
                    rows.append(jnp.concatenate([x[:, 64:], x[:, :64]], axis=1))
                columns.append(jnp.concatenate(rows, axis=0))
            y = jnp.dot(w_ref[i], jnp.concatenate(columns, axis=1), preferred_element_type=F32)
            y = jnp.where(low, y[:96], y[96:]).astype(BF)
            for p in range(NPD):
                s[i, base + p] = y[:, 128 * p : 128 * p + 128]
            return carry

        lax.fori_loop(0, 2, one, 0)

    def regroup(j, carry):
        i = j // 5
        g = lax.rem(j, 5)
        tiles = s[i, pl.ds(16 * g, 16)]
        for e in range(W):
            x = jnp.concatenate(
                [tiles[:, 32 * e + 16 * h : 32 * e + 16 * h + 16].reshape(256, 128) for h in range(2)], axis=1
            )
            y = jnp.dot(perm[...], x, preferred_element_type=F32).astype(BF)
            for h in range(2):
                for q in range(16):
                    qq = 16 * h + q
                    out[qq // 2, i * W + e, pl.ds(pl.multiple_of(16 * g, 16), 16),
                        128 * (qq % 2) : 128 * (qq % 2) + 128] = y[16 * q : 16 * q + 16, 128 * h : 128 * h + 128]
        return carry

    lax.fori_loop(0, 10, regroup, 0)


def first_products(pos, pat, perm, w, tb):
    return pl.pallas_call(
        first_kernel,
        in_specs=[sspec(), sspec(), vspec(), vspec()] + [vspec()] * 8,
        out_specs=vspec(),
        out_shape=jax.ShapeDtypeStruct((16, 2 * W, 80, 256), BF),
        scratch_shapes=[pltpu.VMEM((2, 80, 96, 128), BF)],
        compiler_params=pltpu.CompilerParams(vmem_limit_bytes=VLIM),
        cost_estimate=pl.CostEstimate(flops=3 * 10**9, bytes_accessed=8 * 10**6, transcendentals=0),
        name="first",
    )(pos, pat, perm, w, *tb)


def chi_kernel(pos, first_ref, *rest):
    us, theirs, mine, rhs = rest[:8], rest[8], rest[9], rest[10]
    a = pos[0]
    core0 = lax.rem(a, 2) == 0
    for k in range(8):
        row = pl.multiple_of(src_of(a, k) * 160, 16)
        for kk in range(6):
            rhs[pl.ds(row, 160), 256 * kk : 256 * kk + 256] = us[k][kk]

    def tile(t, carry):
        lhs = jnp.concatenate([first_ref[:, kk].reshape(1280, 256) for kk in range(6)], axis=1)
        r = lax.dot_general(
            lhs,
            rhs[pl.ds(pl.multiple_of(256 * t, 256), 256)],
            (((1,), (1,)), ((), ())),
            preferred_element_type=F32,
        )
        cols = pl.ds(pl.multiple_of(256 * t, 256), 256)
        for b in range(16):
            lo, hi = r[80 * b : 80 * b + 40], r[80 * b + 40 : 80 * b + 80]
            mine[b, :, cols] = jnp.where(core0, lo, hi)
            theirs[b, :, cols] = jnp.where(core0, hi, lo)
        return carry

    lax.fori_loop(0, 5, tile, 0)


def chi_share(pos, first, us):
    return pl.pallas_call(
        chi_kernel,
        in_specs=[sspec(), vspec()] + [vspec()] * 8,
        out_specs=[vspec()] * 2,
        out_shape=[jax.ShapeDtypeStruct((16, 40, 1280), F32)] * 2,
        scratch_shapes=[pltpu.VMEM((1280, 1536), BF)],
        compiler_params=pltpu.CompilerParams(vmem_limit_bytes=VLIM),
        cost_estimate=pl.CostEstimate(flops=5 * 10**9, bytes_accessed=15 * 10**6, transcendentals=0),
        name="chi",
    )(pos, first, *us)


def own_masks(atom_size, n):
    partner = n + jnp.arange(W, dtype=jnp.int32) - R
    inside = (partner >= 0) & (partner < NOB)
    catalog = jnp.arange(NOB, dtype=jnp.int32)
    size_partner = jnp.sum(jnp.where(partner[:, None] == catalog, atom_size, 0), axis=1)
    size_owned = jnp.sum(jnp.where(n == catalog, atom_size, 0))
    funcs = jnp.arange(BS, dtype=jnp.int32)
    rows_ok = (funcs[None, :] < size_partner[:, None]) & inside[:, None]
    return inside, rows_ok[:, :, None] & (funcs < size_owned)[None, None, :]


def deinterleave():
    rows = np.zeros((2, 32, 64), np.float32)
    cols = np.zeros((2, 64, 64), np.float32)
    for g in range(2):
        for q in range(32):
            rows[g, q, 2 * q + g] = 1.0
        for j in range(2):
            for c in range(32):
                cols[g, 2 * c + (g ^ j), 32 * j + c] = 1.0
    return jnp.asarray(rows, BF), jnp.asarray(cols, BF)


def body(three_center, atom_size, tensor_pattern, green_occ, green_virt, green_pattern):
    a, o = lax.axis_index("aux"), lax.axis_index("orb")
    pos = jnp.stack([a, o]).astype(jnp.int32)
    perm = swap16()
    ta, *tb = spread(pos, perm, three_center.transpose(0, 2, 1, 3))
    ta = lax.all_to_all(ta, "orb", split_axis=0, concat_axis=0, tiled=True)
    tb = [tb[0]] + [lax.ppermute(tb[k], "aux", pairs_of(k)) for k in range(1, 8)]

    pat = jnp.pad(tensor_pattern.reshape(NG * W), (0, 2)).reshape(1, 32)
    pat = lax.all_gather(pat, ("aux", "orb"), axis=0, tiled=True)
    pat = pat[:, : NG * W].reshape(-1)
    inside, pair_ok = own_masks(atom_size, o)
    keep = ((green_pattern[0] > 0) | (jnp.arange(W) == R)) & inside
    mask = keep[:, None, None] & pair_ok
    occ = jnp.where(mask, green_occ.reshape(W, BS, BS), jnp.zeros((), BF))
    virt = jnp.where(mask, green_virt.reshape(W, BS, BS), jnp.zeros((), BF))
    rows, cols = deinterleave()
    occ = jnp.einsum("gql,flm->fgqm", rows, occ, preferred_element_type=F32).astype(BF)
    occ = jnp.einsum("fgqm,gmk->fgqk", occ, cols, preferred_element_type=F32).astype(BF)
    packed = jnp.concatenate([virt.reshape(192, 64), occ.reshape(192, 64)], axis=1)
    packed = lax.all_gather(packed[None], "orb", axis=0, tiled=True)
    k4, w = greens(pos, packed)

    us = second_products(pos, pat, perm, ta.reshape(160, W, NOB, 256), k4)
    first = first_products(pos, pat, perm, w, tb)
    first = lax.all_to_all(first, "orb", split_axis=0, concat_axis=0, tiled=True)
    us = [us[0]] + [lax.ppermute(us[k], "aux", pairs_of(k)) for k in range(1, 8)]

    theirs, mine = chi_share(pos, first, us)
    part = (mine + lax.ppermute(theirs, "aux", pairs_of(1))).astype(BF)
    part = lax.all_to_all(part, "orb", split_axis=0, concat_axis=0, tiled=True)
    part = jnp.sum(part.astype(F32), axis=0).reshape(4, NPD, 1280)
    x = a // 2
    total = lax.dynamic_index_in_dim(part, x, 0, keepdims=False)
    for dx in range(1, 4):
        piece = lax.dynamic_index_in_dim(part, lax.rem(x + dx, 4), 0, keepdims=False)
        total = total + lax.ppermute(piece, "aux", pairs_of(2 * dx))
    return total


def solution(mesh):
    return jax.shard_map(
        body,
        mesh=mesh,
        in_specs=(
            P(("aux", "orb"), None, None, None),
            P(),
            P("aux", "orb", None),
            P("orb", None, None),
            P("orb", None, None),
            P("orb", None),
        ),
        out_specs=P(("aux", "orb"), None),
        check_vma=False,
    )
```

time: 545 us -> 308 us (0.57); the launches traced: 537 us -> 307 us
  waiting for transfers between devices: 258 us -> 64.2 us
  local copies, waits for them, and re-layouts: 131 us -> 3.42 us
  blocking collectives: 52.1 us -> 134 us
  Pallas kernels: 0 us -> 53.3 us
  matrix products: 47.1 us -> 0.34 us
  starting transfers between devices: 23.4 us -> 44.1 us
  between operations: 13.9 us -> 0.38 us
    unnamed x2 -> x0, waiting for transfers between devices: 165 us -> none
    unnamed x0 -> x1, blocking collectives: none -> 109 us
    pallas_call x0 -> x5, Pallas kernels: none -> 53.3 us  [the longest x1 13.5 us: second_products(): pl.pallas_call(second_kernel, in_specs=[sspec(), sspec(), vspec(), vspec(...]
    all_to_all x1 -> x0, blocking collectives: 52.1 us -> none  [body(): lax.all_to_all(second, 'aux', split_axis=1, concat_axis=0, tiled=True)]
    dot_general x15 -> x1, matrix products: 47.1 us -> 0.34 us  [body(): jnp.einsum('fgqm,gmk->fgqk', occ, cols, preferred_element_type=F32)]
    another operation x16 -> x0, local copies, waits for them, and re-layouts: 32.2 us -> none
    all_gather x0 -> x1, blocking collectives: none -> 25.4 us  [body(): packed = lax.all_gather(packed[None], 'orb', axis=0, tiled=True)]
    slice x10 -> x0, local copies, waits for them, and re-layouts: 22.4 us -> none  [the longest x6 18.4 us: second_products(): padded_tensor[:, source:source + local_blocks, target - source + R]]
  transfers between devices with their start and end apart: 7 -> 21, of which waited for: 4 -> 10; matrix products, arithmetic and copies ran while one was open for 27% -> 1% of each run, Pallas kernels for 0% -> 10%
where the time goes in v1:
time: 308 us; the launch traced here: 307 us
  blocking collectives  134 us (44%)
  waiting for transfers between devices  64.2 us (21%)
  Pallas kernels  53.3 us (17%)
  starting transfers between devices  44.1 us (14%)
  other arithmetic  6.91 us (2%)
  local copies, waits for them, and re-layouts  3.42 us (1%)
    unnamed x1, blocking collectives  109 us
    all_to_all x1, waiting for transfers between devices, body(): part = lax.all_to_all(part, 'orb', split_axis=0, concat_axis=0, tiled=True)  25.6 us
    all_gather x1, blocking collectives, body(): packed = lax.all_gather(packed[None], 'orb', axis=0, tiled=True)  25.4 us
    ppermute x7, waiting for transfers between devices, body(): lax.ppermute(us[k], 'aux', pairs_of(k))  24.1 us
    pallas_call x1, Pallas kernels, second_products(): pl.pallas_call(second_kernel, in_specs=[sspec(), sspec(), vspec(), vspec(...  13.5 us
    pallas_call x1, Pallas kernels, first_products(): pl.pallas_call(first_kernel, in_specs=[sspec(), sspec(), vspec(), vspec()...  12.7 us
    pallas_call x1, Pallas kernels, chi_share(): pl.pallas_call(chi_kernel, in_specs=[sspec(), vspec()] + [vspec()] * 8, o...  12.2 us
    ppermute x7, starting transfers between devices, body(): lax.ppermute(us[k], 'aux', pairs_of(k))  10.9 us
  transfers between devices with their start and end apart: 21, of which 10 were waited for; matrix products, arithmetic and copies ran while one was open for 1% of the time, Pallas kernels for 10%

profile of v1, /device:TPU:0, one launch (start us, length us, event | category | flops | bytes accessed | tf_op | source)
XLA Modules:
  0.0 306.9 jit_solution(6167501373205441688)
XLA Ops:
  0.6 9.4 %spread.1 = (bf16[16,30,16,256]{3,2,1,0:T(8,128)(2,1)}, bf16[2,3,10,32,128]{4,3,2,1,0:T(8,128)(2,1)}, bf16[2,3,10,32,128]{4,3,2,1,0:T(8,128)(2,1)}, bf16[2,3,10,...) custom-call(s32[2]{0:T(128)} %pad_add_fusion.pos, ...), custom_call_target="tpu_custom_call" | custom-call | flops 1000000000 | bytes 12000000 | tf_op jit(solution)/shard_map/spread/pallas_call | solution.py:77
  10.1 8.3 %all-to-all-start.1 = ((bf16[16,30,16,256]{3,2,1,0:T(8,128)(2,1)}), bf16[16,30,16,256]{3,2,1,0:T(8,128)(2,1)}, u32[]{:S(2)}, u32[]{:S(2)}) async-start(bf16[16,30,16,256]{3,2,1,0:T(8,128)(2,1)} %get-tuple-element.35), calls=%async_computation.1 | async-start | bytes 7864320 | tf_op jit(solution)/shard_map/all_to_all | solution.py:328
  18.5 1.6 collective-permute-start.1
  20.1 1.3 collective-permute-start.2
  21.3 1.7 collective-permute-start.3
  23.0 1.5 collective-permute-start.4
  27.4 108.8 %all-reduce.1 = s32[4096]{0:T(1024)S(1)} all-reduce(s32[4096]{0:T(1024)S(1)} %pad_dynamic-update-slice_fusion), channel_id=2, replica_groups=mesh['aux'=8,'orb'=16] {'aux','orb'}, use_global_device_ids=true, to_apply=%add.1 | all-reduce | flops 4096 | bytes 32768
  138.5 25.4 %all-gather.1 = bf16[3072,128]{1,0:T(8,128)(2,1)} all-gather(bf16[192,128]{1,0:T(8,128)(2,1)S(1)} %pad_maximum_fusion), channel_id=3, replica_groups=mesh['aux'=8,'orb'=16] {'orb'}, dimensions={0}, use_global_device_ids=true | all-gather | bytes 835584 | tf_op jit(solution)/shard_map/all_gather | solution.py:343
  163.9 5.4 %greens.1 = (bf16[16,3,256,256]{3,2,1,0:T(8,128)(2,1)}, bf16[2,192,192]{2,1,0:T(8,128)(2,1)}) custom-call(s32[2]{0:T(128)} %pad_add_fusion.pos, bf16[16,192,128]{2,1,0:T(8,128)(2,1)} %bitcast.46), custom_call_target="tpu_custom_call" | custom-call | flops 1000000 | bytes 8000000 | tf_op jit(solution)/shard_map/greens/pallas_call | solution.py:135
  170.4 12.7 %first.1 = bf16[16,6,80,256]{3,2,1,0:T(8,128)(2,1)} custom-call(s32[2]{0:T(128)} %pad_add_fusion.pos, s32[3840]{0:T(1024)} %reshape.105.pat, bf16[256,256]{1,0:T(8,128)(2,1)} %constant.61.clone.perm, bf16[2,192,192]{2,1,0:T(8,128)(2,1)} %get-tuple-element.26.w_ref, bf16[2,3,10,32,128]{4,3,2,1,0:T(8,128)(2,1)} %get-tuple-element.27.rest_0_, ...), custom_call_target="tpu_custom_call" | custom-call | flops 3000000000 | bytes 8000000 | tf_op jit(solution)/shard_map/first/pallas_call | solution.py:248
  183.1 4.5 %all-to-all-start = ((bf16[16,6,80,256]{3,2,1,0:T(8,128)(2,1)}), bf16[16,6,80,256]{3,2,1,0:T(8,128)(2,1)}, u32[]{:S(2)}, u32[]{:S(2)}) async-start(bf16[16,6,80,256]{3,2,1,0:T(8,128)(2,1)} %first.1), calls=%async_computation | async-start | bytes 7864320 | tf_op jit(solution)/shard_map/all_to_all | solution.py:348
  187.6 13.5 %second.1 = (bf16[6,160,256]{2,1,0:T(8,128)(2,1)}, bf16[6,160,256]{2,1,0:T(8,128)(2,1)}, bf16[6,160,256]{2,1,0:T(8,128)(2,1)}, bf16[6,160,256]{2,1,0:T(8,128)(2,...) custom-call(s32[2]{0:T(128)} %pad_add_fusion.pos, ...), custom_call_target="tpu_custom_call" | custom-call | flops 4000000000 | bytes 15000000 | tf_op jit(solution)/shard_map/second/pallas_call | solution.py:187
  201.2 2.1 collective-permute-start.10
  203.3 1.6 collective-permute-start.12
  204.9 1.9 collective-permute-start.13
  206.8 9.6 %collective-permute-done.10.rest_4_ = bf16[6,160,256]{2,1,0:T(8,128)(2,1)S(1)} collective-permute-done((bf16[6,160,256]{2,1,0:T(8,128)(2,1)}, bf16[6,160,256]{2,1,0:T(8,128)(2,1)S(1)}, u32[]{:S(2)}, u32[]{:S(2)}) %collective-permute-start.10) | collective-permute-done | bytes 491552 | tf_op jit(solution)/shard_map/ppermute | solution.py:349
  216.4 1.8 collective-permute-start.8
  218.2 6.8 %collective-permute-done.11.rest_5_ = bf16[6,160,256]{2,1,0:T(8,128)(2,1)S(1)} collective-permute-done((bf16[6,160,256]{2,1,0:T(8,128)(2,1)}, bf16[6,160,256]{2,1,0:T(8,128)(2,1)S(1)}, u32[]{:S(2)}, u32[]{:S(2)}) %collective-permute-start.11) | collective-permute-done | bytes 491552 | tf_op jit(solution)/shard_map/ppermute | solution.py:349
  225.0 3.5 %collective-permute-start.9 = (bf16[6,160,256]{2,1,0:T(8,128)(2,1)}, bf16[6,160,256]{2,1,0:T(8,128)(2,1)S(1)}, u32[]{:S(2)}, u32[]{:S(2)}) collective-permute-start(bf16[6,160,256]{2,1,0:T(8,128)(2,1)} %get-tuple-element.40), channel_id=1, source_target_pairs={{0,48},{16,32},{32,80},{48,64},{64,112},{80,96},{96,16},{112,0},{1... | collective-permute-start | bytes 1474568 | tf_op jit(solution)/shard_map/ppermute | solution.py:349
  228.5 6.0 %all-to-all-done.first_ref = bf16[16,6,80,256]{3,2,1,0:T(8,128)(2,1)} async-done(((bf16[16,6,80,256]{3,2,1,0:T(8,128)(2,1)}), bf16[16,6,80,256]{3,2,1,0:T(8,128)(2,1)}, u32[]{:S(2)}, u32[]{:S(2)}) %all-to-all-start) | async-done | bytes 3932192 | tf_op jit(solution)/shard_map/all_to_all | solution.py:348
  235.2 6.0 %collective-permute-done.13.rest_7_ = bf16[6,160,256]{2,1,0:T(8,128)(2,1)S(1)} collective-permute-done((bf16[6,160,256]{2,1,0:T(8,128)(2,1)}, bf16[6,160,256]{2,1,0:T(8,128)(2,1)S(1)}, u32[]{:S(2)}, u32[]{:S(2)}) %collective-permute-start.13) | collective-permute-done | bytes 491552 | tf_op jit(solution)/shard_map/ppermute | solution.py:349
  241.2 1.1 collective-permute-done.9.rest_3_
  243.1 12.2 %chi.1 = (f32[16,40,1280]{2,1,0:T(8,128)}, f32[16,40,1280]{2,1,0:T(8,128)}) custom-call(s32[2]{0:T(128)} %pad_add_fusion.pos, bf16[16,6,80,256]{3,2,1,0:T(8,128)(2,1)} %all-to-all-done.first_ref, bf16[6,160,256]{2,1,0:T(8,128)(2,1)} %get-tuple-element.37.rest_0_, bf16[6,160,256]{2,1,0:T(8,128)(2,1)} %copy-done.14, bf16[6,160,256]{2,1,0:T(8,128)(2,1)} %copy-done.16, ...), custom_call_target="tpu_custom_call" | custom-call | flops 5000000000 | bytes 15000000 | tf_op jit(solution)/shard_map/chi/pallas_call | solution.py:288
  255.3 1.3 collective-permute-start.14
  256.6 5.7 %collective-permute-done.14 = f32[16,40,1280]{2,1,0:T(8,128)S(1)} collective-permute-done((f32[16,40,1280]{2,1,0:T(8,128)}, f32[16,40,1280]{2,1,0:T(8,128)S(1)}, u32[]{:S(2)}, u32[]{:S(2)}) %collective-permute-start.14) | collective-permute-done | bytes 3276832 | tf_op jit(solution)/shard_map/ppermute | solution.py:352
  262.3 3.5 %add_convert_fusion = bf16[16,40,1280]{2,1,0:T(8,128)(2,1)} fusion(f32[16,40,1280]{2,1,0:T(8,128)} %get-tuple-element.45, f32[16,40,1280]{2,1,0:T(8,128)S(1)} %collective-permute-done.14), kind=kLoop, calls=%fused_computation.1 | loop fusion | flops 1638400 | bytes 8192000 | tf_op jit(solution)/shard_map/convert_element_type | solution.py:352
  265.8 6.8 %all-to-all-start.2 = ((bf16[16,40,1280]{2,1,0:T(8,128)(2,1)}), bf16[16,40,1280]{2,1,0:T(8,128)(2,1)S(1)}, u32[]{:S(2)}, u32[]{:S(2)}) async-start(bf16[16,40,1280]{2,1,0:T(8,128)(2,1)} %add_convert_fusion), calls=%async_computation.2 | async-start | bytes 3276800 | tf_op jit(solution)/shard_map/all_to_all | solution.py:353
  272.7 25.6 %all-to-all-done.2 = bf16[16,40,1280]{2,1,0:T(8,128)(2,1)S(1)} async-done(((bf16[16,40,1280]{2,1,0:T(8,128)(2,1)}), bf16[16,40,1280]{2,1,0:T(8,128)(2,1)S(1)}, u32[]{:S(2)}, u32[]{:S(2)}) %all-to-all-start.2) | async-done | bytes 1638432 | tf_op jit(solution)/shard_map/all_to_all | solution.py:353
  298.6 1.7 collective-permute-start.15
  300.3 1.5 collective-permute-start.16
  301.8 1.7 collective-permute-start.17
  304.3 1.9 collective-permute-done.16
  (88 shorter events, 10.0 us)
Async XLA Ops:
  10.0 15.5 %copy-start = (bf16[1,3,4096]{2,1,0:T(4,128)(2,1)S(1)}, bf16[1,3,4096]{2,1,0:T(4,128)(2,1)}, u32[]{:S(2)}) copy-start(bf16[1,3,4096]{2,1,0:T(4,128)(2,1)} %param.12) | copy-start | bytes 73732
  10.0 16.4 %copy-start.20 = (bf16[2,64,64,1]{2,1,3,0:T(8,128)(2,1)S(1)}, bf16[2,64,64,1]{2,1,3,0:T(8,128)(2,1)}, u32[]{:S(2)}) copy-start(bf16[2,64,64,1]{2,1,3,0:T(8,128)(2,1)} %constant.76) | copy-start | bytes 49156
  10.0 16.4 %copy-start.21 = (bf16[2,32,64,1]{2,1,3,0:T(8,128)(2,1)S(1)}, bf16[2,32,64,1]{2,1,3,0:T(8,128)(2,1)}, u32[]{:S(2)}) copy-start(bf16[2,32,64,1]{2,1,3,0:T(8,128)(2,1)} %constant.75) | copy-start | bytes 24580
  10.0 16.9 %copy-start.1 = (bf16[1,3,4096]{2,1,0:T(4,128)(2,1)S(1)}, bf16[1,3,4096]{2,1,0:T(4,128)(2,1)}, u32[]{:S(2)}) copy-start(bf16[1,3,4096]{2,1,0:T(4,128)(2,1)} %param.13) | copy-start | bytes 73732
  10.0 17.0 %copy-start.2 = (s32[10,1,3]{0,1,2:T(1,128)S(1)}, s32[10,1,3]{0,1,2:T(1,128)}, u32[]{:S(2)}) copy-start(s32[10,1,3]{0,1,2:T(1,128)} %param.11) | copy-start | bytes 364
  10.1 127.0 %copy-start.5 = (bf16[2,3,10,32,128]{4,3,2,1,0:T(8,128)(2,1)S(1)}, bf16[2,3,10,32,128]{4,3,2,1,0:T(8,128)(2,1)}, u32[]{:S(2)}) copy-start(bf16[2,3,10,32,128]{4,3,2,1,0:T(8,128)(2,1)} %get-tuple-element.33) | copy-start | bytes 1474564
  10.1 127.7 %copy-start.4 = (bf16[2,3,10,32,128]{4,3,2,1,0:T(8,128)(2,1)S(1)}, bf16[2,3,10,32,128]{4,3,2,1,0:T(8,128)(2,1)}, u32[]{:S(2)}) copy-start(bf16[2,3,10,32,128]{4,3,2,1,0:T(8,128)(2,1)} %get-tuple-element.34) | copy-start | bytes 1474564
  10.1 173.0 %all-to-all-start.1 = ((bf16[16,30,16,256]{3,2,1,0:T(8,128)(2,1)}), bf16[16,30,16,256]{3,2,1,0:T(8,128)(2,1)}, u32[]{:S(2)}, u32[]{:S(2)}) async-start(bf16[16,30,16,256]{3,2,1,0:T(8,128)(2,1)} %get-tuple-element.35), calls=%async_computation.1 | async-start | bytes 7864320 | tf_op jit(solution)/shard_map/all_to_all | solution.py:328
  18.4 118.7 %collective-permute-start = (bf16[2,3,10,32,128]{4,3,2,1,0:T(8,128)(2,1)}, bf16[2,3,10,32,128]{4,3,2,1,0:T(8,128)(2,1)S(1)}, u32[]{:S(2)}, u32[]{:S(2)}) collective-permute-start(bf16[2,3,10,32,128]{4,3,2,1,0:T(8,128)(2,1)} %get-tuple-element.28), channel_id=1, source_target_pairs={{0,16},{16,0},{32,48},{48,32},{64,80},{80,64},{96,112},{112,96},{1... | collective-permute-start | bytes 1474568 | tf_op jit(solution)/shard_map/ppermute | solution.py:329
  18.5 119.2 %collective-permute-start.1 = (bf16[2,3,10,32,128]{4,3,2,1,0:T(8,128)(2,1)}, bf16[2,3,10,32,128]{4,3,2,1,0:T(8,128)(2,1)S(1)}, u32[]{:S(2)}, u32[]{:S(2)}) collective-permute-start(bf16[2,3,10,32,128]{4,3,2,1,0:T(8,128)(2,1)} %get-tuple-element.29), channel_id=1, source_target_pairs={{0,32},{16,48},{32,64},{48,80},{64,96},{80,112},{96,0},{112,16},{1... | collective-permute-start | bytes 1474568 | tf_op jit(solution)/shard_map/ppermute | solution.py:329
  20.1 149.3 %collective-permute-start.2 = (bf16[2,3,10,32,128]{4,3,2,1,0:T(8,128)(2,1)}, bf16[2,3,10,32,128]{4,3,2,1,0:T(8,128)(2,1)}, u32[]{:S(2)}, u32[]{:S(2)}) collective-permute-start(bf16[2,3,10,32,128]{4,3,2,1,0:T(8,128)(2,1)} %get-tuple-element.30), channel_id=1, source_target_pairs={{0,48},{16,32},{32,80},{48,64},{64,112},{80,96},{96,16},{112,0},{1... | collective-permute-start | bytes 1474568 | tf_op jit(solution)/shard_map/ppermute | solution.py:329
  21.3 148.1 %collective-permute-start.3 = (bf16[2,3,10,32,128]{4,3,2,1,0:T(8,128)(2,1)S(1)}, bf16[2,3,10,32,128]{4,3,2,1,0:T(8,128)(2,1)}, u32[]{:S(2)}, u32[]{:S(2)}) collective-permute-start(bf16[2,3,10,32,128]{4,3,2,1,0:T(8,128)(2,1)S(1)} %copy-done.9), channel_id=1, source_target_pairs={{0,64},{16,80},{32,96},{48,112},{64,0},{80,16},{96,32},{112,48},{1... | collective-permute-start | bytes 1474568 | tf_op jit(solution)/shard_map/ppermute | solution.py:329
  23.0 146.4 %collective-permute-start.4 = (bf16[2,3,10,32,128]{4,3,2,1,0:T(8,128)(2,1)S(1)}, bf16[2,3,10,32,128]{4,3,2,1,0:T(8,128)(2,1)}, u32[]{:S(2)}, u32[]{:S(2)}) collective-permute-start(bf16[2,3,10,32,128]{4,3,2,1,0:T(8,128)(2,1)S(1)} %copy-done.7), channel_id=1, source_target_pairs={{0,80},{16,64},{32,112},{48,96},{64,16},{80,0},{96,48},{112,32},{1... | collective-permute-start | bytes 1474568 | tf_op jit(solution)/shard_map/ppermute | solution.py:329
  137.1 32.4 %copy-start.6 = (bf16[2,3,10,32,128]{4,3,2,1,0:T(8,128)(2,1)}, bf16[2,3,10,32,128]{4,3,2,1,0:T(8,128)(2,1)S(1)}, u32[]{:S(2)}) copy-start(bf16[2,3,10,32,128]{4,3,2,1,0:T(8,128)(2,1)S(1)} %collective-permute-done.rest_1_) | copy-start | bytes 1474564
  137.1 32.3 %collective-permute-start.5 = (bf16[2,3,10,32,128]{4,3,2,1,0:T(8,128)(2,1)S(1)}, bf16[2,3,10,32,128]{4,3,2,1,0:T(8,128)(2,1)S(1)}, u32[]{:S(2)}, u32[]{:S(2)}) collective-permute-start(bf16[2,3,10,32,128]{4,3,2,1,0:T(8,128)(2,1)S(1)} %copy-done.5), channel_id=1, source_target_pairs={{0,96},{16,112},{32,0},{48,16},{64,32},{80,48},{96,64},{112,80},{1... | collective-permute-start | bytes 1474568 | tf_op jit(solution)/shard_map/ppermute | solution.py:329
  137.7 31.7 %copy-start.8 = (bf16[2,3,10,32,128]{4,3,2,1,0:T(8,128)(2,1)}, bf16[2,3,10,32,128]{4,3,2,1,0:T(8,128)(2,1)S(1)}, u32[]{:S(2)}) copy-start(bf16[2,3,10,32,128]{4,3,2,1,0:T(8,128)(2,1)S(1)} %collective-permute-done.1.rest_2_) | copy-start | bytes 1474564
  137.7 31.7 %collective-permute-start.6 = (bf16[2,3,10,32,128]{4,3,2,1,0:T(8,128)(2,1)S(1)}, bf16[2,3,10,32,128]{4,3,2,1,0:T(8,128)(2,1)S(1)}, u32[]{:S(2)}, u32[]{:S(2)}) collective-permute-start(bf16[2,3,10,32,128]{4,3,2,1,0:T(8,128)(2,1)S(1)} %copy-done.4), channel_id=1, source_target_pairs={{0,112},{16,96},{32,16},{48,0},{64,48},{80,32},{96,80},{112,64},{1... | collective-permute-start | bytes 1474568 | tf_op jit(solution)/shard_map/ppermute | solution.py:329
  183.1 51.4 %all-to-all-start = ((bf16[16,6,80,256]{3,2,1,0:T(8,128)(2,1)}), bf16[16,6,80,256]{3,2,1,0:T(8,128)(2,1)}, u32[]{:S(2)}, u32[]{:S(2)}) async-start(bf16[16,6,80,256]{3,2,1,0:T(8,128)(2,1)} %first.1), calls=%async_computation | async-start | bytes 7864320 | tf_op jit(solution)/shard_map/all_to_all | solution.py:348
  201.2 15.2 %collective-permute-start.10 = (bf16[6,160,256]{2,1,0:T(8,128)(2,1)}, bf16[6,160,256]{2,1,0:T(8,128)(2,1)S(1)}, u32[]{:S(2)}, u32[]{:S(2)}) collective-permute-start(bf16[6,160,256]{2,1,0:T(8,128)(2,1)} %get-tuple-element.41), channel_id=1, source_target_pairs={{0,64},{16,80},{32,96},{48,112},{64,0},{80,16},{96,32},{112,48},{1... | collective-permute-start | bytes 1474568 | tf_op jit(solution)/shard_map/ppermute | solution.py:349
  203.3 21.7 %collective-permute-start.11 = (bf16[6,160,256]{2,1,0:T(8,128)(2,1)}, bf16[6,160,256]{2,1,0:T(8,128)(2,1)S(1)}, u32[]{:S(2)}, u32[]{:S(2)}) collective-permute-start(bf16[6,160,256]{2,1,0:T(8,128)(2,1)} %get-tuple-element.42), channel_id=1, source_target_pairs={{0,80},{16,64},{32,112},{48,96},{64,16},{80,0},{96,48},{112,32},{1... | collective-permute-start | bytes 1474568 | tf_op jit(solution)/shard_map/ppermute | solution.py:349
  203.3 31.9 %collective-permute-start.12 = (bf16[6,160,256]{2,1,0:T(8,128)(2,1)}, bf16[6,160,256]{2,1,0:T(8,128)(2,1)S(1)}, u32[]{:S(2)}, u32[]{:S(2)}) collective-permute-start(bf16[6,160,256]{2,1,0:T(8,128)(2,1)} %get-tuple-element.43), channel_id=1, source_target_pairs={{0,96},{16,112},{32,0},{48,16},{64,32},{80,48},{96,64},{112,80},{1... | collective-permute-start | bytes 1474568 | tf_op jit(solution)/shard_map/ppermute | solution.py:349
  204.9 36.3 %collective-permute-start.13 = (bf16[6,160,256]{2,1,0:T(8,128)(2,1)}, bf16[6,160,256]{2,1,0:T(8,128)(2,1)S(1)}, u32[]{:S(2)}, u32[]{:S(2)}) collective-permute-start(bf16[6,160,256]{2,1,0:T(8,128)(2,1)} %get-tuple-element.44), channel_id=1, source_target_pairs={{0,112},{16,96},{32,16},{48,0},{64,48},{80,32},{96,80},{112,64},{1... | collective-permute-start | bytes 1474568 | tf_op jit(solution)/shard_map/ppermute | solution.py:349
  206.8 34.4 %collective-permute-start.7 = (bf16[6,160,256]{2,1,0:T(8,128)(2,1)}, bf16[6,160,256]{2,1,0:T(8,128)(2,1)S(1)}, u32[]{:S(2)}, u32[]{:S(2)}) collective-permute-start(bf16[6,160,256]{2,1,0:T(8,128)(2,1)} %get-tuple-element.38), channel_id=1, source_target_pairs={{0,16},{16,0},{32,48},{48,32},{64,80},{80,64},{96,112},{112,96},{1... | collective-permute-start | bytes 1474568 | tf_op jit(solution)/shard_map/ppermute | solution.py:349
  216.4 25.9 %copy-start.10 = (bf16[6,160,256]{2,1,0:T(8,128)(2,1)}, bf16[6,160,256]{2,1,0:T(8,128)(2,1)S(1)}, u32[]{:S(2)}) copy-start(bf16[6,160,256]{2,1,0:T(8,128)(2,1)S(1)} %collective-permute-done.10.rest_4_) | copy-start | bytes 1474564
  216.4 24.8 %collective-permute-start.8 = (bf16[6,160,256]{2,1,0:T(8,128)(2,1)}, bf16[6,160,256]{2,1,0:T(8,128)(2,1)S(1)}, u32[]{:S(2)}, u32[]{:S(2)}) collective-permute-start(bf16[6,160,256]{2,1,0:T(8,128)(2,1)} %get-tuple-element.39), channel_id=1, source_target_pairs={{0,32},{16,48},{32,64},{48,80},{64,96},{80,112},{96,0},{112,16},{1... | collective-permute-start | bytes 1474568 | tf_op jit(solution)/shard_map/ppermute | solution.py:349
  225.0 17.3 %copy-start.11 = (bf16[6,160,256]{2,1,0:T(8,128)(2,1)}, bf16[6,160,256]{2,1,0:T(8,128)(2,1)S(1)}, u32[]{:S(2)}) copy-start(bf16[6,160,256]{2,1,0:T(8,128)(2,1)S(1)} %collective-permute-done.11.rest_5_) | copy-start | bytes 1474564
  225.0 17.3 %collective-permute-start.9 = (bf16[6,160,256]{2,1,0:T(8,128)(2,1)}, bf16[6,160,256]{2,1,0:T(8,128)(2,1)S(1)}, u32[]{:S(2)}, u32[]{:S(2)}) collective-permute-start(bf16[6,160,256]{2,1,0:T(8,128)(2,1)} %get-tuple-element.40), channel_id=1, source_target_pairs={{0,48},{16,32},{32,80},{48,64},{64,112},{80,96},{96,16},{112,0},{1... | collective-permute-start | bytes 1474568 | tf_op jit(solution)/shard_map/ppermute | solution.py:349
  255.3 7.0 %collective-permute-start.14 = (f32[16,40,1280]{2,1,0:T(8,128)}, f32[16,40,1280]{2,1,0:T(8,128)S(1)}, u32[]{:S(2)}, u32[]{:S(2)}) collective-permute-start(f32[16,40,1280]{2,1,0:T(8,128)} %get-tuple-element.46), channel_id=1, source_target_pairs={{0,16},{16,0},{32,48},{48,32},{64,80},{80,64},{96,112},{112,96},{1... | collective-permute-start | bytes 9830408 | tf_op jit(solution)/shard_map/ppermute | solution.py:352
  265.8 32.5 %all-to-all-start.2 = ((bf16[16,40,1280]{2,1,0:T(8,128)(2,1)}), bf16[16,40,1280]{2,1,0:T(8,128)(2,1)S(1)}, u32[]{:S(2)}, u32[]{:S(2)}) async-start(bf16[16,40,1280]{2,1,0:T(8,128)(2,1)} %add_convert_fusion), calls=%async_computation.2 | async-start | bytes 3276800 | tf_op jit(solution)/shard_map/all_to_all | solution.py:353
  298.6 5.7 %collective-permute-start.15 = (f32[10,1280]{1,0:T(8,128)S(1)}, f32[10,1280]{1,0:T(8,128)S(1)}, u32[]{:S(2)}, u32[]{:S(2)}) collective-permute-start(f32[10,1280]{1,0:T(8,128)S(1)} %get-tuple-element.47), channel_id=1, source_target_pairs={{0,32},{16,48},{32,64},{48,80},{64,96},{80,112},{96,0},{112,16},{1... | collective-permute-start | bytes 153608 | tf_op jit(solution)/shard_map/ppermute | solution.py:359
  300.3 5.9 %collective-permute-start.16 = (f32[10,1280]{1,0:T(8,128)S(1)}, f32[10,1280]{1,0:T(8,128)S(1)}, u32[]{:S(2)}, u32[]{:S(2)}) collective-permute-start(f32[10,1280]{1,0:T(8,128)S(1)} %get-tuple-element.49), channel_id=1, source_target_pairs={{0,64},{16,80},{32,96},{48,112},{64,0},{80,16},{96,32},{112,48},{1... | collective-permute-start | bytes 153608 | tf_op jit(solution)/shard_map/ppermute | solution.py:359
  301.8 4.4 %collective-permute-start.17 = (f32[10,1280]{1,0:T(8,128)S(1)}, f32[10,1280]{1,0:T(8,128)S(1)}, u32[]{:S(2)}, u32[]{:S(2)}) collective-permute-start(f32[10,1280]{1,0:T(8,128)S(1)} %get-tuple-element.48), channel_id=1, source_target_pairs={{0,96},{16,112},{32,0},{48,16},{64,32},{80,48},{96,64},{112,80},{1... | collective-permute-start | bytes 153608 | tf_op jit(solution)/shard_map/ppermute | solution.py:359
  (11 other events, 66.7 us)

commit v2 on v1

--- a/solution.py
+++ b/solution.py
@@ -32,6 +32,10 @@
     return lax.rem(a // 2 + dx, 4) * 2 + (lax.rem(a, 2) if dc == 0 else 1 - lax.rem(a, 2))
 
 
+def pat_row(o, k, n):
+    return k * NOB + lax.rem(o // 4 + 4 - n // 4, 4) * 4 + lax.rem(lax.rem(o, 4) + 4 - lax.rem(n, 4), 4)
+
+
 def src_of(a, k):
     dx, dc = STEPS[k]
     return lax.rem(a // 2 + 4 - dx, 4) * 2 + (lax.rem(a, 2) if dc == 0 else 1 - lax.rem(a, 2))
@@ -52,13 +56,30 @@
     return pl.BlockSpec(memory_space=pltpu.SMEM)
 
 
-def spread_kernel(pos, perm, x_ref, ta_ref, *rest):
+def rows_kernel(x_ref, ta_ref):
+    for d in range(W):
+        for o in range(16):
+            ta_ref[o, d] = x_ref[0, d, :, 256 * o : 256 * o + 256]
+
+
+def row_slabs(x):
+    return pl.pallas_call(
+        rows_kernel,
+        grid=(NPD,),
+        in_specs=[pl.BlockSpec((1, W, NOB, 4096), lambda i: (i, 0, 0, 0))],
+        out_specs=pl.BlockSpec((16, W, NOB, 256), lambda i: (0, i, 0, 0)),
+        out_shape=jax.ShapeDtypeStruct((16, NPD * W, NOB, 256), BF),
+        compiler_params=pltpu.CompilerParams(vmem_limit_bytes=VLIM),
+        cost_estimate=pl.CostEstimate(flops=0, bytes_accessed=8 * 10**6, transcendentals=0),
+        name="row_slabs",
+    )(x)
+
+
+def pairs_kernel(pos, perm, x_ref, *rest):
     tb, s = rest[:8], rest[8]
     a = pos[0]
     for d in range(W):
         x = x_ref[0, d]
-        for o in range(16):
-            ta_ref[o, d] = x[:, 256 * o : 256 * o + 256]
         halves = [
             jnp.concatenate([x[:, 128 * (16 * h + c) : 128 * (16 * h + c) + 128] for c in range(16)], axis=0)
             for h in range(2)
@@ -73,30 +94,66 @@
             tb[k][i, :, 0] = s[2 * t + i]
 
 
-def spread(pos, perm, x):
-    return pl.pallas_call(
-        spread_kernel,
+def block_pairs(pos, perm, x):
+    return pl.pallas_call(
+        pairs_kernel,
         grid=(NPD,),
         in_specs=[
             sspec(),
             pl.BlockSpec((256, 256), lambda i: (0, 0)),
             pl.BlockSpec((1, W, NOB, 4096), lambda i: (i, 0, 0, 0)),
         ],
-        out_specs=[pl.BlockSpec((16, W, NOB, 256), lambda i: (0, i, 0, 0))]
-        + [pl.BlockSpec((2, W, 1, 32, 128), lambda i: (0, 0, i, 0, 0))] * 8,
-        out_shape=[jax.ShapeDtypeStruct((16, NPD * W, NOB, 256), BF)]
-        + [jax.ShapeDtypeStruct((2, W, NPD, 32, 128), BF)] * 8,
+        out_specs=[pl.BlockSpec((2, W, 1, 32, 128), lambda i: (0, 0, i, 0, 0))] * 8,
+        out_shape=[jax.ShapeDtypeStruct((2, W, NPD, 32, 128), BF)] * 8,
         scratch_shapes=[pltpu.VMEM((NOB, W, 32, 128), BF)],
         compiler_params=pltpu.CompilerParams(vmem_limit_bytes=VLIM),
-        cost_estimate=pl.CostEstimate(flops=10**9, bytes_accessed=12 * 10**6, transcendentals=0),
-        name="spread",
+        cost_estimate=pl.CostEstimate(flops=10**9, bytes_accessed=8 * 10**6, transcendentals=0),
+        name="block_pairs",
     )(pos, perm, x)
 
 
-def greens_kernel(pos, g_ref, k4_ref, w_ref):
-    a = pos[0]
+def prep_kernel(pos, size, gpat, occ_ref, virt_ref, rows_ref, cols_ref, tpat_ref, out):
+    n = pos[1]
+    row = lax.broadcasted_iota(jnp.int32, (BS, BS), 0)
+    col = lax.broadcasted_iota(jnp.int32, (BS, BS), 1)
+    zero = jnp.zeros((BS, BS), BF)
+    for d in range(W):
+        m = n + d - R
+        ok = (m >= 0) & (m < NOB)
+        if d != R:
+            ok = ok & (gpat[d] > 0)
+        rows_in = jnp.where(ok, size[jnp.clip(m, 0, NOB - 1)], 0)
+        mask = (row < rows_in) & (col < size[n])
+        virt = jnp.where(mask, virt_ref[d], zero)
+        occ = jnp.where(mask, occ_ref[d], zero)
+        parts = []
+        for g in range(2):
+            t = jnp.dot(rows_ref[g], occ, preferred_element_type=F32).astype(BF)
+            parts.append(jnp.dot(t, cols_ref[g], preferred_element_type=F32).astype(BF))
+        out[64 * d : 64 * d + 64] = jnp.concatenate([virt, jnp.concatenate(parts, axis=0)], axis=1)
+    out[192:208] = jnp.broadcast_to(tpat_ref[...].astype(F32), (16, 128)).astype(BF)
+
+
+def prep(pos, size, gpat, occ, virt, rows, cols, tpat):
+    return pl.pallas_call(
+        prep_kernel,
+        in_specs=[sspec()] * 3 + [vspec()] * 5,
+        out_specs=vspec(),
+        out_shape=jax.ShapeDtypeStruct((208, 128), BF),
+        cost_estimate=pl.CostEstimate(flops=10**6, bytes_accessed=10**5, transcendentals=0),
+        name="prep",
+    )(pos, size, gpat, occ, virt, rows, cols, tpat)
+
+
+def greens_kernel(pos, *rest):
+    g4, k4_ref, w_ref, g_ref = rest[:4], rest[4], rest[5], rest[6]
+    a, o = pos[0], pos[1]
     lane = lax.broadcasted_iota(jnp.int32, (64, 128), 1)
     zero = jnp.zeros((64, 128), BF)
+    for dy in range(4):
+        for dz in range(4):
+            n = lax.rem(o // 4 + 4 - dy, 4) * 4 + lax.rem(lax.rem(o, 4) + 4 - dz, 4)
+            g_ref[n] = g4[dy][dz, 0:192]
 
     def one(n, carry):
         for d in range(W):
@@ -131,11 +188,12 @@
                 w_ref[i, row : row + 32, :] = jnp.concatenate(cols, axis=1)
 
 
-def greens(pos, g):
+def greens(pos, g4):
     return pl.pallas_call(
         greens_kernel,
-        in_specs=[sspec(), vspec()],
+        in_specs=[sspec()] + [vspec()] * 4,
         out_specs=[vspec(), vspec()],
+        scratch_shapes=[pltpu.VMEM((NOB, 192, 128), BF)],
         out_shape=[
             jax.ShapeDtypeStruct((NOB, W, 256, 256), BF),
             jax.ShapeDtypeStruct((2, 192, 192), BF),
@@ -143,12 +201,12 @@
         compiler_params=pltpu.CompilerParams(vmem_limit_bytes=VLIM),
         cost_estimate=pl.CostEstimate(flops=10**6, bytes_accessed=8 * 10**6, transcendentals=0),
         name="greens",
-    )(pos, g)
+    )(pos, *g4)
 
 
 def second_kernel(pos, pat, perm, ta_ref, k4_ref, *rest):
     outs, s = rest[:8], rest[8]
-    a = pos[0]
+    a, o = pos[0], pos[1]
     s[0] = jnp.zeros(s.shape[1:], BF)
     s[NOB + 1] = jnp.zeros(s.shape[1:], BF)
 
@@ -157,7 +215,7 @@
             x = ta_ref[pl.ds(16 * g, 16), d].reshape(256, 256)
             y = jnp.dot(perm[...], x, preferred_element_type=F32)
             for n in range(NOB):
-                keep = pat[((a * NOB + n) * NG + g) * W + d] > 0
+                keep = pat[pat_row(o, 0, n) * 32 + g * W + d] > 0
                 part = y[16 * n : 16 * n + 16]
                 s[n + 1, d, pl.ds(pl.multiple_of(16 * g, 16), 16)] = jnp.where(
                     keep, part, jnp.zeros_like(part)
@@ -171,13 +229,10 @@
         def one(i, carry, k=k, t=t):
             n = 2 * t + i
             for e in range(W):
-                acc = None
-                for d in range(W):
-                    f = e - d + 1
-                    if 0 <= f < W:
-                        p = jnp.dot(s[n + d, f], k4_ref[n, d], preferred_element_type=F32)
-                        acc = p if acc is None else acc + p
-                outs[k][i * W + e] = acc.astype(BF)
+                ds = [d for d in range(W) if 0 <= e - d + 1 < W]
+                lhs = jnp.concatenate([s[n + d, e - d + 1] for d in ds], axis=1)
+                rhs = k4_ref[n, ds[0] : ds[-1] + 1].reshape(256 * len(ds), 256)
+                outs[k][i * W + e] = jnp.dot(lhs, rhs, preferred_element_type=F32).astype(BF)
             return carry
 
         lax.fori_loop(0, 2, one, 0)
@@ -211,7 +266,7 @@
             for p in range(NPD):
                 rows = []
                 for d in range(W):
-                    keep = pat[((src * NOB + n) * NG + lax.div(o * NPD + p, ABS)) * W + d] > 0
+                    keep = pat[pat_row(o, k, n) * 32 + lax.div(o * NPD + p, ABS) * W + d] > 0
                     x = tb[k][i, d, p]
                     x = jnp.where(keep, x, jnp.zeros_like(x))
                     rows.append(x)
@@ -261,51 +316,41 @@
     us, theirs, mine, rhs = rest[:8], rest[8], rest[9], rest[10]
     a = pos[0]
     core0 = lax.rem(a, 2) == 0
-    for k in range(8):
-        row = pl.multiple_of(src_of(a, k) * 160, 16)
-        for kk in range(6):
-            rhs[pl.ds(row, 160), 256 * kk : 256 * kk + 256] = us[k][kk]
-
-    def tile(t, carry):
-        lhs = jnp.concatenate([first_ref[:, kk].reshape(1280, 256) for kk in range(6)], axis=1)
-        r = lax.dot_general(
-            lhs,
-            rhs[pl.ds(pl.multiple_of(256 * t, 256), 256)],
-            (((1,), (1,)), ((), ())),
-            preferred_element_type=F32,
-        )
-        cols = pl.ds(pl.multiple_of(256 * t, 256), 256)
-        for b in range(16):
-            lo, hi = r[80 * b : 80 * b + 40], r[80 * b + 40 : 80 * b + 80]
-            mine[b, :, cols] = jnp.where(core0, lo, hi)
-            theirs[b, :, cols] = jnp.where(core0, hi, lo)
-        return carry
-
-    lax.fori_loop(0, 5, tile, 0)
+    t = pl.program_id(0)
+
+    @pl.when(t == 0)
+    def _():
+        for k in range(8):
+            row = pl.multiple_of(src_of(a, k) * 160, 16)
+            for kk in range(6):
+                rhs[pl.ds(row, 160), 256 * kk : 256 * kk + 256] = us[k][kk]
+
+
+    lhs = jnp.concatenate([first_ref[:, kk].reshape(1280, 256) for kk in range(6)], axis=1)
+    r = lax.dot_general(
+        lhs,
+        rhs[pl.ds(pl.multiple_of(256 * t, 256), 256)],
+        (((1,), (1,)), ((), ())),
+        preferred_element_type=F32,
+    )
+    for b in range(16):
+        lo, hi = r[80 * b : 80 * b + 40], r[80 * b + 40 : 80 * b + 80]
+        mine[b] = jnp.where(core0, lo, hi)
+        theirs[b] = jnp.where(core0, hi, lo)
 
 
 def chi_share(pos, first, us):
     return pl.pallas_call(
         chi_kernel,
+        grid=(5,),
         in_specs=[sspec(), vspec()] + [vspec()] * 8,
-        out_specs=[vspec()] * 2,
+        out_specs=[pl.BlockSpec((16, 40, 256), lambda t: (0, 0, t))] * 2,
         out_shape=[jax.ShapeDtypeStruct((16, 40, 1280), F32)] * 2,
         scratch_shapes=[pltpu.VMEM((1280, 1536), BF)],
         compiler_params=pltpu.CompilerParams(vmem_limit_bytes=VLIM),
         cost_estimate=pl.CostEstimate(flops=5 * 10**9, bytes_accessed=15 * 10**6, transcendentals=0),
         name="chi",
     )(pos, first, *us)
-
-
-def own_masks(atom_size, n):
-    partner = n + jnp.arange(W, dtype=jnp.int32) - R
-    inside = (partner >= 0) & (partner < NOB)
-    catalog = jnp.arange(NOB, dtype=jnp.int32)
-    size_partner = jnp.sum(jnp.where(partner[:, None] == catalog, atom_size, 0), axis=1)
-    size_owned = jnp.sum(jnp.where(n == catalog, atom_size, 0))
-    funcs = jnp.arange(BS, dtype=jnp.int32)
-    rows_ok = (funcs[None, :] < size_partner[:, None]) & inside[:, None]
-    return inside, rows_ok[:, :, None] & (funcs < size_owned)[None, None, :]
 
 
 def deinterleave():
@@ -320,28 +365,31 @@
     return jnp.asarray(rows, BF), jnp.asarray(cols, BF)
 
 
+def orb_pairs(dy, dz):
+    return [(i, ((i // 4 + dy) % 4) * 4 + (i % 4 + dz) % 4) for i in range(16)]
+
+
 def body(three_center, atom_size, tensor_pattern, green_occ, green_virt, green_pattern):
     a, o = lax.axis_index("aux"), lax.axis_index("orb")
     pos = jnp.stack([a, o]).astype(jnp.int32)
     perm = swap16()
-    ta, *tb = spread(pos, perm, three_center.transpose(0, 2, 1, 3))
-    ta = lax.all_to_all(ta, "orb", split_axis=0, concat_axis=0, tiled=True)
+    rows, cols = deinterleave()
+    tpat = jnp.pad(tensor_pattern.reshape(1, NG * W), ((0, 0), (0, 128 - NG * W)))
+    own = prep(pos, atom_size, green_pattern.reshape(W), green_occ.reshape(W, BS, BS),
+               green_virt.reshape(W, BS, BS), rows, cols, tpat)
+    own, three_center = lax.optimization_barrier((own, three_center))
+    x = three_center.transpose(0, 2, 1, 3)
+    ta = lax.all_to_all(row_slabs(x), "orb", split_axis=0, concat_axis=0, tiled=True)
+    tb = block_pairs(pos, perm, x)
     tb = [tb[0]] + [lax.ppermute(tb[k], "aux", pairs_of(k)) for k in range(1, 8)]
 
-    pat = jnp.pad(tensor_pattern.reshape(NG * W), (0, 2)).reshape(1, 32)
-    pat = lax.all_gather(pat, ("aux", "orb"), axis=0, tiled=True)
-    pat = pat[:, : NG * W].reshape(-1)
-    inside, pair_ok = own_masks(atom_size, o)
-    keep = ((green_pattern[0] > 0) | (jnp.arange(W) == R)) & inside
-    mask = keep[:, None, None] & pair_ok
-    occ = jnp.where(mask, green_occ.reshape(W, BS, BS), jnp.zeros((), BF))
-    virt = jnp.where(mask, green_virt.reshape(W, BS, BS), jnp.zeros((), BF))
-    rows, cols = deinterleave()
-    occ = jnp.einsum("gql,flm->fgqm", rows, occ, preferred_element_type=F32).astype(BF)
-    occ = jnp.einsum("fgqm,gmk->fgqk", occ, cols, preferred_element_type=F32).astype(BF)
-    packed = jnp.concatenate([virt.reshape(192, 64), occ.reshape(192, 64)], axis=1)
-    packed = lax.all_gather(packed[None], "orb", axis=0, tiled=True)
-    k4, w = greens(pos, packed)
+    line = jnp.stack([own] + [lax.ppermute(own, "orb", orb_pairs(0, dz)) for dz in range(1, 4)])
+    plane = [line] + [lax.ppermute(line, "orb", orb_pairs(dy, 0)) for dy in range(1, 4)]
+    k4, w = greens(pos, plane)
+    pat = jnp.concatenate([g[:, 192] for g in plane], axis=0)
+    pat = jnp.stack([pat, lax.ppermute(pat, "aux", pairs_of(1))])
+    pat = jnp.stack([pat] + [lax.ppermute(pat, "aux", pairs_of(2 * dx)) for dx in range(1, 4)])
+    pat = pat[..., :32].astype(jnp.int32).reshape(-1)
 
     us = second_products(pos, pat, perm, ta.reshape(160, W, NOB, 256), k4)
     first = first_products(pos, pat, perm, w, tb)

time: 308 us -> 291 us (0.945)
  blocking collectives: 134 us -> 0 us
  waiting for transfers between devices: 64.2 us -> 146 us
  starting transfers between devices: 44.1 us -> 71.2 us
  Pallas kernels: 53.3 us -> 60.9 us
  local copies, waits for them, and re-layouts: 3.42 us -> 6.95 us
    unnamed x1 -> x0, blocking collectives: 109 us -> none
    ppermute x0 -> x10, waiting for transfers between devices: none -> 37.5 us  [the longest x3 27 us: body(): lax.ppermute(own, 'orb', orb_pairs(0, dz))]
    ppermute x7, waiting for transfers between devices: 0.02 us -> 33.2 us  [body(): lax.ppermute(tb[k], 'aux', pairs_of(k))]
    ppermute x0 -> x10, starting transfers between devices: none -> 27 us  [the longest x3 15.2 us: body(): lax.ppermute(line, 'orb', orb_pairs(dy, 0))]
    all_gather x1 -> x0, blocking collectives: 25.4 us -> none  [body(): packed = lax.all_gather(packed[None], 'orb', axis=0, tiled=True)]
    all_to_all x1, waiting for transfers between devices: 6.05 us -> 29.6 us  [body(): lax.all_to_all(first, 'orb', split_axis=0, concat_axis=0, tiled=True)]
    ppermute x7, waiting for transfers between devices: 24.1 us -> 10.2 us  [body(): lax.ppermute(us[k], 'aux', pairs_of(k))]
    pallas_call x3 -> x5, Pallas kernels: 27.1 us -> 34.5 us  [the longest x1 10.9 us: chi_share(): pl.pallas_call(chi_kernel, grid=(5,), in_specs=[sspec(), vspec()] + [vspe...]
  transfers between devices with their start and end apart: 21 -> 31, of which waited for: 10 -> 18; matrix products, arithmetic and copies ran while one was open for 1% -> 0% of each run, Pallas kernels for 10% -> 14%
where the time goes in v2:
time: 291 us; the launch traced here: 290 us
  waiting for transfers between devices  146 us (50%)
  starting transfers between devices  71.2 us (24%)
  Pallas kernels  60.9 us (21%)
  local copies, waits for them, and re-layouts  6.95 us (2%)
  other arithmetic  5.16 us (2%)
    ppermute x7, waiting for transfers between devices, body(): lax.ppermute(tb[k], 'aux', pairs_of(k))  33.2 us
    all_to_all x1, waiting for transfers between devices, body(): lax.all_to_all(first, 'orb', split_axis=0, concat_axis=0, tiled=True)  29.6 us
    ppermute x3, waiting for transfers between devices, body(): lax.ppermute(own, 'orb', orb_pairs(0, dz))  27 us
    all_to_all x1, waiting for transfers between devices, body(): part = lax.all_to_all(part, 'orb', split_axis=0, concat_axis=0, tiled=True)  25.1 us
    ppermute x3, starting transfers between devices, body(): lax.ppermute(line, 'orb', orb_pairs(dy, 0))  15.2 us
    pallas_call x1, Pallas kernels, second_products(): pl.pallas_call(second_kernel, in_specs=[sspec(), sspec(), vspec(), vspec(...  13.6 us
    pallas_call x1, Pallas kernels, first_products(): pl.pallas_call(first_kernel, in_specs=[sspec(), sspec(), vspec(), vspec()...  12.8 us
    pallas_call x1, Pallas kernels, chi_share(): pl.pallas_call(chi_kernel, grid=(5,), in_specs=[sspec(), vspec()] + [vspe...  10.9 us
  transfers between devices with their start and end apart: 31, of which 18 were waited for; matrix products, arithmetic and copies ran while one was open for 0% of the time, Pallas kernels for 14%

profile of v2, /device:TPU:0, one launch (start us, length us, event | category | flops | bytes accessed | tf_op | source)
XLA Modules:
  0.0 290.4 jit_solution(4737498074645600593)
XLA Ops:
  5.1 1.8 prep.1
  6.9 7.4 %row_slabs.1 = bf16[16,30,16,256]{3,2,1,0:T(8,128)(2,1)} custom-call(bf16[10,3,16,4096]{3,2,1,0:T(8,128)(2,1)} %bitcast.45), custom_call_target="tpu_custom_call" | custom-call | bytes 8000000 | tf_op jit(solution)/shard_map/row_slabs/pallas_call | solution.py:66
  14.3 8.3 %all-to-all-start.1 = ((bf16[16,30,16,256]{3,2,1,0:T(8,128)(2,1)}), bf16[16,30,16,256]{3,2,1,0:T(8,128)(2,1)}, u32[]{:S(2)}, u32[]{:S(2)}) async-start(bf16[16,30,16,256]{3,2,1,0:T(8,128)(2,1)} %row_slabs.1), calls=%async_computation.1 | async-start | bytes 7864320 | tf_op jit(solution)/shard_map/all_to_all | solution.py:382
  22.6 1.9 collective-permute-start
  24.6 2.7 collective-permute-start.1
  28.7 8.7 %block_pairs.1 = (bf16[2,3,10,32,128]{4,3,2,1,0:T(8,128)(2,1)}, bf16[2,3,10,32,128]{4,3,2,1,0:T(8,128)(2,1)}, bf16[2,3,10,32,128]{4,3,2,1,0:T(8,128)(2,1)}, bf16...) custom-call(s32[2]{0:T(128)} %pad_add_fusion.pos, ...), custom_call_target="tpu_custom_call" | custom-call | flops 1000000000 | bytes 8000000 | tf_op jit(solution)/shard_map/block_pairs/pallas_call | solution.py:98
  39.0 27.0 %collective-permute-done = bf16[208,128]{1,0:T(8,128)(2,1)S(1)} collective-permute-done((bf16[208,128]{1,0:T(8,128)(2,1)S(1)}, bf16[208,128]{1,0:T(8,128)(2,1)S(1)}, u32[]{:S(2)}, u32[]{:S(2)}) %collective-permute-start) | collective-permute-done | bytes 53280 | tf_op jit(solution)/shard_map/ppermute | solution.py:386
  66.0 11.6 %collective-permute-start.5 = (bf16[4,208,128]{2,1,0:T(8,128)(2,1)S(1)}, bf16[4,208,128]{2,1,0:T(8,128)(2,1)S(1)}, u32[]{:S(2)}, u32[]{:S(2)}) collective-permute-start(bf16[4,208,128]{2,1,0:T(8,128)(2,1)S(1)} %pad_maximum_fusion.rest_0_), channel_id=1, source_target_pairs={{0,12},{1,13},{2,14},{3,15},{4,0},{5,1},{6,2},{7,3},{8,4},{9,5},{1... | collective-permute-start | bytes 638984 | tf_op jit(solution)/shard_map/ppermute | solution.py:387
  77.6 3.5 %collective-permute-start.4 = (bf16[4,208,128]{2,1,0:T(8,128)(2,1)S(1)}, bf16[4,208,128]{2,1,0:T(8,128)(2,1)S(1)}, u32[]{:S(2)}, u32[]{:S(2)}) collective-permute-start(bf16[4,208,128]{2,1,0:T(8,128)(2,1)S(1)} %pad_maximum_fusion.rest_0_), channel_id=1, source_target_pairs={{0,8},{1,9},{2,10},{3,11},{4,12},{5,13},{6,14},{7,15},{8,0},{9,1},... | collective-permute-start | bytes 638984 | tf_op jit(solution)/shard_map/ppermute | solution.py:387
  81.2 4.0 %collective-permute-done.5.rest_3_ = bf16[4,208,128]{2,1,0:T(8,128)(2,1)S(1)} collective-permute-done((bf16[4,208,128]{2,1,0:T(8,128)(2,1)S(1)}, bf16[4,208,128]{2,1,0:T(8,128)(2,1)S(1)}, u32[]{:S(2)}, u32[]{:S(2)}) %collective-permute-start.5) | collective-permute-done | bytes 213024 | tf_op jit(solution)/shard_map/ppermute | solution.py:387
  85.2 1.9 collective-permute-done.4.rest_2_
  87.1 2.6 collective-permute-done.3.rest_1_
  92.4 2.7 collective-permute-start.8
  97.6 2.7 collective-permute-start.13
  100.4 2.5 collective-permute-start.15
  103.9 5.7 %greens.1 = (bf16[16,3,256,256]{3,2,1,0:T(8,128)(2,1)}, bf16[2,192,192]{2,1,0:T(8,128)(2,1)}) custom-call(s32[2]{0:T(128)} %pad_add_fusion.pos, bf16[4,208,128]{2,1,0:T(8,128)(2,1)} %copy-done, bf16[4,208,128]{2,1,0:T(8,128)(2,1)} %copy-done.3, bf16[4,208,128]{2,1,0:T(8,128)(2,1)} %copy-done.2, bf16[4,208,128]{2,1,0:T(8,128)(2,1)} %copy-done.1), custom_call_target="tpu_custom_call" | custom-call | flops 1000000 | bytes 8000000 | tf_op jit(solution)/shard_map/greens/pallas_call | solution.py:192
  110.3 21.9 %collective-permute-done.12.rest_3_ = bf16[2,3,10,32,128]{4,3,2,1,0:T(8,128)(2,1)S(1)} collective-permute-done((bf16[2,3,10,32,128]{4,3,2,1,0:T(8,128)(2,1)}, bf16[2,3,10,32,128]{4,3,2,1,0:T(8,128)(2,1)S(1)}, u32[]{:S(2)}, u32[]{:S(2)}) %collective-permute-start.12) | collective-permute-done | bytes 491552 | tf_op jit(solution)/shard_map/ppermute | solution.py:384
  133.5 10.0 %collective-permute-done.16.rest_7_ = bf16[2,3,10,32,128]{4,3,2,1,0:T(8,128)(2,1)S(1)} collective-permute-done((bf16[2,3,10,32,128]{4,3,2,1,0:T(8,128)(2,1)}, bf16[2,3,10,32,128]{4,3,2,1,0:T(8,128)(2,1)S(1)}, u32[]{:S(2)}, u32[]{:S(2)}) %collective-permute-start.16) | collective-permute-done | bytes 491552 | tf_op jit(solution)/shard_map/ppermute | solution.py:384
  144.3 12.8 %first.1 = bf16[16,6,80,256]{3,2,1,0:T(8,128)(2,1)} custom-call(s32[2]{0:T(128)} %pad_add_fusion.pos, s32[4096]{0:T(1024)} %reshape.32.pat, bf16[256,256]{1,0:T(8,128)(2,1)} %constant.54.clone.perm, bf16[2,192,192]{2,1,0:T(8,128)(2,1)} %get-tuple-element.28.w_ref, bf16[2,3,10,32,128]{4,3,2,1,0:T(8,128)(2,1)} %get-tuple-element.30.rest_0_, ...), custom_call_target="tpu_custom_call" | custom-call | flops 3000000000 | bytes 8000000 | tf_op jit(solution)/shard_map/first/pallas_call | solution.py:303
  157.1 6.0 %all-to-all-start = ((bf16[16,6,80,256]{3,2,1,0:T(8,128)(2,1)}), bf16[16,6,80,256]{3,2,1,0:T(8,128)(2,1)}, u32[]{:S(2)}, u32[]{:S(2)}) async-start(bf16[16,6,80,256]{3,2,1,0:T(8,128)(2,1)} %first.1), calls=%async_computation | async-start | bytes 7864320 | tf_op jit(solution)/shard_map/all_to_all | solution.py:396
  163.1 13.6 %second.1 = (bf16[6,160,256]{2,1,0:T(8,128)(2,1)}, bf16[6,160,256]{2,1,0:T(8,128)(2,1)}, bf16[6,160,256]{2,1,0:T(8,128)(2,1)}, bf16[6,160,256]{2,1,0:T(8,128)(2,...) custom-call(s32[2]{0:T(128)} %pad_add_fusion.pos, ...), custom_call_target="tpu_custom_call" | custom-call | flops 4000000000 | bytes 15000000 | tf_op jit(solution)/shard_map/second/pallas_call | solution.py:242
  177.6 3.7 %collective-permute-start.20 = (bf16[6,160,256]{2,1,0:T(8,128)(2,1)}, bf16[6,160,256]{2,1,0:T(8,128)(2,1)S(1)}, u32[]{:S(2)}, u32[]{:S(2)}) collective-permute-start(bf16[6,160,256]{2,1,0:T(8,128)(2,1)} %get-tuple-element.43), channel_id=1, source_target_pairs={{0,64},{16,80},{32,96},{48,112},{64,0},{80,16},{96,32},{112,48},{1... | collective-permute-start | bytes 1474568 | tf_op jit(solution)/shard_map/ppermute | solution.py:397
  181.3 2.5 collective-permute-start.22
  183.8 8.5 %collective-permute-done.18.rest_2_ = bf16[6,160,256]{2,1,0:T(8,128)(2,1)S(1)} collective-permute-done((bf16[6,160,256]{2,1,0:T(8,128)(2,1)}, bf16[6,160,256]{2,1,0:T(8,128)(2,1)S(1)}, u32[]{:S(2)}, u32[]{:S(2)}) %collective-permute-start.18) | collective-permute-done | bytes 491552 | tf_op jit(solution)/shard_map/ppermute | solution.py:397
  192.8 29.6 %all-to-all-done.first_ref = bf16[16,6,80,256]{3,2,1,0:T(8,128)(2,1)} async-done(((bf16[16,6,80,256]{3,2,1,0:T(8,128)(2,1)}), bf16[16,6,80,256]{3,2,1,0:T(8,128)(2,1)}, u32[]{:S(2)}, u32[]{:S(2)}) %all-to-all-start) | async-done | bytes 3932192 | tf_op jit(solution)/shard_map/all_to_all | solution.py:396
  225.1 10.9 %chi.1 = (f32[16,40,1280]{2,1,0:T(8,128)}, f32[16,40,1280]{2,1,0:T(8,128)}) custom-call(s32[2]{0:T(128)} %pad_add_fusion.pos, bf16[16,6,80,256]{3,2,1,0:T(8,128)(2,1)} %all-to-all-done.first_ref, bf16[6,160,256]{2,1,0:T(8,128)(2,1)} %get-tuple-element.39.rest_0_, bf16[6,160,256]{2,1,0:T(8,128)(2,1)} %copy-done.9, bf16[6,160,256]{2,1,0:T(8,128)(2,1)} %copy-done.10, ...), custom_call_target="tpu_custom_call" | custom-call | flops 5000000000 | bytes 15000000 | tf_op jit(solution)/shard_map/chi/pallas_call | solution.py:343
  236.3 5.8 %collective-permute-done.24 = f32[16,40,1280]{2,1,0:T(8,128)S(1)} collective-permute-done((f32[16,40,1280]{2,1,0:T(8,128)}, f32[16,40,1280]{2,1,0:T(8,128)S(1)}, u32[]{:S(2)}, u32[]{:S(2)}) %collective-permute-start.24) | collective-permute-done | bytes 3276832 | tf_op jit(solution)/shard_map/ppermute | solution.py:400
  242.1 3.6 %add_convert_fusion = bf16[16,40,1280]{2,1,0:T(8,128)(2,1)} fusion(f32[16,40,1280]{2,1,0:T(8,128)} %get-tuple-element.47, f32[16,40,1280]{2,1,0:T(8,128)S(1)} %collective-permute-done.24), kind=kLoop, calls=%fused_computation.1 | loop fusion | flops 1638400 | bytes 8192000 | tf_op jit(solution)/shard_map/convert_element_type | solution.py:400
  245.7 9.8 %all-to-all-start.2 = ((bf16[16,40,1280]{2,1,0:T(8,128)(2,1)}), bf16[16,40,1280]{2,1,0:T(8,128)(2,1)S(1)}, u32[]{:S(2)}, u32[]{:S(2)}) async-start(bf16[16,40,1280]{2,1,0:T(8,128)(2,1)} %add_convert_fusion), calls=%async_computation.2 | async-start | bytes 3276800 | tf_op jit(solution)/shard_map/all_to_all | solution.py:401
  255.6 25.1 %all-to-all-done.2 = bf16[16,40,1280]{2,1,0:T(8,128)(2,1)S(1)} async-done(((bf16[16,40,1280]{2,1,0:T(8,128)(2,1)}), bf16[16,40,1280]{2,1,0:T(8,128)(2,1)S(1)}, u32[]{:S(2)}, u32[]{:S(2)}) %all-to-all-start.2) | async-done | bytes 1638432 | tf_op jit(solution)/shard_map/all_to_all | solution.py:401
  281.6 3.7 %collective-permute-start.26 = (f32[10,1280]{1,0:T(8,128)S(1)}, f32[10,1280]{1,0:T(8,128)S(1)}, u32[]{:S(2)}, u32[]{:S(2)}) collective-permute-start(f32[10,1280]{1,0:T(8,128)S(1)} %get-tuple-element.51), channel_id=1, source_target_pairs={{0,64},{16,80},{32,96},{48,112},{64,0},{80,16},{96,32},{112,48},{1... | collective-permute-start | bytes 153608 | tf_op jit(solution)/shard_map/ppermute | solution.py:407
  286.7 1.9 collective-permute-done.26
  (99 shorter events, 25.8 us)
Async XLA Ops:
  14.3 142.8 %all-to-all-start.1 = ((bf16[16,30,16,256]{3,2,1,0:T(8,128)(2,1)}), bf16[16,30,16,256]{3,2,1,0:T(8,128)(2,1)}, u32[]{:S(2)}, u32[]{:S(2)}) async-start(bf16[16,30,16,256]{3,2,1,0:T(8,128)(2,1)} %row_slabs.1), calls=%async_computation.1 | async-start | bytes 7864320 | tf_op jit(solution)/shard_map/all_to_all | solution.py:382
  22.6 43.3 %collective-permute-start = (bf16[208,128]{1,0:T(8,128)(2,1)S(1)}, bf16[208,128]{1,0:T(8,128)(2,1)S(1)}, u32[]{:S(2)}, u32[]{:S(2)}) collective-permute-start(bf16[208,128]{1,0:T(8,128)(2,1)S(1)} %copy-done.4), channel_id=1, source_target_pairs={{0,1},{1,2},{2,3},{3,0},{4,5},{5,6},{6,7},{7,4},{8,9},{9,10},{10,1... | collective-permute-start | bytes 159752 | tf_op jit(solution)/shard_map/ppermute | solution.py:386
  24.6 41.4 %collective-permute-start.1 = (bf16[208,128]{1,0:T(8,128)(2,1)S(1)}, bf16[208,128]{1,0:T(8,128)(2,1)S(1)}, u32[]{:S(2)}, u32[]{:S(2)}) collective-permute-start(bf16[208,128]{1,0:T(8,128)(2,1)S(1)} %copy-done.4), channel_id=1, source_target_pairs={{0,2},{1,3},{2,0},{3,1},{4,6},{5,7},{6,4},{7,5},{8,10},{9,11},{10,... | collective-permute-start | bytes 159752 | tf_op jit(solution)/shard_map/ppermute | solution.py:386
  27.3 38.7 %collective-permute-start.2 = (bf16[208,128]{1,0:T(8,128)(2,1)S(1)}, bf16[208,128]{1,0:T(8,128)(2,1)S(1)}, u32[]{:S(2)}, u32[]{:S(2)}) collective-permute-start(bf16[208,128]{1,0:T(8,128)(2,1)S(1)} %copy-done.4), channel_id=1, source_target_pairs={{0,3},{1,0},{2,1},{3,2},{4,7},{5,4},{6,5},{7,6},{8,11},{9,8},{10,9... | collective-permute-start | bytes 159752 | tf_op jit(solution)/shard_map/ppermute | solution.py:386
  37.4 62.9 %collective-permute-start.10 = (bf16[2,3,10,32,128]{4,3,2,1,0:T(8,128)(2,1)}, bf16[2,3,10,32,128]{4,3,2,1,0:T(8,128)(2,1)S(1)}, u32[]{:S(2)}, u32[]{:S(2)}) collective-permute-start(bf16[2,3,10,32,128]{4,3,2,1,0:T(8,128)(2,1)} %get-tuple-element.31), channel_id=1, source_target_pairs={{0,16},{16,0},{32,48},{48,32},{64,80},{80,64},{96,112},{112,96},{1... | collective-permute-start | bytes 1474568 | tf_op jit(solution)/shard_map/ppermute | solution.py:384
  37.5 65.4 %collective-permute-start.11 = (bf16[2,3,10,32,128]{4,3,2,1,0:T(8,128)(2,1)}, bf16[2,3,10,32,128]{4,3,2,1,0:T(8,128)(2,1)S(1)}, u32[]{:S(2)}, u32[]{:S(2)}) collective-permute-start(bf16[2,3,10,32,128]{4,3,2,1,0:T(8,128)(2,1)} %get-tuple-element.32), channel_id=1, source_target_pairs={{0,32},{16,48},{32,64},{48,80},{64,96},{80,112},{96,0},{112,16},{1... | collective-permute-start | bytes 1474568 | tf_op jit(solution)/shard_map/ppermute | solution.py:384
  66.0 19.1 %collective-permute-start.5 = (bf16[4,208,128]{2,1,0:T(8,128)(2,1)S(1)}, bf16[4,208,128]{2,1,0:T(8,128)(2,1)S(1)}, u32[]{:S(2)}, u32[]{:S(2)}) collective-permute-start(bf16[4,208,128]{2,1,0:T(8,128)(2,1)S(1)} %pad_maximum_fusion.rest_0_), channel_id=1, source_target_pairs={{0,12},{1,13},{2,14},{3,15},{4,0},{5,1},{6,2},{7,3},{8,4},{9,5},{1... | collective-permute-start | bytes 638984 | tf_op jit(solution)/shard_map/ppermute | solution.py:387
  77.6 9.4 %collective-permute-start.4 = (bf16[4,208,128]{2,1,0:T(8,128)(2,1)S(1)}, bf16[4,208,128]{2,1,0:T(8,128)(2,1)S(1)}, u32[]{:S(2)}, u32[]{:S(2)}) collective-permute-start(bf16[4,208,128]{2,1,0:T(8,128)(2,1)S(1)} %pad_maximum_fusion.rest_0_), channel_id=1, source_target_pairs={{0,8},{1,9},{2,10},{3,11},{4,12},{5,13},{6,14},{7,15},{8,0},{9,1},... | collective-permute-start | bytes 638984 | tf_op jit(solution)/shard_map/ppermute | solution.py:387
  81.2 8.5 %collective-permute-start.3 = (bf16[4,208,128]{2,1,0:T(8,128)(2,1)S(1)}, bf16[4,208,128]{2,1,0:T(8,128)(2,1)S(1)}, u32[]{:S(2)}, u32[]{:S(2)}) collective-permute-start(bf16[4,208,128]{2,1,0:T(8,128)(2,1)S(1)} %pad_maximum_fusion.rest_0_), channel_id=1, source_target_pairs={{0,4},{1,5},{2,6},{3,7},{4,8},{5,9},{6,10},{7,11},{8,12},{9,13},{1... | collective-permute-start | bytes 638984 | tf_op jit(solution)/shard_map/ppermute | solution.py:387
  89.7 1.2 collective-permute-start.6
  91.0 5.7 %collective-permute-start.7 = (bf16[2,16,128]{2,1,0:T(8,128)(2,1)S(1)}, bf16[2,16,128]{2,1,0:T(8,128)(2,1)S(1)}, u32[]{:S(2)}, u32[]{:S(2)}) collective-permute-start(bf16[2,16,128]{2,1,0:T(8,128)(2,1)S(1)} %get-tuple-element.53), channel_id=1, source_target_pairs={{0,32},{16,48},{32,64},{48,80},{64,96},{80,112},{96,0},{112,16},{1... | collective-permute-start | bytes 24584 | tf_op jit(solution)/shard_map/ppermute | solution.py:391
  92.4 5.2 %collective-permute-start.8 = (bf16[2,16,128]{2,1,0:T(8,128)(2,1)S(1)}, bf16[2,16,128]{2,1,0:T(8,128)(2,1)S(1)}, u32[]{:S(2)}, u32[]{:S(2)}) collective-permute-start(bf16[2,16,128]{2,1,0:T(8,128)(2,1)S(1)} %get-tuple-element.53), channel_id=1, source_target_pairs={{0,64},{16,80},{32,96},{48,112},{64,0},{80,16},{96,32},{112,48},{1... | collective-permute-start | bytes 24584 | tf_op jit(solution)/shard_map/ppermute | solution.py:391
  95.2 5.2 %collective-permute-start.9 = (bf16[2,16,128]{2,1,0:T(8,128)(2,1)S(1)}, bf16[2,16,128]{2,1,0:T(8,128)(2,1)S(1)}, u32[]{:S(2)}, u32[]{:S(2)}) collective-permute-start(bf16[2,16,128]{2,1,0:T(8,128)(2,1)S(1)} %get-tuple-element.53), channel_id=1, source_target_pairs={{0,96},{16,112},{32,0},{48,16},{64,32},{80,48},{96,64},{112,80},{1... | collective-permute-start | bytes 24584 | tf_op jit(solution)/shard_map/ppermute | solution.py:391
  96.6 35.5 %collective-permute-start.12 = (bf16[2,3,10,32,128]{4,3,2,1,0:T(8,128)(2,1)}, bf16[2,3,10,32,128]{4,3,2,1,0:T(8,128)(2,1)S(1)}, u32[]{:S(2)}, u32[]{:S(2)}) collective-permute-start(bf16[2,3,10,32,128]{4,3,2,1,0:T(8,128)(2,1)} %get-tuple-element.33), channel_id=1, source_target_pairs={{0,48},{16,32},{32,80},{48,64},{64,112},{80,96},{96,16},{112,0},{1... | collective-permute-start | bytes 1474568 | tf_op jit(solution)/shard_map/ppermute | solution.py:384
  97.6 34.5 %collective-permute-start.13 = (bf16[2,3,10,32,128]{4,3,2,1,0:T(8,128)(2,1)}, bf16[2,3,10,32,128]{4,3,2,1,0:T(8,128)(2,1)S(1)}, u32[]{:S(2)}, u32[]{:S(2)}) collective-permute-start(bf16[2,3,10,32,128]{4,3,2,1,0:T(8,128)(2,1)} %get-tuple-element.34), channel_id=1, source_target_pairs={{0,64},{16,80},{32,96},{48,112},{64,0},{80,16},{96,32},{112,48},{1... | collective-permute-start | bytes 1474568 | tf_op jit(solution)/shard_map/ppermute | solution.py:384
  100.3 31.8 %collective-permute-start.14 = (bf16[2,3,10,32,128]{4,3,2,1,0:T(8,128)(2,1)}, bf16[2,3,10,32,128]{4,3,2,1,0:T(8,128)(2,1)S(1)}, u32[]{:S(2)}, u32[]{:S(2)}) collective-permute-start(bf16[2,3,10,32,128]{4,3,2,1,0:T(8,128)(2,1)} %get-tuple-element.35), channel_id=1, source_target_pairs={{0,80},{16,64},{32,112},{48,96},{64,16},{80,0},{96,48},{112,32},{1... | collective-permute-start | bytes 1474568 | tf_op jit(solution)/shard_map/ppermute | solution.py:384
  100.3 43.2 %copy-start.5 = (bf16[2,3,10,32,128]{4,3,2,1,0:T(8,128)(2,1)}, bf16[2,3,10,32,128]{4,3,2,1,0:T(8,128)(2,1)S(1)}, u32[]{:S(2)}) copy-start(bf16[2,3,10,32,128]{4,3,2,1,0:T(8,128)(2,1)S(1)} %collective-permute-done.10.rest_1_) | copy-start | bytes 1474564
  100.4 33.1 %collective-permute-start.15 = (bf16[2,3,10,32,128]{4,3,2,1,0:T(8,128)(2,1)}, bf16[2,3,10,32,128]{4,3,2,1,0:T(8,128)(2,1)S(1)}, u32[]{:S(2)}, u32[]{:S(2)}) collective-permute-start(bf16[2,3,10,32,128]{4,3,2,1,0:T(8,128)(2,1)} %get-tuple-element.36), channel_id=1, source_target_pairs={{0,96},{16,112},{32,0},{48,16},{64,32},{80,48},{96,64},{112,80},{1... | collective-permute-start | bytes 1474568 | tf_op jit(solution)/shard_map/ppermute | solution.py:384
  102.8 40.7 %collective-permute-start.16 = (bf16[2,3,10,32,128]{4,3,2,1,0:T(8,128)(2,1)}, bf16[2,3,10,32,128]{4,3,2,1,0:T(8,128)(2,1)S(1)}, u32[]{:S(2)}, u32[]{:S(2)}) collective-permute-start(bf16[2,3,10,32,128]{4,3,2,1,0:T(8,128)(2,1)} %get-tuple-element.37), channel_id=1, source_target_pairs={{0,112},{16,96},{32,16},{48,0},{64,48},{80,32},{96,80},{112,64},{1... | collective-permute-start | bytes 1474568 | tf_op jit(solution)/shard_map/ppermute | solution.py:384
  157.1 65.2 %all-to-all-start = ((bf16[16,6,80,256]{3,2,1,0:T(8,128)(2,1)}), bf16[16,6,80,256]{3,2,1,0:T(8,128)(2,1)}, u32[]{:S(2)}, u32[]{:S(2)}) async-start(bf16[16,6,80,256]{3,2,1,0:T(8,128)(2,1)} %first.1), calls=%async_computation | async-start | bytes 7864320 | tf_op jit(solution)/shard_map/all_to_all | solution.py:396
  176.7 4.6 %collective-permute-start.17 = (bf16[6,160,256]{2,1,0:T(8,128)(2,1)}, bf16[6,160,256]{2,1,0:T(8,128)(2,1)S(1)}, u32[]{:S(2)}, u32[]{:S(2)}) collective-permute-start(bf16[6,160,256]{2,1,0:T(8,128)(2,1)} %get-tuple-element.40), channel_id=1, source_target_pairs={{0,16},{16,0},{32,48},{48,32},{64,80},{80,64},{96,112},{112,96},{1... | collective-permute-start | bytes 1474568 | tf_op jit(solution)/shard_map/ppermute | solution.py:397
  176.7 15.5 %collective-permute-start.18 = (bf16[6,160,256]{2,1,0:T(8,128)(2,1)}, bf16[6,160,256]{2,1,0:T(8,128)(2,1)S(1)}, u32[]{:S(2)}, u32[]{:S(2)}) collective-permute-start(bf16[6,160,256]{2,1,0:T(8,128)(2,1)} %get-tuple-element.41), channel_id=1, source_target_pairs={{0,32},{16,48},{32,64},{48,80},{64,96},{80,112},{96,0},{112,16},{1... | collective-permute-start | bytes 1474568 | tf_op jit(solution)/shard_map/ppermute | solution.py:397
  177.6 44.8 %collective-permute-start.19 = (bf16[6,160,256]{2,1,0:T(8,128)(2,1)}, bf16[6,160,256]{2,1,0:T(8,128)(2,1)S(1)}, u32[]{:S(2)}, u32[]{:S(2)}) collective-permute-start(bf16[6,160,256]{2,1,0:T(8,128)(2,1)} %get-tuple-element.42), channel_id=1, source_target_pairs={{0,48},{16,32},{32,80},{48,64},{64,112},{80,96},{96,16},{112,0},{1... | collective-permute-start | bytes 1474568 | tf_op jit(solution)/shard_map/ppermute | solution.py:397
  177.6 44.8 %collective-permute-start.20 = (bf16[6,160,256]{2,1,0:T(8,128)(2,1)}, bf16[6,160,256]{2,1,0:T(8,128)(2,1)S(1)}, u32[]{:S(2)}, u32[]{:S(2)}) collective-permute-start(bf16[6,160,256]{2,1,0:T(8,128)(2,1)} %get-tuple-element.43), channel_id=1, source_target_pairs={{0,64},{16,80},{32,96},{48,112},{64,0},{80,16},{96,32},{112,48},{1... | collective-permute-start | bytes 1474568 | tf_op jit(solution)/shard_map/ppermute | solution.py:397
  181.3 42.7 %collective-permute-start.21 = (bf16[6,160,256]{2,1,0:T(8,128)(2,1)}, bf16[6,160,256]{2,1,0:T(8,128)(2,1)S(1)}, u32[]{:S(2)}, u32[]{:S(2)}) collective-permute-start(bf16[6,160,256]{2,1,0:T(8,128)(2,1)} %get-tuple-element.44), channel_id=1, source_target_pairs={{0,80},{16,64},{32,112},{48,96},{64,16},{80,0},{96,48},{112,32},{1... | collective-permute-start | bytes 1474568 | tf_op jit(solution)/shard_map/ppermute | solution.py:397
  181.3 42.7 %collective-permute-start.22 = (bf16[6,160,256]{2,1,0:T(8,128)(2,1)}, bf16[6,160,256]{2,1,0:T(8,128)(2,1)S(1)}, u32[]{:S(2)}, u32[]{:S(2)}) collective-permute-start(bf16[6,160,256]{2,1,0:T(8,128)(2,1)} %get-tuple-element.45), channel_id=1, source_target_pairs={{0,96},{16,112},{32,0},{48,16},{64,32},{80,48},{96,64},{112,80},{1... | collective-permute-start | bytes 1474568 | tf_op jit(solution)/shard_map/ppermute | solution.py:397
  192.3 31.9 %collective-permute-start.23 = (bf16[6,160,256]{2,1,0:T(8,128)(2,1)}, bf16[6,160,256]{2,1,0:T(8,128)(2,1)S(1)}, u32[]{:S(2)}, u32[]{:S(2)}) collective-permute-start(bf16[6,160,256]{2,1,0:T(8,128)(2,1)} %get-tuple-element.46), channel_id=1, source_target_pairs={{0,112},{16,96},{32,16},{48,0},{64,48},{80,32},{96,80},{112,64},{1... | collective-permute-start | bytes 1474568 | tf_op jit(solution)/shard_map/ppermute | solution.py:397
  236.0 6.1 %collective-permute-start.24 = (f32[16,40,1280]{2,1,0:T(8,128)}, f32[16,40,1280]{2,1,0:T(8,128)S(1)}, u32[]{:S(2)}, u32[]{:S(2)}) collective-permute-start(f32[16,40,1280]{2,1,0:T(8,128)} %get-tuple-element.48), channel_id=1, source_target_pairs={{0,16},{16,0},{32,48},{48,32},{64,80},{80,64},{96,112},{112,96},{1... | collective-permute-start | bytes 9830408 | tf_op jit(solution)/shard_map/ppermute | solution.py:400
  245.7 35.0 %all-to-all-start.2 = ((bf16[16,40,1280]{2,1,0:T(8,128)(2,1)}), bf16[16,40,1280]{2,1,0:T(8,128)(2,1)S(1)}, u32[]{:S(2)}, u32[]{:S(2)}) async-start(bf16[16,40,1280]{2,1,0:T(8,128)(2,1)} %add_convert_fusion), calls=%async_computation.2 | async-start | bytes 3276800 | tf_op jit(solution)/shard_map/all_to_all | solution.py:401
  281.0 5.7 %collective-permute-start.25 = (f32[10,1280]{1,0:T(8,128)S(1)}, f32[10,1280]{1,0:T(8,128)S(1)}, u32[]{:S(2)}, u32[]{:S(2)}) collective-permute-start(f32[10,1280]{1,0:T(8,128)S(1)} %get-tuple-element.49), channel_id=1, source_target_pairs={{0,32},{16,48},{32,64},{48,80},{64,96},{80,112},{96,0},{112,16},{1... | collective-permute-start | bytes 153608 | tf_op jit(solution)/shard_map/ppermute | solution.py:407
  281.6 7.0 %collective-permute-start.26 = (f32[10,1280]{1,0:T(8,128)S(1)}, f32[10,1280]{1,0:T(8,128)S(1)}, u32[]{:S(2)}, u32[]{:S(2)}) collective-permute-start(f32[10,1280]{1,0:T(8,128)S(1)} %get-tuple-element.51), channel_id=1, source_target_pairs={{0,64},{16,80},{32,96},{48,112},{64,0},{80,16},{96,32},{112,48},{1... | collective-permute-start | bytes 153608 | tf_op jit(solution)/shard_map/ppermute | solution.py:407
  285.3 4.4 %collective-permute-start.27 = (f32[10,1280]{1,0:T(8,128)S(1)}, f32[10,1280]{1,0:T(8,128)S(1)}, u32[]{:S(2)}, u32[]{:S(2)}) collective-permute-start(f32[10,1280]{1,0:T(8,128)S(1)} %get-tuple-element.50), channel_id=1, source_target_pairs={{0,96},{16,112},{32,0},{48,16},{64,32},{80,48},{96,64},{112,80},{1... | collective-permute-start | bytes 153608 | tf_op jit(solution)/shard_map/ppermute | solution.py:407
  (18 other events, 262.7 us)

commit v3 on v2

--- a/solution.py
+++ b/solution.py
@@ -32,8 +32,8 @@
     return lax.rem(a // 2 + dx, 4) * 2 + (lax.rem(a, 2) if dc == 0 else 1 - lax.rem(a, 2))
 
 
-def pat_row(o, k, n):
-    return k * NOB + lax.rem(o // 4 + 4 - n // 4, 4) * 4 + lax.rem(lax.rem(o, 4) + 4 - lax.rem(n, 4), 4)
+def meta_row(o, n):
+    return lax.rem(o // 4 + 4 - n // 4, 4) * 4 + lax.rem(lax.rem(o, 4) + 4 - lax.rem(n, 4), 4)
 
 
 def src_of(a, k):
@@ -57,17 +57,18 @@
 
 
 def rows_kernel(x_ref, ta_ref):
-    for d in range(W):
-        for o in range(16):
-            ta_ref[o, d] = x_ref[0, d, :, 256 * o : 256 * o + 256]
+    for p in range(2):
+        for d in range(W):
+            for o in range(16):
+                ta_ref[o, p * W + d] = x_ref[p, d, :, 256 * o : 256 * o + 256]
 
 
 def row_slabs(x):
     return pl.pallas_call(
         rows_kernel,
-        grid=(NPD,),
-        in_specs=[pl.BlockSpec((1, W, NOB, 4096), lambda i: (i, 0, 0, 0))],
-        out_specs=pl.BlockSpec((16, W, NOB, 256), lambda i: (0, i, 0, 0)),
+        grid=(NPD // 2,),
+        in_specs=[pl.BlockSpec((2, W, NOB, 4096), lambda i: (i, 0, 0, 0))],
+        out_specs=pl.BlockSpec((16, 2 * W, NOB, 256), lambda i: (0, i, 0, 0)),
         out_shape=jax.ShapeDtypeStruct((16, NPD * W, NOB, 256), BF),
         compiler_params=pltpu.CompilerParams(vmem_limit_bytes=VLIM),
         cost_estimate=pl.CostEstimate(flops=0, bytes_accessed=8 * 10**6, transcendentals=0),
@@ -75,96 +76,79 @@
     )(x)
 
 
-def pairs_kernel(pos, perm, x_ref, *rest):
+def pairs_kernel(pos, meta, perm, x_ref, *rest):
     tb, s = rest[:8], rest[8]
-    a = pos[0]
-    for d in range(W):
-        x = x_ref[0, d]
-        halves = [
-            jnp.concatenate([x[:, 128 * (16 * h + c) : 128 * (16 * h + c) + 128] for c in range(16)], axis=0)
-            for h in range(2)
-        ]
-        y = jnp.dot(perm[...], jnp.concatenate(halves, axis=1), preferred_element_type=F32).astype(BF)
-        for n in range(NOB):
-            for h in range(2):
-                s[n, d, 16 * h : 16 * h + 16] = y[16 * n : 16 * n + 16, 128 * h : 128 * h + 128]
+    a, o = pos[0], pos[1]
+    for p in range(2):
+        g = lax.div(o * NPD + pl.program_id(0) * 2 + p, ABS)
+        for d in range(W):
+            x = x_ref[p, d]
+            halves = [
+                jnp.concatenate([x[:, 128 * (16 * h + c) : 128 * (16 * h + c) + 128] for c in range(16)], axis=0)
+                for h in range(2)
+            ]
+            y = jnp.dot(perm[...], jnp.concatenate(halves, axis=1), preferred_element_type=F32)
+            for n in range(NOB):
+                part = y[16 * n : 16 * n + 16]
+                keep = meta[meta_row(o, n) * 128 + g * W + d] > 0
+                part = jnp.where(keep, part, jnp.zeros_like(part)).astype(BF)
+                for h in range(2):
+                    s[n, d, p, 16 * h : 16 * h + 16] = part[:, 128 * h : 128 * h + 128]
     for k in range(8):
         t = dest_of(a, k)
         for i in range(2):
-            tb[k][i, :, 0] = s[2 * t + i]
-
-
-def block_pairs(pos, perm, x):
+            tb[k][i] = s[2 * t + i]
+
+
+def block_pairs(pos, meta, perm, x):
     return pl.pallas_call(
         pairs_kernel,
-        grid=(NPD,),
+        grid=(NPD // 2,),
         in_specs=[
             sspec(),
+            sspec(),
             pl.BlockSpec((256, 256), lambda i: (0, 0)),
-            pl.BlockSpec((1, W, NOB, 4096), lambda i: (i, 0, 0, 0)),
+            pl.BlockSpec((2, W, NOB, 4096), lambda i: (i, 0, 0, 0)),
         ],
-        out_specs=[pl.BlockSpec((2, W, 1, 32, 128), lambda i: (0, 0, i, 0, 0))] * 8,
+        out_specs=[pl.BlockSpec((2, W, 2, 32, 128), lambda i: (0, 0, i, 0, 0))] * 8,
         out_shape=[jax.ShapeDtypeStruct((2, W, NPD, 32, 128), BF)] * 8,
-        scratch_shapes=[pltpu.VMEM((NOB, W, 32, 128), BF)],
+        scratch_shapes=[pltpu.VMEM((NOB, W, 2, 32, 128), BF)],
         compiler_params=pltpu.CompilerParams(vmem_limit_bytes=VLIM),
         cost_estimate=pl.CostEstimate(flops=10**9, bytes_accessed=8 * 10**6, transcendentals=0),
         name="block_pairs",
-    )(pos, perm, x)
-
-
-def prep_kernel(pos, size, gpat, occ_ref, virt_ref, rows_ref, cols_ref, tpat_ref, out):
-    n = pos[1]
-    row = lax.broadcasted_iota(jnp.int32, (BS, BS), 0)
-    col = lax.broadcasted_iota(jnp.int32, (BS, BS), 1)
-    zero = jnp.zeros((BS, BS), BF)
-    for d in range(W):
-        m = n + d - R
-        ok = (m >= 0) & (m < NOB)
-        if d != R:
-            ok = ok & (gpat[d] > 0)
-        rows_in = jnp.where(ok, size[jnp.clip(m, 0, NOB - 1)], 0)
-        mask = (row < rows_in) & (col < size[n])
-        virt = jnp.where(mask, virt_ref[d], zero)
-        occ = jnp.where(mask, occ_ref[d], zero)
-        parts = []
-        for g in range(2):
-            t = jnp.dot(rows_ref[g], occ, preferred_element_type=F32).astype(BF)
-            parts.append(jnp.dot(t, cols_ref[g], preferred_element_type=F32).astype(BF))
-        out[64 * d : 64 * d + 64] = jnp.concatenate([virt, jnp.concatenate(parts, axis=0)], axis=1)
-    out[192:208] = jnp.broadcast_to(tpat_ref[...].astype(F32), (16, 128)).astype(BF)
-
-
-def prep(pos, size, gpat, occ, virt, rows, cols, tpat):
-    return pl.pallas_call(
-        prep_kernel,
-        in_specs=[sspec()] * 3 + [vspec()] * 5,
-        out_specs=vspec(),
-        out_shape=jax.ShapeDtypeStruct((208, 128), BF),
-        cost_estimate=pl.CostEstimate(flops=10**6, bytes_accessed=10**5, transcendentals=0),
-        name="prep",
-    )(pos, size, gpat, occ, virt, rows, cols, tpat)
-
-
-def greens_kernel(pos, *rest):
-    g4, k4_ref, w_ref, g_ref = rest[:4], rest[4], rest[5], rest[6]
+    )(pos, meta, perm, x)
+
+
+def greens_kernel(pos, size, meta, g_ref, rows_ref, cols_ref, k4_ref, w_ref, o_ref):
     a, o = pos[0], pos[1]
     lane = lax.broadcasted_iota(jnp.int32, (64, 128), 1)
     zero = jnp.zeros((64, 128), BF)
-    for dy in range(4):
-        for dz in range(4):
-            n = lax.rem(o // 4 + 4 - dy, 4) * 4 + lax.rem(lax.rem(o, 4) + 4 - dz, 4)
-            g_ref[n] = g4[dy][dz, 0:192]
+    row = lax.broadcasted_iota(jnp.int32, (BS, BS), 0)
+    col = lax.broadcasted_iota(jnp.int32, (BS, BS), 1)
 
     def one(n, carry):
+        r = meta_row(o, n)
         for d in range(W):
-            v = g_ref[n, 64 * d : 64 * d + 64, 0:64]
+            m = n + d - R
+            ok = (m >= 0) & (m < NOB)
+            if d != R:
+                ok = ok & (meta[r * 128 + NG * W + d] > 0)
+            rows_in = jnp.where(ok, size[jnp.clip(m, 0, NOB - 1)], 0)
+            mask = (row < rows_in) & (col < size[n])
+            occ = jnp.where(mask, g_ref[r, d], jnp.zeros((BS, BS), BF))
+            v = jnp.where(mask, g_ref[r, W + d], jnp.zeros((BS, BS), BF))
+            for g in range(2):
+                t = jnp.dot(rows_ref[g], occ, preferred_element_type=F32).astype(BF)
+                o_ref[n, d, 32 * g : 32 * g + 32] = jnp.dot(
+                    t, cols_ref[g], preferred_element_type=F32
+                ).astype(BF)
             vv = jnp.concatenate([v, v], axis=1)
             lo = jnp.where(lane < 64, vv, zero)
             hi = jnp.where(lane < 64, zero, vv)
-            for r in range(4):
+            for q in range(4):
                 for t in range(2):
-                    part = zero if r // 2 != t else (lo if r % 2 == 0 else hi)
-                    k4_ref[n, d, 64 * r : 64 * r + 64, 128 * t : 128 * t + 128] = part
+                    part = zero if q // 2 != t else (lo if q % 2 == 0 else hi)
+                    k4_ref[n, d, 64 * q : 64 * q + 64, 128 * t : 128 * t + 128] = part
         return carry
 
     lax.fori_loop(0, NOB, one, 0)
@@ -181,19 +165,18 @@
                     m = 2 * a + i + d - 1
                     ok = (m >= 0) & (m < NOB)
                     mc = jnp.clip(m, 0, NOB - 1)
-                    row = (f * 2 + g) * 32
-                    v = g_ref[mc, row : row + 32, :][:, 64:128]
+                    v = o_ref[mc, f, 32 * g : 32 * g + 32]
                     cols.append(jnp.where(ok, v, z))
                 row = (g * W + e) * 32
                 w_ref[i, row : row + 32, :] = jnp.concatenate(cols, axis=1)
 
 
-def greens(pos, g4):
+def greens(pos, size, meta, g, rows, cols):
     return pl.pallas_call(
         greens_kernel,
-        in_specs=[sspec()] + [vspec()] * 4,
+        in_specs=[sspec()] * 3 + [vspec()] * 3,
         out_specs=[vspec(), vspec()],
-        scratch_shapes=[pltpu.VMEM((NOB, 192, 128), BF)],
+        scratch_shapes=[pltpu.VMEM((NOB, W, 64, 64), BF)],
         out_shape=[
             jax.ShapeDtypeStruct((NOB, W, 256, 256), BF),
             jax.ShapeDtypeStruct((2, 192, 192), BF),
@@ -201,7 +184,7 @@
         compiler_params=pltpu.CompilerParams(vmem_limit_bytes=VLIM),
         cost_estimate=pl.CostEstimate(flops=10**6, bytes_accessed=8 * 10**6, transcendentals=0),
         name="greens",
-    )(pos, *g4)
+    )(pos, size, meta, g, rows, cols)
 
 
 def second_kernel(pos, pat, perm, ta_ref, k4_ref, *rest):
@@ -215,7 +198,7 @@
             x = ta_ref[pl.ds(16 * g, 16), d].reshape(256, 256)
             y = jnp.dot(perm[...], x, preferred_element_type=F32)
             for n in range(NOB):
-                keep = pat[pat_row(o, 0, n) * 32 + g * W + d] > 0
+                keep = pat[meta_row(o, n) * 128 + g * W + d] > 0
                 part = y[16 * n : 16 * n + 16]
                 s[n + 1, d, pl.ds(pl.multiple_of(16 * g, 16), 16)] = jnp.where(
                     keep, part, jnp.zeros_like(part)
@@ -251,24 +234,21 @@
     )(pos, pat, perm, ta, k4)
 
 
-def first_kernel(pos, pat, perm, w_ref, *rest):
+def first_kernel(pos, perm, w_ref, *rest):
     tb, out, s = rest[:8], rest[8], rest[9]
-    a, o = pos[0], pos[1]
+    a = pos[0]
     lane = lax.broadcasted_iota(jnp.int32, (96, NPD * 128), 1)
     low = lax.rem(lane, 128) < 64
     for k in range(8):
         src = src_of(a, k)
         base = lax.rem(src, 2) * 40 + (src // 2) * 10
 
-        def one(i, carry, k=k, src=src, base=base):
-            n = 2 * a + i
+        def one(i, carry, k=k, base=base):
             columns = []
             for p in range(NPD):
                 rows = []
                 for d in range(W):
-                    keep = pat[pat_row(o, k, n) * 32 + lax.div(o * NPD + p, ABS) * W + d] > 0
                     x = tb[k][i, d, p]
-                    x = jnp.where(keep, x, jnp.zeros_like(x))
                     rows.append(x)
                     rows.append(jnp.concatenate([x[:, 64:], x[:, :64]], axis=1))
                 columns.append(jnp.concatenate(rows, axis=0))
@@ -299,17 +279,17 @@
     lax.fori_loop(0, 10, regroup, 0)
 
 
-def first_products(pos, pat, perm, w, tb):
+def first_products(pos, perm, w, tb):
     return pl.pallas_call(
         first_kernel,
-        in_specs=[sspec(), sspec(), vspec(), vspec()] + [vspec()] * 8,
+        in_specs=[sspec(), vspec(), vspec()] + [vspec()] * 8,
         out_specs=vspec(),
         out_shape=jax.ShapeDtypeStruct((16, 2 * W, 80, 256), BF),
         scratch_shapes=[pltpu.VMEM((2, 80, 96, 128), BF)],
         compiler_params=pltpu.CompilerParams(vmem_limit_bytes=VLIM),
         cost_estimate=pl.CostEstimate(flops=3 * 10**9, bytes_accessed=8 * 10**6, transcendentals=0),
         name="first",
-    )(pos, pat, perm, w, *tb)
+    )(pos, perm, w, *tb)
 
 
 def chi_kernel(pos, first_ref, *rest):
@@ -374,25 +354,23 @@
     pos = jnp.stack([a, o]).astype(jnp.int32)
     perm = swap16()
     rows, cols = deinterleave()
-    tpat = jnp.pad(tensor_pattern.reshape(1, NG * W), ((0, 0), (0, 128 - NG * W)))
-    own = prep(pos, atom_size, green_pattern.reshape(W), green_occ.reshape(W, BS, BS),
-               green_virt.reshape(W, BS, BS), rows, cols, tpat)
-    own, three_center = lax.optimization_barrier((own, three_center))
     x = three_center.transpose(0, 2, 1, 3)
-    ta = lax.all_to_all(row_slabs(x), "orb", split_axis=0, concat_axis=0, tiled=True)
-    tb = block_pairs(pos, perm, x)
-    tb = [tb[0]] + [lax.ppermute(tb[k], "aux", pairs_of(k)) for k in range(1, 8)]
-
+
+    marks = jnp.concatenate([tensor_pattern.reshape(1, NG * W), green_pattern], axis=1).astype(BF)
+    marks = jnp.pad(marks, ((0, 1), (0, 4096 - NG * W - W)))
+    own = jnp.concatenate([green_occ[0], green_virt[0], marks], axis=0)
     line = jnp.stack([own] + [lax.ppermute(own, "orb", orb_pairs(0, dz)) for dz in range(1, 4)])
     plane = [line] + [lax.ppermute(line, "orb", orb_pairs(dy, 0)) for dy in range(1, 4)]
-    k4, w = greens(pos, plane)
-    pat = jnp.concatenate([g[:, 192] for g in plane], axis=0)
-    pat = jnp.stack([pat, lax.ppermute(pat, "aux", pairs_of(1))])
-    pat = jnp.stack([pat] + [lax.ppermute(pat, "aux", pairs_of(2 * dx)) for dx in range(1, 4)])
-    pat = pat[..., :32].astype(jnp.int32).reshape(-1)
-
-    us = second_products(pos, pat, perm, ta.reshape(160, W, NOB, 256), k4)
-    first = first_products(pos, pat, perm, w, tb)
+    *plane, ta = lax.optimization_barrier((*plane, row_slabs(x)))
+    ta = lax.all_to_all(ta, "orb", split_axis=0, concat_axis=0, tiled=True)
+    meta = jnp.concatenate([g[:, 2 * W, :128] for g in plane], axis=0).astype(jnp.int32).reshape(-1)
+    tb = block_pairs(pos, meta, perm, x)
+    tb = [tb[0]] + [lax.ppermute(tb[k], "aux", pairs_of(k)) for k in range(1, 8)]
+    blocks = jnp.concatenate([g[:, : 2 * W] for g in plane], axis=0).reshape(NOB, 2 * W, BS, BS)
+    k4, w = greens(pos, atom_size, meta, blocks, rows, cols)
+
+    us = second_products(pos, meta, perm, ta.reshape(160, W, NOB, 256), k4)
+    first = first_products(pos, perm, w, tb)
     first = lax.all_to_all(first, "orb", split_axis=0, concat_axis=0, tiled=True)
     us = [us[0]] + [lax.ppermute(us[k], "aux", pairs_of(k)) for k in range(1, 8)]
 

time: 291 us -> 232 us (0.80)
  waiting for transfers between devices: 146 us -> 109 us
  starting transfers between devices: 71.2 us -> 52.7 us
  local copies, waits for them, and re-layouts: 6.95 us -> 3.85 us
  other arithmetic: 5.16 us -> 8.19 us
  Pallas kernels: 60.9 us -> 57.9 us
    ppermute x7, waiting for transfers between devices: 10.2 us -> 40.2 us  [body(): lax.ppermute(us[k], 'aux', pairs_of(k))]
    all_to_all x1, waiting for transfers between devices: 29.6 us -> 0.01 us  [body(): lax.all_to_all(first, 'orb', split_axis=0, concat_axis=0, tiled=True)]
    ppermute x3, waiting for transfers between devices: 27 us -> 3.26 us  [body(): lax.ppermute(own, 'orb', orb_pairs(0, dz))]
    ppermute x3, starting transfers between devices: 15.2 us -> 5.89 us  [body(): lax.ppermute(line, 'orb', orb_pairs(dy, 0))]
    ppermute x7, waiting for transfers between devices: 33.2 us -> 26.7 us  [body(): lax.ppermute(tb[k], 'aux', pairs_of(k))]
    ppermute x4 -> x0, starting transfers between devices: 5.74 us -> none  [the longest x3 5.65 us: body(): lax.ppermute(pat, 'aux', pairs_of(2 * dx))]
    ppermute x3, waiting for transfers between devices: 8.45 us -> 3.16 us  [body(): lax.ppermute(line, 'orb', orb_pairs(dy, 0))]
    pallas_call x5 -> x4, Pallas kernels: 36.4 us -> 33.4 us  [the longest x1 12.5 us: first_products(): pl.pallas_call(first_kernel, in_specs=[sspec(), vspec(), vspec()] + [vspe...]
  transfers between devices with their start and end apart: 31 -> 27, of which waited for: 18 -> 14; matrix products, arithmetic and copies ran while one was open for 0% -> 2% of each run, Pallas kernels for 14% -> 20%
where the time goes in v3:
time: 232 us; the launch traced here: 231 us
  waiting for transfers between devices  109 us (47%)
  Pallas kernels  57.9 us (25%)
  starting transfers between devices  52.7 us (23%)
  other arithmetic  8.19 us (4%)
  local copies, waits for them, and re-layouts  3.85 us (2%)
    ppermute x7, waiting for transfers between devices, body(): lax.ppermute(us[k], 'aux', pairs_of(k))  40.2 us
    ppermute x7, waiting for transfers between devices, body(): lax.ppermute(tb[k], 'aux', pairs_of(k))  26.7 us
    all_to_all x1, waiting for transfers between devices, body(): part = lax.all_to_all(part, 'orb', split_axis=0, concat_axis=0, tiled=True)  25.1 us
    pallas_call x1, Pallas kernels, second_products(): pl.pallas_call(second_kernel, in_specs=[sspec(), sspec(), vspec(), vspec(...  13.6 us
    pallas_call x1, Pallas kernels, first_products(): pl.pallas_call(first_kernel, in_specs=[sspec(), vspec(), vspec()] + [vspe...  12.5 us
    pallas_call x1, Pallas kernels, chi_share(): pl.pallas_call(chi_kernel, grid=(5,), in_specs=[sspec(), vspec()] + [vspe...  10.9 us
    pallas_call x1, Pallas kernels, greens(): pl.pallas_call(greens_kernel, in_specs=[sspec()] * 3 + [vspec()] * 3, out...  8.87 us
    ppermute x7, starting transfers between devices, body(): lax.ppermute(tb[k], 'aux', pairs_of(k))  8.59 us
  transfers between devices with their start and end apart: 27, of which 14 were waited for; matrix products, arithmetic and copies ran while one was open for 2% of the time, Pallas kernels for 20%

profile of v3, /device:TPU:0, one launch (start us, length us, event | category | flops | bytes accessed | tf_op | source)
XLA Modules:
  0.0 231.4 jit_solution(7218597369374091037)
XLA Ops:
  2.5 2.1 collective-permute-start
  4.5 3.6 %collective-permute-start.1 = (bf16[8,4096]{1,0:T(8,128)(2,1)S(1)}, bf16[8,4096]{1,0:T(8,128)(2,1)S(1)}, u32[]{:S(2)}, u32[]{:S(2)}) collective-permute-start(bf16[8,4096]{1,0:T(8,128)(2,1)S(1)} %pad_maximum_fusion.2), channel_id=1, source_target_pairs={{0,2},{1,3},{2,0},{3,1},{4,6},{5,7},{6,4},{7,5},{8,10},{9,11},{10,... | collective-permute-start | bytes 196616 | tf_op jit(solution)/shard_map/ppermute | solution.py:362
  9.1 2.2 collective-permute-done.1
  12.4 1.6 collective-permute-start.3
  14.1 2.9 %collective-permute-start.4 = (bf16[4,8,4096]{2,1,0:T(8,128)(2,1)S(1)}, bf16[4,8,4096]{2,1,0:T(8,128)(2,1)S(1)}, u32[]{:S(2)}, u32[]{:S(2)}) collective-permute-start(bf16[4,8,4096]{2,1,0:T(8,128)(2,1)S(1)} %pad_maximum_fusion.1), channel_id=1, source_target_pairs={{0,8},{1,9},{2,10},{3,11},{4,12},{5,13},{6,14},{7,15},{8,0},{9,1},... | collective-permute-start | bytes 786440 | tf_op jit(solution)/shard_map/ppermute | solution.py:363
  17.0 1.3 collective-permute-start.5
  18.3 5.7 %row_slabs.1 = bf16[16,30,16,256]{3,2,1,0:T(8,128)(2,1)} custom-call(bf16[10,3,16,4096]{3,2,1,0:T(8,128)(2,1)} %bitcast.41), custom_call_target="tpu_custom_call" | custom-call | bytes 8000000 | tf_op jit(solution)/shard_map/row_slabs/pallas_call | solution.py:67
  24.0 3.2 %collective-permute-done.4 = bf16[4,8,4096]{2,1,0:T(8,128)(2,1)S(1)} collective-permute-done((bf16[4,8,4096]{2,1,0:T(8,128)(2,1)S(1)}, bf16[4,8,4096]{2,1,0:T(8,128)(2,1)S(1)}, u32[]{:S(2)}, u32[]{:S(2)}) %collective-permute-start.4) | collective-permute-done | bytes 262176 | tf_op jit(solution)/shard_map/ppermute | solution.py:363
  27.2 5.7 %all-to-all-start.1 = ((bf16[16,30,16,256]{3,2,1,0:T(8,128)(2,1)}), bf16[16,30,16,256]{3,2,1,0:T(8,128)(2,1)}, u32[]{:S(2)}, u32[]{:S(2)}) async-start(bf16[16,30,16,256]{3,2,1,0:T(8,128)(2,1)} %row_slabs.1), calls=%async_computation.1 | async-start | bytes 7864320 | tf_op jit(solution)/shard_map/all_to_all | solution.py:365
  34.1 6.3 %block_pairs.1 = (bf16[2,3,10,32,128]{4,3,2,1,0:T(8,128)(2,1)}, bf16[2,3,10,32,128]{4,3,2,1,0:T(8,128)(2,1)}, bf16[2,3,10,32,128]{4,3,2,1,0:T(8,128)(2,1)}, bf16...) custom-call(s32[2]{0:T(128)} %pad_add_fusion.pos, ...), custom_call_target="tpu_custom_call" | custom-call | flops 1000000000 | bytes 8000000 | tf_op jit(solution)/shard_map/block_pairs/pallas_call | solution.py:104
  41.4 1.9 collective-permute-start.11
  44.5 1.6 collective-permute-start.7
  46.1 9.6 %collective-permute-done.10.rest_5_ = bf16[2,3,10,32,128]{4,3,2,1,0:T(8,128)(2,1)S(1)} collective-permute-done((bf16[2,3,10,32,128]{4,3,2,1,0:T(8,128)(2,1)}, bf16[2,3,10,32,128]{4,3,2,1,0:T(8,128)(2,1)S(1)}, u32[]{:S(2)}, u32[]{:S(2)}) %collective-permute-start.10) | collective-permute-done | bytes 491552 | tf_op jit(solution)/shard_map/ppermute | solution.py:368
  55.8 8.1 %collective-permute-done.11.rest_6_ = bf16[2,3,10,32,128]{4,3,2,1,0:T(8,128)(2,1)S(1)} collective-permute-done((bf16[2,3,10,32,128]{4,3,2,1,0:T(8,128)(2,1)}, bf16[2,3,10,32,128]{4,3,2,1,0:T(8,128)(2,1)S(1)}, u32[]{:S(2)}, u32[]{:S(2)}) %collective-permute-start.11) | collective-permute-done | bytes 491552 | tf_op jit(solution)/shard_map/ppermute | solution.py:368
  63.9 2.9 %collective-permute-start.9 = (bf16[2,3,10,32,128]{4,3,2,1,0:T(8,128)(2,1)}, bf16[2,3,10,32,128]{4,3,2,1,0:T(8,128)(2,1)}, u32[]{:S(2)}, u32[]{:S(2)}) collective-permute-start(bf16[2,3,10,32,128]{4,3,2,1,0:T(8,128)(2,1)} %get-tuple-element.39), channel_id=1, source_target_pairs={{0,64},{16,80},{32,96},{48,112},{64,0},{80,16},{96,32},{112,48},{1... | collective-permute-start | bytes 1474568 | tf_op jit(solution)/shard_map/ppermute | solution.py:368
  67.1 2.6 %reshape.51.g_ref = bf16[16,6,64,64]{3,2,1,0:T(8,128)(2,1)} reshape(bf16[16,6,4096]{2,1,0:T(8,128)(2,1)S(1)} %pad_maximum_fusion) | data formatting | bytes 1572864 | tf_op jit(solution)/shard_map/reshape | solution.py:369
  69.7 8.9 %greens.1 = (bf16[16,3,256,256]{3,2,1,0:T(8,128)(2,1)}, bf16[2,192,192]{2,1,0:T(8,128)(2,1)}) custom-call(s32[2]{0:T(128)} %pad_add_fusion.pos, s32[16]{0:T(128)} %size.1, s32[2048]{0:T(1024)} %fusion.7.meta.pat, bf16[16,6,64,64]{3,2,1,0:T(8,128)(2,1)} %reshape.51.g_ref, bf16[2,32,64]{2,1,0:T(8,128)(2,1)} %constant.57.clone.rows_ref, ...), custom_call_target="tpu_custom_call" | custom-call | flops 1000000 | bytes 8000000 | tf_op jit(solution)/shard_map/greens/pallas_call | solution.py:175
  78.6 8.9 %collective-permute-done.9.rest_4_ = bf16[2,3,10,32,128]{4,3,2,1,0:T(8,128)(2,1)} collective-permute-done((bf16[2,3,10,32,128]{4,3,2,1,0:T(8,128)(2,1)}, bf16[2,3,10,32,128]{4,3,2,1,0:T(8,128)(2,1)}, u32[]{:S(2)}, u32[]{:S(2)}) %collective-permute-start.9) | collective-permute-done | bytes 491552 | tf_op jit(solution)/shard_map/ppermute | solution.py:368
  87.5 12.5 %first.1 = bf16[16,6,80,256]{3,2,1,0:T(8,128)(2,1)} custom-call(s32[2]{0:T(128)} %pad_add_fusion.pos, bf16[256,256]{1,0:T(8,128)(2,1)} %constant.56.clone.perm, bf16[2,192,192]{2,1,0:T(8,128)(2,1)} %get-tuple-element.34.w_ref, bf16[2,3,10,32,128]{4,3,2,1,0:T(8,128)(2,1)} %get-tuple-element.35.rest_0_, ...), custom_call_target="tpu_custom_call" | custom-call | flops 3000000000 | bytes 8000000 | tf_op jit(solution)/shard_map/first/pallas_call | solution.py:283
  100.0 7.2 %all-to-all-start = ((bf16[16,6,80,256]{3,2,1,0:T(8,128)(2,1)}), bf16[16,6,80,256]{3,2,1,0:T(8,128)(2,1)}, u32[]{:S(2)}, u32[]{:S(2)}) async-start(bf16[16,6,80,256]{3,2,1,0:T(8,128)(2,1)} %first.1), calls=%async_computation | async-start | bytes 7864320 | tf_op jit(solution)/shard_map/all_to_all | solution.py:374
  107.3 13.6 %second.1 = (bf16[6,160,256]{2,1,0:T(8,128)(2,1)}, bf16[6,160,256]{2,1,0:T(8,128)(2,1)}, bf16[6,160,256]{2,1,0:T(8,128)(2,1)}, bf16[6,160,256]{2,1,0:T(8,128)(2,...) custom-call(s32[2]{0:T(128)} %pad_add_fusion.pos, ...), custom_call_target="tpu_custom_call" | custom-call | flops 4000000000 | bytes 15000000 | tf_op jit(solution)/shard_map/second/pallas_call | solution.py:225
  121.1 4.2 %collective-permute-start.16 = (bf16[6,160,256]{2,1,0:T(8,128)(2,1)}, bf16[6,160,256]{2,1,0:T(8,128)(2,1)S(1)}, u32[]{:S(2)}, u32[]{:S(2)}) collective-permute-start(bf16[6,160,256]{2,1,0:T(8,128)(2,1)} %get-tuple-element.49), channel_id=1, source_target_pairs={{0,64},{16,80},{32,96},{48,112},{64,0},{80,16},{96,32},{112,48},{1... | collective-permute-start | bytes 1474568 | tf_op jit(solution)/shard_map/ppermute | solution.py:375
  125.4 2.0 collective-permute-start.18
  127.3 9.0 %collective-permute-done.14.rest_2_ = bf16[6,160,256]{2,1,0:T(8,128)(2,1)S(1)} collective-permute-done((bf16[6,160,256]{2,1,0:T(8,128)(2,1)}, bf16[6,160,256]{2,1,0:T(8,128)(2,1)S(1)}, u32[]{:S(2)}, u32[]{:S(2)}) %collective-permute-start.14) | collective-permute-done | bytes 491552 | tf_op jit(solution)/shard_map/ppermute | solution.py:375
  136.3 30.7 %collective-permute-done.15.rest_3_ = bf16[6,160,256]{2,1,0:T(8,128)(2,1)S(1)} collective-permute-done((bf16[6,160,256]{2,1,0:T(8,128)(2,1)}, bf16[6,160,256]{2,1,0:T(8,128)(2,1)S(1)}, u32[]{:S(2)}, u32[]{:S(2)}) %collective-permute-start.15) | collective-permute-done | bytes 491552 | tf_op jit(solution)/shard_map/ppermute | solution.py:375
  168.6 10.9 %chi.1 = (f32[16,40,1280]{2,1,0:T(8,128)}, f32[16,40,1280]{2,1,0:T(8,128)}) custom-call(s32[2]{0:T(128)} %pad_add_fusion.pos, bf16[16,6,80,256]{3,2,1,0:T(8,128)(2,1)} %all-to-all-done.first_ref, bf16[6,160,256]{2,1,0:T(8,128)(2,1)} %get-tuple-element.45.rest_0_, bf16[6,160,256]{2,1,0:T(8,128)(2,1)} %copy-done.2, bf16[6,160,256]{2,1,0:T(8,128)(2,1)} %copy-done.3, ...), custom_call_target="tpu_custom_call" | custom-call | flops 5000000000 | bytes 15000000 | tf_op jit(solution)/shard_map/chi/pallas_call | solution.py:323
  179.8 5.7 %collective-permute-done.20 = f32[16,40,1280]{2,1,0:T(8,128)S(1)} collective-permute-done((f32[16,40,1280]{2,1,0:T(8,128)}, f32[16,40,1280]{2,1,0:T(8,128)S(1)}, u32[]{:S(2)}, u32[]{:S(2)}) %collective-permute-start.20) | collective-permute-done | bytes 3276832 | tf_op jit(solution)/shard_map/ppermute | solution.py:378
  185.5 3.6 %add_convert_fusion = bf16[16,40,1280]{2,1,0:T(8,128)(2,1)} fusion(f32[16,40,1280]{2,1,0:T(8,128)} %get-tuple-element.53, f32[16,40,1280]{2,1,0:T(8,128)S(1)} %collective-permute-done.20), kind=kLoop, calls=%fused_computation.1 | loop fusion | flops 1638400 | bytes 8192000 | tf_op jit(solution)/shard_map/convert_element_type | solution.py:378
  189.0 8.3 %all-to-all-start.2 = ((bf16[16,40,1280]{2,1,0:T(8,128)(2,1)}), bf16[16,40,1280]{2,1,0:T(8,128)(2,1)S(1)}, u32[]{:S(2)}, u32[]{:S(2)}) async-start(bf16[16,40,1280]{2,1,0:T(8,128)(2,1)} %add_convert_fusion), calls=%async_computation.2 | async-start | bytes 3276800 | tf_op jit(solution)/shard_map/all_to_all | solution.py:379
  197.4 25.1 %all-to-all-done.2 = bf16[16,40,1280]{2,1,0:T(8,128)(2,1)S(1)} async-done(((bf16[16,40,1280]{2,1,0:T(8,128)(2,1)}), bf16[16,40,1280]{2,1,0:T(8,128)(2,1)S(1)}, u32[]{:S(2)}, u32[]{:S(2)}) %all-to-all-start.2) | async-done | bytes 1638432 | tf_op jit(solution)/shard_map/all_to_all | solution.py:379
  223.3 3.1 %collective-permute-start.22 = (f32[10,1280]{1,0:T(8,128)S(1)}, f32[10,1280]{1,0:T(8,128)S(1)}, u32[]{:S(2)}, u32[]{:S(2)}) collective-permute-start(f32[10,1280]{1,0:T(8,128)S(1)} %get-tuple-element.57), channel_id=1, source_target_pairs={{0,64},{16,80},{32,96},{48,112},{64,0},{80,16},{96,32},{112,48},{1... | collective-permute-start | bytes 153608 | tf_op jit(solution)/shard_map/ppermute | solution.py:385
  226.4 2.2 collective-permute-done.21
  (68 shorter events, 14.0 us)
Async XLA Ops:
  2.5 6.7 %collective-permute-start = (bf16[8,4096]{1,0:T(8,128)(2,1)S(1)}, bf16[8,4096]{1,0:T(8,128)(2,1)S(1)}, u32[]{:S(2)}, u32[]{:S(2)}) collective-permute-start(bf16[8,4096]{1,0:T(8,128)(2,1)S(1)} %pad_maximum_fusion.2), channel_id=1, source_target_pairs={{0,1},{1,2},{2,3},{3,0},{4,5},{5,6},{6,7},{7,4},{8,9},{9,10},{10,1... | collective-permute-start | bytes 196616 | tf_op jit(solution)/shard_map/ppermute | solution.py:362
  4.5 6.8 %collective-permute-start.1 = (bf16[8,4096]{1,0:T(8,128)(2,1)S(1)}, bf16[8,4096]{1,0:T(8,128)(2,1)S(1)}, u32[]{:S(2)}, u32[]{:S(2)}) collective-permute-start(bf16[8,4096]{1,0:T(8,128)(2,1)S(1)} %pad_maximum_fusion.2), channel_id=1, source_target_pairs={{0,2},{1,3},{2,0},{3,1},{4,6},{5,7},{6,4},{7,5},{8,10},{9,11},{10,... | collective-permute-start | bytes 196616 | tf_op jit(solution)/shard_map/ppermute | solution.py:362
  8.1 4.3 %collective-permute-start.2 = (bf16[8,4096]{1,0:T(8,128)(2,1)S(1)}, bf16[8,4096]{1,0:T(8,128)(2,1)S(1)}, u32[]{:S(2)}, u32[]{:S(2)}) collective-permute-start(bf16[8,4096]{1,0:T(8,128)(2,1)S(1)} %pad_maximum_fusion.2), channel_id=1, source_target_pairs={{0,3},{1,0},{2,1},{3,2},{4,7},{5,4},{6,5},{7,6},{8,11},{9,8},{10,9... | collective-permute-start | bytes 196616 | tf_op jit(solution)/shard_map/ppermute | solution.py:362
  12.4 11.6 %collective-permute-start.3 = (bf16[4,8,4096]{2,1,0:T(8,128)(2,1)S(1)}, bf16[4,8,4096]{2,1,0:T(8,128)(2,1)S(1)}, u32[]{:S(2)}, u32[]{:S(2)}) collective-permute-start(bf16[4,8,4096]{2,1,0:T(8,128)(2,1)S(1)} %pad_maximum_fusion.1), channel_id=1, source_target_pairs={{0,4},{1,5},{2,6},{3,7},{4,8},{5,9},{6,10},{7,11},{8,12},{9,13},{1... | collective-permute-start | bytes 786440 | tf_op jit(solution)/shard_map/ppermute | solution.py:363
  14.1 13.1 %collective-permute-start.4 = (bf16[4,8,4096]{2,1,0:T(8,128)(2,1)S(1)}, bf16[4,8,4096]{2,1,0:T(8,128)(2,1)S(1)}, u32[]{:S(2)}, u32[]{:S(2)}) collective-permute-start(bf16[4,8,4096]{2,1,0:T(8,128)(2,1)S(1)} %pad_maximum_fusion.1), channel_id=1, source_target_pairs={{0,8},{1,9},{2,10},{3,11},{4,12},{5,13},{6,14},{7,15},{8,0},{9,1},... | collective-permute-start | bytes 786440 | tf_op jit(solution)/shard_map/ppermute | solution.py:363
  17.0 10.2 %collective-permute-start.5 = (bf16[4,8,4096]{2,1,0:T(8,128)(2,1)S(1)}, bf16[4,8,4096]{2,1,0:T(8,128)(2,1)S(1)}, u32[]{:S(2)}, u32[]{:S(2)}) collective-permute-start(bf16[4,8,4096]{2,1,0:T(8,128)(2,1)S(1)} %pad_maximum_fusion.1), channel_id=1, source_target_pairs={{0,12},{1,13},{2,14},{3,15},{4,0},{5,1},{6,2},{7,3},{8,4},{9,5},{1... | collective-permute-start | bytes 786440 | tf_op jit(solution)/shard_map/ppermute | solution.py:363
  27.2 72.8 %all-to-all-start.1 = ((bf16[16,30,16,256]{3,2,1,0:T(8,128)(2,1)}), bf16[16,30,16,256]{3,2,1,0:T(8,128)(2,1)}, u32[]{:S(2)}, u32[]{:S(2)}) async-start(bf16[16,30,16,256]{3,2,1,0:T(8,128)(2,1)} %row_slabs.1), calls=%async_computation.1 | async-start | bytes 7864320 | tf_op jit(solution)/shard_map/all_to_all | solution.py:365
  40.4 15.3 %collective-permute-start.10 = (bf16[2,3,10,32,128]{4,3,2,1,0:T(8,128)(2,1)}, bf16[2,3,10,32,128]{4,3,2,1,0:T(8,128)(2,1)S(1)}, u32[]{:S(2)}, u32[]{:S(2)}) collective-permute-start(bf16[2,3,10,32,128]{4,3,2,1,0:T(8,128)(2,1)} %get-tuple-element.40), channel_id=1, source_target_pairs={{0,80},{16,64},{32,112},{48,96},{64,16},{80,0},{96,48},{112,32},{1... | collective-permute-start | bytes 1474568 | tf_op jit(solution)/shard_map/ppermute | solution.py:368
  41.4 22.5 %collective-permute-start.11 = (bf16[2,3,10,32,128]{4,3,2,1,0:T(8,128)(2,1)}, bf16[2,3,10,32,128]{4,3,2,1,0:T(8,128)(2,1)S(1)}, u32[]{:S(2)}, u32[]{:S(2)}) collective-permute-start(bf16[2,3,10,32,128]{4,3,2,1,0:T(8,128)(2,1)} %get-tuple-element.41), channel_id=1, source_target_pairs={{0,96},{16,112},{32,0},{48,16},{64,32},{80,48},{96,64},{112,80},{1... | collective-permute-start | bytes 1474568 | tf_op jit(solution)/shard_map/ppermute | solution.py:368
  43.4 35.2 %collective-permute-start.12 = (bf16[2,3,10,32,128]{4,3,2,1,0:T(8,128)(2,1)}, bf16[2,3,10,32,128]{4,3,2,1,0:T(8,128)(2,1)}, u32[]{:S(2)}, u32[]{:S(2)}) collective-permute-start(bf16[2,3,10,32,128]{4,3,2,1,0:T(8,128)(2,1)} %get-tuple-element.42), channel_id=1, source_target_pairs={{0,112},{16,96},{32,16},{48,0},{64,48},{80,32},{96,80},{112,64},{1... | collective-permute-start | bytes 1474568 | tf_op jit(solution)/shard_map/ppermute | solution.py:368
  44.4 34.1 %collective-permute-start.6 = (bf16[2,3,10,32,128]{4,3,2,1,0:T(8,128)(2,1)}, bf16[2,3,10,32,128]{4,3,2,1,0:T(8,128)(2,1)}, u32[]{:S(2)}, u32[]{:S(2)}) collective-permute-start(bf16[2,3,10,32,128]{4,3,2,1,0:T(8,128)(2,1)} %get-tuple-element.36), channel_id=1, source_target_pairs={{0,16},{16,0},{32,48},{48,32},{64,80},{80,64},{96,112},{112,96},{1... | collective-permute-start | bytes 1474568 | tf_op jit(solution)/shard_map/ppermute | solution.py:368
  44.5 34.1 %collective-permute-start.7 = (bf16[2,3,10,32,128]{4,3,2,1,0:T(8,128)(2,1)}, bf16[2,3,10,32,128]{4,3,2,1,0:T(8,128)(2,1)}, u32[]{:S(2)}, u32[]{:S(2)}) collective-permute-start(bf16[2,3,10,32,128]{4,3,2,1,0:T(8,128)(2,1)} %get-tuple-element.37), channel_id=1, source_target_pairs={{0,32},{16,48},{32,64},{48,80},{64,96},{80,112},{96,0},{112,16},{1... | collective-permute-start | bytes 1474568 | tf_op jit(solution)/shard_map/ppermute | solution.py:368
  55.8 31.7 %copy-start = (bf16[2,3,10,32,128]{4,3,2,1,0:T(8,128)(2,1)}, bf16[2,3,10,32,128]{4,3,2,1,0:T(8,128)(2,1)S(1)}, u32[]{:S(2)}) copy-start(bf16[2,3,10,32,128]{4,3,2,1,0:T(8,128)(2,1)S(1)} %collective-permute-done.10.rest_5_) | copy-start | bytes 1474564
  55.8 22.8 %collective-permute-start.8 = (bf16[2,3,10,32,128]{4,3,2,1,0:T(8,128)(2,1)}, bf16[2,3,10,32,128]{4,3,2,1,0:T(8,128)(2,1)}, u32[]{:S(2)}, u32[]{:S(2)}) collective-permute-start(bf16[2,3,10,32,128]{4,3,2,1,0:T(8,128)(2,1)} %get-tuple-element.38), channel_id=1, source_target_pairs={{0,48},{16,32},{32,80},{48,64},{64,112},{80,96},{96,16},{112,0},{1... | collective-permute-start | bytes 1474568 | tf_op jit(solution)/shard_map/ppermute | solution.py:368
  63.9 23.6 %copy-start.1 = (bf16[2,3,10,32,128]{4,3,2,1,0:T(8,128)(2,1)}, bf16[2,3,10,32,128]{4,3,2,1,0:T(8,128)(2,1)S(1)}, u32[]{:S(2)}) copy-start(bf16[2,3,10,32,128]{4,3,2,1,0:T(8,128)(2,1)S(1)} %collective-permute-done.11.rest_6_) | copy-start | bytes 1474564
  63.9 23.6 %collective-permute-start.9 = (bf16[2,3,10,32,128]{4,3,2,1,0:T(8,128)(2,1)}, bf16[2,3,10,32,128]{4,3,2,1,0:T(8,128)(2,1)}, u32[]{:S(2)}, u32[]{:S(2)}) collective-permute-start(bf16[2,3,10,32,128]{4,3,2,1,0:T(8,128)(2,1)} %get-tuple-element.39), channel_id=1, source_target_pairs={{0,64},{16,80},{32,96},{48,112},{64,0},{80,16},{96,32},{112,48},{1... | collective-permute-start | bytes 1474568 | tf_op jit(solution)/shard_map/ppermute | solution.py:368
  100.0 67.6 %all-to-all-start = ((bf16[16,6,80,256]{3,2,1,0:T(8,128)(2,1)}), bf16[16,6,80,256]{3,2,1,0:T(8,128)(2,1)}, u32[]{:S(2)}, u32[]{:S(2)}) async-start(bf16[16,6,80,256]{3,2,1,0:T(8,128)(2,1)} %first.1), calls=%async_computation | async-start | bytes 7864320 | tf_op jit(solution)/shard_map/all_to_all | solution.py:374
  120.8 4.5 %collective-permute-start.13 = (bf16[6,160,256]{2,1,0:T(8,128)(2,1)}, bf16[6,160,256]{2,1,0:T(8,128)(2,1)S(1)}, u32[]{:S(2)}, u32[]{:S(2)}) collective-permute-start(bf16[6,160,256]{2,1,0:T(8,128)(2,1)} %get-tuple-element.46), channel_id=1, source_target_pairs={{0,16},{16,0},{32,48},{48,32},{64,80},{80,64},{96,112},{112,96},{1... | collective-permute-start | bytes 1474568 | tf_op jit(solution)/shard_map/ppermute | solution.py:375
  120.8 15.5 %collective-permute-start.14 = (bf16[6,160,256]{2,1,0:T(8,128)(2,1)}, bf16[6,160,256]{2,1,0:T(8,128)(2,1)S(1)}, u32[]{:S(2)}, u32[]{:S(2)}) collective-permute-start(bf16[6,160,256]{2,1,0:T(8,128)(2,1)} %get-tuple-element.47), channel_id=1, source_target_pairs={{0,32},{16,48},{32,64},{48,80},{64,96},{80,112},{96,0},{112,16},{1... | collective-permute-start | bytes 1474568 | tf_op jit(solution)/shard_map/ppermute | solution.py:375
  121.0 46.0 %collective-permute-start.15 = (bf16[6,160,256]{2,1,0:T(8,128)(2,1)}, bf16[6,160,256]{2,1,0:T(8,128)(2,1)S(1)}, u32[]{:S(2)}, u32[]{:S(2)}) collective-permute-start(bf16[6,160,256]{2,1,0:T(8,128)(2,1)} %get-tuple-element.48), channel_id=1, source_target_pairs={{0,48},{16,32},{32,80},{48,64},{64,112},{80,96},{96,16},{112,0},{1... | collective-permute-start | bytes 1474568 | tf_op jit(solution)/shard_map/ppermute | solution.py:375
  121.1 45.9 %collective-permute-start.16 = (bf16[6,160,256]{2,1,0:T(8,128)(2,1)}, bf16[6,160,256]{2,1,0:T(8,128)(2,1)S(1)}, u32[]{:S(2)}, u32[]{:S(2)}) collective-permute-start(bf16[6,160,256]{2,1,0:T(8,128)(2,1)} %get-tuple-element.49), channel_id=1, source_target_pairs={{0,64},{16,80},{32,96},{48,112},{64,0},{80,16},{96,32},{112,48},{1... | collective-permute-start | bytes 1474568 | tf_op jit(solution)/shard_map/ppermute | solution.py:375
  125.4 41.7 %collective-permute-start.17 = (bf16[6,160,256]{2,1,0:T(8,128)(2,1)}, bf16[6,160,256]{2,1,0:T(8,128)(2,1)S(1)}, u32[]{:S(2)}, u32[]{:S(2)}) collective-permute-start(bf16[6,160,256]{2,1,0:T(8,128)(2,1)} %get-tuple-element.50), channel_id=1, source_target_pairs={{0,80},{16,64},{32,112},{48,96},{64,16},{80,0},{96,48},{112,32},{1... | collective-permute-start | bytes 1474568 | tf_op jit(solution)/shard_map/ppermute | solution.py:375
  125.4 42.3 %copy-start.2 = (bf16[6,160,256]{2,1,0:T(8,128)(2,1)}, bf16[6,160,256]{2,1,0:T(8,128)(2,1)S(1)}, u32[]{:S(2)}) copy-start(bf16[6,160,256]{2,1,0:T(8,128)(2,1)S(1)} %collective-permute-done.13.rest_1_) | copy-start | bytes 1474564
  125.4 41.7 %collective-permute-start.18 = (bf16[6,160,256]{2,1,0:T(8,128)(2,1)}, bf16[6,160,256]{2,1,0:T(8,128)(2,1)S(1)}, u32[]{:S(2)}, u32[]{:S(2)}) collective-permute-start(bf16[6,160,256]{2,1,0:T(8,128)(2,1)} %get-tuple-element.51), channel_id=1, source_target_pairs={{0,96},{16,112},{32,0},{48,16},{64,32},{80,48},{96,64},{112,80},{1... | collective-permute-start | bytes 1474568 | tf_op jit(solution)/shard_map/ppermute | solution.py:375
  136.3 31.3 %copy-start.3 = (bf16[6,160,256]{2,1,0:T(8,128)(2,1)}, bf16[6,160,256]{2,1,0:T(8,128)(2,1)S(1)}, u32[]{:S(2)}) copy-start(bf16[6,160,256]{2,1,0:T(8,128)(2,1)S(1)} %collective-permute-done.14.rest_2_) | copy-start | bytes 1474564
  136.3 31.3 %collective-permute-start.19 = (bf16[6,160,256]{2,1,0:T(8,128)(2,1)}, bf16[6,160,256]{2,1,0:T(8,128)(2,1)S(1)}, u32[]{:S(2)}, u32[]{:S(2)}) collective-permute-start(bf16[6,160,256]{2,1,0:T(8,128)(2,1)} %get-tuple-element.52), channel_id=1, source_target_pairs={{0,112},{16,96},{32,16},{48,0},{64,48},{80,32},{96,80},{112,64},{1... | collective-permute-start | bytes 1474568 | tf_op jit(solution)/shard_map/ppermute | solution.py:375
  167.1 1.3 copy-start.7
  179.4 6.1 %collective-permute-start.20 = (f32[16,40,1280]{2,1,0:T(8,128)}, f32[16,40,1280]{2,1,0:T(8,128)S(1)}, u32[]{:S(2)}, u32[]{:S(2)}) collective-permute-start(f32[16,40,1280]{2,1,0:T(8,128)} %get-tuple-element.54), channel_id=1, source_target_pairs={{0,16},{16,0},{32,48},{48,32},{64,80},{80,64},{96,112},{112,96},{1... | collective-permute-start | bytes 9830408 | tf_op jit(solution)/shard_map/ppermute | solution.py:378
  189.0 33.5 %all-to-all-start.2 = ((bf16[16,40,1280]{2,1,0:T(8,128)(2,1)}), bf16[16,40,1280]{2,1,0:T(8,128)(2,1)S(1)}, u32[]{:S(2)}, u32[]{:S(2)}) async-start(bf16[16,40,1280]{2,1,0:T(8,128)(2,1)} %add_convert_fusion), calls=%async_computation.2 | async-start | bytes 3276800 | tf_op jit(solution)/shard_map/all_to_all | solution.py:379
  222.8 5.7 %collective-permute-start.21 = (f32[10,1280]{1,0:T(8,128)S(1)}, f32[10,1280]{1,0:T(8,128)S(1)}, u32[]{:S(2)}, u32[]{:S(2)}) collective-permute-start(f32[10,1280]{1,0:T(8,128)S(1)} %get-tuple-element.55), channel_id=1, source_target_pairs={{0,32},{16,48},{32,64},{48,80},{64,96},{80,112},{96,0},{112,16},{1... | collective-permute-start | bytes 153608 | tf_op jit(solution)/shard_map/ppermute | solution.py:385
  223.3 6.4 %collective-permute-start.22 = (f32[10,1280]{1,0:T(8,128)S(1)}, f32[10,1280]{1,0:T(8,128)S(1)}, u32[]{:S(2)}, u32[]{:S(2)}) collective-permute-start(f32[10,1280]{1,0:T(8,128)S(1)} %get-tuple-element.57), channel_id=1, source_target_pairs={{0,64},{16,80},{32,96},{48,112},{64,0},{80,16},{96,32},{112,48},{1... | collective-permute-start | bytes 153608 | tf_op jit(solution)/shard_map/ppermute | solution.py:385
  226.3 4.4 %collective-permute-start.23 = (f32[10,1280]{1,0:T(8,128)S(1)}, f32[10,1280]{1,0:T(8,128)S(1)}, u32[]{:S(2)}, u32[]{:S(2)}) collective-permute-start(f32[10,1280]{1,0:T(8,128)S(1)} %get-tuple-element.56), channel_id=1, source_target_pairs={{0,96},{16,112},{32,0},{48,16},{64,32},{80,48},{96,64},{112,80},{1... | collective-permute-start | bytes 153608 | tf_op jit(solution)/shard_map/ppermute | solution.py:385
  (4 other events, 3.9 us)

commit v4 on v3

v4 whole, which is shorter than its diff:
```python
import functools

import jax
import jax.numpy as jnp
import numpy as np
from jax import lax
from jax.experimental import pallas as pl
from jax.experimental.pallas import tpu as pltpu
from jax.sharding import PartitionSpec as P

BS = 64
R = 1
W = 3
ABS = 16
NOB = 16
NPD = 10
NG = 10
BF = jnp.bfloat16
F32 = jnp.float32
VLIM = 56 * 1024 * 1024

STEPS = [(k // 2, k % 2) for k in range(8)]


def pairs_of(k):
    dx, dc = STEPS[k]
    return [(i, ((i // 2 + dx) % 4) * 2 + ((i % 2) ^ dc)) for i in range(8)]


def dest_of(a, k):
    dx, dc = STEPS[k]
    return lax.rem(a // 2 + dx, 4) * 2 + (lax.rem(a, 2) if dc == 0 else 1 - lax.rem(a, 2))


def src_of(a, k):
    dx, dc = STEPS[k]
    return lax.rem(a // 2 + 4 - dx, 4) * 2 + (lax.rem(a, 2) if dc == 0 else 1 - lax.rem(a, 2))


def swap16():
    r = np.arange(256)
    m = np.zeros((256, 256), np.float32)
    m[r, (r % 16) * 16 + r // 16] = 1.0
    return jnp.asarray(m, BF)


def vspec():
    return pl.BlockSpec(memory_space=pltpu.VMEM)


def sspec():
    return pl.BlockSpec(memory_space=pltpu.SMEM)


def rows_kernel(x_ref, ta_ref):
    for p in range(2):
        for d in range(W):
            for o in range(16):
                ta_ref[o, p * W + d] = x_ref[p, d, :, 256 * o : 256 * o + 256]


def row_slabs(x):
    return pl.pallas_call(
        rows_kernel,
        grid=(NPD // 2,),
        in_specs=[pl.BlockSpec((2, W, NOB, 4096), lambda i: (i, 0, 0, 0))],
        out_specs=pl.BlockSpec((16, 2 * W, NOB, 256), lambda i: (0, i, 0, 0)),
        out_shape=jax.ShapeDtypeStruct((16, NPD * W, NOB, 256), BF),
        compiler_params=pltpu.CompilerParams(vmem_limit_bytes=VLIM),
        cost_estimate=pl.CostEstimate(flops=0, bytes_accessed=8 * 10**6, transcendentals=0),
        name="row_slabs",
    )(x)


def pairs_kernel(pos, perm, x_ref, *rest):
    tb, s = rest[:8], rest[8]
    a = pos[0]
    for p in range(2):
        for d in range(W):
            x = x_ref[p, d]
            halves = [
                jnp.concatenate([x[:, 128 * (16 * h + c) : 128 * (16 * h + c) + 128] for c in range(16)], axis=0)
                for h in range(2)
            ]
            y = jnp.dot(perm[...], jnp.concatenate(halves, axis=1), preferred_element_type=F32).astype(BF)
            for n in range(NOB):
                part = y[16 * n : 16 * n + 16]
                for h in range(2):
                    s[n, d, p, 16 * h : 16 * h + 16] = part[:, 128 * h : 128 * h + 128]
    for k in range(8):
        t = dest_of(a, k)
        for i in range(2):
            tb[k][i] = s[2 * t + i]


def block_pairs(pos, perm, x):
    return pl.pallas_call(
        pairs_kernel,
        grid=(NPD // 2,),
        in_specs=[
            sspec(),
            pl.BlockSpec((256, 256), lambda i: (0, 0)),
            pl.BlockSpec((2, W, NOB, 4096), lambda i: (i, 0, 0, 0)),
        ],
        out_specs=[pl.BlockSpec((2, W, 2, 32, 128), lambda i: (0, 0, i, 0, 0))] * 8,
        out_shape=[jax.ShapeDtypeStruct((2, W, NPD, 32, 128), BF)] * 8,
        scratch_shapes=[pltpu.VMEM((NOB, W, 2, 32, 128), BF)],
        compiler_params=pltpu.CompilerParams(vmem_limit_bytes=VLIM),
        cost_estimate=pl.CostEstimate(flops=10**9, bytes_accessed=8 * 10**6, transcendentals=0),
        name="block_pairs",
    )(pos, perm, x)


def greens_kernel(pos, size, meta, g_ref, rows_ref, cols_ref, v_ref, w_ref, o_ref):
    a = pos[0]
    row = lax.broadcasted_iota(jnp.int32, (BS, BS), 0)
    col = lax.broadcasted_iota(jnp.int32, (BS, BS), 1)

    def one(n, carry):
        for d in range(W):
            m = n + d - R
            ok = (m >= 0) & (m < NOB)
            if d != R:
                ok = ok & (meta[n * 128 + NG * W + d] > 0)
            rows_in = jnp.where(ok, size[jnp.clip(m, 0, NOB - 1)], 0)
            mask = (row < rows_in) & (col < size[n])
            occ = jnp.where(mask, g_ref[n, d], jnp.zeros((BS, BS), BF))
            v = jnp.where(mask, g_ref[n, W + d], jnp.zeros((BS, BS), BF))
            for g in range(2):
                t = jnp.dot(rows_ref[g], occ, preferred_element_type=F32).astype(BF)
                o_ref[n, d, 32 * g : 32 * g + 32] = jnp.dot(
                    t, cols_ref[g], preferred_element_type=F32
                ).astype(BF)
            v_ref[n, d] = jnp.concatenate([v, v], axis=1)
        return carry

    lax.fori_loop(0, NOB, one, 0)
    z = jnp.zeros((32, 64), BF)
    for i in range(2):
        for g in range(2):
            for e in range(W):
                cols = []
                for d in range(W):
                    f = e - d + 1
                    if f < 0 or f >= W:
                        cols.append(z)
                        continue
                    m = 2 * a + i + d - 1
                    ok = (m >= 0) & (m < NOB)
                    mc = jnp.clip(m, 0, NOB - 1)
                    v = o_ref[mc, f, 32 * g : 32 * g + 32]
                    cols.append(jnp.where(ok, v, z))
                row = (g * W + e) * 32
                w_ref[i, row : row + 32, :] = jnp.concatenate(cols, axis=1)


def greens(pos, size, meta, g, rows, cols):
    return pl.pallas_call(
        greens_kernel,
        in_specs=[sspec()] * 3 + [vspec()] * 3,
        out_specs=[vspec(), vspec()],
        scratch_shapes=[pltpu.VMEM((NOB, W, 64, 64), BF)],
        out_shape=[
            jax.ShapeDtypeStruct((NOB, W, BS, 128), BF),
            jax.ShapeDtypeStruct((2, 192, 192), BF),
        ],
        compiler_params=pltpu.CompilerParams(vmem_limit_bytes=VLIM),
        cost_estimate=pl.CostEstimate(flops=10**6, bytes_accessed=8 * 10**6, transcendentals=0),
        name="greens",
    )(pos, size, meta, g, rows, cols)


def second_kernel(pos, pat, perm, ta_ref, v_ref, *rest):
    outs, s, kb = rest[:8], rest[8], rest[9]
    a = pos[0]
    low = lax.broadcasted_iota(jnp.int32, (BS, 128), 1) < 64
    zero = jnp.zeros((BS, 128), BF)
    kb[...] = jnp.zeros(kb.shape, BF)
    s[0] = jnp.zeros(s.shape[1:], BF)
    s[NOB + 1] = jnp.zeros(s.shape[1:], BF)

    def regroup(g, carry):
        for d in range(W):
            x = ta_ref[pl.ds(16 * g, 16), d].reshape(256, 256)
            y = jnp.dot(perm[...], x, preferred_element_type=F32)
            for n in range(NOB):
                keep = pat[n * 128 + g * W + d] > 0
                part = y[16 * n : 16 * n + 16]
                s[n + 1, d, pl.ds(pl.multiple_of(16 * g, 16), 16)] = jnp.where(
                    keep, part, jnp.zeros_like(part)
                ).astype(BF)
        return carry

    lax.fori_loop(0, NG, regroup, 0)
    for k in range(8):
        t = dest_of(a, k)

        def one(i, carry, k=k, t=t):
            n = 2 * t + i
            for d in range(W):
                v = v_ref[n, d]
                lo, hi = jnp.where(low, v, zero), jnp.where(low, zero, v)
                for q in range(4):
                    row, col = 256 * d + 64 * q, 128 * (q // 2)
                    kb[row : row + 64, col : col + 128] = hi if q % 2 else lo
            for e in range(W):
                ds = [d for d in range(W) if 0 <= e - d + 1 < W]
                lhs = jnp.concatenate([s[n + d, e - d + 1] for d in ds], axis=1)
                rhs = kb[256 * ds[0] : 256 * ds[-1] + 256]
                outs[k][i * W + e] = jnp.dot(lhs, rhs, preferred_element_type=F32).astype(BF)
            return carry

        lax.fori_loop(0, 2, one, 0)


def second_products(pos, pat, perm, ta, v):
    return pl.pallas_call(
        second_kernel,
        in_specs=[sspec(), sspec(), vspec(), vspec(), vspec()],
        out_specs=[vspec()] * 8,
        out_shape=[jax.ShapeDtypeStruct((2 * W, 160, 256), BF)] * 8,
        scratch_shapes=[pltpu.VMEM((NOB + 2, W, 160, 256), BF), pltpu.VMEM((256 * W, 256), BF)],
        compiler_params=pltpu.CompilerParams(vmem_limit_bytes=VLIM),
        cost_estimate=pl.CostEstimate(flops=4 * 10**9, bytes_accessed=15 * 10**6, transcendentals=0),
        name="second",
    )(pos, pat, perm, ta, v)


def first_kernel(pos, pat, perm, w_ref, *rest):
    tb, out, s = rest[:8], rest[8], rest[9]
    a, o = pos[0], pos[1]
    lane = lax.broadcasted_iota(jnp.int32, (96, NPD * 128), 1)
    low = lax.rem(lane, 128) < 64
    for k in range(8):
        src = src_of(a, k)
        base = lax.rem(src, 2) * 40 + (src // 2) * 10

        def one(i, carry, k=k, base=base):
            n = 2 * a + i
            columns = []
            for p in range(NPD):
                rows = []
                for d in range(W):
                    keep = pat[(k * NOB + n) * 32 + lax.div(o * NPD + p, ABS) * W + d] > 0
                    x = tb[k][i, d, p]
                    x = jnp.where(keep, x, jnp.zeros_like(x))
                    rows.append(x)
                    rows.append(jnp.concatenate([x[:, 64:], x[:, :64]], axis=1))
                columns.append(jnp.concatenate(rows, axis=0))
            y = jnp.dot(w_ref[i], jnp.concatenate(columns, axis=1), preferred_element_type=F32)
            y = jnp.where(low, y[:96], y[96:]).astype(BF)
            for p in range(NPD):
                s[i, base + p] = y[:, 128 * p : 128 * p + 128]
            return carry

        lax.fori_loop(0, 2, one, 0)

    def regroup(j, carry):
        i = j // 5
        g = lax.rem(j, 5)
        tiles = s[i, pl.ds(16 * g, 16)]
        for e in range(W):
            x = jnp.concatenate(
                [tiles[:, 32 * e + 16 * h : 32 * e + 16 * h + 16].reshape(256, 128) for h in range(2)], axis=1
            )
            y = jnp.dot(perm[...], x, preferred_element_type=F32).astype(BF)
            for h in range(2):
                for q in range(16):
                    qq = 16 * h + q
                    out[qq // 2, i * W + e, pl.ds(pl.multiple_of(16 * g, 16), 16),
                        128 * (qq % 2) : 128 * (qq % 2) + 128] = y[16 * q : 16 * q + 16, 128 * h : 128 * h + 128]
        return carry

    lax.fori_loop(0, 10, regroup, 0)


def first_products(pos, pat, perm, w, tb):
    return pl.pallas_call(
        first_kernel,
        in_specs=[sspec(), sspec(), vspec(), vspec()] + [vspec()] * 8,
        out_specs=vspec(),
        out_shape=jax.ShapeDtypeStruct((16, 2 * W, 80, 256), BF),
        scratch_shapes=[pltpu.VMEM((2, 80, 96, 128), BF)],
        compiler_params=pltpu.CompilerParams(vmem_limit_bytes=VLIM),
        cost_estimate=pl.CostEstimate(flops=3 * 10**9, bytes_accessed=8 * 10**6, transcendentals=0),
        name="first",
    )(pos, pat, perm, w, *tb)


HALVES = [(0, 1, 6, 7), (4, 5, 2, 3)]


def chi_kernel(half, pos, first_ref, *rest):
    us, theirs, mine, rhs = rest[:4], rest[4], rest[5], rest[6]
    core = lax.rem(pos[0], 2)
    for j, k in enumerate(HALVES[half]):
        c = core if k % 2 == 0 else 1 - core
        row = pl.multiple_of((j // 2) * 320 + c * 160, 32)
        for kk in range(6):
            rhs[pl.ds(row, 160), 256 * kk : 256 * kk + 256] = us[j][kk]
    for c0, cw in ((0, 256), (256, 256), (512, 128)):
        lhs = jnp.concatenate([first_ref[:, kk].reshape(1280, 256) for kk in range(6)], axis=1)
        r = lax.dot_general(
            lhs, rhs[c0 : c0 + cw], (((1,), (1,)), ((), ())), preferred_element_type=F32
        )
        for b in range(16):
            lo, hi = r[80 * b : 80 * b + 40], r[80 * b + 40 : 80 * b + 80]
            mine[b, :, c0 : c0 + cw] = jnp.where(core == 0, lo, hi)
            theirs[b, :, c0 : c0 + cw] = jnp.where(core == 0, hi, lo).astype(BF)


def chi_share(half, pos, first, us):
    return pl.pallas_call(
        functools.partial(chi_kernel, half),
        in_specs=[sspec(), vspec()] + [vspec()] * 4,
        out_specs=[vspec()] * 2,
        out_shape=[jax.ShapeDtypeStruct((16, 40, 640), BF), jax.ShapeDtypeStruct((16, 40, 640), F32)],
        scratch_shapes=[pltpu.VMEM((640, 1536), BF)],
        compiler_params=pltpu.CompilerParams(vmem_limit_bytes=VLIM),
        cost_estimate=pl.CostEstimate(flops=25 * 10**8, bytes_accessed=10 * 10**6, transcendentals=0),
        name="chi",
    )(pos, first, *[us[k] for k in HALVES[half]])


def deinterleave():
    rows = np.zeros((2, 32, 64), np.float32)
    cols = np.zeros((2, 64, 64), np.float32)
    for g in range(2):
        for q in range(32):
            rows[g, q, 2 * q + g] = 1.0
        for j in range(2):
            for c in range(32):
                cols[g, 2 * c + (g ^ j), 32 * j + c] = 1.0
    return jnp.asarray(rows, BF), jnp.asarray(cols, BF)


def body(three_center, atom_size, tensor_pattern, green_occ, green_virt, green_pattern):
    a, o = lax.axis_index("aux"), lax.axis_index("orb")
    pos = jnp.stack([a, o]).astype(jnp.int32)
    perm = swap16()
    rows, cols = deinterleave()
    x = three_center.transpose(0, 2, 1, 3)

    marks = jnp.concatenate([tensor_pattern.reshape(1, NG * W), green_pattern], axis=1).astype(BF)
    marks = jnp.pad(marks, ((0, 1), (0, 4096 - NG * W - W)))
    own = jnp.concatenate([green_occ[0], green_virt[0], marks], axis=0)
    every = jnp.broadcast_to(own[None], (NOB,) + own.shape)
    every = lax.all_to_all(every, "orb", split_axis=0, concat_axis=0, tiled=True)

    *tb, x = lax.optimization_barrier((*block_pairs(pos, perm, x), x))
    tb = [tb[0]] + [lax.ppermute(tb[k], "aux", pairs_of(k)) for k in range(1, 8)]
    every, tb[1], tb[2], tb[6], ta = lax.optimization_barrier((every, tb[1], tb[2], tb[6], row_slabs(x)))
    ta = lax.all_to_all(ta, "orb", split_axis=0, concat_axis=0, tiled=True)

    marks = every[:, 2 * W, :128]
    meta = marks.astype(jnp.int32).reshape(-1)
    pat = jnp.stack([marks, lax.ppermute(marks, "aux", pairs_of(1))])
    pat = jnp.stack([pat] + [lax.ppermute(pat, "aux", pairs_of(2 * dx)) for dx in range(1, 4)])
    pat = pat[..., :32].astype(jnp.int32).reshape(-1)
    blocks = every[:, : 2 * W].reshape(NOB, 2 * W, BS, BS)
    v, w = greens(pos, atom_size, meta, blocks, rows, cols)

    first = first_products(pos, pat, perm, w, tb)
    first = lax.all_to_all(first, "orb", split_axis=0, concat_axis=0, tiled=True)
    us = second_products(pos, meta, perm, ta.reshape(160, W, NOB, 256), v)
    us = [us[0]] + [lax.ppermute(us[k], "aux", pairs_of(k)) for k in range(1, 8)]

    parts = []
    for half in range(2):
        theirs, mine = chi_share(half, pos, first, us)
        parts.append(mine + lax.ppermute(theirs, "aux", pairs_of(1)).astype(F32))
    part = jnp.concatenate(parts, axis=2).astype(BF)
    part = lax.all_to_all(part, "orb", split_axis=0, concat_axis=0, tiled=True)
    part = jnp.sum(part.astype(F32), axis=0)
    x = a // 2
    part = lax.dynamic_slice(
        jnp.concatenate([part, part], axis=1), (0, lax.rem(4 - x, 4) * 320), (40, 1280)
    ).reshape(4, NPD, 1280)
    total = lax.dynamic_index_in_dim(part, x, 0, keepdims=False)
    for dx in range(1, 4):
        piece = lax.dynamic_index_in_dim(part, lax.rem(x + dx, 4), 0, keepdims=False)
        total = total + lax.ppermute(piece, "aux", pairs_of(2 * dx))
    return total


def solution(mesh):
    return jax.shard_map(
        body,
        mesh=mesh,
        in_specs=(
            P(("aux", "orb"), None, None, None),
            P(),
            P("aux", "orb", None),
            P("orb", None, None),
            P("orb", None, None),
            P("orb", None),
        ),
        out_specs=P(("aux", "orb"), None),
        check_vma=False,
    )
```

time: 232 us -> 237 us (1.022)
  local copies, waits for them, and re-layouts: 3.85 us -> 9.48 us
    ppermute x7, waiting for transfers between devices: 40.2 us -> 13.8 us  [body(): lax.ppermute(us[k], 'aux', pairs_of(k))]
    all_to_all x1, waiting for transfers between devices: 0.01 us -> 24 us  [body(): lax.all_to_all(first, 'orb', split_axis=0, concat_axis=0, tiled=True)]
    ppermute x7 -> x6, waiting for transfers between devices: 12.1 us -> 33.8 us  [the longest x3 30.7 us: body(): lax.ppermute(pat, 'aux', pairs_of(2 * dx))]
    ppermute x7, waiting for transfers between devices: 26.7 us -> 6.11 us  [body(): lax.ppermute(tb[k], 'aux', pairs_of(k))]
    ppermute x7 -> x6, starting transfers between devices: 12.9 us -> 2.5 us  [the longest x3 1.98 us: body(): lax.ppermute(pat, 'aux', pairs_of(2 * dx))]
    all_to_all x0 -> x1, starting transfers between devices: none -> 8.13 us  [body(): lax.all_to_all(every, 'orb', split_axis=0, concat_axis=0, tiled=True)]
    pallas_call x3 -> x4, Pallas kernels: 29.7 us -> 34 us  [the longest x2 15 us: chi_share(): pl.pallas_call(functools.partial(chi_kernel, half), in_specs=[sspec(), vs...]
    convert_element_type x2 -> x1, other arithmetic: 4.17 us -> 0.6 us  [body(): meta = marks.astype(jnp.int32).reshape(-1)]
  transfers between devices with their start and end apart: 27 -> 27, of which waited for: 14 -> 13; matrix products, arithmetic and copies ran while one was open for 2% -> 2% of each run, Pallas kernels for 20% -> 25%
where the time goes in v4:
time: 237 us; the launch traced here: 236 us
  waiting for transfers between devices  108 us (46%)
  Pallas kernels  58.8 us (25%)
  starting transfers between devices  53.8 us (23%)
  local copies, waits for them, and re-layouts  9.48 us (4%)
  other arithmetic  6.19 us (3%)
    ppermute x3, waiting for transfers between devices, body(): lax.ppermute(pat, 'aux', pairs_of(2 * dx))  30.7 us
    all_to_all x1, waiting for transfers between devices, body(): part = lax.all_to_all(part, 'orb', split_axis=0, concat_axis=0, tiled=True)  25.6 us
    all_to_all x1, waiting for transfers between devices, body(): lax.all_to_all(first, 'orb', split_axis=0, concat_axis=0, tiled=True)  24 us
    pallas_call x2, Pallas kernels, chi_share(): pl.pallas_call(functools.partial(chi_kernel, half), in_specs=[sspec(), vs...  15 us
    ppermute x7, waiting for transfers between devices, body(): lax.ppermute(us[k], 'aux', pairs_of(k))  13.8 us
    pallas_call x1, Pallas kernels, first_products(): pl.pallas_call(first_kernel, in_specs=[sspec(), sspec(), vspec(), vspec()...  12.7 us
    pallas_call x1, Pallas kernels, second_products(): pl.pallas_call(second_kernel, in_specs=[sspec(), sspec(), vspec(), vspec(...  12.1 us
    ppermute x7, starting transfers between devices, body(): lax.ppermute(tb[k], 'aux', pairs_of(k))  8.79 us
  transfers between devices with their start and end apart: 27, of which 13 were waited for; matrix products, arithmetic and copies ran while one was open for 2% of the time, Pallas kernels for 25%

profile of v4, /device:TPU:0, one launch (start us, length us, event | category | flops | bytes accessed | tf_op | source)
XLA Modules:
  0.0 236.3 jit_solution(1502384353347089875)
XLA Ops:
  3.6 8.1 %all-to-all-start = ((bf16[16,8,4096]{2,1,0:T(8,128)(2,1)}), bf16[16,8,4096]{2,1,0:T(8,128)(2,1)S(1)}, u32[]{:S(2)}, u32[]{:S(2)}) async-start(bf16[16,8,4096]{2,1,0:T(8,128)(2,1)} %broadcast_in_dim.2), calls=%async_computation | async-start | bytes 2097152 | tf_op jit(solution)/shard_map/all_to_all | solution.py:348
  12.4 6.3 %block_pairs.1 = (bf16[2,3,10,32,128]{4,3,2,1,0:T(8,128)(2,1)}, bf16[2,3,10,32,128]{4,3,2,1,0:T(8,128)(2,1)}, bf16[2,3,10,32,128]{4,3,2,1,0:T(8,128)(2,1)}, bf16...) custom-call(s32[2]{0:T(128)} %pad_add_fusion.pos, ...), custom_call_target="tpu_custom_call" | custom-call | flops 1000000000 | bytes 8000000 | tf_op jit(solution)/shard_map/block_pairs/pallas_call | solution.py:97
  18.8 1.6 collective-permute-start.1
  20.3 1.7 collective-permute-start.2
  22.1 5.7 %row_slabs.1 = bf16[16,30,16,256]{3,2,1,0:T(8,128)(2,1)} custom-call(bf16[10,3,16,4096]{3,2,1,0:T(8,128)(2,1)} %bitcast.37), custom_call_target="tpu_custom_call" | custom-call | bytes 8000000 | tf_op jit(solution)/shard_map/row_slabs/pallas_call | solution.py:63
  27.8 6.0 %collective-permute-done.1.rest_2_ = bf16[2,3,10,32,128]{4,3,2,1,0:T(8,128)(2,1)S(1)} collective-permute-done((bf16[2,3,10,32,128]{4,3,2,1,0:T(8,128)(2,1)}, bf16[2,3,10,32,128]{4,3,2,1,0:T(8,128)(2,1)S(1)}, u32[]{:S(2)}, u32[]{:S(2)}) %collective-permute-start.1) | collective-permute-done | bytes 491552 | tf_op jit(solution)/shard_map/ppermute | solution.py:351
  34.6 7.2 %all-to-all-start.2 = ((bf16[16,30,16,256]{3,2,1,0:T(8,128)(2,1)}), bf16[16,30,16,256]{3,2,1,0:T(8,128)(2,1)}, u32[]{:S(2)}, u32[]{:S(2)}) async-start(bf16[16,30,16,256]{3,2,1,0:T(8,128)(2,1)} %row_slabs.1), calls=%async_computation.2 | async-start | bytes 7864320 | tf_op jit(solution)/shard_map/all_to_all | solution.py:353
  43.7 2.1 collective-permute-start.8
  45.8 1.5 collective-permute-start.9
  49.6 1.8 collective-permute-start.5
  51.4 27.2 %collective-permute-done.5 = bf16[2,16,128]{2,1,0:T(8,128)(2,1)S(1)} collective-permute-done((bf16[2,16,128]{2,1,0:T(8,128)(2,1)S(1)}, bf16[2,16,128]{2,1,0:T(8,128)(2,1)S(1)}, u32[]{:S(2)}, u32[]{:S(2)}) %collective-permute-start.5) | collective-permute-done | bytes 8224 | tf_op jit(solution)/shard_map/ppermute | solution.py:358
  78.8 3.5 %collective-permute-done.6 = bf16[2,16,128]{2,1,0:T(8,128)(2,1)S(1)} collective-permute-done((bf16[2,16,128]{2,1,0:T(8,128)(2,1)S(1)}, bf16[2,16,128]{2,1,0:T(8,128)(2,1)S(1)}, u32[]{:S(2)}, u32[]{:S(2)}) %collective-permute-start.6) | collective-permute-done | bytes 8224 | tf_op jit(solution)/shard_map/ppermute | solution.py:358
  82.3 2.6 %reshape.61.g_ref = bf16[16,6,64,64]{3,2,1,0:T(8,128)(2,1)} reshape(bf16[16,6,4096]{2,1,0:T(8,128)(2,1)S(1)} %bitcast.38) | data formatting | bytes 1572864 | tf_op jit(solution)/shard_map/reshape | solution.py:360
  84.9 7.1 %greens.1 = (bf16[16,3,64,128]{3,2,1,0:T(8,128)(2,1)}, bf16[2,192,192]{2,1,0:T(8,128)(2,1)}) custom-call(s32[2]{0:T(128)} %pad_add_fusion.pos, s32[16]{0:T(128)} %size.1, s32[2048]{0:T(1024)} %get-tuple-element.77.meta.pat, bf16[16,6,64,64]{3,2,1,0:T(8,128)(2,1)} %reshape.61.g_ref, bf16[2,32,64]{2,1,0:T(8,128)(2,1)} %constant.63.clone.rows_ref, ...), custom_call_target="tpu_custom_call" | custom-call | flops 1000000 | bytes 8000000 | tf_op jit(solution)/shard_map/greens/pallas_call | solution.py:158
  93.6 12.7 %first.1 = bf16[16,6,80,256]{3,2,1,0:T(8,128)(2,1)} custom-call(s32[2]{0:T(128)} %pad_add_fusion.pos, s32[4096]{0:T(1024)} %reshape.59.pat, bf16[256,256]{1,0:T(8,128)(2,1)} %constant.62.clone.perm, bf16[2,192,192]{2,1,0:T(8,128)(2,1)} %get-tuple-element.54.w_ref, bf16[2,3,10,32,128]{4,3,2,1,0:T(8,128)(2,1)} %get-tuple-element.55.rest_0_, ...), custom_call_target="tpu_custom_call" | custom-call | flops 3000000000 | bytes 8000000 | tf_op jit(solution)/shard_map/first/pallas_call | solution.py:278
  106.3 7.1 %all-to-all-start.1 = ((bf16[16,6,80,256]{3,2,1,0:T(8,128)(2,1)}), bf16[16,6,80,256]{3,2,1,0:T(8,128)(2,1)}, u32[]{:S(2)}, u32[]{:S(2)}) async-start(bf16[16,6,80,256]{3,2,1,0:T(8,128)(2,1)} %first.1), calls=%async_computation.1 | async-start | bytes 7864320 | tf_op jit(solution)/shard_map/all_to_all | solution.py:364
  113.3 12.1 %second.1 = (bf16[6,160,256]{2,1,0:T(8,128)(2,1)}, bf16[6,160,256]{2,1,0:T(8,128)(2,1)}, bf16[6,160,256]{2,1,0:T(8,128)(2,1)}, bf16[6,160,256]{2,1,0:T(8,128)(2,...) custom-call(s32[2]{0:T(128)} %pad_add_fusion.pos, ...), custom_call_target="tpu_custom_call" | custom-call | flops 4000000000 | bytes 15000000 | tf_op jit(solution)/shard_map/second/pallas_call | solution.py:217
  125.5 3.5 %collective-permute-start.12 = (bf16[6,160,256]{2,1,0:T(8,128)(2,1)}, bf16[6,160,256]{2,1,0:T(8,128)(2,1)S(1)}, u32[]{:S(2)}, u32[]{:S(2)}) collective-permute-start(bf16[6,160,256]{2,1,0:T(8,128)(2,1)} %get-tuple-element.67), channel_id=1, source_target_pairs={{0,96},{16,112},{32,0},{48,16},{64,32},{80,48},{96,64},{112,80},{1... | collective-permute-start | bytes 1474568 | tf_op jit(solution)/shard_map/ppermute | solution.py:366
  129.6 2.3 collective-permute-start.16
  132.0 2.0 collective-permute-start.17
  133.9 6.8 %collective-permute-done.12.rest_2_ = bf16[6,160,256]{2,1,0:T(8,128)(2,1)S(1)} collective-permute-done((bf16[6,160,256]{2,1,0:T(8,128)(2,1)}, bf16[6,160,256]{2,1,0:T(8,128)(2,1)S(1)}, u32[]{:S(2)}, u32[]{:S(2)}) %collective-permute-start.12) | collective-permute-done | bytes 491552 | tf_op jit(solution)/shard_map/ppermute | solution.py:366
  140.8 24.0 %all-to-all-done.1.first_ref = bf16[16,6,80,256]{3,2,1,0:T(8,128)(2,1)} async-done(((bf16[16,6,80,256]{3,2,1,0:T(8,128)(2,1)}), bf16[16,6,80,256]{3,2,1,0:T(8,128)(2,1)}, u32[]{:S(2)}, u32[]{:S(2)}) %all-to-all-start.1) | async-done | bytes 3932192 | tf_op jit(solution)/shard_map/all_to_all | solution.py:364
  164.8 7.0 %collective-permute-done.13.rest_3_ = bf16[6,160,256]{2,1,0:T(8,128)(2,1)S(1)} collective-permute-done((bf16[6,160,256]{2,1,0:T(8,128)(2,1)}, bf16[6,160,256]{2,1,0:T(8,128)(2,1)S(1)}, u32[]{:S(2)}, u32[]{:S(2)}) %collective-permute-start.13) | collective-permute-done | bytes 491552 | tf_op jit(solution)/shard_map/ppermute | solution.py:366
  172.6 7.5 %chi.2 = (bf16[16,40,640]{2,1,0:T(8,128)(2,1)}, f32[16,40,640]{2,1,0:T(8,128)}) custom-call(s32[2]{0:T(128)} %pad_add_fusion.pos, bf16[16,6,80,256]{3,2,1,0:T(8,128)(2,1)} %all-to-all-done.1.first_ref, bf16[6,160,256]{2,1,0:T(8,128)(2,1)} %get-tuple-element.65.rest_0_, bf16[6,160,256]{2,1,0:T(8,128)(2,1)} %copy-done.12, bf16[6,160,256]{2,1,0:T(8,128)(2,1)} %copy-done.14, ...), custom_call_target="tpu_custom_call" | custom-call | flops 2500000000 | bytes 10000000 | tf_op jit(solution)/shard_map/chi/pallas_call | solution.py:313
  182.0 7.4 %chi.3 = (bf16[16,40,640]{2,1,0:T(8,128)(2,1)}, f32[16,40,640]{2,1,0:T(8,128)}) custom-call(s32[2]{0:T(128)} %pad_add_fusion.pos, bf16[16,6,80,256]{3,2,1,0:T(8,128)(2,1)} %all-to-all-done.1.first_ref, bf16[6,160,256]{2,1,0:T(8,128)(2,1)} %copy-done.9, bf16[6,160,256]{2,1,0:T(8,128)(2,1)} %copy-done.10, bf16[6,160,256]{2,1,0:T(8,128)(2,1)} %copy-done.11, ...), custom_call_target="tpu_custom_call" | custom-call | flops 2500000000 | bytes 10000000 | tf_op jit(solution)/shard_map/chi/pallas_call | solution.py:313
  190.1 2.0 collective-permute-done.19
  192.2 1.3 pad_maximum_fusion
  193.6 7.2 %all-to-all-start.3 = ((bf16[16,40,1280]{2,1,0:T(8,128)(2,1)}), bf16[16,40,1280]{2,1,0:T(8,128)(2,1)S(1)}, u32[]{:S(2)}, u32[]{:S(2)}) async-start(bf16[16,40,1280]{2,1,0:T(8,128)(2,1)} %pad_maximum_fusion), calls=%async_computation.3 | async-start | bytes 3276800 | tf_op jit(solution)/shard_map/all_to_all | solution.py:373
  200.8 25.6 %all-to-all-done.3 = bf16[16,40,1280]{2,1,0:T(8,128)(2,1)S(1)} async-done(((bf16[16,40,1280]{2,1,0:T(8,128)(2,1)}), bf16[16,40,1280]{2,1,0:T(8,128)(2,1)S(1)}, u32[]{:S(2)}, u32[]{:S(2)}) %all-to-all-start.3) | async-done | bytes 1638432 | tf_op jit(solution)/shard_map/all_to_all | solution.py:373
  227.0 4.2 %collective-permute-start.21 = (f32[10,1280]{1,0:T(8,128)S(1)}, f32[10,1280]{1,0:T(8,128)S(1)}, u32[]{:S(2)}, u32[]{:S(2)}) collective-permute-start(f32[10,1280]{1,0:T(8,128)S(1)} %get-tuple-element.82), channel_id=1, source_target_pairs={{0,64},{16,80},{32,96},{48,112},{64,0},{80,16},{96,32},{112,48},{1... | collective-permute-start | bytes 153608 | tf_op jit(solution)/shard_map/ppermute | solution.py:382
  231.2 1.4 collective-permute-done.20
  232.6 1.9 collective-permute-done.21
  (83 shorter events, 17.6 us)
Async XLA Ops:
  3.6 30.3 %all-to-all-start = ((bf16[16,8,4096]{2,1,0:T(8,128)(2,1)}), bf16[16,8,4096]{2,1,0:T(8,128)(2,1)S(1)}, u32[]{:S(2)}, u32[]{:S(2)}) async-start(bf16[16,8,4096]{2,1,0:T(8,128)(2,1)} %broadcast_in_dim.2), calls=%async_computation | async-start | bytes 2097152 | tf_op jit(solution)/shard_map/all_to_all | solution.py:348
  18.7 9.1 %collective-permute-start = (bf16[2,3,10,32,128]{4,3,2,1,0:T(8,128)(2,1)}, bf16[2,3,10,32,128]{4,3,2,1,0:T(8,128)(2,1)S(1)}, u32[]{:S(2)}, u32[]{:S(2)}) collective-permute-start(bf16[2,3,10,32,128]{4,3,2,1,0:T(8,128)(2,1)} %get-tuple-element.49), channel_id=1, source_target_pairs={{0,16},{16,0},{32,48},{48,32},{64,80},{80,64},{96,112},{112,96},{1... | collective-permute-start | bytes 1474568 | tf_op jit(solution)/shard_map/ppermute | solution.py:351
  18.8 15.1 %collective-permute-start.1 = (bf16[2,3,10,32,128]{4,3,2,1,0:T(8,128)(2,1)}, bf16[2,3,10,32,128]{4,3,2,1,0:T(8,128)(2,1)S(1)}, u32[]{:S(2)}, u32[]{:S(2)}) collective-permute-start(bf16[2,3,10,32,128]{4,3,2,1,0:T(8,128)(2,1)} %get-tuple-element.50), channel_id=1, source_target_pairs={{0,32},{16,48},{32,64},{48,80},{64,96},{80,112},{96,0},{112,16},{1... | collective-permute-start | bytes 1474568 | tf_op jit(solution)/shard_map/ppermute | solution.py:351
  20.3 13.6 %collective-permute-start.2 = (bf16[2,3,10,32,128]{4,3,2,1,0:T(8,128)(2,1)}, bf16[2,3,10,32,128]{4,3,2,1,0:T(8,128)(2,1)}, u32[]{:S(2)}, u32[]{:S(2)}) collective-permute-start(bf16[2,3,10,32,128]{4,3,2,1,0:T(8,128)(2,1)} %get-tuple-element.51), channel_id=1, source_target_pairs={{0,96},{16,112},{32,0},{48,16},{64,32},{80,48},{96,64},{112,80},{1... | collective-permute-start | bytes 1474568 | tf_op jit(solution)/shard_map/ppermute | solution.py:351
  27.8 15.1 %copy-start.6 = (bf16[2,3,10,32,128]{4,3,2,1,0:T(8,128)(2,1)S(1)}, bf16[2,3,10,32,128]{4,3,2,1,0:T(8,128)(2,1)}, u32[]{:S(2)}) copy-start(bf16[2,3,10,32,128]{4,3,2,1,0:T(8,128)(2,1)} %get-tuple-element.58) | copy-start | bytes 1474564
  27.8 15.9 %copy-start.4 = (bf16[2,3,10,32,128]{4,3,2,1,0:T(8,128)(2,1)S(1)}, bf16[2,3,10,32,128]{4,3,2,1,0:T(8,128)(2,1)}, u32[]{:S(2)}) copy-start(bf16[2,3,10,32,128]{4,3,2,1,0:T(8,128)(2,1)} %get-tuple-element.59) | copy-start | bytes 1474564
  27.8 17.9 %copy-start.2 = (bf16[2,3,10,32,128]{4,3,2,1,0:T(8,128)(2,1)S(1)}, bf16[2,3,10,32,128]{4,3,2,1,0:T(8,128)(2,1)}, u32[]{:S(2)}) copy-start(bf16[2,3,10,32,128]{4,3,2,1,0:T(8,128)(2,1)} %get-tuple-element.60) | copy-start | bytes 1474564
  34.6 71.7 %all-to-all-start.2 = ((bf16[16,30,16,256]{3,2,1,0:T(8,128)(2,1)}), bf16[16,30,16,256]{3,2,1,0:T(8,128)(2,1)}, u32[]{:S(2)}, u32[]{:S(2)}) async-start(bf16[16,30,16,256]{3,2,1,0:T(8,128)(2,1)} %row_slabs.1), calls=%async_computation.2 | async-start | bytes 7864320 | tf_op jit(solution)/shard_map/all_to_all | solution.py:353
  41.8 50.8 %collective-permute-start.10 = (bf16[2,3,10,32,128]{4,3,2,1,0:T(8,128)(2,1)}, bf16[2,3,10,32,128]{4,3,2,1,0:T(8,128)(2,1)S(1)}, u32[]{:S(2)}, u32[]{:S(2)}) collective-permute-start(bf16[2,3,10,32,128]{4,3,2,1,0:T(8,128)(2,1)} %get-tuple-element.62), channel_id=1, source_target_pairs={{0,112},{16,96},{32,16},{48,0},{64,48},{80,32},{96,80},{112,64},{1... | collective-permute-start | bytes 1474568 | tf_op jit(solution)/shard_map/ppermute | solution.py:351
  42.9 49.8 %collective-permute-start.7 = (bf16[2,3,10,32,128]{4,3,2,1,0:T(8,128)(2,1)S(1)}, bf16[2,3,10,32,128]{4,3,2,1,0:T(8,128)(2,1)S(1)}, u32[]{:S(2)}, u32[]{:S(2)}) collective-permute-start(bf16[2,3,10,32,128]{4,3,2,1,0:T(8,128)(2,1)S(1)} %copy-done.6), channel_id=1, source_target_pairs={{0,48},{16,32},{32,80},{48,64},{64,112},{80,96},{96,16},{112,0},{1... | collective-permute-start | bytes 1474568 | tf_op jit(solution)/shard_map/ppermute | solution.py:351
  43.7 49.0 %collective-permute-start.8 = (bf16[2,3,10,32,128]{4,3,2,1,0:T(8,128)(2,1)S(1)}, bf16[2,3,10,32,128]{4,3,2,1,0:T(8,128)(2,1)}, u32[]{:S(2)}, u32[]{:S(2)}) collective-permute-start(bf16[2,3,10,32,128]{4,3,2,1,0:T(8,128)(2,1)S(1)} %copy-done.4), channel_id=1, source_target_pairs={{0,64},{16,80},{32,96},{48,112},{64,0},{80,16},{96,32},{112,48},{1... | collective-permute-start | bytes 1474568 | tf_op jit(solution)/shard_map/ppermute | solution.py:351
  45.8 46.9 %collective-permute-start.9 = (bf16[2,3,10,32,128]{4,3,2,1,0:T(8,128)(2,1)S(1)}, bf16[2,3,10,32,128]{4,3,2,1,0:T(8,128)(2,1)}, u32[]{:S(2)}, u32[]{:S(2)}) collective-permute-start(bf16[2,3,10,32,128]{4,3,2,1,0:T(8,128)(2,1)S(1)} %copy-done.2), channel_id=1, source_target_pairs={{0,80},{16,64},{32,112},{48,96},{64,16},{80,0},{96,48},{112,32},{1... | collective-permute-start | bytes 1474568 | tf_op jit(solution)/shard_map/ppermute | solution.py:351
  48.5 1.2 collective-permute-start.3
  49.6 29.0 %collective-permute-start.5 = (bf16[2,16,128]{2,1,0:T(8,128)(2,1)S(1)}, bf16[2,16,128]{2,1,0:T(8,128)(2,1)S(1)}, u32[]{:S(2)}, u32[]{:S(2)}) collective-permute-start(bf16[2,16,128]{2,1,0:T(8,128)(2,1)S(1)} %get-tuple-element.84), channel_id=1, source_target_pairs={{0,64},{16,80},{32,96},{48,112},{64,0},{80,16},{96,32},{112,48},{1... | collective-permute-start | bytes 24584 | tf_op jit(solution)/shard_map/ppermute | solution.py:358
  78.6 3.7 %collective-permute-start.6 = (bf16[2,16,128]{2,1,0:T(8,128)(2,1)S(1)}, bf16[2,16,128]{2,1,0:T(8,128)(2,1)S(1)}, u32[]{:S(2)}, u32[]{:S(2)}) collective-permute-start(bf16[2,16,128]{2,1,0:T(8,128)(2,1)S(1)} %get-tuple-element.84), channel_id=1, source_target_pairs={{0,96},{16,112},{32,0},{48,16},{64,32},{80,48},{96,64},{112,80},{1... | collective-permute-start | bytes 24584 | tf_op jit(solution)/shard_map/ppermute | solution.py:358
  82.3 9.6 %collective-permute-start.4 = (bf16[2,16,128]{2,1,0:T(8,128)(2,1)S(1)}, bf16[2,16,128]{2,1,0:T(8,128)(2,1)S(1)}, u32[]{:S(2)}, u32[]{:S(2)}) collective-permute-start(bf16[2,16,128]{2,1,0:T(8,128)(2,1)S(1)} %get-tuple-element.84), channel_id=1, source_target_pairs={{0,32},{16,48},{32,64},{48,80},{64,96},{80,112},{96,0},{112,16},{1... | collective-permute-start | bytes 24584 | tf_op jit(solution)/shard_map/ppermute | solution.py:358
  106.3 58.5 %all-to-all-start.1 = ((bf16[16,6,80,256]{3,2,1,0:T(8,128)(2,1)}), bf16[16,6,80,256]{3,2,1,0:T(8,128)(2,1)}, u32[]{:S(2)}, u32[]{:S(2)}) async-start(bf16[16,6,80,256]{3,2,1,0:T(8,128)(2,1)} %first.1), calls=%async_computation.1 | async-start | bytes 7864320 | tf_op jit(solution)/shard_map/all_to_all | solution.py:364
  125.5 6.5 %collective-permute-start.11 = (bf16[6,160,256]{2,1,0:T(8,128)(2,1)}, bf16[6,160,256]{2,1,0:T(8,128)(2,1)S(1)}, u32[]{:S(2)}, u32[]{:S(2)}) collective-permute-start(bf16[6,160,256]{2,1,0:T(8,128)(2,1)} %get-tuple-element.66), channel_id=1, source_target_pairs={{0,16},{16,0},{32,48},{48,32},{64,80},{80,64},{96,112},{112,96},{1... | collective-permute-start | bytes 1474568 | tf_op jit(solution)/shard_map/ppermute | solution.py:366
  125.5 15.3 %collective-permute-start.12 = (bf16[6,160,256]{2,1,0:T(8,128)(2,1)}, bf16[6,160,256]{2,1,0:T(8,128)(2,1)S(1)}, u32[]{:S(2)}, u32[]{:S(2)}) collective-permute-start(bf16[6,160,256]{2,1,0:T(8,128)(2,1)} %get-tuple-element.67), channel_id=1, source_target_pairs={{0,96},{16,112},{32,0},{48,16},{64,32},{80,48},{96,64},{112,80},{1... | collective-permute-start | bytes 1474568 | tf_op jit(solution)/shard_map/ppermute | solution.py:366
  128.9 42.9 %collective-permute-start.13 = (bf16[6,160,256]{2,1,0:T(8,128)(2,1)}, bf16[6,160,256]{2,1,0:T(8,128)(2,1)S(1)}, u32[]{:S(2)}, u32[]{:S(2)}) collective-permute-start(bf16[6,160,256]{2,1,0:T(8,128)(2,1)} %get-tuple-element.68), channel_id=1, source_target_pairs={{0,112},{16,96},{32,16},{48,0},{64,48},{80,32},{96,80},{112,64},{1... | collective-permute-start | bytes 1474568 | tf_op jit(solution)/shard_map/ppermute | solution.py:366
  128.9 51.2 %collective-permute-start.15 = (bf16[6,160,256]{2,1,0:T(8,128)(2,1)}, bf16[6,160,256]{2,1,0:T(8,128)(2,1)S(1)}, u32[]{:S(2)}, u32[]{:S(2)}) collective-permute-start(bf16[6,160,256]{2,1,0:T(8,128)(2,1)} %get-tuple-element.71), channel_id=1, source_target_pairs={{0,64},{16,80},{32,96},{48,112},{64,0},{80,16},{96,32},{112,48},{1... | collective-permute-start | bytes 1474568 | tf_op jit(solution)/shard_map/ppermute | solution.py:366
  129.6 50.5 %collective-permute-start.16 = (bf16[6,160,256]{2,1,0:T(8,128)(2,1)}, bf16[6,160,256]{2,1,0:T(8,128)(2,1)S(1)}, u32[]{:S(2)}, u32[]{:S(2)}) collective-permute-start(bf16[6,160,256]{2,1,0:T(8,128)(2,1)} %get-tuple-element.72), channel_id=1, source_target_pairs={{0,80},{16,64},{32,112},{48,96},{64,16},{80,0},{96,48},{112,32},{1... | collective-permute-start | bytes 1474568 | tf_op jit(solution)/shard_map/ppermute | solution.py:366
  132.0 39.8 %copy-start.12 = (bf16[6,160,256]{2,1,0:T(8,128)(2,1)}, bf16[6,160,256]{2,1,0:T(8,128)(2,1)S(1)}, u32[]{:S(2)}) copy-start(bf16[6,160,256]{2,1,0:T(8,128)(2,1)S(1)} %collective-permute-done.11.rest_1_) | copy-start | bytes 1474564
  132.0 48.2 %collective-permute-start.17 = (bf16[6,160,256]{2,1,0:T(8,128)(2,1)}, bf16[6,160,256]{2,1,0:T(8,128)(2,1)S(1)}, u32[]{:S(2)}, u32[]{:S(2)}) collective-permute-start(bf16[6,160,256]{2,1,0:T(8,128)(2,1)} %get-tuple-element.73), channel_id=1, source_target_pairs={{0,32},{16,48},{32,64},{48,80},{64,96},{80,112},{96,0},{112,16},{1... | collective-permute-start | bytes 1474568 | tf_op jit(solution)/shard_map/ppermute | solution.py:366
  140.8 31.0 %copy-start.14 = (bf16[6,160,256]{2,1,0:T(8,128)(2,1)}, bf16[6,160,256]{2,1,0:T(8,128)(2,1)S(1)}, u32[]{:S(2)}) copy-start(bf16[6,160,256]{2,1,0:T(8,128)(2,1)S(1)} %collective-permute-done.12.rest_2_) | copy-start | bytes 1474564
  140.8 39.4 %collective-permute-start.18 = (bf16[6,160,256]{2,1,0:T(8,128)(2,1)}, bf16[6,160,256]{2,1,0:T(8,128)(2,1)S(1)}, u32[]{:S(2)}, u32[]{:S(2)}) collective-permute-start(bf16[6,160,256]{2,1,0:T(8,128)(2,1)} %get-tuple-element.74), channel_id=1, source_target_pairs={{0,48},{16,32},{32,80},{48,64},{64,112},{80,96},{96,16},{112,0},{1... | collective-permute-start | bytes 1474568 | tf_op jit(solution)/shard_map/ppermute | solution.py:366
  180.1 9.8 %collective-permute-start.14 = (bf16[16,40,640]{2,1,0:T(8,128)(2,1)}, bf16[16,40,640]{2,1,0:T(8,128)(2,1)S(1)}, u32[]{:S(2)}, u32[]{:S(2)}) collective-permute-start(bf16[16,40,640]{2,1,0:T(8,128)(2,1)} %get-tuple-element.70), channel_id=1, source_target_pairs={{0,16},{16,0},{32,48},{48,32},{64,80},{80,64},{96,112},{112,96},{1... | collective-permute-start | bytes 2457608 | tf_op jit(solution)/shard_map/ppermute | solution.py:371
  189.4 2.7 %collective-permute-start.19 = (bf16[16,40,640]{2,1,0:T(8,128)(2,1)}, bf16[16,40,640]{2,1,0:T(8,128)(2,1)S(1)}, u32[]{:S(2)}, u32[]{:S(2)}) collective-permute-start(bf16[16,40,640]{2,1,0:T(8,128)(2,1)} %get-tuple-element.76), channel_id=1, source_target_pairs={{0,16},{16,0},{32,48},{48,32},{64,80},{80,64},{96,112},{112,96},{1... | collective-permute-start | bytes 2457608 | tf_op jit(solution)/shard_map/ppermute | solution.py:371
  193.6 32.8 %all-to-all-start.3 = ((bf16[16,40,1280]{2,1,0:T(8,128)(2,1)}), bf16[16,40,1280]{2,1,0:T(8,128)(2,1)S(1)}, u32[]{:S(2)}, u32[]{:S(2)}) async-start(bf16[16,40,1280]{2,1,0:T(8,128)(2,1)} %pad_maximum_fusion), calls=%async_computation.3 | async-start | bytes 3276800 | tf_op jit(solution)/shard_map/all_to_all | solution.py:373
  226.9 5.7 %collective-permute-start.20 = (f32[10,1280]{1,0:T(8,128)S(1)}, f32[10,1280]{1,0:T(8,128)S(1)}, u32[]{:S(2)}, u32[]{:S(2)}) collective-permute-start(f32[10,1280]{1,0:T(8,128)S(1)} %get-tuple-element.80), channel_id=1, source_target_pairs={{0,32},{16,48},{32,64},{48,80},{64,96},{80,112},{96,0},{112,16},{1... | collective-permute-start | bytes 153608 | tf_op jit(solution)/shard_map/ppermute | solution.py:382
  227.0 7.5 %collective-permute-start.21 = (f32[10,1280]{1,0:T(8,128)S(1)}, f32[10,1280]{1,0:T(8,128)S(1)}, u32[]{:S(2)}, u32[]{:S(2)}) collective-permute-start(f32[10,1280]{1,0:T(8,128)S(1)} %get-tuple-element.82), channel_id=1, source_target_pairs={{0,64},{16,80},{32,96},{48,112},{64,0},{80,16},{96,32},{112,48},{1... | collective-permute-start | bytes 153608 | tf_op jit(solution)/shard_map/ppermute | solution.py:382
  231.2 4.4 %collective-permute-start.22 = (f32[10,1280]{1,0:T(8,128)S(1)}, f32[10,1280]{1,0:T(8,128)S(1)}, u32[]{:S(2)}, u32[]{:S(2)}) collective-permute-start(f32[10,1280]{1,0:T(8,128)S(1)} %get-tuple-element.81), channel_id=1, source_target_pairs={{0,96},{16,112},{32,0},{48,16},{64,32},{80,48},{96,64},{112,80},{1... | collective-permute-start | bytes 153608 | tf_op jit(solution)/shard_map/ppermute | solution.py:382
  (11 other events, 25.0 us)

commit v5 on v4

--- a/solution.py
+++ b/solution.py
@@ -182,13 +182,13 @@
     def regroup(g, carry):
         for d in range(W):
             x = ta_ref[pl.ds(16 * g, 16), d].reshape(256, 256)
-            y = jnp.dot(perm[...], x, preferred_element_type=F32)
+            y = jnp.dot(perm[...], x, preferred_element_type=F32).astype(BF)
             for n in range(NOB):
                 keep = pat[n * 128 + g * W + d] > 0
                 part = y[16 * n : 16 * n + 16]
                 s[n + 1, d, pl.ds(pl.multiple_of(16 * g, 16), 16)] = jnp.where(
                     keep, part, jnp.zeros_like(part)
-                ).astype(BF)
+                )
         return carry
 
     lax.fori_loop(0, NG, regroup, 0)
@@ -287,39 +287,44 @@
     )(pos, pat, perm, w, *tb)
 
 
-HALVES = [(0, 1, 6, 7), (4, 5, 2, 3)]
-
-
-def chi_kernel(half, pos, first_ref, *rest):
-    us, theirs, mine, rhs = rest[:4], rest[4], rest[5], rest[6]
-    core = lax.rem(pos[0], 2)
-    for j, k in enumerate(HALVES[half]):
-        c = core if k % 2 == 0 else 1 - core
-        row = pl.multiple_of((j // 2) * 320 + c * 160, 32)
-        for kk in range(6):
-            rhs[pl.ds(row, 160), 256 * kk : 256 * kk + 256] = us[j][kk]
-    for c0, cw in ((0, 256), (256, 256), (512, 128)):
-        lhs = jnp.concatenate([first_ref[:, kk].reshape(1280, 256) for kk in range(6)], axis=1)
-        r = lax.dot_general(
-            lhs, rhs[c0 : c0 + cw], (((1,), (1,)), ((), ())), preferred_element_type=F32
-        )
-        for b in range(16):
-            lo, hi = r[80 * b : 80 * b + 40], r[80 * b + 40 : 80 * b + 80]
-            mine[b, :, c0 : c0 + cw] = jnp.where(core == 0, lo, hi)
-            theirs[b, :, c0 : c0 + cw] = jnp.where(core == 0, hi, lo).astype(BF)
-
-
-def chi_share(half, pos, first, us):
-    return pl.pallas_call(
-        functools.partial(chi_kernel, half),
-        in_specs=[sspec(), vspec()] + [vspec()] * 4,
-        out_specs=[vspec()] * 2,
-        out_shape=[jax.ShapeDtypeStruct((16, 40, 640), BF), jax.ShapeDtypeStruct((16, 40, 640), F32)],
-        scratch_shapes=[pltpu.VMEM((640, 1536), BF)],
-        compiler_params=pltpu.CompilerParams(vmem_limit_bytes=VLIM),
-        cost_estimate=pl.CostEstimate(flops=25 * 10**8, bytes_accessed=10 * 10**6, transcendentals=0),
+def chi_kernel(pos, first_ref, *rest):
+    us, theirs, mine, rhs = rest[:8], rest[8], rest[9], rest[10]
+    a = pos[0]
+    core0 = lax.rem(a, 2) == 0
+    t = pl.program_id(0)
+
+    @pl.when(t == 0)
+    def _():
+        for k in range(8):
+            row = pl.multiple_of(src_of(a, k) * 160, 32)
+            for kk in range(6):
+                rhs[pl.ds(row, 160), 256 * kk : 256 * kk + 256] = us[k][kk]
+
+    lhs = jnp.concatenate([first_ref[:, kk].reshape(1280, 256) for kk in range(6)], axis=1)
+    r = lax.dot_general(
+        lhs,
+        rhs[pl.ds(pl.multiple_of(256 * t, 256), 256)],
+        (((1,), (1,)), ((), ())),
+        preferred_element_type=F32,
+    )
+    for b in range(16):
+        lo, hi = r[80 * b : 80 * b + 40], r[80 * b + 40 : 80 * b + 80]
+        mine[b] = jnp.where(core0, lo, hi)
+        theirs[b] = jnp.where(core0, hi, lo).astype(BF)
+
+
+def chi_share(pos, first, us):
+    return pl.pallas_call(
+        chi_kernel,
+        grid=(5,),
+        in_specs=[sspec(), vspec()] + [vspec()] * 8,
+        out_specs=[pl.BlockSpec((16, 40, 256), lambda t: (0, 0, t))] * 2,
+        out_shape=[jax.ShapeDtypeStruct((16, 40, 1280), BF), jax.ShapeDtypeStruct((16, 40, 1280), F32)],
+        scratch_shapes=[pltpu.VMEM((1280, 1536), BF)],
+        compiler_params=pltpu.CompilerParams(vmem_limit_bytes=VLIM),
+        cost_estimate=pl.CostEstimate(flops=5 * 10**9, bytes_accessed=13 * 10**6, transcendentals=0),
         name="chi",
-    )(pos, first, *[us[k] for k in HALVES[half]])
+    )(pos, first, *us)
 
 
 def deinterleave():
@@ -354,28 +359,22 @@
 
     marks = every[:, 2 * W, :128]
     meta = marks.astype(jnp.int32).reshape(-1)
+    blocks = every[:, : 2 * W].reshape(NOB, 2 * W, BS, BS)
+    v, w, marks = lax.optimization_barrier((*greens(pos, atom_size, meta, blocks, rows, cols), marks))
     pat = jnp.stack([marks, lax.ppermute(marks, "aux", pairs_of(1))])
     pat = jnp.stack([pat] + [lax.ppermute(pat, "aux", pairs_of(2 * dx)) for dx in range(1, 4)])
     pat = pat[..., :32].astype(jnp.int32).reshape(-1)
-    blocks = every[:, : 2 * W].reshape(NOB, 2 * W, BS, BS)
-    v, w = greens(pos, atom_size, meta, blocks, rows, cols)
 
     first = first_products(pos, pat, perm, w, tb)
     first = lax.all_to_all(first, "orb", split_axis=0, concat_axis=0, tiled=True)
     us = second_products(pos, meta, perm, ta.reshape(160, W, NOB, 256), v)
     us = [us[0]] + [lax.ppermute(us[k], "aux", pairs_of(k)) for k in range(1, 8)]
 
-    parts = []
-    for half in range(2):
-        theirs, mine = chi_share(half, pos, first, us)
-        parts.append(mine + lax.ppermute(theirs, "aux", pairs_of(1)).astype(F32))
-    part = jnp.concatenate(parts, axis=2).astype(BF)
+    theirs, mine = chi_share(pos, first, us)
+    part = (mine + lax.ppermute(theirs, "aux", pairs_of(1)).astype(F32)).astype(BF)
     part = lax.all_to_all(part, "orb", split_axis=0, concat_axis=0, tiled=True)
-    part = jnp.sum(part.astype(F32), axis=0)
+    part = jnp.sum(part.astype(F32), axis=0).reshape(4, NPD, 1280)
     x = a // 2
-    part = lax.dynamic_slice(
-        jnp.concatenate([part, part], axis=1), (0, lax.rem(4 - x, 4) * 320), (40, 1280)
-    ).reshape(4, NPD, 1280)
     total = lax.dynamic_index_in_dim(part, x, 0, keepdims=False)
     for dx in range(1, 4):
         piece = lax.dynamic_index_in_dim(part, lax.rem(x + dx, 4), 0, keepdims=False)

time: 237 us -> 230 us (0.970)
  Pallas kernels: 58.8 us -> 54.7 us
  local copies, waits for them, and re-layouts: 9.48 us -> 7.01 us
    ppermute x3, waiting for transfers between devices: 30.7 us -> 26.3 us  [body(): lax.ppermute(pat, 'aux', pairs_of(2 * dx))]
    pallas_call x2 -> x1, Pallas kernels: 15 us -> 10.8 us  [chi_share(): pl.pallas_call(chi_kernel, grid=(5,), in_specs=[sspec(), vspec()] + [vspe...]
    ppermute x7, waiting for transfers between devices: 13.8 us -> 17.2 us  [body(): lax.ppermute(us[k], 'aux', pairs_of(k))]
    convert_element_type x1, other arithmetic: 0.6 us -> 3.45 us  [body(): (mine + lax.ppermute(theirs, 'aux', pairs_of(1)).astype(F32)).astype(BF)]
    unnamed x32 -> x24, local copies, waits for them, and re-layouts: 4.25 us -> 1.76 us
  transfers between devices with their start and end apart: 27 -> 26, of which waited for: 13 -> 14; matrix products, arithmetic and copies ran while one was open for 2% -> 2% of each run, Pallas kernels for 25% -> 19%
where the time goes in v5:
time: 230 us; the launch traced here: 229 us
  waiting for transfers between devices  106 us (46%)
  Pallas kernels  54.7 us (24%)
  starting transfers between devices  53.7 us (23%)
  other arithmetic  7.84 us (3%)
  local copies, waits for them, and re-layouts  7.01 us (3%)
    ppermute x3, waiting for transfers between devices, body(): lax.ppermute(pat, 'aux', pairs_of(2 * dx))  26.3 us
    all_to_all x1, waiting for transfers between devices, body(): part = lax.all_to_all(part, 'orb', split_axis=0, concat_axis=0, tiled=True)  25.6 us
    all_to_all x1, waiting for transfers between devices, body(): lax.all_to_all(first, 'orb', split_axis=0, concat_axis=0, tiled=True)  23 us
    ppermute x7, waiting for transfers between devices, body(): lax.ppermute(us[k], 'aux', pairs_of(k))  17.2 us
    pallas_call x1, Pallas kernels, first_products(): pl.pallas_call(first_kernel, in_specs=[sspec(), sspec(), vspec(), vspec()...  12.7 us
    pallas_call x1, Pallas kernels, second_products(): pl.pallas_call(second_kernel, in_specs=[sspec(), sspec(), vspec(), vspec(...  12.1 us
    pallas_call x1, Pallas kernels, chi_share(): pl.pallas_call(chi_kernel, grid=(5,), in_specs=[sspec(), vspec()] + [vspe...  10.8 us
    ppermute x7, starting transfers between devices, body(): lax.ppermute(tb[k], 'aux', pairs_of(k))  9.18 us
  transfers between devices with their start and end apart: 26, of which 14 were waited for; matrix products, arithmetic and copies ran while one was open for 2% of the time, Pallas kernels for 19%

profile of v5, /device:TPU:0, one launch (start us, length us, event | category | flops | bytes accessed | tf_op | source)
XLA Modules:
  0.0 229.1 jit_solution(778368732581208104)
XLA Ops:
  3.6 8.1 %all-to-all-start = ((bf16[16,8,4096]{2,1,0:T(8,128)(2,1)}), bf16[16,8,4096]{2,1,0:T(8,128)(2,1)S(1)}, u32[]{:S(2)}, u32[]{:S(2)}) async-start(bf16[16,8,4096]{2,1,0:T(8,128)(2,1)} %broadcast_in_dim.2), calls=%async_computation | async-start | bytes 2097152 | tf_op jit(solution)/shard_map/all_to_all | solution.py:353
  12.3 6.3 %block_pairs.1 = (bf16[2,3,10,32,128]{4,3,2,1,0:T(8,128)(2,1)}, bf16[2,3,10,32,128]{4,3,2,1,0:T(8,128)(2,1)}, bf16[2,3,10,32,128]{4,3,2,1,0:T(8,128)(2,1)}, bf16...) custom-call(s32[2]{0:T(128)} %pad_add_fusion.pos, ...), custom_call_target="tpu_custom_call" | custom-call | flops 1000000000 | bytes 8000000 | tf_op jit(solution)/shard_map/block_pairs/pallas_call | solution.py:97
  18.7 1.5 collective-permute-start.1
  20.3 1.8 collective-permute-start.2
  22.0 5.7 %row_slabs.1 = bf16[16,30,16,256]{3,2,1,0:T(8,128)(2,1)} custom-call(bf16[10,3,16,4096]{3,2,1,0:T(8,128)(2,1)} %bitcast.36), custom_call_target="tpu_custom_call" | custom-call | bytes 8000000 | tf_op jit(solution)/shard_map/row_slabs/pallas_call | solution.py:63
  27.8 6.0 %collective-permute-done.1.rest_2_ = bf16[2,3,10,32,128]{4,3,2,1,0:T(8,128)(2,1)S(1)} collective-permute-done((bf16[2,3,10,32,128]{4,3,2,1,0:T(8,128)(2,1)}, bf16[2,3,10,32,128]{4,3,2,1,0:T(8,128)(2,1)S(1)}, u32[]{:S(2)}, u32[]{:S(2)}) %collective-permute-start.1) | collective-permute-done | bytes 491552 | tf_op jit(solution)/shard_map/ppermute | solution.py:356
  34.8 7.2 %all-to-all-start.2 = ((bf16[16,30,16,256]{3,2,1,0:T(8,128)(2,1)}), bf16[16,30,16,256]{3,2,1,0:T(8,128)(2,1)}, u32[]{:S(2)}, u32[]{:S(2)}) async-start(bf16[16,30,16,256]{3,2,1,0:T(8,128)(2,1)} %row_slabs.1), calls=%async_computation.2 | async-start | bytes 7864320 | tf_op jit(solution)/shard_map/all_to_all | solution.py:358
  42.0 1.5 collective-permute-start.10
  43.8 2.6 %collective-permute-start.8 = (bf16[2,3,10,32,128]{4,3,2,1,0:T(8,128)(2,1)}, bf16[2,3,10,32,128]{4,3,2,1,0:T(8,128)(2,1)}, u32[]{:S(2)}, u32[]{:S(2)}) collective-permute-start(bf16[2,3,10,32,128]{4,3,2,1,0:T(8,128)(2,1)} %get-tuple-element.63), channel_id=1, source_target_pairs={{0,64},{16,80},{32,96},{48,112},{64,0},{80,16},{96,32},{112,48},{1... | collective-permute-start | bytes 1474568 | tf_op jit(solution)/shard_map/ppermute | solution.py:356
  46.4 1.4 collective-permute-start.9
  48.4 2.6 %reshape.61.g_ref = bf16[16,6,64,64]{3,2,1,0:T(8,128)(2,1)} reshape(bf16[16,6,4096]{2,1,0:T(8,128)(2,1)S(1)} %bitcast.37) | data formatting | bytes 1572864 | tf_op jit(solution)/shard_map/reshape | solution.py:362
  51.6 7.1 %greens.1 = (bf16[16,3,64,128]{3,2,1,0:T(8,128)(2,1)}, bf16[2,192,192]{2,1,0:T(8,128)(2,1)}) custom-call(s32[2]{0:T(128)} %pad_add_fusion.pos, s32[16]{0:T(128)} %size.1, s32[2048]{0:T(1024)} %get-tuple-element.80.meta.pat, bf16[16,6,64,64]{3,2,1,0:T(8,128)(2,1)} %reshape.61.g_ref, bf16[2,32,64]{2,1,0:T(8,128)(2,1)} %constant.57.clone.rows_ref, ...), custom_call_target="tpu_custom_call" | custom-call | flops 1000000 | bytes 8000000 | tf_op jit(solution)/shard_map/greens/pallas_call | solution.py:158
  60.7 19.0 %collective-permute-done.4 = bf16[2,16,128]{2,1,0:T(8,128)(2,1)S(1)} collective-permute-done((bf16[2,16,128]{2,1,0:T(8,128)(2,1)S(1)}, bf16[2,16,128]{2,1,0:T(8,128)(2,1)S(1)}, u32[]{:S(2)}, u32[]{:S(2)}) %collective-permute-start.4) | collective-permute-done | bytes 8224 | tf_op jit(solution)/shard_map/ppermute | solution.py:365
  80.9 4.0 %collective-permute-done.5 = bf16[2,16,128]{2,1,0:T(8,128)(2,1)S(1)} collective-permute-done((bf16[2,16,128]{2,1,0:T(8,128)(2,1)S(1)}, bf16[2,16,128]{2,1,0:T(8,128)(2,1)S(1)}, u32[]{:S(2)}, u32[]{:S(2)}) %collective-permute-start.5) | collective-permute-done | bytes 8224 | tf_op jit(solution)/shard_map/ppermute | solution.py:365
  85.1 3.4 %collective-permute-done.6 = bf16[2,16,128]{2,1,0:T(8,128)(2,1)S(1)} collective-permute-done((bf16[2,16,128]{2,1,0:T(8,128)(2,1)S(1)}, bf16[2,16,128]{2,1,0:T(8,128)(2,1)S(1)}, u32[]{:S(2)}, u32[]{:S(2)}) %collective-permute-start.6) | collective-permute-done | bytes 8224 | tf_op jit(solution)/shard_map/ppermute | solution.py:365
  89.2 12.7 %first.1 = bf16[16,6,80,256]{3,2,1,0:T(8,128)(2,1)} custom-call(s32[2]{0:T(128)} %pad_add_fusion.pos, s32[4096]{0:T(1024)} %reshape.60.pat, bf16[256,256]{1,0:T(8,128)(2,1)} %constant.56.clone.perm, bf16[2,192,192]{2,1,0:T(8,128)(2,1)} %get-tuple-element.58.w_ref, bf16[2,3,10,32,128]{4,3,2,1,0:T(8,128)(2,1)} %get-tuple-element.59.rest_0_, ...), custom_call_target="tpu_custom_call" | custom-call | flops 3000000000 | bytes 8000000 | tf_op jit(solution)/shard_map/first/pallas_call | solution.py:278
  101.9 6.9 %all-to-all-start.1 = ((bf16[16,6,80,256]{3,2,1,0:T(8,128)(2,1)}), bf16[16,6,80,256]{3,2,1,0:T(8,128)(2,1)}, u32[]{:S(2)}, u32[]{:S(2)}) async-start(bf16[16,6,80,256]{3,2,1,0:T(8,128)(2,1)} %first.1), calls=%async_computation.1 | async-start | bytes 7864320 | tf_op jit(solution)/shard_map/all_to_all | solution.py:369
  108.9 12.1 %second.1 = (bf16[6,160,256]{2,1,0:T(8,128)(2,1)}, bf16[6,160,256]{2,1,0:T(8,128)(2,1)}, bf16[6,160,256]{2,1,0:T(8,128)(2,1)}, bf16[6,160,256]{2,1,0:T(8,128)(2,...) custom-call(s32[2]{0:T(128)} %pad_add_fusion.pos, ...), custom_call_target="tpu_custom_call" | custom-call | flops 4000000000 | bytes 15000000 | tf_op jit(solution)/shard_map/second/pallas_call | solution.py:217
  122.2 3.3 %collective-permute-start.14 = (bf16[6,160,256]{2,1,0:T(8,128)(2,1)}, bf16[6,160,256]{2,1,0:T(8,128)(2,1)S(1)}, u32[]{:S(2)}, u32[]{:S(2)}) collective-permute-start(bf16[6,160,256]{2,1,0:T(8,128)(2,1)} %get-tuple-element.73), channel_id=1, source_target_pairs={{0,64},{16,80},{32,96},{48,112},{64,0},{80,16},{96,32},{112,48},{1... | collective-permute-start | bytes 1474568 | tf_op jit(solution)/shard_map/ppermute | solution.py:371
  125.6 1.8 collective-permute-start.16
  127.4 9.2 %collective-permute-done.12.rest_2_ = bf16[6,160,256]{2,1,0:T(8,128)(2,1)S(1)} collective-permute-done((bf16[6,160,256]{2,1,0:T(8,128)(2,1)}, bf16[6,160,256]{2,1,0:T(8,128)(2,1)S(1)}, u32[]{:S(2)}, u32[]{:S(2)}) %collective-permute-start.12) | collective-permute-done | bytes 491552 | tf_op jit(solution)/shard_map/ppermute | solution.py:371
  136.6 23.0 %all-to-all-done.1.first_ref = bf16[16,6,80,256]{3,2,1,0:T(8,128)(2,1)} async-done(((bf16[16,6,80,256]{3,2,1,0:T(8,128)(2,1)}), bf16[16,6,80,256]{3,2,1,0:T(8,128)(2,1)}, u32[]{:S(2)}, u32[]{:S(2)}) %all-to-all-start.1) | async-done | bytes 3932192 | tf_op jit(solution)/shard_map/all_to_all | solution.py:369
  159.6 7.4 %collective-permute-done.15.rest_5_ = bf16[6,160,256]{2,1,0:T(8,128)(2,1)S(1)} collective-permute-done((bf16[6,160,256]{2,1,0:T(8,128)(2,1)}, bf16[6,160,256]{2,1,0:T(8,128)(2,1)S(1)}, u32[]{:S(2)}, u32[]{:S(2)}) %collective-permute-start.15) | collective-permute-done | bytes 491552 | tf_op jit(solution)/shard_map/ppermute | solution.py:371
  168.5 10.8 %chi.1 = (bf16[16,40,1280]{2,1,0:T(8,128)(2,1)}, f32[16,40,1280]{2,1,0:T(8,128)}) custom-call(s32[2]{0:T(128)} %pad_add_fusion.pos, bf16[16,6,80,256]{3,2,1,0:T(8,128)(2,1)} %all-to-all-done.1.first_ref, bf16[6,160,256]{2,1,0:T(8,128)(2,1)} %get-tuple-element.69.rest_0_, bf16[6,160,256]{2,1,0:T(8,128)(2,1)} %copy-done.5, bf16[6,160,256]{2,1,0:T(8,128)(2,1)} %copy-done.6, ...), custom_call_target="tpu_custom_call" | custom-call | flops 5000000000 | bytes 13000000 | tf_op jit(solution)/shard_map/chi/pallas_call | solution.py:317
  179.8 3.3 %collective-permute-done.18 = bf16[16,40,1280]{2,1,0:T(8,128)(2,1)S(1)} collective-permute-done((bf16[16,40,1280]{2,1,0:T(8,128)(2,1)}, bf16[16,40,1280]{2,1,0:T(8,128)(2,1)S(1)}, u32[]{:S(2)}, u32[]{:S(2)}) %collective-permute-start.18) | collective-permute-done | bytes 1638432 | tf_op jit(solution)/shard_map/ppermute | solution.py:374
  183.2 3.4 %add_convert_fusion = bf16[16,40,1280]{2,1,0:T(8,128)(2,1)} fusion(f32[16,40,1280]{2,1,0:T(8,128)} %get-tuple-element.77, bf16[16,40,1280]{2,1,0:T(8,128)(2,1)S(1)} %collective-permute-done.18), kind=kLoop, calls=%fused_computation.1 | loop fusion | flops 2457600 | bytes 6553600 | tf_op jit(solution)/shard_map/convert_element_type | solution.py:374
  186.6 7.2 %all-to-all-start.3 = ((bf16[16,40,1280]{2,1,0:T(8,128)(2,1)}), bf16[16,40,1280]{2,1,0:T(8,128)(2,1)S(1)}, u32[]{:S(2)}, u32[]{:S(2)}) async-start(bf16[16,40,1280]{2,1,0:T(8,128)(2,1)} %add_convert_fusion), calls=%async_computation.3 | async-start | bytes 3276800 | tf_op jit(solution)/shard_map/all_to_all | solution.py:375
  193.9 25.6 %all-to-all-done.3 = bf16[16,40,1280]{2,1,0:T(8,128)(2,1)S(1)} async-done(((bf16[16,40,1280]{2,1,0:T(8,128)(2,1)}), bf16[16,40,1280]{2,1,0:T(8,128)(2,1)S(1)}, u32[]{:S(2)}, u32[]{:S(2)}) %all-to-all-start.3) | async-done | bytes 1638432 | tf_op jit(solution)/shard_map/all_to_all | solution.py:375
  219.8 2.6 %collective-permute-start.19 = (f32[10,1280]{1,0:T(8,128)S(1)}, f32[10,1280]{1,0:T(8,128)S(1)}, u32[]{:S(2)}, u32[]{:S(2)}) collective-permute-start(f32[10,1280]{1,0:T(8,128)S(1)} %get-tuple-element.81), channel_id=1, source_target_pairs={{0,32},{16,48},{32,64},{48,80},{64,96},{80,112},{96,0},{112,16},{1... | collective-permute-start | bytes 153608 | tf_op jit(solution)/shard_map/ppermute | solution.py:381
  222.3 1.6 collective-permute-start.20
  224.0 1.5 collective-permute-start.21
  225.8 2.5 %collective-permute-done.20 = f32[10,1280]{1,0:T(8,128)S(1)} collective-permute-done((f32[10,1280]{1,0:T(8,128)S(1)}, f32[10,1280]{1,0:T(8,128)S(1)}, u32[]{:S(2)}, u32[]{:S(2)}) %collective-permute-start.20) | collective-permute-done | bytes 51232 | tf_op jit(solution)/shard_map/ppermute | solution.py:381
  (69 shorter events, 15.7 us)
Async XLA Ops:
  3.6 30.2 %all-to-all-start = ((bf16[16,8,4096]{2,1,0:T(8,128)(2,1)}), bf16[16,8,4096]{2,1,0:T(8,128)(2,1)S(1)}, u32[]{:S(2)}, u32[]{:S(2)}) async-start(bf16[16,8,4096]{2,1,0:T(8,128)(2,1)} %broadcast_in_dim.2), calls=%async_computation | async-start | bytes 2097152 | tf_op jit(solution)/shard_map/all_to_all | solution.py:353
  18.7 9.1 %collective-permute-start = (bf16[2,3,10,32,128]{4,3,2,1,0:T(8,128)(2,1)}, bf16[2,3,10,32,128]{4,3,2,1,0:T(8,128)(2,1)S(1)}, u32[]{:S(2)}, u32[]{:S(2)}) collective-permute-start(bf16[2,3,10,32,128]{4,3,2,1,0:T(8,128)(2,1)} %get-tuple-element.50), channel_id=1, source_target_pairs={{0,16},{16,0},{32,48},{48,32},{64,80},{80,64},{96,112},{112,96},{1... | collective-permute-start | bytes 1474568 | tf_op jit(solution)/shard_map/ppermute | solution.py:356
  18.7 15.1 %collective-permute-start.1 = (bf16[2,3,10,32,128]{4,3,2,1,0:T(8,128)(2,1)}, bf16[2,3,10,32,128]{4,3,2,1,0:T(8,128)(2,1)S(1)}, u32[]{:S(2)}, u32[]{:S(2)}) collective-permute-start(bf16[2,3,10,32,128]{4,3,2,1,0:T(8,128)(2,1)} %get-tuple-element.51), channel_id=1, source_target_pairs={{0,32},{16,48},{32,64},{48,80},{64,96},{80,112},{96,0},{112,16},{1... | collective-permute-start | bytes 1474568 | tf_op jit(solution)/shard_map/ppermute | solution.py:356
  20.3 13.5 %collective-permute-start.2 = (bf16[2,3,10,32,128]{4,3,2,1,0:T(8,128)(2,1)}, bf16[2,3,10,32,128]{4,3,2,1,0:T(8,128)(2,1)S(1)}, u32[]{:S(2)}, u32[]{:S(2)}) collective-permute-start(bf16[2,3,10,32,128]{4,3,2,1,0:T(8,128)(2,1)} %get-tuple-element.52), channel_id=1, source_target_pairs={{0,96},{16,112},{32,0},{48,16},{64,32},{80,48},{96,64},{112,80},{1... | collective-permute-start | bytes 1474568 | tf_op jit(solution)/shard_map/ppermute | solution.py:356
  27.8 14.2 %copy-start.4 = (bf16[2,3,10,32,128]{4,3,2,1,0:T(8,128)(2,1)S(1)}, bf16[2,3,10,32,128]{4,3,2,1,0:T(8,128)(2,1)}, u32[]{:S(2)}) copy-start(bf16[2,3,10,32,128]{4,3,2,1,0:T(8,128)(2,1)} %get-tuple-element.66) | copy-start | bytes 1474564
  27.8 18.6 %copy-start = (bf16[2,3,10,32,128]{4,3,2,1,0:T(8,128)(2,1)S(1)}, bf16[2,3,10,32,128]{4,3,2,1,0:T(8,128)(2,1)}, u32[]{:S(2)}) copy-start(bf16[2,3,10,32,128]{4,3,2,1,0:T(8,128)(2,1)} %get-tuple-element.64) | copy-start | bytes 1474564
  34.8 67.1 %all-to-all-start.2 = ((bf16[16,30,16,256]{3,2,1,0:T(8,128)(2,1)}), bf16[16,30,16,256]{3,2,1,0:T(8,128)(2,1)}, u32[]{:S(2)}, u32[]{:S(2)}) async-start(bf16[16,30,16,256]{3,2,1,0:T(8,128)(2,1)} %row_slabs.1), calls=%async_computation.2 | async-start | bytes 7864320 | tf_op jit(solution)/shard_map/all_to_all | solution.py:358
  42.0 47.2 %collective-permute-start.10 = (bf16[2,3,10,32,128]{4,3,2,1,0:T(8,128)(2,1)S(1)}, bf16[2,3,10,32,128]{4,3,2,1,0:T(8,128)(2,1)}, u32[]{:S(2)}, u32[]{:S(2)}) collective-permute-start(bf16[2,3,10,32,128]{4,3,2,1,0:T(8,128)(2,1)S(1)} %copy-done.4), channel_id=1, source_target_pairs={{0,112},{16,96},{32,16},{48,0},{64,48},{80,32},{96,80},{112,64},{1... | collective-permute-start | bytes 1474568 | tf_op jit(solution)/shard_map/ppermute | solution.py:356
  43.5 45.7 %collective-permute-start.7 = (bf16[2,3,10,32,128]{4,3,2,1,0:T(8,128)(2,1)}, bf16[2,3,10,32,128]{4,3,2,1,0:T(8,128)(2,1)}, u32[]{:S(2)}, u32[]{:S(2)}) collective-permute-start(bf16[2,3,10,32,128]{4,3,2,1,0:T(8,128)(2,1)} %get-tuple-element.62), channel_id=1, source_target_pairs={{0,48},{16,32},{32,80},{48,64},{64,112},{80,96},{96,16},{112,0},{1... | collective-permute-start | bytes 1474568 | tf_op jit(solution)/shard_map/ppermute | solution.py:356
  43.8 45.4 %collective-permute-start.8 = (bf16[2,3,10,32,128]{4,3,2,1,0:T(8,128)(2,1)}, bf16[2,3,10,32,128]{4,3,2,1,0:T(8,128)(2,1)}, u32[]{:S(2)}, u32[]{:S(2)}) collective-permute-start(bf16[2,3,10,32,128]{4,3,2,1,0:T(8,128)(2,1)} %get-tuple-element.63), channel_id=1, source_target_pairs={{0,64},{16,80},{32,96},{48,112},{64,0},{80,16},{96,32},{112,48},{1... | collective-permute-start | bytes 1474568 | tf_op jit(solution)/shard_map/ppermute | solution.py:356
  46.4 42.8 %collective-permute-start.9 = (bf16[2,3,10,32,128]{4,3,2,1,0:T(8,128)(2,1)S(1)}, bf16[2,3,10,32,128]{4,3,2,1,0:T(8,128)(2,1)}, u32[]{:S(2)}, u32[]{:S(2)}) collective-permute-start(bf16[2,3,10,32,128]{4,3,2,1,0:T(8,128)(2,1)S(1)} %copy-done), channel_id=1, source_target_pairs={{0,80},{16,64},{32,112},{48,96},{64,16},{80,0},{96,48},{112,32},{1... | collective-permute-start | bytes 1474568 | tf_op jit(solution)/shard_map/ppermute | solution.py:356
  58.7 1.2 collective-permute-start.3
  59.9 19.8 %collective-permute-start.4 = (bf16[2,16,128]{2,1,0:T(8,128)(2,1)S(1)}, bf16[2,16,128]{2,1,0:T(8,128)(2,1)S(1)}, u32[]{:S(2)}, u32[]{:S(2)}) collective-permute-start(bf16[2,16,128]{2,1,0:T(8,128)(2,1)S(1)} %get-tuple-element.85), channel_id=1, source_target_pairs={{0,32},{16,48},{32,64},{48,80},{64,96},{80,112},{96,0},{112,16},{1... | collective-permute-start | bytes 24584 | tf_op jit(solution)/shard_map/ppermute | solution.py:365
  79.7 5.2 %collective-permute-start.5 = (bf16[2,16,128]{2,1,0:T(8,128)(2,1)S(1)}, bf16[2,16,128]{2,1,0:T(8,128)(2,1)S(1)}, u32[]{:S(2)}, u32[]{:S(2)}) collective-permute-start(bf16[2,16,128]{2,1,0:T(8,128)(2,1)S(1)} %get-tuple-element.85), channel_id=1, source_target_pairs={{0,64},{16,80},{32,96},{48,112},{64,0},{80,16},{96,32},{112,48},{1... | collective-permute-start | bytes 24584 | tf_op jit(solution)/shard_map/ppermute | solution.py:365
  84.8 3.7 %collective-permute-start.6 = (bf16[2,16,128]{2,1,0:T(8,128)(2,1)S(1)}, bf16[2,16,128]{2,1,0:T(8,128)(2,1)S(1)}, u32[]{:S(2)}, u32[]{:S(2)}) collective-permute-start(bf16[2,16,128]{2,1,0:T(8,128)(2,1)S(1)} %get-tuple-element.85), channel_id=1, source_target_pairs={{0,96},{16,112},{32,0},{48,16},{64,32},{80,48},{96,64},{112,80},{1... | collective-permute-start | bytes 24584 | tf_op jit(solution)/shard_map/ppermute | solution.py:365
  101.9 57.7 %all-to-all-start.1 = ((bf16[16,6,80,256]{3,2,1,0:T(8,128)(2,1)}), bf16[16,6,80,256]{3,2,1,0:T(8,128)(2,1)}, u32[]{:S(2)}, u32[]{:S(2)}) async-start(bf16[16,6,80,256]{3,2,1,0:T(8,128)(2,1)} %first.1), calls=%async_computation.1 | async-start | bytes 7864320 | tf_op jit(solution)/shard_map/all_to_all | solution.py:369
  120.9 4.7 %collective-permute-start.11 = (bf16[6,160,256]{2,1,0:T(8,128)(2,1)}, bf16[6,160,256]{2,1,0:T(8,128)(2,1)S(1)}, u32[]{:S(2)}, u32[]{:S(2)}) collective-permute-start(bf16[6,160,256]{2,1,0:T(8,128)(2,1)} %get-tuple-element.70), channel_id=1, source_target_pairs={{0,16},{16,0},{32,48},{48,32},{64,80},{80,64},{96,112},{112,96},{1... | collective-permute-start | bytes 1474568 | tf_op jit(solution)/shard_map/ppermute | solution.py:371
  120.9 15.7 %collective-permute-start.12 = (bf16[6,160,256]{2,1,0:T(8,128)(2,1)}, bf16[6,160,256]{2,1,0:T(8,128)(2,1)S(1)}, u32[]{:S(2)}, u32[]{:S(2)}) collective-permute-start(bf16[6,160,256]{2,1,0:T(8,128)(2,1)} %get-tuple-element.71), channel_id=1, source_target_pairs={{0,32},{16,48},{32,64},{48,80},{64,96},{80,112},{96,0},{112,16},{1... | collective-permute-start | bytes 1474568 | tf_op jit(solution)/shard_map/ppermute | solution.py:371
  121.2 38.4 %collective-permute-start.13 = (bf16[6,160,256]{2,1,0:T(8,128)(2,1)}, bf16[6,160,256]{2,1,0:T(8,128)(2,1)S(1)}, u32[]{:S(2)}, u32[]{:S(2)}) collective-permute-start(bf16[6,160,256]{2,1,0:T(8,128)(2,1)} %get-tuple-element.72), channel_id=1, source_target_pairs={{0,48},{16,32},{32,80},{48,64},{64,112},{80,96},{96,16},{112,0},{1... | collective-permute-start | bytes 1474568 | tf_op jit(solution)/shard_map/ppermute | solution.py:371
  122.2 37.4 %collective-permute-start.14 = (bf16[6,160,256]{2,1,0:T(8,128)(2,1)}, bf16[6,160,256]{2,1,0:T(8,128)(2,1)S(1)}, u32[]{:S(2)}, u32[]{:S(2)}) collective-permute-start(bf16[6,160,256]{2,1,0:T(8,128)(2,1)} %get-tuple-element.73), channel_id=1, source_target_pairs={{0,64},{16,80},{32,96},{48,112},{64,0},{80,16},{96,32},{112,48},{1... | collective-permute-start | bytes 1474568 | tf_op jit(solution)/shard_map/ppermute | solution.py:371
  125.5 41.5 %collective-permute-start.15 = (bf16[6,160,256]{2,1,0:T(8,128)(2,1)}, bf16[6,160,256]{2,1,0:T(8,128)(2,1)S(1)}, u32[]{:S(2)}, u32[]{:S(2)}) collective-permute-start(bf16[6,160,256]{2,1,0:T(8,128)(2,1)} %get-tuple-element.74), channel_id=1, source_target_pairs={{0,80},{16,64},{32,112},{48,96},{64,16},{80,0},{96,48},{112,32},{1... | collective-permute-start | bytes 1474568 | tf_op jit(solution)/shard_map/ppermute | solution.py:371
  125.6 42.0 %copy-start.5 = (bf16[6,160,256]{2,1,0:T(8,128)(2,1)}, bf16[6,160,256]{2,1,0:T(8,128)(2,1)S(1)}, u32[]{:S(2)}) copy-start(bf16[6,160,256]{2,1,0:T(8,128)(2,1)S(1)} %collective-permute-done.11.rest_1_) | copy-start | bytes 1474564
  125.6 41.4 %collective-permute-start.16 = (bf16[6,160,256]{2,1,0:T(8,128)(2,1)}, bf16[6,160,256]{2,1,0:T(8,128)(2,1)S(1)}, u32[]{:S(2)}, u32[]{:S(2)}) collective-permute-start(bf16[6,160,256]{2,1,0:T(8,128)(2,1)} %get-tuple-element.75), channel_id=1, source_target_pairs={{0,96},{16,112},{32,0},{48,16},{64,32},{80,48},{96,64},{112,80},{1... | collective-permute-start | bytes 1474568 | tf_op jit(solution)/shard_map/ppermute | solution.py:371
  136.6 31.0 %copy-start.6 = (bf16[6,160,256]{2,1,0:T(8,128)(2,1)}, bf16[6,160,256]{2,1,0:T(8,128)(2,1)S(1)}, u32[]{:S(2)}) copy-start(bf16[6,160,256]{2,1,0:T(8,128)(2,1)S(1)} %collective-permute-done.12.rest_2_) | copy-start | bytes 1474564
  136.6 31.0 %collective-permute-start.17 = (bf16[6,160,256]{2,1,0:T(8,128)(2,1)}, bf16[6,160,256]{2,1,0:T(8,128)(2,1)S(1)}, u32[]{:S(2)}, u32[]{:S(2)}) collective-permute-start(bf16[6,160,256]{2,1,0:T(8,128)(2,1)} %get-tuple-element.76), channel_id=1, source_target_pairs={{0,112},{16,96},{32,16},{48,0},{64,48},{80,32},{96,80},{112,64},{1... | collective-permute-start | bytes 1474568 | tf_op jit(solution)/shard_map/ppermute | solution.py:371
  159.6 8.1 %copy-start.7 = (bf16[6,160,256]{2,1,0:T(8,128)(2,1)}, bf16[6,160,256]{2,1,0:T(8,128)(2,1)S(1)}, u32[]{:S(2)}) copy-start(bf16[6,160,256]{2,1,0:T(8,128)(2,1)S(1)} %collective-permute-done.13.rest_3_) | copy-start | bytes 1474564
  159.6 8.1 %copy-start.8 = (bf16[6,160,256]{2,1,0:T(8,128)(2,1)}, bf16[6,160,256]{2,1,0:T(8,128)(2,1)S(1)}, u32[]{:S(2)}) copy-start(bf16[6,160,256]{2,1,0:T(8,128)(2,1)S(1)} %collective-permute-done.14.rest_4_) | copy-start | bytes 1474564
  179.3 3.9 %collective-permute-start.18 = (bf16[16,40,1280]{2,1,0:T(8,128)(2,1)}, bf16[16,40,1280]{2,1,0:T(8,128)(2,1)S(1)}, u32[]{:S(2)}, u32[]{:S(2)}) collective-permute-start(bf16[16,40,1280]{2,1,0:T(8,128)(2,1)} %get-tuple-element.78), channel_id=1, source_target_pairs={{0,16},{16,0},{32,48},{48,32},{64,80},{80,64},{96,112},{112,96},{1... | collective-permute-start | bytes 4915208 | tf_op jit(solution)/shard_map/ppermute | solution.py:374
  186.6 32.8 %all-to-all-start.3 = ((bf16[16,40,1280]{2,1,0:T(8,128)(2,1)}), bf16[16,40,1280]{2,1,0:T(8,128)(2,1)S(1)}, u32[]{:S(2)}, u32[]{:S(2)}) async-start(bf16[16,40,1280]{2,1,0:T(8,128)(2,1)} %add_convert_fusion), calls=%async_computation.3 | async-start | bytes 3276800 | tf_op jit(solution)/shard_map/all_to_all | solution.py:375
  219.8 6.0 %collective-permute-start.19 = (f32[10,1280]{1,0:T(8,128)S(1)}, f32[10,1280]{1,0:T(8,128)S(1)}, u32[]{:S(2)}, u32[]{:S(2)}) collective-permute-start(f32[10,1280]{1,0:T(8,128)S(1)} %get-tuple-element.81), channel_id=1, source_target_pairs={{0,32},{16,48},{32,64},{48,80},{64,96},{80,112},{96,0},{112,16},{1... | collective-permute-start | bytes 153608 | tf_op jit(solution)/shard_map/ppermute | solution.py:381
  222.3 5.9 %collective-permute-start.20 = (f32[10,1280]{1,0:T(8,128)S(1)}, f32[10,1280]{1,0:T(8,128)S(1)}, u32[]{:S(2)}, u32[]{:S(2)}) collective-permute-start(f32[10,1280]{1,0:T(8,128)S(1)} %get-tuple-element.83), channel_id=1, source_target_pairs={{0,64},{16,80},{32,96},{48,112},{64,0},{80,16},{96,32},{112,48},{1... | collective-permute-start | bytes 153608 | tf_op jit(solution)/shard_map/ppermute | solution.py:381
  224.0 4.4 %collective-permute-start.21 = (f32[10,1280]{1,0:T(8,128)S(1)}, f32[10,1280]{1,0:T(8,128)S(1)}, u32[]{:S(2)}, u32[]{:S(2)}) collective-permute-start(f32[10,1280]{1,0:T(8,128)S(1)} %get-tuple-element.82), channel_id=1, source_target_pairs={{0,96},{16,112},{32,0},{48,16},{64,32},{80,48},{96,64},{112,80},{1... | collective-permute-start | bytes 153608 | tf_op jit(solution)/shard_map/ppermute | solution.py:381
  (6 other events, 10.3 us)

commit v6 on v5

--- a/solution.py
+++ b/solution.py
@@ -17,7 +17,7 @@
 NG = 10
 BF = jnp.bfloat16
 F32 = jnp.float32
-VLIM = 56 * 1024 * 1024
+VLIM = 24 * 1024 * 1024
 
 STEPS = [(k // 2, k % 2) for k in range(8)]
 
@@ -354,16 +354,18 @@
 
     *tb, x = lax.optimization_barrier((*block_pairs(pos, perm, x), x))
     tb = [tb[0]] + [lax.ppermute(tb[k], "aux", pairs_of(k)) for k in range(1, 8)]
-    every, tb[1], tb[2], tb[6], ta = lax.optimization_barrier((every, tb[1], tb[2], tb[6], row_slabs(x)))
-    ta = lax.all_to_all(ta, "orb", split_axis=0, concat_axis=0, tiled=True)
-
+    every, ta = lax.optimization_barrier((every, row_slabs(x)))
     marks = every[:, 2 * W, :128]
-    meta = marks.astype(jnp.int32).reshape(-1)
-    blocks = every[:, : 2 * W].reshape(NOB, 2 * W, BS, BS)
-    v, w, marks = lax.optimization_barrier((*greens(pos, atom_size, meta, blocks, rows, cols), marks))
     pat = jnp.stack([marks, lax.ppermute(marks, "aux", pairs_of(1))])
     pat = jnp.stack([pat] + [lax.ppermute(pat, "aux", pairs_of(2 * dx)) for dx in range(1, 4)])
+    every, pat, tb[1], tb[2], tb[6], ta = lax.optimization_barrier(
+        (every, pat, tb[1], tb[2], tb[6], ta)
+    )
+    ta = lax.all_to_all(ta, "orb", split_axis=0, concat_axis=0, tiled=True)
     pat = pat[..., :32].astype(jnp.int32).reshape(-1)
+    meta = every[:, 2 * W, :128].astype(jnp.int32).reshape(-1)
+    blocks = every[:, : 2 * W].reshape(NOB, 2 * W, BS, BS)
+    v, w = greens(pos, atom_size, meta, blocks, rows, cols)
 
     first = first_products(pos, pat, perm, w, tb)
     first = lax.all_to_all(first, "orb", split_axis=0, concat_axis=0, tiled=True)

time: 230 us -> 228 us (level)
  Pallas kernels: 54.7 us -> 41 us
  local copies, waits for them, and re-layouts: 7.01 us -> 18 us
    ppermute x3, waiting for transfers between devices: 26.3 us -> 4.68 us  [body(): lax.ppermute(pat, 'aux', pairs_of(2 * dx))]
    ppermute x7, waiting for transfers between devices: 6.01 us -> 21.9 us  [body(): lax.ppermute(tb[k], 'aux', pairs_of(k))]
    unnamed x24 -> x32, local copies, waits for them, and re-layouts: 1.76 us -> 11.9 us
    ppermute x7, waiting for transfers between devices: 17.2 us -> 9.98 us  [body(): lax.ppermute(us[k], 'aux', pairs_of(k))]
    all_to_all x1, waiting for transfers between devices: 23 us -> 30 us  [body(): lax.all_to_all(first, 'orb', split_axis=0, concat_axis=0, tiled=True)]
    all_to_all x1, waiting for transfers between devices: 0.01 us -> 5.44 us  [body(): lax.all_to_all(every, 'orb', split_axis=0, concat_axis=0, tiled=True)]
    pallas_call x1, Pallas kernels: 5.74 us -> 0.58 us  [row_slabs(): pl.pallas_call(rows_kernel, grid=(NPD // 2,), in_specs=[pl.BlockSpec((2,...]
    all_to_all x1, starting transfers between devices: 7.22 us -> 4.52 us  [body(): ta = lax.all_to_all(ta, 'orb', split_axis=0, concat_axis=0, tiled=True)]
  transfers between devices with their start and end apart: 26 -> 26, of which waited for: 14 -> 15; matrix products, arithmetic and copies ran while one was open for 2% -> 2% of each run, Pallas kernels for 19% -> 14%
where the time goes in v6:
time: 228 us; the launch traced here: 227 us
  waiting for transfers between devices  107 us (47%)
  starting transfers between devices  55.1 us (24%)
  Pallas kernels  41 us (18%)
  local copies, waits for them, and re-layouts  18 us (8%)
  other arithmetic  5.58 us (2%)
    all_to_all x1, waiting for transfers between devices, body(): lax.all_to_all(first, 'orb', split_axis=0, concat_axis=0, tiled=True)  30 us
    all_to_all x1, waiting for transfers between devices, body(): part = lax.all_to_all(part, 'orb', split_axis=0, concat_axis=0, tiled=True)  25.1 us
    ppermute x7, waiting for transfers between devices, body(): lax.ppermute(tb[k], 'aux', pairs_of(k))  21.9 us
    unnamed x32, local copies, waits for them, and re-layouts  11.9 us
    pallas_call x1, Pallas kernels, second_products(): pl.pallas_call(second_kernel, in_specs=[sspec(), sspec(), vspec(), vspec(...  11 us
    pallas_call x1, Pallas kernels, first_products(): pl.pallas_call(first_kernel, in_specs=[sspec(), sspec(), vspec(), vspec()...  10 us
    ppermute x7, waiting for transfers between devices, body(): lax.ppermute(us[k], 'aux', pairs_of(k))  9.98 us
    pallas_call x1, Pallas kernels, chi_share(): pl.pallas_call(chi_kernel, grid=(5,), in_specs=[sspec(), vspec()] + [vspe...  9.53 us
  transfers between devices with their start and end apart: 26, of which 15 were waited for; matrix products, arithmetic and copies ran while one was open for 2% of the time, Pallas kernels for 14%

profile of v6, /device:TPU:0, one launch (start us, length us, event | category | flops | bytes accessed | tf_op | source)
XLA Modules:
  0.0 227.1 jit_solution(6319280040107367559)
XLA Ops:
  3.6 8.2 %all-to-all-start = ((bf16[16,8,4096]{2,1,0:T(8,128)(2,1)}), bf16[16,8,4096]{2,1,0:T(8,128)(2,1)}, u32[]{:S(2)}, u32[]{:S(2)}) async-start(bf16[16,8,4096]{2,1,0:T(8,128)(2,1)} %broadcast_in_dim.2), calls=%async_computation | async-start | bytes 2097152 | tf_op jit(solution)/shard_map/all_to_all | solution.py:353
  11.9 2.1 copy-done
  14.0 4.4 %block_pairs.1 = (bf16[2,3,10,32,128]{4,3,2,1,0:T(8,128)(2,1)S(1)}, bf16[2,3,10,32,128]{4,3,2,1,0:T(8,128)(2,1)}, bf16[2,3,10,32,128]{4,3,2,1,0:T(8,128)(2,1)}, ...) custom-call(s32[2]{0:T(128)S(1)} %pad_add_fusion.pos, ...), custom_call_target="tpu_custom_call" | custom-call | flops 1000000000 | bytes 8000000 | tf_op jit(solution)/shard_map/block_pairs/pallas_call | solution.py:97
  18.4 1.5 collective-permute-start.5
  19.9 1.8 collective-permute-start.6
  22.3 1.9 copy-done.2
  24.1 5.4 %all-to-all-done = bf16[16,8,4096]{2,1,0:T(8,128)(2,1)} async-done(((bf16[16,8,4096]{2,1,0:T(8,128)(2,1)}), bf16[16,8,4096]{2,1,0:T(8,128)(2,1)}, u32[]{:S(2)}, u32[]{:S(2)}) %all-to-all-start) | async-done | bytes 1048608 | tf_op jit(solution)/shard_map/all_to_all | solution.py:353
  29.6 1.8 copy.14
  32.7 2.8 %collective-permute-start.3 = (bf16[2,16,128]{2,1,0:T(8,128)(2,1)S(1)}, bf16[2,16,128]{2,1,0:T(8,128)(2,1)S(1)}, u32[]{:S(2)}, u32[]{:S(2)}) collective-permute-start(bf16[2,16,128]{2,1,0:T(8,128)(2,1)S(1)} %get-tuple-element.85), channel_id=1, source_target_pairs={{0,96},{16,112},{32,0},{48,16},{64,32},{80,48},{96,64},{112,80},{1... | collective-permute-start | bytes 24584 | tf_op jit(solution)/shard_map/ppermute | solution.py:360
  37.8 2.8 %collective-permute-done.2 = bf16[2,16,128]{2,1,0:T(8,128)(2,1)S(1)} collective-permute-done((bf16[2,16,128]{2,1,0:T(8,128)(2,1)S(1)}, bf16[2,16,128]{2,1,0:T(8,128)(2,1)S(1)}, u32[]{:S(2)}, u32[]{:S(2)}) %collective-permute-start.2) | collective-permute-done | bytes 8224 | tf_op jit(solution)/shard_map/ppermute | solution.py:360
  43.1 4.5 %all-to-all-start.2 = ((bf16[16,30,16,256]{3,2,1,0:T(8,128)(2,1)}), bf16[16,30,16,256]{3,2,1,0:T(8,128)(2,1)}, u32[]{:S(2)}, u32[]{:S(2)}) async-start(bf16[16,30,16,256]{3,2,1,0:T(8,128)(2,1)} %copy-done.2), calls=%async_computation.2 | async-start | bytes 7864320 | tf_op jit(solution)/shard_map/all_to_all | solution.py:364
  49.0 1.9 collective-permute-start.9
  50.9 2.1 collective-permute-start.10
  53.2 2.8 %reshape.61.g_ref = bf16[16,6,64,64]{3,2,1,0:T(8,128)(2,1)S(1)} reshape(bf16[16,6,4096]{2,1,0:T(8,128)(2,1)} %bitcast.33) | data formatting | bytes 1572864 | tf_op jit(solution)/shard_map/reshape | solution.py:367
  56.8 5.5 %greens.1 = (bf16[16,3,64,128]{3,2,1,0:T(8,128)(2,1)S(1)}, bf16[2,192,192]{2,1,0:T(8,128)(2,1)S(1)}) custom-call(s32[2]{0:T(128)S(1)} %pad_add_fusion.pos, s32[16]{0:T(128)S(1)} %copy-done.7, s32[2048]{0:T(1024)S(1)} %bitcast.36, bf16[16,6,64,64]{3,2,1,0:T(8,128)(2,1)S(1)} %reshape.61.g_ref, bf16[2,32,64]{2,1,0:T(8,128)(2,1)S(1)} %copy-done.6, ...), custom_call_target="tpu_custom_call" | custom-call | flops 1000000 | bytes 8000000 | tf_op jit(solution)/shard_map/greens/pallas_call | solution.py:158
  62.3 20.9 %collective-permute-done.7.rest_3_ = bf16[2,3,10,32,128]{4,3,2,1,0:T(8,128)(2,1)} collective-permute-done((bf16[2,3,10,32,128]{4,3,2,1,0:T(8,128)(2,1)}, bf16[2,3,10,32,128]{4,3,2,1,0:T(8,128)(2,1)}, u32[]{:S(2)}, u32[]{:S(2)}) %collective-permute-start.7) | collective-permute-done | bytes 491552 | tf_op jit(solution)/shard_map/ppermute | solution.py:356
  87.3 10.0 %first.1 = bf16[16,6,80,256]{3,2,1,0:T(8,128)(2,1)S(1)} custom-call(s32[2]{0:T(128)S(1)} %pad_add_fusion.pos, s32[4096]{0:T(1024)S(1)} %reshape.59.pat, bf16[256,256]{1,0:T(8,128)(2,1)S(1)} %copy-done.4, bf16[2,192,192]{2,1,0:T(8,128)(2,1)S(1)} %get-tuple-element.58.w_ref, bf16[2,3,10,32,128]{4,3,2,1,0:T(8,128)(2,1)S(1)} %get-tuple-element.59.rest_0_, ...), custom_call_target="tpu_custom_call" | custom-call | flops 3000000000 | bytes 8000000 | tf_op jit(solution)/shard_map/first/pallas_call | solution.py:278
  97.3 1.9 copy-done.3
  99.2 7.1 %all-to-all-start.1 = ((bf16[16,6,80,256]{3,2,1,0:T(8,128)(2,1)}), bf16[16,6,80,256]{3,2,1,0:T(8,128)(2,1)}, u32[]{:S(2)}, u32[]{:S(2)}) async-start(bf16[16,6,80,256]{3,2,1,0:T(8,128)(2,1)} %copy-done.3), calls=%async_computation.1 | async-start | bytes 7864320 | tf_op jit(solution)/shard_map/all_to_all | solution.py:371
  106.2 11.0 %second.1 = (bf16[6,160,256]{2,1,0:T(8,128)(2,1)S(1)}, bf16[6,160,256]{2,1,0:T(8,128)(2,1)S(1)}, bf16[6,160,256]{2,1,0:T(8,128)(2,1)S(1)}, bf16[6,160,256]{2,1,0...) custom-call(s32[2]{0:T(128)S(1)} %pad_add_fusion.pos, ...), custom_call_target="tpu_custom_call" | custom-call | flops 4000000000 | bytes 15000000 | tf_op jit(solution)/shard_map/second/pallas_call | solution.py:217
  118.6 4.0 %collective-permute-start.14 = (bf16[6,160,256]{2,1,0:T(8,128)(2,1)}, bf16[6,160,256]{2,1,0:T(8,128)(2,1)}, u32[]{:S(2)}, u32[]{:S(2)}) collective-permute-start(bf16[6,160,256]{2,1,0:T(8,128)(2,1)} %get-tuple-element.73), channel_id=1, source_target_pairs={{0,64},{16,80},{32,96},{48,112},{64,0},{80,16},{96,32},{112,48},{1... | collective-permute-start | bytes 1474568 | tf_op jit(solution)/shard_map/ppermute | solution.py:373
  122.6 2.0 collective-permute-start.16
  124.6 8.7 %collective-permute-done.12.rest_2_ = bf16[6,160,256]{2,1,0:T(8,128)(2,1)S(1)} collective-permute-done((bf16[6,160,256]{2,1,0:T(8,128)(2,1)S(1)}, bf16[6,160,256]{2,1,0:T(8,128)(2,1)S(1)}, u32[]{:S(2)}, u32[]{:S(2)}) %collective-permute-start.12) | collective-permute-done | bytes 491552 | tf_op jit(solution)/shard_map/ppermute | solution.py:373
  133.8 30.0 %all-to-all-done.1.first_ref = bf16[16,6,80,256]{3,2,1,0:T(8,128)(2,1)} async-done(((bf16[16,6,80,256]{3,2,1,0:T(8,128)(2,1)}), bf16[16,6,80,256]{3,2,1,0:T(8,128)(2,1)}, u32[]{:S(2)}, u32[]{:S(2)}) %all-to-all-start.1) | async-done | bytes 3932192 | tf_op jit(solution)/shard_map/all_to_all | solution.py:371
  166.1 9.5 %chi.1 = (bf16[16,40,1280]{2,1,0:T(8,128)(2,1)S(1)}, f32[16,40,1280]{2,1,0:T(8,128)S(1)}) custom-call(s32[2]{0:T(128)S(1)} %pad_add_fusion.pos, bf16[16,6,80,256]{3,2,1,0:T(8,128)(2,1)} %all-to-all-done.1.first_ref, bf16[6,160,256]{2,1,0:T(8,128)(2,1)S(1)} %copy-done.15, bf16[6,160,256]{2,1,0:T(8,128)(2,1)S(1)} %collective-permute-done.11.rest_1_, ...), custom_call_target="tpu_custom_call" | custom-call | flops 5000000000 | bytes 13000000 | tf_op jit(solution)/shard_map/chi/pallas_call | solution.py:317
  176.0 3.2 %collective-permute-done.18 = bf16[16,40,1280]{2,1,0:T(8,128)(2,1)S(1)} collective-permute-done((bf16[16,40,1280]{2,1,0:T(8,128)(2,1)S(1)}, bf16[16,40,1280]{2,1,0:T(8,128)(2,1)S(1)}, u32[]{:S(2)}, u32[]{:S(2)}) %collective-permute-start.18) | collective-permute-done | bytes 1638432 | tf_op jit(solution)/shard_map/ppermute | solution.py:376
  179.2 1.5 add_convert_fusion
  180.7 9.2 %all-to-all-start.3 = ((bf16[16,40,1280]{2,1,0:T(8,128)(2,1)}), bf16[16,40,1280]{2,1,0:T(8,128)(2,1)S(1)}, u32[]{:S(2)}, u32[]{:S(2)}) async-start(bf16[16,40,1280]{2,1,0:T(8,128)(2,1)} %add_convert_fusion), calls=%async_computation.3 | async-start | bytes 3276800 | tf_op jit(solution)/shard_map/all_to_all | solution.py:377
  190.0 25.1 %all-to-all-done.3 = bf16[16,40,1280]{2,1,0:T(8,128)(2,1)S(1)} async-done(((bf16[16,40,1280]{2,1,0:T(8,128)(2,1)}), bf16[16,40,1280]{2,1,0:T(8,128)(2,1)S(1)}, u32[]{:S(2)}, u32[]{:S(2)}) %all-to-all-start.3) | async-done | bytes 1638432 | tf_op jit(solution)/shard_map/all_to_all | solution.py:377
  215.4 4.5 %collective-permute-start.21 = (f32[10,1280]{1,0:T(8,128)S(1)}, f32[10,1280]{1,0:T(8,128)S(1)}, u32[]{:S(2)}, u32[]{:S(2)}) collective-permute-start(f32[10,1280]{1,0:T(8,128)S(1)} %get-tuple-element.82), channel_id=1, source_target_pairs={{0,96},{16,112},{32,0},{48,16},{64,32},{80,48},{96,64},{112,80},{1... | collective-permute-start | bytes 153608 | tf_op jit(solution)/shard_map/ppermute | solution.py:383
  220.8 1.9 collective-permute-done.21
  222.8 3.2 %collective-permute-done.20 = f32[10,1280]{1,0:T(8,128)S(1)} collective-permute-done((f32[10,1280]{1,0:T(8,128)S(1)}, f32[10,1280]{1,0:T(8,128)S(1)}, u32[]{:S(2)}, u32[]{:S(2)}) %collective-permute-start.20) | collective-permute-done | bytes 51232 | tf_op jit(solution)/shard_map/ppermute | solution.py:383
  (79 shorter events, 23.7 us)
Async XLA Ops:
  0.0 11.9 %copy-start.4 = (bf16[256,256]{1,0:T(8,128)(2,1)S(1)}, bf16[256,256]{1,0:T(8,128)(2,1)}, u32[]{:S(2)}) copy-start(bf16[256,256]{1,0:T(8,128)(2,1)} %constant.56.clone.perm) | copy-start | bytes 393220
  3.6 25.9 %all-to-all-start = ((bf16[16,8,4096]{2,1,0:T(8,128)(2,1)}), bf16[16,8,4096]{2,1,0:T(8,128)(2,1)}, u32[]{:S(2)}, u32[]{:S(2)}) async-start(bf16[16,8,4096]{2,1,0:T(8,128)(2,1)} %broadcast_in_dim.2), calls=%async_computation | async-start | bytes 2097152 | tf_op jit(solution)/shard_map/all_to_all | solution.py:353
  11.9 2.1 copy-start
  14.0 7.6 %copy-start.1 = (bf16[10,16,3,4096]{3,1,2,0:T(8,128)(2,1)S(1)}, bf16[10,16,3,4096]{3,1,2,0:T(8,128)(2,1)}, u32[]{:S(2)}) copy-start(bf16[10,16,3,4096]{3,1,2,0:T(8,128)(2,1)} %param.9) | copy-start | bytes 11796484
  18.4 23.6 %collective-permute-start.4 = (bf16[2,3,10,32,128]{4,3,2,1,0:T(8,128)(2,1)}, bf16[2,3,10,32,128]{4,3,2,1,0:T(8,128)(2,1)S(1)}, u32[]{:S(2)}, u32[]{:S(2)}) collective-permute-start(bf16[2,3,10,32,128]{4,3,2,1,0:T(8,128)(2,1)} %get-tuple-element.52), channel_id=1, source_target_pairs={{0,16},{16,0},{32,48},{48,32},{64,80},{80,64},{96,112},{112,96},{1... | collective-permute-start | bytes 1474568 | tf_op jit(solution)/shard_map/ppermute | solution.py:356
  18.4 23.6 %collective-permute-start.5 = (bf16[2,3,10,32,128]{4,3,2,1,0:T(8,128)(2,1)}, bf16[2,3,10,32,128]{4,3,2,1,0:T(8,128)(2,1)S(1)}, u32[]{:S(2)}, u32[]{:S(2)}) collective-permute-start(bf16[2,3,10,32,128]{4,3,2,1,0:T(8,128)(2,1)} %get-tuple-element.53), channel_id=1, source_target_pairs={{0,32},{16,48},{32,64},{48,80},{64,96},{80,112},{96,0},{112,16},{1... | collective-permute-start | bytes 1474568 | tf_op jit(solution)/shard_map/ppermute | solution.py:356
  19.9 22.1 %collective-permute-start.6 = (bf16[2,3,10,32,128]{4,3,2,1,0:T(8,128)(2,1)S(1)}, bf16[2,3,10,32,128]{4,3,2,1,0:T(8,128)(2,1)S(1)}, u32[]{:S(2)}, u32[]{:S(2)}) collective-permute-start(bf16[2,3,10,32,128]{4,3,2,1,0:T(8,128)(2,1)S(1)} %get-tuple-element.54), channel_id=1, source_target_pairs={{0,96},{16,112},{32,0},{48,16},{64,32},{80,48},{96,64},{112,80},{1... | collective-permute-start | bytes 1474568 | tf_op jit(solution)/shard_map/ppermute | solution.py:356
  31.4 1.2 collective-permute-start
  32.7 4.1 %collective-permute-start.3 = (bf16[2,16,128]{2,1,0:T(8,128)(2,1)S(1)}, bf16[2,16,128]{2,1,0:T(8,128)(2,1)S(1)}, u32[]{:S(2)}, u32[]{:S(2)}) collective-permute-start(bf16[2,16,128]{2,1,0:T(8,128)(2,1)S(1)} %get-tuple-element.85), channel_id=1, source_target_pairs={{0,96},{16,112},{32,0},{48,16},{64,32},{80,48},{96,64},{112,80},{1... | collective-permute-start | bytes 24584 | tf_op jit(solution)/shard_map/ppermute | solution.py:360
  35.4 5.2 %collective-permute-start.2 = (bf16[2,16,128]{2,1,0:T(8,128)(2,1)S(1)}, bf16[2,16,128]{2,1,0:T(8,128)(2,1)S(1)}, u32[]{:S(2)}, u32[]{:S(2)}) collective-permute-start(bf16[2,16,128]{2,1,0:T(8,128)(2,1)S(1)} %get-tuple-element.85), channel_id=1, source_target_pairs={{0,64},{16,80},{32,96},{48,112},{64,0},{80,16},{96,32},{112,48},{1... | collective-permute-start | bytes 24584 | tf_op jit(solution)/shard_map/ppermute | solution.py:360
  36.8 5.1 %collective-permute-start.1 = (bf16[2,16,128]{2,1,0:T(8,128)(2,1)S(1)}, bf16[2,16,128]{2,1,0:T(8,128)(2,1)S(1)}, u32[]{:S(2)}, u32[]{:S(2)}) collective-permute-start(bf16[2,16,128]{2,1,0:T(8,128)(2,1)S(1)} %get-tuple-element.85), channel_id=1, source_target_pairs={{0,32},{16,48},{32,64},{48,80},{64,96},{80,112},{96,0},{112,16},{1... | collective-permute-start | bytes 24584 | tf_op jit(solution)/shard_map/ppermute | solution.py:360
  41.9 14.8 %copy-start.5 = (bf16[2,64,64]{2,1,0:T(8,128)(2,1)S(1)}, bf16[2,64,64]{2,1,0:T(8,128)(2,1)}, u32[]{:S(2)}) copy-start(bf16[2,64,64]{2,1,0:T(8,128)(2,1)} %constant.58.clone.cols_ref) | copy-start | bytes 49156
  41.9 14.8 %copy-start.6 = (bf16[2,32,64]{2,1,0:T(8,128)(2,1)S(1)}, bf16[2,32,64]{2,1,0:T(8,128)(2,1)}, u32[]{:S(2)}) copy-start(bf16[2,32,64]{2,1,0:T(8,128)(2,1)} %constant.57.clone.rows_ref) | copy-start | bytes 24580
  41.9 14.8 %copy-start.7 = (s32[16]{0:T(128)S(1)}, s32[16]{0:T(128)}, u32[]{:S(2)}) copy-start(s32[16]{0:T(128)} %size.1) | copy-start | bytes 196
  43.1 56.1 %all-to-all-start.2 = ((bf16[16,30,16,256]{3,2,1,0:T(8,128)(2,1)}), bf16[16,30,16,256]{3,2,1,0:T(8,128)(2,1)}, u32[]{:S(2)}, u32[]{:S(2)}) async-start(bf16[16,30,16,256]{3,2,1,0:T(8,128)(2,1)} %copy-done.2), calls=%async_computation.2 | async-start | bytes 7864320 | tf_op jit(solution)/shard_map/all_to_all | solution.py:364
  47.6 35.6 %collective-permute-start.7 = (bf16[2,3,10,32,128]{4,3,2,1,0:T(8,128)(2,1)}, bf16[2,3,10,32,128]{4,3,2,1,0:T(8,128)(2,1)}, u32[]{:S(2)}, u32[]{:S(2)}) collective-permute-start(bf16[2,3,10,32,128]{4,3,2,1,0:T(8,128)(2,1)} %get-tuple-element.62), channel_id=1, source_target_pairs={{0,48},{16,32},{32,80},{48,64},{64,112},{80,96},{96,16},{112,0},{1... | collective-permute-start | bytes 1474568 | tf_op jit(solution)/shard_map/ppermute | solution.py:356
  47.7 35.5 %collective-permute-start.8 = (bf16[2,3,10,32,128]{4,3,2,1,0:T(8,128)(2,1)}, bf16[2,3,10,32,128]{4,3,2,1,0:T(8,128)(2,1)}, u32[]{:S(2)}, u32[]{:S(2)}) collective-permute-start(bf16[2,3,10,32,128]{4,3,2,1,0:T(8,128)(2,1)} %get-tuple-element.63), channel_id=1, source_target_pairs={{0,64},{16,80},{32,96},{48,112},{64,0},{80,16},{96,32},{112,48},{1... | collective-permute-start | bytes 1474568 | tf_op jit(solution)/shard_map/ppermute | solution.py:356
  49.0 34.2 %collective-permute-start.9 = (bf16[2,3,10,32,128]{4,3,2,1,0:T(8,128)(2,1)}, bf16[2,3,10,32,128]{4,3,2,1,0:T(8,128)(2,1)}, u32[]{:S(2)}, u32[]{:S(2)}) collective-permute-start(bf16[2,3,10,32,128]{4,3,2,1,0:T(8,128)(2,1)} %get-tuple-element.64), channel_id=1, source_target_pairs={{0,80},{16,64},{32,112},{48,96},{64,16},{80,0},{96,48},{112,32},{1... | collective-permute-start | bytes 1474568 | tf_op jit(solution)/shard_map/ppermute | solution.py:356
  50.9 33.2 %collective-permute-start.10 = (bf16[2,3,10,32,128]{4,3,2,1,0:T(8,128)(2,1)S(1)}, bf16[2,3,10,32,128]{4,3,2,1,0:T(8,128)(2,1)}, u32[]{:S(2)}, u32[]{:S(2)}) collective-permute-start(bf16[2,3,10,32,128]{4,3,2,1,0:T(8,128)(2,1)S(1)} %get-tuple-element.66), channel_id=1, source_target_pairs={{0,112},{16,96},{32,16},{48,0},{64,48},{80,32},{96,80},{112,64},{1... | collective-permute-start | bytes 1474568 | tf_op jit(solution)/shard_map/ppermute | solution.py:356
  99.2 64.6 %all-to-all-start.1 = ((bf16[16,6,80,256]{3,2,1,0:T(8,128)(2,1)}), bf16[16,6,80,256]{3,2,1,0:T(8,128)(2,1)}, u32[]{:S(2)}, u32[]{:S(2)}) async-start(bf16[16,6,80,256]{3,2,1,0:T(8,128)(2,1)} %copy-done.3), calls=%async_computation.1 | async-start | bytes 7864320 | tf_op jit(solution)/shard_map/all_to_all | solution.py:371
  118.0 4.5 %collective-permute-start.11 = (bf16[6,160,256]{2,1,0:T(8,128)(2,1)S(1)}, bf16[6,160,256]{2,1,0:T(8,128)(2,1)S(1)}, u32[]{:S(2)}, u32[]{:S(2)}) collective-permute-start(bf16[6,160,256]{2,1,0:T(8,128)(2,1)S(1)} %get-tuple-element.70), channel_id=1, source_target_pairs={{0,16},{16,0},{32,48},{48,32},{64,80},{80,64},{96,112},{112,96},{1... | collective-permute-start | bytes 1474568 | tf_op jit(solution)/shard_map/ppermute | solution.py:373
  118.1 15.2 %collective-permute-start.12 = (bf16[6,160,256]{2,1,0:T(8,128)(2,1)S(1)}, bf16[6,160,256]{2,1,0:T(8,128)(2,1)S(1)}, u32[]{:S(2)}, u32[]{:S(2)}) collective-permute-start(bf16[6,160,256]{2,1,0:T(8,128)(2,1)S(1)} %get-tuple-element.71), channel_id=1, source_target_pairs={{0,32},{16,48},{32,64},{48,80},{64,96},{80,112},{96,0},{112,16},{1... | collective-permute-start | bytes 1474568 | tf_op jit(solution)/shard_map/ppermute | solution.py:373
  118.1 45.7 %collective-permute-start.13 = (bf16[6,160,256]{2,1,0:T(8,128)(2,1)}, bf16[6,160,256]{2,1,0:T(8,128)(2,1)S(1)}, u32[]{:S(2)}, u32[]{:S(2)}) collective-permute-start(bf16[6,160,256]{2,1,0:T(8,128)(2,1)} %get-tuple-element.72), channel_id=1, source_target_pairs={{0,48},{16,32},{32,80},{48,64},{64,112},{80,96},{96,16},{112,0},{1... | collective-permute-start | bytes 1474568 | tf_op jit(solution)/shard_map/ppermute | solution.py:373
  118.6 45.1 %collective-permute-start.14 = (bf16[6,160,256]{2,1,0:T(8,128)(2,1)}, bf16[6,160,256]{2,1,0:T(8,128)(2,1)}, u32[]{:S(2)}, u32[]{:S(2)}) collective-permute-start(bf16[6,160,256]{2,1,0:T(8,128)(2,1)} %get-tuple-element.73), channel_id=1, source_target_pairs={{0,64},{16,80},{32,96},{48,112},{64,0},{80,16},{96,32},{112,48},{1... | collective-permute-start | bytes 1474568 | tf_op jit(solution)/shard_map/ppermute | solution.py:373
  122.6 42.5 %collective-permute-start.15 = (bf16[6,160,256]{2,1,0:T(8,128)(2,1)S(1)}, bf16[6,160,256]{2,1,0:T(8,128)(2,1)}, u32[]{:S(2)}, u32[]{:S(2)}) collective-permute-start(bf16[6,160,256]{2,1,0:T(8,128)(2,1)S(1)} %get-tuple-element.74), channel_id=1, source_target_pairs={{0,80},{16,64},{32,112},{48,96},{64,16},{80,0},{96,48},{112,32},{1... | collective-permute-start | bytes 1474568 | tf_op jit(solution)/shard_map/ppermute | solution.py:373
  122.6 42.5 %collective-permute-start.16 = (bf16[6,160,256]{2,1,0:T(8,128)(2,1)S(1)}, bf16[6,160,256]{2,1,0:T(8,128)(2,1)}, u32[]{:S(2)}, u32[]{:S(2)}) collective-permute-start(bf16[6,160,256]{2,1,0:T(8,128)(2,1)S(1)} %get-tuple-element.75), channel_id=1, source_target_pairs={{0,96},{16,112},{32,0},{48,16},{64,32},{80,48},{96,64},{112,80},{1... | collective-permute-start | bytes 1474568 | tf_op jit(solution)/shard_map/ppermute | solution.py:373
  133.3 31.8 %collective-permute-start.17 = (bf16[6,160,256]{2,1,0:T(8,128)(2,1)S(1)}, bf16[6,160,256]{2,1,0:T(8,128)(2,1)}, u32[]{:S(2)}, u32[]{:S(2)}) collective-permute-start(bf16[6,160,256]{2,1,0:T(8,128)(2,1)S(1)} %get-tuple-element.76), channel_id=1, source_target_pairs={{0,112},{16,96},{32,16},{48,0},{64,48},{80,32},{96,80},{112,64},{1... | collective-permute-start | bytes 1474568 | tf_op jit(solution)/shard_map/ppermute | solution.py:373
  175.6 3.6 %collective-permute-start.18 = (bf16[16,40,1280]{2,1,0:T(8,128)(2,1)S(1)}, bf16[16,40,1280]{2,1,0:T(8,128)(2,1)S(1)}, u32[]{:S(2)}, u32[]{:S(2)}) collective-permute-start(bf16[16,40,1280]{2,1,0:T(8,128)(2,1)S(1)} %get-tuple-element.78), channel_id=1, source_target_pairs={{0,16},{16,0},{32,48},{48,32},{64,80},{80,64},{96,112},{112,96},{1... | collective-permute-start | bytes 4915208 | tf_op jit(solution)/shard_map/ppermute | solution.py:376
  180.7 34.3 %all-to-all-start.3 = ((bf16[16,40,1280]{2,1,0:T(8,128)(2,1)}), bf16[16,40,1280]{2,1,0:T(8,128)(2,1)S(1)}, u32[]{:S(2)}, u32[]{:S(2)}) async-start(bf16[16,40,1280]{2,1,0:T(8,128)(2,1)} %add_convert_fusion), calls=%async_computation.3 | async-start | bytes 3276800 | tf_op jit(solution)/shard_map/all_to_all | solution.py:377
  215.4 7.4 %collective-permute-start.21 = (f32[10,1280]{1,0:T(8,128)S(1)}, f32[10,1280]{1,0:T(8,128)S(1)}, u32[]{:S(2)}, u32[]{:S(2)}) collective-permute-start(f32[10,1280]{1,0:T(8,128)S(1)} %get-tuple-element.82), channel_id=1, source_target_pairs={{0,96},{16,112},{32,0},{48,16},{64,32},{80,48},{96,64},{112,80},{1... | collective-permute-start | bytes 153608 | tf_op jit(solution)/shard_map/ppermute | solution.py:383
  219.9 6.0 %collective-permute-start.20 = (f32[10,1280]{1,0:T(8,128)S(1)}, f32[10,1280]{1,0:T(8,128)S(1)}, u32[]{:S(2)}, u32[]{:S(2)}) collective-permute-start(f32[10,1280]{1,0:T(8,128)S(1)} %get-tuple-element.83), channel_id=1, source_target_pairs={{0,64},{16,80},{32,96},{48,112},{64,0},{80,16},{96,32},{112,48},{1... | collective-permute-start | bytes 153608 | tf_op jit(solution)/shard_map/ppermute | solution.py:383
  219.9 6.5 %collective-permute-start.19 = (f32[10,1280]{1,0:T(8,128)S(1)}, f32[10,1280]{1,0:T(8,128)S(1)}, u32[]{:S(2)}, u32[]{:S(2)}) collective-permute-start(f32[10,1280]{1,0:T(8,128)S(1)} %get-tuple-element.81), channel_id=1, source_target_pairs={{0,32},{16,48},{32,64},{48,80},{64,96},{80,112},{96,0},{112,16},{1... | collective-permute-start | bytes 153608 | tf_op jit(solution)/shard_map/ppermute | solution.py:383
  (10 other events, 11.5 us)

commit v7 on v5

--- a/solution.py
+++ b/solution.py
@@ -17,9 +17,13 @@
 NG = 10
 BF = jnp.bfloat16
 F32 = jnp.float32
-VLIM = 56 * 1024 * 1024
+VLIM = 24 * 1024 * 1024
 
 STEPS = [(k // 2, k % 2) for k in range(8)]
+
+
+TROWS = 2 * W * NPD * 32
+CARRIERS = (3, 4, 7)
 
 
 def pairs_of(k):
@@ -242,7 +246,8 @@
                 rows = []
                 for d in range(W):
                     keep = pat[(k * NOB + n) * 32 + lax.div(o * NPD + p, ABS) * W + d] > 0
-                    x = tb[k][i, d, p]
+                    row = pl.multiple_of(((i * W + d) * NPD + p) * 32, 32)
+                    x = tb[k][pl.ds(row, 32)]
                     x = jnp.where(keep, x, jnp.zeros_like(x))
                     rows.append(x)
                     rows.append(jnp.concatenate([x[:, 64:], x[:, :64]], axis=1))
@@ -353,17 +358,23 @@
     every = lax.all_to_all(every, "orb", split_axis=0, concat_axis=0, tiled=True)
 
     *tb, x = lax.optimization_barrier((*block_pairs(pos, perm, x), x))
-    tb = [tb[0]] + [lax.ppermute(tb[k], "aux", pairs_of(k)) for k in range(1, 8)]
-    every, tb[1], tb[2], tb[6], ta = lax.optimization_barrier((every, tb[1], tb[2], tb[6], row_slabs(x)))
+    tb = [t.reshape(TROWS, 128) for t in tb]
+    for k in (1, 2, 6):
+        tb[k] = lax.ppermute(tb[k], "aux", pairs_of(k))
+    marks, ta = lax.optimization_barrier((every[:, 2 * W, :128], row_slabs(x)))
+    both = jnp.concatenate([marks, lax.ppermute(marks, "aux", pairs_of(1))], axis=0)
+    both, tb[1], tb[2], tb[6], ta = lax.optimization_barrier((both, tb[1], tb[2], tb[6], ta))
     ta = lax.all_to_all(ta, "orb", split_axis=0, concat_axis=0, tiled=True)
-
-    marks = every[:, 2 * W, :128]
+    for k in CARRIERS:
+        tb[k] = jnp.concatenate([tb[k], both], axis=0)
+    for k in (3, 4, 5, 7):
+        tb[k] = lax.ppermute(tb[k], "aux", pairs_of(k))
+    back, far, ahead = [tb[k][TROWS:, :32] for k in CARRIERS]
+    pat = jnp.concatenate([both[:, :32], back[16:], back[:16], far, ahead[16:], ahead[:16]], axis=0)
+    pat = pat.astype(jnp.int32).reshape(-1)
     meta = marks.astype(jnp.int32).reshape(-1)
     blocks = every[:, : 2 * W].reshape(NOB, 2 * W, BS, BS)
-    v, w, marks = lax.optimization_barrier((*greens(pos, atom_size, meta, blocks, rows, cols), marks))
-    pat = jnp.stack([marks, lax.ppermute(marks, "aux", pairs_of(1))])
-    pat = jnp.stack([pat] + [lax.ppermute(pat, "aux", pairs_of(2 * dx)) for dx in range(1, 4)])
-    pat = pat[..., :32].astype(jnp.int32).reshape(-1)
+    v, w = greens(pos, atom_size, meta, blocks, rows, cols)
 
     first = first_products(pos, pat, perm, w, tb)
     first = lax.all_to_all(first, "orb", split_axis=0, concat_axis=0, tiled=True)

time: 230 us -> 228 us (level)
  Pallas kernels: 54.7 us -> 39.1 us
  local copies, waits for them, and re-layouts: 7.01 us -> 22.2 us
    all_to_all x1, waiting for transfers between devices: 23 us -> 0.01 us  [body(): lax.all_to_all(first, 'orb', split_axis=0, concat_axis=0, tiled=True)]
    ppermute x7, waiting for transfers between devices: 17.2 us -> 39.9 us  [body(): lax.ppermute(us[k], 'aux', pairs_of(k))]
    unnamed x24 -> x45, local copies, waits for them, and re-layouts: 1.76 us -> 16.5 us
    ppermute x11 -> x8, waiting for transfers between devices: 33.5 us -> 26.6 us  [the longest x7 25.5 us: body(): tb[k] = lax.ppermute(tb[k], 'aux', pairs_of(k))]
    pallas_call x1, Pallas kernels: 5.74 us -> 0.58 us  [row_slabs(): pl.pallas_call(rows_kernel, grid=(NPD // 2,), in_specs=[pl.BlockSpec((2,...]
    all_to_all x1, waiting for transfers between devices: 0.01 us -> 4.79 us  [body(): lax.all_to_all(every, 'orb', split_axis=0, concat_axis=0, tiled=True)]
    all_to_all x1, starting transfers between devices: 6.93 us -> 10.6 us  [body(): lax.all_to_all(first, 'orb', split_axis=0, concat_axis=0, tiled=True)]
    pallas_call x1, Pallas kernels: 12.7 us -> 9.56 us  [first_products(): pl.pallas_call(first_kernel, in_specs=[sspec(), sspec(), vspec(), vspec()...]
  transfers between devices with their start and end apart: 26 -> 23, of which waited for: 14 -> 14; matrix products, arithmetic and copies ran while one was open for 2% -> 2% of each run, Pallas kernels for 19% -> 13%
where the time goes in v7:
time: 228 us; the launch traced here: 227 us
  waiting for transfers between devices  105 us (46%)
  starting transfers between devices  53.6 us (24%)
  Pallas kernels  39.1 us (17%)
  local copies, waits for them, and re-layouts  22.2 us (10%)
  other arithmetic  5.98 us (3%)
    ppermute x7, waiting for transfers between devices, body(): lax.ppermute(us[k], 'aux', pairs_of(k))  39.9 us
    all_to_all x1, waiting for transfers between devices, body(): part = lax.all_to_all(part, 'orb', split_axis=0, concat_axis=0, tiled=True)  25.6 us
    ppermute x7, waiting for transfers between devices, body(): tb[k] = lax.ppermute(tb[k], 'aux', pairs_of(k))  25.5 us
    unnamed x45, local copies, waits for them, and re-layouts  16.5 us
    all_to_all x1, starting transfers between devices, body(): lax.all_to_all(first, 'orb', split_axis=0, concat_axis=0, tiled=True)  10.6 us
    pallas_call x1, Pallas kernels, second_products(): pl.pallas_call(second_kernel, in_specs=[sspec(), sspec(), vspec(), vspec(...  10.3 us
    pallas_call x1, Pallas kernels, first_products(): pl.pallas_call(first_kernel, in_specs=[sspec(), sspec(), vspec(), vspec()...  9.56 us
    ppermute x7, starting transfers between devices, body(): tb[k] = lax.ppermute(tb[k], 'aux', pairs_of(k))  9.01 us
  transfers between devices with their start and end apart: 23, of which 14 were waited for; matrix products, arithmetic and copies ran while one was open for 2% of the time, Pallas kernels for 13%

profile of v7, /device:TPU:0, one launch (start us, length us, event | category | flops | bytes accessed | tf_op | source)
XLA Modules:
  0.0 226.7 jit_solution(13991191856465952185)
XLA Ops:
  3.6 8.2 %all-to-all-start = ((bf16[16,8,4096]{2,1,0:T(8,128)(2,1)}), bf16[16,8,4096]{2,1,0:T(8,128)(2,1)}, u32[]{:S(2)}, u32[]{:S(2)}) async-start(bf16[16,8,4096]{2,1,0:T(8,128)(2,1)} %broadcast_in_dim.2), calls=%async_computation | async-start | bytes 2097152 | tf_op jit(solution)/shard_map/all_to_all | solution.py:358
  11.9 2.1 copy-done
  14.0 4.2 %block_pairs.1 = (bf16[2,3,10,32,128]{4,3,2,1,0:T(8,128)(2,1)S(1)}, bf16[2,3,10,32,128]{4,3,2,1,0:T(8,128)(2,1)}, bf16[2,3,10,32,128]{4,3,2,1,0:T(8,128)(2,1)}, ...) custom-call(s32[2]{0:T(128)S(1)} %pad_add_fusion.pos, ...), custom_call_target="tpu_custom_call" | custom-call | flops 1000000000 | bytes 8000000 | tf_op jit(solution)/shard_map/block_pairs/pallas_call | solution.py:101
  19.1 1.5 collective-permute-start.2
  20.5 1.8 collective-permute-start.3
  22.9 1.9 copy-done.2
  24.8 4.8 %all-to-all-done = bf16[16,8,4096]{2,1,0:T(8,128)(2,1)} async-done(((bf16[16,8,4096]{2,1,0:T(8,128)(2,1)}), bf16[16,8,4096]{2,1,0:T(8,128)(2,1)}, u32[]{:S(2)}, u32[]{:S(2)}) %all-to-all-start) | async-done | bytes 1048608 | tf_op jit(solution)/shard_map/all_to_all | solution.py:358
  31.6 2.5 %collective-permute-done.2.rest_2_ = bf16[1920,128]{1,0:T(8,128)(2,1)S(1)} collective-permute-done((bf16[1920,128]{1,0:T(8,128)(2,1)}, bf16[1920,128]{1,0:T(8,128)(2,1)S(1)}, u32[]{:S(2)}, u32[]{:S(2)}) %collective-permute-start.2) | collective-permute-done | bytes 491552 | tf_op jit(solution)/shard_map/ppermute | solution.py:363
  35.1 7.2 %all-to-all-start.2 = ((bf16[16,30,16,256]{3,2,1,0:T(8,128)(2,1)}), bf16[16,30,16,256]{3,2,1,0:T(8,128)(2,1)}, u32[]{:S(2)}, u32[]{:S(2)}) async-start(bf16[16,30,16,256]{3,2,1,0:T(8,128)(2,1)} %copy-done.2), calls=%async_computation.2 | async-start | bytes 7864320 | tf_op jit(solution)/shard_map/all_to_all | solution.py:367
  43.5 1.5 collective-permute-start.6
  46.9 2.3 %collective-permute-start.7 = (bf16[1920,128]{1,0:T(8,128)(2,1)}, bf16[1920,128]{1,0:T(8,128)(2,1)}, u32[]{:S(2)}, u32[]{:S(2)}) collective-permute-start(bf16[1920,128]{1,0:T(8,128)(2,1)} %bitcast.14), channel_id=1, source_target_pairs={{0,80},{16,64},{32,112},{48,96},{64,16},{80,0},{96,48},{112,32},{1... | collective-permute-start | bytes 1474568 | tf_op jit(solution)/shard_map/ppermute | solution.py:371
  49.3 2.8 %reshape.93.g_ref = bf16[16,6,64,64]{3,2,1,0:T(8,128)(2,1)S(1)} reshape(bf16[16,6,4096]{2,1,0:T(8,128)(2,1)} %bitcast.35) | data formatting | bytes 1572864 | tf_op jit(solution)/shard_map/reshape | solution.py:376
  52.1 5.5 %greens.1 = (bf16[16,3,64,128]{3,2,1,0:T(8,128)(2,1)S(1)}, bf16[2,192,192]{2,1,0:T(8,128)(2,1)S(1)}) custom-call(s32[2]{0:T(128)S(1)} %pad_add_fusion.pos, s32[16]{0:T(128)S(1)} %copy-done.7, s32[2048]{0:T(1024)S(1)} %bitcast_convert_fusion.meta.pat, bf16[16,6,64,64]{3,2,1,0:T(8,128)(2,1)S(1)} %reshape.93.g_ref, bf16[2,32,64]{2,1,0:T(8,128)(2,1)S(1)} %copy-done.6, ...), custom_call_target="tpu_custom_call" | custom-call | flops 1000000 | bytes 8000000 | tf_op jit(solution)/shard_map/greens/pallas_call | solution.py:162
  58.9 1.9 collective-permute-done.5.rest_4_
  60.8 11.0 %collective-permute-done.4.rest_3_ = bf16[1952,128]{1,0:T(8,128)(2,1)S(1)} collective-permute-done((bf16[1952,128]{1,0:T(8,128)(2,1)}, bf16[1952,128]{1,0:T(8,128)(2,1)S(1)}, u32[]{:S(2)}, u32[]{:S(2)}) %collective-permute-start.4) | collective-permute-done | bytes 499744 | tf_op jit(solution)/shard_map/ppermute | solution.py:371
  72.3 10.1 %collective-permute-done.7.rest_5_ = bf16[1920,128]{1,0:T(8,128)(2,1)} collective-permute-done((bf16[1920,128]{1,0:T(8,128)(2,1)}, bf16[1920,128]{1,0:T(8,128)(2,1)}, u32[]{:S(2)}, u32[]{:S(2)}) %collective-permute-start.7) | collective-permute-done | bytes 491552 | tf_op jit(solution)/shard_map/ppermute | solution.py:371
  86.5 9.6 %first.1 = bf16[16,6,80,256]{3,2,1,0:T(8,128)(2,1)S(1)} custom-call(s32[2]{0:T(128)S(1)} %pad_add_fusion.pos, s32[4096]{0:T(1024)S(1)} %reshape.90.pat, bf16[256,256]{1,0:T(8,128)(2,1)S(1)} %copy-done.4, bf16[2,192,192]{2,1,0:T(8,128)(2,1)S(1)} %get-tuple-element.59.w_ref, bf16[1920,128]{1,0:T(8,128)(2,1)S(1)} %bitcast.41, bf16[1920,128]{1,0:T(8,128)(2,1)S(1)} %copy-done.13, ...), custom_call_target="tpu_custom_call" | custom-call | flops 3000000000 | bytes 8000000 | tf_op jit(solution)/shard_map/first/pallas_call | solution.py:283
  96.1 2.0 copy-done.3
  98.5 10.6 %all-to-all-start.1 = ((bf16[16,6,80,256]{3,2,1,0:T(8,128)(2,1)}), bf16[16,6,80,256]{3,2,1,0:T(8,128)(2,1)}, u32[]{:S(2)}, u32[]{:S(2)}) async-start(bf16[16,6,80,256]{3,2,1,0:T(8,128)(2,1)} %copy-done.3), calls=%async_computation.1 | async-start | bytes 7864320 | tf_op jit(solution)/shard_map/all_to_all | solution.py:380
  109.1 10.3 %second.1 = (bf16[6,160,256]{2,1,0:T(8,128)(2,1)S(1)}, bf16[6,160,256]{2,1,0:T(8,128)(2,1)S(1)}, bf16[6,160,256]{2,1,0:T(8,128)(2,1)S(1)}, bf16[6,160,256]{2,1,0...) custom-call(s32[2]{0:T(128)S(1)} %pad_add_fusion.pos, ...), custom_call_target="tpu_custom_call" | custom-call | flops 4000000000 | bytes 15000000 | tf_op jit(solution)/shard_map/second/pallas_call | solution.py:221
  120.2 4.5 %collective-permute-start.11 = (bf16[6,160,256]{2,1,0:T(8,128)(2,1)S(1)}, bf16[6,160,256]{2,1,0:T(8,128)(2,1)S(1)}, u32[]{:S(2)}, u32[]{:S(2)}) collective-permute-start(bf16[6,160,256]{2,1,0:T(8,128)(2,1)S(1)} %get-tuple-element.71), channel_id=1, source_target_pairs={{0,64},{16,80},{32,96},{48,112},{64,0},{80,16},{96,32},{112,48},{1... | collective-permute-start | bytes 1474568 | tf_op jit(solution)/shard_map/ppermute | solution.py:382
  124.7 1.8 collective-permute-start.13
  126.5 8.9 %collective-permute-done.9.rest_2_ = bf16[6,160,256]{2,1,0:T(8,128)(2,1)S(1)} collective-permute-done((bf16[6,160,256]{2,1,0:T(8,128)(2,1)S(1)}, bf16[6,160,256]{2,1,0:T(8,128)(2,1)S(1)}, u32[]{:S(2)}, u32[]{:S(2)}) %collective-permute-start.9) | collective-permute-done | bytes 491552 | tf_op jit(solution)/shard_map/ppermute | solution.py:382
  135.4 30.8 %collective-permute-done.10.rest_3_ = bf16[6,160,256]{2,1,0:T(8,128)(2,1)S(1)} collective-permute-done((bf16[6,160,256]{2,1,0:T(8,128)(2,1)S(1)}, bf16[6,160,256]{2,1,0:T(8,128)(2,1)S(1)}, u32[]{:S(2)}, u32[]{:S(2)}) %collective-permute-start.10) | collective-permute-done | bytes 491552 | tf_op jit(solution)/shard_map/ppermute | solution.py:382
  169.3 9.0 %chi.1 = (bf16[16,40,1280]{2,1,0:T(8,128)(2,1)S(1)}, f32[16,40,1280]{2,1,0:T(8,128)S(1)}) custom-call(s32[2]{0:T(128)S(1)} %pad_add_fusion.pos, bf16[16,6,80,256]{3,2,1,0:T(8,128)(2,1)} %all-to-all-done.1.first_ref, bf16[6,160,256]{2,1,0:T(8,128)(2,1)S(1)} %copy-done.21, bf16[6,160,256]{2,1,0:T(8,128)(2,1)S(1)} %collective-permute-done.8.rest_1_, ...), custom_call_target="tpu_custom_call" | custom-call | flops 5000000000 | bytes 13000000 | tf_op jit(solution)/shard_map/chi/pallas_call | solution.py:322
  179.0 3.1 %collective-permute-done.15 = bf16[16,40,1280]{2,1,0:T(8,128)(2,1)S(1)} collective-permute-done((bf16[16,40,1280]{2,1,0:T(8,128)(2,1)S(1)}, bf16[16,40,1280]{2,1,0:T(8,128)(2,1)S(1)}, u32[]{:S(2)}, u32[]{:S(2)}) %collective-permute-start.15) | collective-permute-done | bytes 1638432 | tf_op jit(solution)/shard_map/ppermute | solution.py:385
  182.1 1.5 add_convert_fusion
  183.6 7.2 %all-to-all-start.3 = ((bf16[16,40,1280]{2,1,0:T(8,128)(2,1)}), bf16[16,40,1280]{2,1,0:T(8,128)(2,1)S(1)}, u32[]{:S(2)}, u32[]{:S(2)}) async-start(bf16[16,40,1280]{2,1,0:T(8,128)(2,1)} %add_convert_fusion), calls=%async_computation.3 | async-start | bytes 3276800 | tf_op jit(solution)/shard_map/all_to_all | solution.py:386
  190.9 25.6 %all-to-all-done.3 = bf16[16,40,1280]{2,1,0:T(8,128)(2,1)S(1)} async-done(((bf16[16,40,1280]{2,1,0:T(8,128)(2,1)}), bf16[16,40,1280]{2,1,0:T(8,128)(2,1)S(1)}, u32[]{:S(2)}, u32[]{:S(2)}) %all-to-all-start.3) | async-done | bytes 1638432 | tf_op jit(solution)/shard_map/all_to_all | solution.py:386
  217.2 2.9 %collective-permute-start.18 = (f32[10,1280]{1,0:T(8,128)S(1)}, f32[10,1280]{1,0:T(8,128)S(1)}, u32[]{:S(2)}, u32[]{:S(2)}) collective-permute-start(f32[10,1280]{1,0:T(8,128)S(1)} %get-tuple-element.82), channel_id=1, source_target_pairs={{0,96},{16,112},{32,0},{48,16},{64,32},{80,48},{96,64},{112,80},{1... | collective-permute-start | bytes 153608 | tf_op jit(solution)/shard_map/ppermute | solution.py:392
  221.0 1.9 collective-permute-done.16
  222.9 3.1 %collective-permute-done.17 = f32[10,1280]{1,0:T(8,128)S(1)} collective-permute-done((f32[10,1280]{1,0:T(8,128)S(1)}, f32[10,1280]{1,0:T(8,128)S(1)}, u32[]{:S(2)}, u32[]{:S(2)}) %collective-permute-start.17) | collective-permute-done | bytes 51232 | tf_op jit(solution)/shard_map/ppermute | solution.py:392
  (96 shorter events, 24.3 us)
Async XLA Ops:
  0.0 11.9 %copy-start.4 = (bf16[256,256]{1,0:T(8,128)(2,1)S(1)}, bf16[256,256]{1,0:T(8,128)(2,1)}, u32[]{:S(2)}) copy-start(bf16[256,256]{1,0:T(8,128)(2,1)} %constant.56.clone.perm) | copy-start | bytes 393220
  3.6 25.9 %all-to-all-start = ((bf16[16,8,4096]{2,1,0:T(8,128)(2,1)}), bf16[16,8,4096]{2,1,0:T(8,128)(2,1)}, u32[]{:S(2)}, u32[]{:S(2)}) async-start(bf16[16,8,4096]{2,1,0:T(8,128)(2,1)} %broadcast_in_dim.2), calls=%async_computation | async-start | bytes 2097152 | tf_op jit(solution)/shard_map/all_to_all | solution.py:358
  11.9 2.1 copy-start
  14.0 8.3 %copy-start.1 = (bf16[10,16,3,4096]{3,1,2,0:T(8,128)(2,1)S(1)}, bf16[10,16,3,4096]{3,1,2,0:T(8,128)(2,1)}, u32[]{:S(2)}) copy-start(bf16[10,16,3,4096]{3,1,2,0:T(8,128)(2,1)} %param.9) | copy-start | bytes 11796484
  19.0 12.5 %collective-permute-start.1 = (bf16[1920,128]{1,0:T(8,128)(2,1)}, bf16[1920,128]{1,0:T(8,128)(2,1)S(1)}, u32[]{:S(2)}, u32[]{:S(2)}) collective-permute-start(bf16[1920,128]{1,0:T(8,128)(2,1)} %bitcast.6), channel_id=1, source_target_pairs={{0,16},{16,0},{32,48},{48,32},{64,80},{80,64},{96,112},{112,96},{1... | collective-permute-start | bytes 1474568 | tf_op jit(solution)/shard_map/ppermute | solution.py:363
  19.1 15.1 %collective-permute-start.2 = (bf16[1920,128]{1,0:T(8,128)(2,1)}, bf16[1920,128]{1,0:T(8,128)(2,1)S(1)}, u32[]{:S(2)}, u32[]{:S(2)}) collective-permute-start(bf16[1920,128]{1,0:T(8,128)(2,1)} %bitcast.7), channel_id=1, source_target_pairs={{0,32},{16,48},{32,64},{48,80},{64,96},{80,112},{96,0},{112,16},{1... | collective-permute-start | bytes 1474568 | tf_op jit(solution)/shard_map/ppermute | solution.py:363
  20.5 13.6 %collective-permute-start.3 = (bf16[1920,128]{1,0:T(8,128)(2,1)}, bf16[1920,128]{1,0:T(8,128)(2,1)S(1)}, u32[]{:S(2)}, u32[]{:S(2)}) collective-permute-start(bf16[1920,128]{1,0:T(8,128)(2,1)} %bitcast.8), channel_id=1, source_target_pairs={{0,96},{16,112},{32,0},{48,16},{64,32},{80,48},{96,64},{112,80},{1... | collective-permute-start | bytes 1474568 | tf_op jit(solution)/shard_map/ppermute | solution.py:363
  30.3 1.2 collective-permute-start
  31.6 2.5 %copy-start.12 = (bf16[1920,128]{1,0:T(8,128)(2,1)}, bf16[1920,128]{1,0:T(8,128)(2,1)S(1)}, u32[]{:S(2)}) copy-start(bf16[1920,128]{1,0:T(8,128)(2,1)S(1)} %collective-permute-done.1.rest_1_) | copy-start | bytes 1474564
  35.1 63.4 %all-to-all-start.2 = ((bf16[16,30,16,256]{3,2,1,0:T(8,128)(2,1)}), bf16[16,30,16,256]{3,2,1,0:T(8,128)(2,1)}, u32[]{:S(2)}, u32[]{:S(2)}) async-start(bf16[16,30,16,256]{3,2,1,0:T(8,128)(2,1)} %copy-done.2), calls=%async_computation.2 | async-start | bytes 7864320 | tf_op jit(solution)/shard_map/all_to_all | solution.py:367
  42.3 9.8 %copy-start.5 = (bf16[2,64,64]{2,1,0:T(8,128)(2,1)S(1)}, bf16[2,64,64]{2,1,0:T(8,128)(2,1)}, u32[]{:S(2)}) copy-start(bf16[2,64,64]{2,1,0:T(8,128)(2,1)} %constant.58.clone.cols_ref) | copy-start | bytes 49156
  42.3 9.8 %copy-start.6 = (bf16[2,32,64]{2,1,0:T(8,128)(2,1)S(1)}, bf16[2,32,64]{2,1,0:T(8,128)(2,1)}, u32[]{:S(2)}) copy-start(bf16[2,32,64]{2,1,0:T(8,128)(2,1)} %constant.57.clone.rows_ref) | copy-start | bytes 24580
  42.3 9.8 %copy-start.7 = (s32[16]{0:T(128)S(1)}, s32[16]{0:T(128)}, u32[]{:S(2)}) copy-start(s32[16]{0:T(128)} %size.1) | copy-start | bytes 196
  43.5 15.2 %collective-permute-start.6 = (bf16[1952,128]{1,0:T(8,128)(2,1)}, bf16[1952,128]{1,0:T(8,128)(2,1)S(1)}, u32[]{:S(2)}, u32[]{:S(2)}) collective-permute-start(bf16[1952,128]{1,0:T(8,128)(2,1)} %get-tuple-element.84), channel_id=1, source_target_pairs={{0,112},{16,96},{32,16},{48,0},{64,48},{80,32},{96,80},{112,64},{1... | collective-permute-start | bytes 1499144 | tf_op jit(solution)/shard_map/ppermute | solution.py:371
  45.0 15.8 %collective-permute-start.5 = (bf16[1952,128]{1,0:T(8,128)(2,1)}, bf16[1952,128]{1,0:T(8,128)(2,1)S(1)}, u32[]{:S(2)}, u32[]{:S(2)}) collective-permute-start(bf16[1952,128]{1,0:T(8,128)(2,1)} %get-tuple-element.85), channel_id=1, source_target_pairs={{0,64},{16,80},{32,96},{48,112},{64,0},{80,16},{96,32},{112,48},{1... | collective-permute-start | bytes 1499144 | tf_op jit(solution)/shard_map/ppermute | solution.py:371
  46.1 25.8 %collective-permute-start.4 = (bf16[1952,128]{1,0:T(8,128)(2,1)}, bf16[1952,128]{1,0:T(8,128)(2,1)S(1)}, u32[]{:S(2)}, u32[]{:S(2)}) collective-permute-start(bf16[1952,128]{1,0:T(8,128)(2,1)} %get-tuple-element.86), channel_id=1, source_target_pairs={{0,48},{16,32},{32,80},{48,64},{64,112},{80,96},{96,16},{112,0},{1... | collective-permute-start | bytes 1499144 | tf_op jit(solution)/shard_map/ppermute | solution.py:371
  46.9 35.5 %collective-permute-start.7 = (bf16[1920,128]{1,0:T(8,128)(2,1)}, bf16[1920,128]{1,0:T(8,128)(2,1)}, u32[]{:S(2)}, u32[]{:S(2)}) collective-permute-start(bf16[1920,128]{1,0:T(8,128)(2,1)} %bitcast.14), channel_id=1, source_target_pairs={{0,80},{16,64},{32,112},{48,96},{64,16},{80,0},{96,48},{112,32},{1... | collective-permute-start | bytes 1474568 | tf_op jit(solution)/shard_map/ppermute | solution.py:371
  96.1 2.0 copy-start.3
  98.1 11.0 %copy-start.9 = (bf16[16,3,64,128]{3,2,1,0:T(8,128)(2,1)S(1)}, bf16[16,3,64,128]{3,2,1,0:T(8,128)(2,1)}, u32[]{:S(2)}) copy-start(bf16[16,3,64,128]{3,2,1,0:T(8,128)(2,1)} %copy-done.8) | copy-start | bytes 2359300
  98.5 68.7 %all-to-all-start.1 = ((bf16[16,6,80,256]{3,2,1,0:T(8,128)(2,1)}), bf16[16,6,80,256]{3,2,1,0:T(8,128)(2,1)}, u32[]{:S(2)}, u32[]{:S(2)}) async-start(bf16[16,6,80,256]{3,2,1,0:T(8,128)(2,1)} %copy-done.3), calls=%async_computation.1 | async-start | bytes 7864320 | tf_op jit(solution)/shard_map/all_to_all | solution.py:380
  120.2 4.5 %collective-permute-start.8 = (bf16[6,160,256]{2,1,0:T(8,128)(2,1)S(1)}, bf16[6,160,256]{2,1,0:T(8,128)(2,1)S(1)}, u32[]{:S(2)}, u32[]{:S(2)}) collective-permute-start(bf16[6,160,256]{2,1,0:T(8,128)(2,1)S(1)} %get-tuple-element.68), channel_id=1, source_target_pairs={{0,16},{16,0},{32,48},{48,32},{64,80},{80,64},{96,112},{112,96},{1... | collective-permute-start | bytes 1474568 | tf_op jit(solution)/shard_map/ppermute | solution.py:382
  120.2 15.2 %collective-permute-start.9 = (bf16[6,160,256]{2,1,0:T(8,128)(2,1)S(1)}, bf16[6,160,256]{2,1,0:T(8,128)(2,1)S(1)}, u32[]{:S(2)}, u32[]{:S(2)}) collective-permute-start(bf16[6,160,256]{2,1,0:T(8,128)(2,1)S(1)} %get-tuple-element.69), channel_id=1, source_target_pairs={{0,32},{16,48},{32,64},{48,80},{64,96},{80,112},{96,0},{112,16},{1... | collective-permute-start | bytes 1474568 | tf_op jit(solution)/shard_map/ppermute | solution.py:382
  120.2 46.1 %collective-permute-start.10 = (bf16[6,160,256]{2,1,0:T(8,128)(2,1)S(1)}, bf16[6,160,256]{2,1,0:T(8,128)(2,1)S(1)}, u32[]{:S(2)}, u32[]{:S(2)}) collective-permute-start(bf16[6,160,256]{2,1,0:T(8,128)(2,1)S(1)} %get-tuple-element.70), channel_id=1, source_target_pairs={{0,48},{16,32},{32,80},{48,64},{64,112},{80,96},{96,16},{112,0},{1... | collective-permute-start | bytes 1474568 | tf_op jit(solution)/shard_map/ppermute | solution.py:382
  120.2 46.0 %collective-permute-start.11 = (bf16[6,160,256]{2,1,0:T(8,128)(2,1)S(1)}, bf16[6,160,256]{2,1,0:T(8,128)(2,1)S(1)}, u32[]{:S(2)}, u32[]{:S(2)}) collective-permute-start(bf16[6,160,256]{2,1,0:T(8,128)(2,1)S(1)} %get-tuple-element.71), channel_id=1, source_target_pairs={{0,64},{16,80},{32,96},{48,112},{64,0},{80,16},{96,32},{112,48},{1... | collective-permute-start | bytes 1474568 | tf_op jit(solution)/shard_map/ppermute | solution.py:382
  124.7 41.5 %collective-permute-start.12 = (bf16[6,160,256]{2,1,0:T(8,128)(2,1)S(1)}, bf16[6,160,256]{2,1,0:T(8,128)(2,1)S(1)}, u32[]{:S(2)}, u32[]{:S(2)}) collective-permute-start(bf16[6,160,256]{2,1,0:T(8,128)(2,1)S(1)} %get-tuple-element.72), channel_id=1, source_target_pairs={{0,80},{16,64},{32,112},{48,96},{64,16},{80,0},{96,48},{112,32},{1... | collective-permute-start | bytes 1474568 | tf_op jit(solution)/shard_map/ppermute | solution.py:382
  124.7 41.5 %collective-permute-start.13 = (bf16[6,160,256]{2,1,0:T(8,128)(2,1)S(1)}, bf16[6,160,256]{2,1,0:T(8,128)(2,1)S(1)}, u32[]{:S(2)}, u32[]{:S(2)}) collective-permute-start(bf16[6,160,256]{2,1,0:T(8,128)(2,1)S(1)} %get-tuple-element.73), channel_id=1, source_target_pairs={{0,96},{16,112},{32,0},{48,16},{64,32},{80,48},{96,64},{112,80},{1... | collective-permute-start | bytes 1474568 | tf_op jit(solution)/shard_map/ppermute | solution.py:382
  135.4 31.0 %collective-permute-start.14 = (bf16[6,160,256]{2,1,0:T(8,128)(2,1)S(1)}, bf16[6,160,256]{2,1,0:T(8,128)(2,1)S(1)}, u32[]{:S(2)}, u32[]{:S(2)}) collective-permute-start(bf16[6,160,256]{2,1,0:T(8,128)(2,1)S(1)} %get-tuple-element.74), channel_id=1, source_target_pairs={{0,112},{16,96},{32,16},{48,0},{64,48},{80,32},{96,80},{112,64},{1... | collective-permute-start | bytes 1474568 | tf_op jit(solution)/shard_map/ppermute | solution.py:382
  178.2 3.9 %collective-permute-start.15 = (bf16[16,40,1280]{2,1,0:T(8,128)(2,1)S(1)}, bf16[16,40,1280]{2,1,0:T(8,128)(2,1)S(1)}, u32[]{:S(2)}, u32[]{:S(2)}) collective-permute-start(bf16[16,40,1280]{2,1,0:T(8,128)(2,1)S(1)} %get-tuple-element.76), channel_id=1, source_target_pairs={{0,16},{16,0},{32,48},{48,32},{64,80},{80,64},{96,112},{112,96},{1... | collective-permute-start | bytes 4915208 | tf_op jit(solution)/shard_map/ppermute | solution.py:385
  183.6 32.8 %all-to-all-start.3 = ((bf16[16,40,1280]{2,1,0:T(8,128)(2,1)}), bf16[16,40,1280]{2,1,0:T(8,128)(2,1)S(1)}, u32[]{:S(2)}, u32[]{:S(2)}) async-start(bf16[16,40,1280]{2,1,0:T(8,128)(2,1)} %add_convert_fusion), calls=%async_computation.3 | async-start | bytes 3276800 | tf_op jit(solution)/shard_map/all_to_all | solution.py:386
  216.8 6.1 %collective-permute-start.16 = (f32[10,1280]{1,0:T(8,128)S(1)}, f32[10,1280]{1,0:T(8,128)S(1)}, u32[]{:S(2)}, u32[]{:S(2)}) collective-permute-start(f32[10,1280]{1,0:T(8,128)S(1)} %get-tuple-element.81), channel_id=1, source_target_pairs={{0,32},{16,48},{32,64},{48,80},{64,96},{80,112},{96,0},{112,16},{1... | collective-permute-start | bytes 153608 | tf_op jit(solution)/shard_map/ppermute | solution.py:392
  217.2 5.8 %collective-permute-start.18 = (f32[10,1280]{1,0:T(8,128)S(1)}, f32[10,1280]{1,0:T(8,128)S(1)}, u32[]{:S(2)}, u32[]{:S(2)}) collective-permute-start(f32[10,1280]{1,0:T(8,128)S(1)} %get-tuple-element.82), channel_id=1, source_target_pairs={{0,96},{16,112},{32,0},{48,16},{64,32},{80,48},{96,64},{112,80},{1... | collective-permute-start | bytes 153608 | tf_op jit(solution)/shard_map/ppermute | solution.py:392
  220.1 5.9 %collective-permute-start.17 = (f32[10,1280]{1,0:T(8,128)S(1)}, f32[10,1280]{1,0:T(8,128)S(1)}, u32[]{:S(2)}, u32[]{:S(2)}) collective-permute-start(f32[10,1280]{1,0:T(8,128)S(1)} %get-tuple-element.83), channel_id=1, source_target_pairs={{0,64},{16,80},{32,96},{48,112},{64,0},{80,16},{96,32},{112,48},{1... | collective-permute-start | bytes 153608 | tf_op jit(solution)/shard_map/ppermute | solution.py:392
  (13 other events, 13.2 us)

commit v8 on v7

--- a/solution.py
+++ b/solution.py
@@ -17,7 +17,8 @@
 NG = 10
 BF = jnp.bfloat16
 F32 = jnp.float32
-VLIM = 24 * 1024 * 1024
+VLIM = 56 * 1024 * 1024
+VSMALL = 24 * 1024 * 1024
 
 STEPS = [(k // 2, k % 2) for k in range(8)]
 
@@ -70,7 +71,7 @@
         in_specs=[pl.BlockSpec((2, W, NOB, 4096), lambda i: (i, 0, 0, 0))],
         out_specs=pl.BlockSpec((16, 2 * W, NOB, 256), lambda i: (0, i, 0, 0)),
         out_shape=jax.ShapeDtypeStruct((16, NPD * W, NOB, 256), BF),
-        compiler_params=pltpu.CompilerParams(vmem_limit_bytes=VLIM),
+        compiler_params=pltpu.CompilerParams(vmem_limit_bytes=VSMALL),
         cost_estimate=pl.CostEstimate(flops=0, bytes_accessed=8 * 10**6, transcendentals=0),
         name="row_slabs",
     )(x)
@@ -109,7 +110,7 @@
         out_specs=[pl.BlockSpec((2, W, 2, 32, 128), lambda i: (0, 0, i, 0, 0))] * 8,
         out_shape=[jax.ShapeDtypeStruct((2, W, NPD, 32, 128), BF)] * 8,
         scratch_shapes=[pltpu.VMEM((NOB, W, 2, 32, 128), BF)],
-        compiler_params=pltpu.CompilerParams(vmem_limit_bytes=VLIM),
+        compiler_params=pltpu.CompilerParams(vmem_limit_bytes=VSMALL),
         cost_estimate=pl.CostEstimate(flops=10**9, bytes_accessed=8 * 10**6, transcendentals=0),
         name="block_pairs",
     )(pos, perm, x)
@@ -174,8 +175,8 @@
     )(pos, size, meta, g, rows, cols)
 
 
-def second_kernel(pos, pat, perm, ta_ref, v_ref, *rest):
-    outs, s, kb = rest[:8], rest[8], rest[9]
+def second_kernel(steps, pos, pat, perm, ta_ref, v_ref, *rest):
+    outs, s, kb = rest[:4], rest[4], rest[5]
     a = pos[0]
     low = lax.broadcasted_iota(jnp.int32, (BS, 128), 1) < 64
     zero = jnp.zeros((BS, 128), BF)
@@ -196,10 +197,10 @@
         return carry
 
     lax.fori_loop(0, NG, regroup, 0)
-    for k in range(8):
+    for j, k in enumerate(steps):
         t = dest_of(a, k)
 
-        def one(i, carry, k=k, t=t):
+        def one(i, carry, j=j, t=t):
             n = 2 * t + i
             for d in range(W):
                 v = v_ref[n, d]
@@ -211,21 +212,21 @@
                 ds = [d for d in range(W) if 0 <= e - d + 1 < W]
                 lhs = jnp.concatenate([s[n + d, e - d + 1] for d in ds], axis=1)
                 rhs = kb[256 * ds[0] : 256 * ds[-1] + 256]
-                outs[k][i * W + e] = jnp.dot(lhs, rhs, preferred_element_type=F32).astype(BF)
+                outs[j][i * W + e] = jnp.dot(lhs, rhs, preferred_element_type=F32).astype(BF)
             return carry
 
         lax.fori_loop(0, 2, one, 0)
 
 
-def second_products(pos, pat, perm, ta, v):
-    return pl.pallas_call(
-        second_kernel,
+def second_products(steps, pos, pat, perm, ta, v):
+    return pl.pallas_call(
+        functools.partial(second_kernel, steps),
         in_specs=[sspec(), sspec(), vspec(), vspec(), vspec()],
-        out_specs=[vspec()] * 8,
-        out_shape=[jax.ShapeDtypeStruct((2 * W, 160, 256), BF)] * 8,
+        out_specs=[vspec()] * 4,
+        out_shape=[jax.ShapeDtypeStruct((2 * W, 160, 256), BF)] * 4,
         scratch_shapes=[pltpu.VMEM((NOB + 2, W, 160, 256), BF), pltpu.VMEM((256 * W, 256), BF)],
         compiler_params=pltpu.CompilerParams(vmem_limit_bytes=VLIM),
-        cost_estimate=pl.CostEstimate(flops=4 * 10**9, bytes_accessed=15 * 10**6, transcendentals=0),
+        cost_estimate=pl.CostEstimate(flops=2 * 10**9, bytes_accessed=15 * 10**6, transcendentals=0),
         name="second",
     )(pos, pat, perm, ta, v)
 
@@ -378,8 +379,15 @@
 
     first = first_products(pos, pat, perm, w, tb)
     first = lax.all_to_all(first, "orb", split_axis=0, concat_axis=0, tiled=True)
-    us = second_products(pos, meta, perm, ta.reshape(160, W, NOB, 256), v)
-    us = [us[0]] + [lax.ppermute(us[k], "aux", pairs_of(k)) for k in range(1, 8)]
+    us = [None] * 8
+    ta = ta.reshape(160, W, NOB, 256)
+    late = (4, 5, 1)
+    for k, u in zip((2, 6, 3, 7), second_products((2, 6, 3, 7), pos, meta, perm, ta, v)):
+        us[k] = lax.ppermute(u, "aux", pairs_of(k))
+    *parts, us[0] = second_products(late + (0,), pos, meta, perm, ta, v)
+    *parts, us[2], us[6] = lax.optimization_barrier((*parts, us[2], us[6]))
+    for k, u in zip(late, parts):
+        us[k] = lax.ppermute(u, "aux", pairs_of(k))
 
     theirs, mine = chi_share(pos, first, us)
     part = (mine + lax.ppermute(theirs, "aux", pairs_of(1)).astype(F32)).astype(BF)

time: 228 us -> 223 us (0.978)
  Pallas kernels: 39.1 us -> 52.6 us
  waiting for transfers between devices: 105 us -> 92.1 us
  local copies, waits for them, and re-layouts: 22.2 us -> 13.2 us
  starting transfers between devices: 53.6 us -> 55.9 us
    ppermute x7, waiting for transfers between devices: 39.9 us -> 24.9 us  [body(): us[k] = lax.ppermute(u, 'aux', pairs_of(k))]
    unnamed x45 -> x33, local copies, waits for them, and re-layouts: 16.5 us -> 6.05 us
    pallas_call x1 -> x2, Pallas kernels: 10.3 us -> 17.7 us  [second_products(): pl.pallas_call(functools.partial(second_kernel, steps), in_specs=[sspec()...]
    all_to_all x1, waiting for transfers between devices: 0.38 us -> 5.62 us  [body(): ta = lax.all_to_all(ta, 'orb', split_axis=0, concat_axis=0, tiled=True)]
    ppermute x7, waiting for transfers between devices: 25.5 us -> 20.6 us  [body(): tb[k] = lax.ppermute(tb[k], 'aux', pairs_of(k))]
    ppermute x7, starting transfers between devices: 6.32 us -> 9.64 us  [body(): us[k] = lax.ppermute(u, 'aux', pairs_of(k))]
    pallas_call x1, Pallas kernels: 9.56 us -> 12.6 us  [first_products(): pl.pallas_call(first_kernel, in_specs=[sspec(), sspec(), vspec(), vspec()...]
  transfers between devices with their start and end apart: 23 -> 23, of which waited for: 14 -> 14; matrix products, arithmetic and copies ran while one was open for 2% -> 3% of each run, Pallas kernels for 13% -> 19%
where the time goes in v8:
time: 223 us; the launch traced here: 222 us
  waiting for transfers between devices  92.1 us (41%)
  starting transfers between devices  55.9 us (25%)
  Pallas kernels  52.6 us (24%)
  local copies, waits for them, and re-layouts  13.2 us (6%)
  other arithmetic  8.19 us (4%)
    all_to_all x1, waiting for transfers between devices, body(): part = lax.all_to_all(part, 'orb', split_axis=0, concat_axis=0, tiled=True)  25.6 us
    ppermute x7, waiting for transfers between devices, body(): us[k] = lax.ppermute(u, 'aux', pairs_of(k))  24.9 us
    ppermute x7, waiting for transfers between devices, body(): tb[k] = lax.ppermute(tb[k], 'aux', pairs_of(k))  20.6 us
    pallas_call x2, Pallas kernels, second_products(): pl.pallas_call(functools.partial(second_kernel, steps), in_specs=[sspec()...  17.7 us
    pallas_call x1, Pallas kernels, first_products(): pl.pallas_call(first_kernel, in_specs=[sspec(), sspec(), vspec(), vspec()...  12.6 us
    pallas_call x1, Pallas kernels, chi_share(): pl.pallas_call(chi_kernel, grid=(5,), in_specs=[sspec(), vspec()] + [vspe...  10.8 us
    all_to_all x1, starting transfers between devices, body(): lax.all_to_all(first, 'orb', split_axis=0, concat_axis=0, tiled=True)  10.7 us
    ppermute x7, starting transfers between devices, body(): us[k] = lax.ppermute(u, 'aux', pairs_of(k))  9.64 us
  transfers between devices with their start and end apart: 23, of which 14 were waited for; matrix products, arithmetic and copies ran while one was open for 3% of the time, Pallas kernels for 19%

profile of v8, /device:TPU:0, one launch (start us, length us, event | category | flops | bytes accessed | tf_op | source)
XLA Modules:
  0.0 222.2 jit_solution(16114661025018053453)
XLA Ops:
  3.6 8.2 %all-to-all-start = ((bf16[16,8,4096]{2,1,0:T(8,128)(2,1)}), bf16[16,8,4096]{2,1,0:T(8,128)(2,1)}, u32[]{:S(2)}, u32[]{:S(2)}) async-start(bf16[16,8,4096]{2,1,0:T(8,128)(2,1)} %broadcast_in_dim.2), calls=%async_computation | async-start | bytes 2097152 | tf_op jit(solution)/shard_map/all_to_all | solution.py:359
  11.9 2.1 copy-done
  14.0 3.8 %block_pairs.1 = (bf16[2,3,10,32,128]{4,3,2,1,0:T(8,128)(2,1)S(1)}, bf16[2,3,10,32,128]{4,3,2,1,0:T(8,128)(2,1)}, bf16[2,3,10,32,128]{4,3,2,1,0:T(8,128)(2,1)S(1...) custom-call(s32[2]{0:T(128)S(1)} %pad_add_fusion.pos, ...), custom_call_target="tpu_custom_call" | custom-call | flops 1000000000 | bytes 8000000 | tf_op jit(solution)/shard_map/block_pairs/pallas_call | solution.py:102
  20.1 1.7 collective-permute-start.3
  22.5 1.9 copy-done.2
  24.3 5.2 %all-to-all-done = bf16[16,8,4096]{2,1,0:T(8,128)(2,1)} async-done(((bf16[16,8,4096]{2,1,0:T(8,128)(2,1)}), bf16[16,8,4096]{2,1,0:T(8,128)(2,1)}, u32[]{:S(2)}, u32[]{:S(2)}) %all-to-all-start) | async-done | bytes 1048608 | tf_op jit(solution)/shard_map/all_to_all | solution.py:359
  31.6 2.0 collective-permute-done.2.rest_2_
  33.6 7.2 %all-to-all-start.2 = ((bf16[16,30,16,256]{3,2,1,0:T(8,128)(2,1)}), bf16[16,30,16,256]{3,2,1,0:T(8,128)(2,1)}, u32[]{:S(2)}, u32[]{:S(2)}) async-start(bf16[16,30,16,256]{3,2,1,0:T(8,128)(2,1)} %copy-done.2), calls=%async_computation.2 | async-start | bytes 7864320 | tf_op jit(solution)/shard_map/all_to_all | solution.py:368
  41.9 2.9 %collective-permute-start.5 = (bf16[1952,128]{1,0:T(8,128)(2,1)S(1)}, bf16[1952,128]{1,0:T(8,128)(2,1)S(1)}, u32[]{:S(2)}, u32[]{:S(2)}) collective-permute-start(bf16[1952,128]{1,0:T(8,128)(2,1)S(1)} %get-tuple-element.95), channel_id=1, source_target_pairs={{0,64},{16,80},{32,96},{48,112},{64,0},{80,16},{96,32},{112,48},{1... | collective-permute-start | bytes 1499144 | tf_op jit(solution)/shard_map/ppermute | solution.py:372
  44.8 1.7 collective-permute-start.6
  47.9 3.6 %reshape.93.g_ref = bf16[16,6,64,64]{3,2,1,0:T(8,128)(2,1)} reshape(bf16[16,6,4096]{2,1,0:T(8,128)(2,1)} %bitcast.35) | data formatting | bytes 1572864 | tf_op jit(solution)/shard_map/reshape | solution.py:377
  51.5 7.0 %greens.1 = (bf16[16,3,64,128]{3,2,1,0:T(8,128)(2,1)}, bf16[2,192,192]{2,1,0:T(8,128)(2,1)}) custom-call(s32[2]{0:T(128)} %copy-done.4, s32[16]{0:T(128)} %size.1, s32[2048]{0:T(1024)} %bitcast_convert_fusion.meta.pat, bf16[16,6,64,64]{3,2,1,0:T(8,128)(2,1)} %reshape.93.g_ref, bf16[2,32,64]{2,1,0:T(8,128)(2,1)} %constant.57.clone.rows_ref, ...), custom_call_target="tpu_custom_call" | custom-call | flops 1000000 | bytes 8000000 | tf_op jit(solution)/shard_map/greens/pallas_call | solution.py:163
  58.8 8.5 %collective-permute-done.5.rest_4_ = bf16[1952,128]{1,0:T(8,128)(2,1)S(1)} collective-permute-done((bf16[1952,128]{1,0:T(8,128)(2,1)S(1)}, bf16[1952,128]{1,0:T(8,128)(2,1)S(1)}, u32[]{:S(2)}, u32[]{:S(2)}) %collective-permute-start.5) | collective-permute-done | bytes 499744 | tf_op jit(solution)/shard_map/ppermute | solution.py:372
  68.5 10.1 %collective-permute-done.7.rest_5_ = bf16[1920,128]{1,0:T(8,128)(2,1)} collective-permute-done((bf16[1920,128]{1,0:T(8,128)(2,1)S(1)}, bf16[1920,128]{1,0:T(8,128)(2,1)}, u32[]{:S(2)}, u32[]{:S(2)}) %collective-permute-start.7) | collective-permute-done | bytes 491552 | tf_op jit(solution)/shard_map/ppermute | solution.py:372
  78.6 12.6 %first.1 = bf16[16,6,80,256]{3,2,1,0:T(8,128)(2,1)} custom-call(s32[2]{0:T(128)} %copy-done.4, s32[4096]{0:T(1024)} %reshape.90.pat, bf16[256,256]{1,0:T(8,128)(2,1)} %constant.56.clone.perm, bf16[2,192,192]{2,1,0:T(8,128)(2,1)} %get-tuple-element.64.w_ref, bf16[1920,128]{1,0:T(8,128)(2,1)} %bitcast.41, bf16[1920,128]{1,0:T(8,128)(2,1)} %collective-permute-done.1.rest_1_, ...), custom_call_target="tpu_custom_call" | custom-call | flops 3000000000 | bytes 8000000 | tf_op jit(solution)/shard_map/first/pallas_call | solution.py:284
  91.3 5.6 %all-to-all-done.2 = bf16[16,30,16,256]{3,2,1,0:T(8,128)(2,1)} async-done(((bf16[16,30,16,256]{3,2,1,0:T(8,128)(2,1)}), bf16[16,30,16,256]{3,2,1,0:T(8,128)(2,1)}, u32[]{:S(2)}, u32[]{:S(2)}) %all-to-all-start.2) | async-done | bytes 3932192 | tf_op jit(solution)/shard_map/all_to_all | solution.py:368
  96.9 10.7 %all-to-all-start.1 = ((bf16[16,6,80,256]{3,2,1,0:T(8,128)(2,1)}), bf16[16,6,80,256]{3,2,1,0:T(8,128)(2,1)}, u32[]{:S(2)}, u32[]{:S(2)}) async-start(bf16[16,6,80,256]{3,2,1,0:T(8,128)(2,1)} %first.1), calls=%async_computation.1 | async-start | bytes 7864320 | tf_op jit(solution)/shard_map/all_to_all | solution.py:381
  107.6 8.8 %second.3 = (bf16[6,160,256]{2,1,0:T(8,128)(2,1)}, bf16[6,160,256]{2,1,0:T(8,128)(2,1)}, bf16[6,160,256]{2,1,0:T(8,128)(2,1)}, bf16[6,160,256]{2,1,0:T(8,128)(2,1)}) custom-call(s32[2]{0:T(128)} %copy-done.4, s32[2048]{0:T(1024)} %bitcast_convert_fusion.meta.pat, bf16[256,256]{1,0:T(8,128)(2,1)} %constant.56.clone.perm, ...), custom_call_target="tpu_custom_call" | custom-call | flops 2000000000 | bytes 15000000 | tf_op jit(solution)/shard_map/second/pallas_call | solution.py:222
  116.4 3.2 %collective-permute-start.9 = (bf16[6,160,256]{2,1,0:T(8,128)(2,1)}, bf16[6,160,256]{2,1,0:T(8,128)(2,1)S(1)}, u32[]{:S(2)}, u32[]{:S(2)}) collective-permute-start(bf16[6,160,256]{2,1,0:T(8,128)(2,1)} %get-tuple-element.77), channel_id=1, source_target_pairs={{0,96},{16,112},{32,0},{48,16},{64,32},{80,48},{96,64},{112,80},{1... | collective-permute-start | bytes 1474568 | tf_op jit(solution)/shard_map/ppermute | solution.py:386
  119.6 3.0 %collective-permute-start.14 = (bf16[6,160,256]{2,1,0:T(8,128)(2,1)}, bf16[6,160,256]{2,1,0:T(8,128)(2,1)S(1)}, u32[]{:S(2)}, u32[]{:S(2)}) collective-permute-start(bf16[6,160,256]{2,1,0:T(8,128)(2,1)} %get-tuple-element.84), channel_id=1, source_target_pairs={{0,112},{16,96},{32,16},{48,0},{64,48},{80,32},{96,80},{112,64},{1... | collective-permute-start | bytes 1474568 | tf_op jit(solution)/shard_map/ppermute | solution.py:386
  122.6 8.9 %second.2 = (bf16[6,160,256]{2,1,0:T(8,128)(2,1)}, bf16[6,160,256]{2,1,0:T(8,128)(2,1)}, bf16[6,160,256]{2,1,0:T(8,128)(2,1)}, bf16[6,160,256]{2,1,0:T(8,128)(2,1)}) custom-call(s32[2]{0:T(128)} %copy-done.4, s32[2048]{0:T(1024)} %bitcast_convert_fusion.meta.pat, bf16[256,256]{1,0:T(8,128)(2,1)} %constant.56.clone.perm, ...), custom_call_target="tpu_custom_call" | custom-call | flops 2000000000 | bytes 15000000 | tf_op jit(solution)/shard_map/second/pallas_call | solution.py:222
  133.5 2.0 collective-permute-start.13
  135.4 2.3 %collective-permute-done.11.rest_3_ = bf16[6,160,256]{2,1,0:T(8,128)(2,1)S(1)} collective-permute-done((bf16[6,160,256]{2,1,0:T(8,128)(2,1)}, bf16[6,160,256]{2,1,0:T(8,128)(2,1)S(1)}, u32[]{:S(2)}, u32[]{:S(2)}) %collective-permute-start.11) | collective-permute-done | bytes 491552 | tf_op jit(solution)/shard_map/ppermute | solution.py:386
  137.8 22.1 %collective-permute-done.14.rest_7_ = bf16[6,160,256]{2,1,0:T(8,128)(2,1)S(1)} collective-permute-done((bf16[6,160,256]{2,1,0:T(8,128)(2,1)}, bf16[6,160,256]{2,1,0:T(8,128)(2,1)S(1)}, u32[]{:S(2)}, u32[]{:S(2)}) %collective-permute-start.14) | collective-permute-done | bytes 491552 | tf_op jit(solution)/shard_map/ppermute | solution.py:386
  161.2 10.8 %chi.1 = (bf16[16,40,1280]{2,1,0:T(8,128)(2,1)}, f32[16,40,1280]{2,1,0:T(8,128)}) custom-call(s32[2]{0:T(128)} %copy-done.4, bf16[16,6,80,256]{3,2,1,0:T(8,128)(2,1)} %all-to-all-done.1.first_ref, bf16[6,160,256]{2,1,0:T(8,128)(2,1)} %get-tuple-element.72.rest_0_, bf16[6,160,256]{2,1,0:T(8,128)(2,1)} %copy-done.13, bf16[6,160,256]{2,1,0:T(8,128)(2,1)} %copy-done.9, ...), custom_call_target="tpu_custom_call" | custom-call | flops 5000000000 | bytes 13000000 | tf_op jit(solution)/shard_map/chi/pallas_call | solution.py:323
  172.6 3.3 %collective-permute-done.15 = bf16[16,40,1280]{2,1,0:T(8,128)(2,1)S(1)} collective-permute-done((bf16[16,40,1280]{2,1,0:T(8,128)(2,1)}, bf16[16,40,1280]{2,1,0:T(8,128)(2,1)S(1)}, u32[]{:S(2)}, u32[]{:S(2)}) %collective-permute-start.15) | collective-permute-done | bytes 1638432 | tf_op jit(solution)/shard_map/ppermute | solution.py:393
  175.9 3.4 %add_convert_fusion = bf16[16,40,1280]{2,1,0:T(8,128)(2,1)} fusion(f32[16,40,1280]{2,1,0:T(8,128)} %get-tuple-element.85, bf16[16,40,1280]{2,1,0:T(8,128)(2,1)S(1)} %collective-permute-done.15), kind=kLoop, calls=%fused_computation.1 | loop fusion | flops 2457600 | bytes 6553600 | tf_op jit(solution)/shard_map/convert_element_type | solution.py:393
  179.3 6.9 %all-to-all-start.3 = ((bf16[16,40,1280]{2,1,0:T(8,128)(2,1)}), bf16[16,40,1280]{2,1,0:T(8,128)(2,1)S(1)}, u32[]{:S(2)}, u32[]{:S(2)}) async-start(bf16[16,40,1280]{2,1,0:T(8,128)(2,1)} %add_convert_fusion), calls=%async_computation.3 | async-start | bytes 3276800 | tf_op jit(solution)/shard_map/all_to_all | solution.py:394
  186.3 25.6 %all-to-all-done.3 = bf16[16,40,1280]{2,1,0:T(8,128)(2,1)S(1)} async-done(((bf16[16,40,1280]{2,1,0:T(8,128)(2,1)}), bf16[16,40,1280]{2,1,0:T(8,128)(2,1)S(1)}, u32[]{:S(2)}, u32[]{:S(2)}) %all-to-all-start.3) | async-done | bytes 1638432 | tf_op jit(solution)/shard_map/all_to_all | solution.py:394
  212.2 2.9 %collective-permute-start.18 = (f32[10,1280]{1,0:T(8,128)S(1)}, f32[10,1280]{1,0:T(8,128)S(1)}, u32[]{:S(2)}, u32[]{:S(2)}) collective-permute-start(f32[10,1280]{1,0:T(8,128)S(1)} %get-tuple-element.92), channel_id=1, source_target_pairs={{0,96},{16,112},{32,0},{48,16},{64,32},{80,48},{96,64},{112,80},{1... | collective-permute-start | bytes 153608 | tf_op jit(solution)/shard_map/ppermute | solution.py:400
  216.0 1.9 collective-permute-done.18
  217.9 3.2 %collective-permute-done.17 = f32[10,1280]{1,0:T(8,128)S(1)} collective-permute-done((f32[10,1280]{1,0:T(8,128)S(1)}, f32[10,1280]{1,0:T(8,128)S(1)}, u32[]{:S(2)}, u32[]{:S(2)}) %collective-permute-start.17) | collective-permute-done | bytes 51232 | tf_op jit(solution)/shard_map/ppermute | solution.py:400
  (85 shorter events, 18.8 us)
Async XLA Ops:
  0.0 11.9 %copy-start.3 = (bf16[256,256]{1,0:T(8,128)(2,1)S(1)}, bf16[256,256]{1,0:T(8,128)(2,1)}, u32[]{:S(2)}) copy-start(bf16[256,256]{1,0:T(8,128)(2,1)} %constant.56.clone.perm) | copy-start | bytes 393220
  3.6 25.9 %all-to-all-start = ((bf16[16,8,4096]{2,1,0:T(8,128)(2,1)}), bf16[16,8,4096]{2,1,0:T(8,128)(2,1)}, u32[]{:S(2)}, u32[]{:S(2)}) async-start(bf16[16,8,4096]{2,1,0:T(8,128)(2,1)} %broadcast_in_dim.2), calls=%async_computation | async-start | bytes 2097152 | tf_op jit(solution)/shard_map/all_to_all | solution.py:359
  11.9 10.6 %copy-start.4 = (s32[2]{0:T(128)}, s32[2]{0:T(128)S(1)}, u32[]{:S(2)}) copy-start(s32[2]{0:T(128)S(1)} %pad_add_fusion.pos) | copy-start | bytes 28
  14.0 7.9 %copy-start.1 = (bf16[10,16,3,4096]{3,1,2,0:T(8,128)(2,1)S(1)}, bf16[10,16,3,4096]{3,1,2,0:T(8,128)(2,1)}, u32[]{:S(2)}) copy-start(bf16[10,16,3,4096]{3,1,2,0:T(8,128)(2,1)} %param.9) | copy-start | bytes 11796484
  18.6 13.0 %collective-permute-start.1 = (bf16[1920,128]{1,0:T(8,128)(2,1)}, bf16[1920,128]{1,0:T(8,128)(2,1)}, u32[]{:S(2)}, u32[]{:S(2)}) collective-permute-start(bf16[1920,128]{1,0:T(8,128)(2,1)} %bitcast.6), channel_id=1, source_target_pairs={{0,16},{16,0},{32,48},{48,32},{64,80},{80,64},{96,112},{112,96},{1... | collective-permute-start | bytes 1474568 | tf_op jit(solution)/shard_map/ppermute | solution.py:364
  18.6 14.9 %collective-permute-start.2 = (bf16[1920,128]{1,0:T(8,128)(2,1)S(1)}, bf16[1920,128]{1,0:T(8,128)(2,1)}, u32[]{:S(2)}, u32[]{:S(2)}) collective-permute-start(bf16[1920,128]{1,0:T(8,128)(2,1)S(1)} %bitcast.44), channel_id=1, source_target_pairs={{0,32},{16,48},{32,64},{48,80},{64,96},{80,112},{96,0},{112,16},{1... | collective-permute-start | bytes 1474568 | tf_op jit(solution)/shard_map/ppermute | solution.py:364
  20.1 13.5 %collective-permute-start.3 = (bf16[1920,128]{1,0:T(8,128)(2,1)S(1)}, bf16[1920,128]{1,0:T(8,128)(2,1)}, u32[]{:S(2)}, u32[]{:S(2)}) collective-permute-start(bf16[1920,128]{1,0:T(8,128)(2,1)S(1)} %bitcast.43), channel_id=1, source_target_pairs={{0,96},{16,112},{32,0},{48,16},{64,32},{80,48},{96,64},{112,80},{1... | collective-permute-start | bytes 1474568 | tf_op jit(solution)/shard_map/ppermute | solution.py:364
  30.3 1.2 collective-permute-start
  33.6 63.3 %all-to-all-start.2 = ((bf16[16,30,16,256]{3,2,1,0:T(8,128)(2,1)}), bf16[16,30,16,256]{3,2,1,0:T(8,128)(2,1)}, u32[]{:S(2)}, u32[]{:S(2)}) async-start(bf16[16,30,16,256]{3,2,1,0:T(8,128)(2,1)} %copy-done.2), calls=%async_computation.2 | async-start | bytes 7864320 | tf_op jit(solution)/shard_map/all_to_all | solution.py:368
  41.7 16.9 %collective-permute-start.4 = (bf16[1952,128]{1,0:T(8,128)(2,1)}, bf16[1952,128]{1,0:T(8,128)(2,1)S(1)}, u32[]{:S(2)}, u32[]{:S(2)}) collective-permute-start(bf16[1952,128]{1,0:T(8,128)(2,1)} %get-tuple-element.96), channel_id=1, source_target_pairs={{0,48},{16,32},{32,80},{48,64},{64,112},{80,96},{96,16},{112,0},{1... | collective-permute-start | bytes 1499144 | tf_op jit(solution)/shard_map/ppermute | solution.py:372
  41.9 25.4 %collective-permute-start.5 = (bf16[1952,128]{1,0:T(8,128)(2,1)S(1)}, bf16[1952,128]{1,0:T(8,128)(2,1)S(1)}, u32[]{:S(2)}, u32[]{:S(2)}) collective-permute-start(bf16[1952,128]{1,0:T(8,128)(2,1)S(1)} %get-tuple-element.95), channel_id=1, source_target_pairs={{0,64},{16,80},{32,96},{48,112},{64,0},{80,16},{96,32},{112,48},{1... | collective-permute-start | bytes 1499144 | tf_op jit(solution)/shard_map/ppermute | solution.py:372
  44.8 22.6 %collective-permute-start.6 = (bf16[1952,128]{1,0:T(8,128)(2,1)S(1)}, bf16[1952,128]{1,0:T(8,128)(2,1)S(1)}, u32[]{:S(2)}, u32[]{:S(2)}) collective-permute-start(bf16[1952,128]{1,0:T(8,128)(2,1)S(1)} %get-tuple-element.94), channel_id=1, source_target_pairs={{0,112},{16,96},{32,16},{48,0},{64,48},{80,32},{96,80},{112,64},{1... | collective-permute-start | bytes 1499144 | tf_op jit(solution)/shard_map/ppermute | solution.py:372
  46.5 32.1 %collective-permute-start.7 = (bf16[1920,128]{1,0:T(8,128)(2,1)S(1)}, bf16[1920,128]{1,0:T(8,128)(2,1)}, u32[]{:S(2)}, u32[]{:S(2)}) collective-permute-start(bf16[1920,128]{1,0:T(8,128)(2,1)S(1)} %bitcast.42), channel_id=1, source_target_pairs={{0,80},{16,64},{32,112},{48,96},{64,16},{80,0},{96,48},{112,32},{1... | collective-permute-start | bytes 1474568 | tf_op jit(solution)/shard_map/ppermute | solution.py:372
  58.6 20.0 %copy-start.6 = (bf16[1952,128]{1,0:T(8,128)(2,1)}, bf16[1952,128]{1,0:T(8,128)(2,1)S(1)}, u32[]{:S(2)}) copy-start(bf16[1952,128]{1,0:T(8,128)(2,1)S(1)} %collective-permute-done.4.rest_3_) | copy-start | bytes 1499140
  67.3 11.3 %copy-start.7 = (bf16[1952,128]{1,0:T(8,128)(2,1)}, bf16[1952,128]{1,0:T(8,128)(2,1)S(1)}, u32[]{:S(2)}) copy-start(bf16[1952,128]{1,0:T(8,128)(2,1)S(1)} %collective-permute-done.5.rest_4_) | copy-start | bytes 1499140
  67.5 11.2 %copy-start.8 = (bf16[1952,128]{1,0:T(8,128)(2,1)}, bf16[1952,128]{1,0:T(8,128)(2,1)S(1)}, u32[]{:S(2)}) copy-start(bf16[1952,128]{1,0:T(8,128)(2,1)S(1)} %collective-permute-done.6.rest_7_) | copy-start | bytes 1499140
  96.9 63.0 %all-to-all-start.1 = ((bf16[16,6,80,256]{3,2,1,0:T(8,128)(2,1)}), bf16[16,6,80,256]{3,2,1,0:T(8,128)(2,1)}, u32[]{:S(2)}, u32[]{:S(2)}) async-start(bf16[16,6,80,256]{3,2,1,0:T(8,128)(2,1)} %first.1), calls=%async_computation.1 | async-start | bytes 7864320 | tf_op jit(solution)/shard_map/all_to_all | solution.py:381
  116.4 15.6 %collective-permute-start.8 = (bf16[6,160,256]{2,1,0:T(8,128)(2,1)}, bf16[6,160,256]{2,1,0:T(8,128)(2,1)S(1)}, u32[]{:S(2)}, u32[]{:S(2)}) collective-permute-start(bf16[6,160,256]{2,1,0:T(8,128)(2,1)} %get-tuple-element.76), channel_id=1, source_target_pairs={{0,32},{16,48},{32,64},{48,80},{64,96},{80,112},{96,0},{112,16},{1... | collective-permute-start | bytes 1474568 | tf_op jit(solution)/shard_map/ppermute | solution.py:386
  116.4 15.6 %collective-permute-start.9 = (bf16[6,160,256]{2,1,0:T(8,128)(2,1)}, bf16[6,160,256]{2,1,0:T(8,128)(2,1)S(1)}, u32[]{:S(2)}, u32[]{:S(2)}) collective-permute-start(bf16[6,160,256]{2,1,0:T(8,128)(2,1)} %get-tuple-element.77), channel_id=1, source_target_pairs={{0,96},{16,112},{32,0},{48,16},{64,32},{80,48},{96,64},{112,80},{1... | collective-permute-start | bytes 1474568 | tf_op jit(solution)/shard_map/ppermute | solution.py:386
  119.6 18.1 %collective-permute-start.11 = (bf16[6,160,256]{2,1,0:T(8,128)(2,1)}, bf16[6,160,256]{2,1,0:T(8,128)(2,1)S(1)}, u32[]{:S(2)}, u32[]{:S(2)}) collective-permute-start(bf16[6,160,256]{2,1,0:T(8,128)(2,1)} %get-tuple-element.80), channel_id=1, source_target_pairs={{0,48},{16,32},{32,80},{48,64},{64,112},{80,96},{96,16},{112,0},{1... | collective-permute-start | bytes 1474568 | tf_op jit(solution)/shard_map/ppermute | solution.py:386
  119.6 40.2 %collective-permute-start.14 = (bf16[6,160,256]{2,1,0:T(8,128)(2,1)}, bf16[6,160,256]{2,1,0:T(8,128)(2,1)S(1)}, u32[]{:S(2)}, u32[]{:S(2)}) collective-permute-start(bf16[6,160,256]{2,1,0:T(8,128)(2,1)} %get-tuple-element.84), channel_id=1, source_target_pairs={{0,112},{16,96},{32,16},{48,0},{64,48},{80,32},{96,80},{112,64},{1... | collective-permute-start | bytes 1474568 | tf_op jit(solution)/shard_map/ppermute | solution.py:386
  132.0 27.9 %copy-start.9 = (bf16[6,160,256]{2,1,0:T(8,128)(2,1)}, bf16[6,160,256]{2,1,0:T(8,128)(2,1)S(1)}, u32[]{:S(2)}) copy-start(bf16[6,160,256]{2,1,0:T(8,128)(2,1)S(1)} %collective-permute-done.8.rest_2_) | copy-start | bytes 1474564
  132.0 27.9 %copy-start.10 = (bf16[6,160,256]{2,1,0:T(8,128)(2,1)}, bf16[6,160,256]{2,1,0:T(8,128)(2,1)S(1)}, u32[]{:S(2)}) copy-start(bf16[6,160,256]{2,1,0:T(8,128)(2,1)S(1)} %collective-permute-done.9.rest_6_) | copy-start | bytes 1474564
  132.0 27.9 %collective-permute-start.10 = (bf16[6,160,256]{2,1,0:T(8,128)(2,1)}, bf16[6,160,256]{2,1,0:T(8,128)(2,1)S(1)}, u32[]{:S(2)}, u32[]{:S(2)}) collective-permute-start(bf16[6,160,256]{2,1,0:T(8,128)(2,1)} %get-tuple-element.78), channel_id=1, source_target_pairs={{0,16},{16,0},{32,48},{48,32},{64,80},{80,64},{96,112},{112,96},{1... | collective-permute-start | bytes 1474568 | tf_op jit(solution)/shard_map/ppermute | solution.py:390
  132.1 27.8 %collective-permute-start.12 = (bf16[6,160,256]{2,1,0:T(8,128)(2,1)}, bf16[6,160,256]{2,1,0:T(8,128)(2,1)S(1)}, u32[]{:S(2)}, u32[]{:S(2)}) collective-permute-start(bf16[6,160,256]{2,1,0:T(8,128)(2,1)} %get-tuple-element.81), channel_id=1, source_target_pairs={{0,64},{16,80},{32,96},{48,112},{64,0},{80,16},{96,32},{112,48},{1... | collective-permute-start | bytes 1474568 | tf_op jit(solution)/shard_map/ppermute | solution.py:390
  133.5 26.4 %collective-permute-start.13 = (bf16[6,160,256]{2,1,0:T(8,128)(2,1)}, bf16[6,160,256]{2,1,0:T(8,128)(2,1)S(1)}, u32[]{:S(2)}, u32[]{:S(2)}) collective-permute-start(bf16[6,160,256]{2,1,0:T(8,128)(2,1)} %get-tuple-element.82), channel_id=1, source_target_pairs={{0,80},{16,64},{32,112},{48,96},{64,16},{80,0},{96,48},{112,32},{1... | collective-permute-start | bytes 1474568 | tf_op jit(solution)/shard_map/ppermute | solution.py:390
  137.8 22.2 %copy-start.11 = (bf16[6,160,256]{2,1,0:T(8,128)(2,1)}, bf16[6,160,256]{2,1,0:T(8,128)(2,1)S(1)}, u32[]{:S(2)}) copy-start(bf16[6,160,256]{2,1,0:T(8,128)(2,1)S(1)} %collective-permute-done.11.rest_3_) | copy-start | bytes 1474564
  172.0 3.9 %collective-permute-start.15 = (bf16[16,40,1280]{2,1,0:T(8,128)(2,1)}, bf16[16,40,1280]{2,1,0:T(8,128)(2,1)S(1)}, u32[]{:S(2)}, u32[]{:S(2)}) collective-permute-start(bf16[16,40,1280]{2,1,0:T(8,128)(2,1)} %get-tuple-element.86), channel_id=1, source_target_pairs={{0,16},{16,0},{32,48},{48,32},{64,80},{80,64},{96,112},{112,96},{1... | collective-permute-start | bytes 4915208 | tf_op jit(solution)/shard_map/ppermute | solution.py:393
  179.3 32.5 %all-to-all-start.3 = ((bf16[16,40,1280]{2,1,0:T(8,128)(2,1)}), bf16[16,40,1280]{2,1,0:T(8,128)(2,1)S(1)}, u32[]{:S(2)}, u32[]{:S(2)}) async-start(bf16[16,40,1280]{2,1,0:T(8,128)(2,1)} %add_convert_fusion), calls=%async_computation.3 | async-start | bytes 3276800 | tf_op jit(solution)/shard_map/all_to_all | solution.py:394
  212.2 5.7 %collective-permute-start.18 = (f32[10,1280]{1,0:T(8,128)S(1)}, f32[10,1280]{1,0:T(8,128)S(1)}, u32[]{:S(2)}, u32[]{:S(2)}) collective-permute-start(f32[10,1280]{1,0:T(8,128)S(1)} %get-tuple-element.92), channel_id=1, source_target_pairs={{0,96},{16,112},{32,0},{48,16},{64,32},{80,48},{96,64},{112,80},{1... | collective-permute-start | bytes 153608 | tf_op jit(solution)/shard_map/ppermute | solution.py:400
  215.1 6.0 %collective-permute-start.17 = (f32[10,1280]{1,0:T(8,128)S(1)}, f32[10,1280]{1,0:T(8,128)S(1)}, u32[]{:S(2)}, u32[]{:S(2)}) collective-permute-start(f32[10,1280]{1,0:T(8,128)S(1)} %get-tuple-element.93), channel_id=1, source_target_pairs={{0,64},{16,80},{32,96},{48,112},{64,0},{80,16},{96,32},{112,48},{1... | collective-permute-start | bytes 153608 | tf_op jit(solution)/shard_map/ppermute | solution.py:400
  215.1 6.5 %collective-permute-start.16 = (f32[10,1280]{1,0:T(8,128)S(1)}, f32[10,1280]{1,0:T(8,128)S(1)}, u32[]{:S(2)}, u32[]{:S(2)}) collective-permute-start(f32[10,1280]{1,0:T(8,128)S(1)} %get-tuple-element.91), channel_id=1, source_target_pairs={{0,32},{16,48},{32,64},{48,80},{64,96},{80,112},{96,0},{112,16},{1... | collective-permute-start | bytes 153608 | tf_op jit(solution)/shard_map/ppermute | solution.py:400
  (7 other events, 8.9 us)

commit v9 on v8

--- a/solution.py
+++ b/solution.py
@@ -116,6 +116,32 @@
     )(pos, perm, x)
 
 
+def pack_kernel(tpat, gpat, occ_ref, virt_ref, out):
+    lane = lax.broadcasted_iota(jnp.int32, (1, 128), 1)
+    row = jnp.zeros((1, 128), jnp.int32)
+    for d in range(W):
+        for g in range(NG):
+            row = jnp.where(lane == g * W + d, tpat[d, 0, g], row)
+        row = jnp.where(lane == NG * W + d, gpat[0, d], row)
+    tail = jnp.concatenate([row, jnp.zeros((1, 128), jnp.int32)], axis=0).astype(F32).astype(BF)
+    rest = jnp.zeros((2, 4096 - 128), BF)
+    own = jnp.concatenate([occ_ref[0], virt_ref[0], jnp.concatenate([tail, rest], axis=1)], axis=0)
+    for o in range(NOB):
+        out[o] = own
+
+
+def pack(tpat, gpat, occ, virt):
+    return pl.pallas_call(
+        pack_kernel,
+        in_specs=[sspec(), sspec(), vspec(), vspec()],
+        out_specs=vspec(),
+        out_shape=jax.ShapeDtypeStruct((NOB, 8, 4096), BF),
+        compiler_params=pltpu.CompilerParams(vmem_limit_bytes=VSMALL),
+        cost_estimate=pl.CostEstimate(flops=0, bytes_accessed=11 * 10**5, transcendentals=0),
+        name="pack",
+    )(tpat, gpat, occ, virt)
+
+
 def greens_kernel(pos, size, meta, g_ref, rows_ref, cols_ref, v_ref, w_ref, o_ref):
     a = pos[0]
     row = lax.broadcasted_iota(jnp.int32, (BS, BS), 0)
@@ -352,10 +378,7 @@
     rows, cols = deinterleave()
     x = three_center.transpose(0, 2, 1, 3)
 
-    marks = jnp.concatenate([tensor_pattern.reshape(1, NG * W), green_pattern], axis=1).astype(BF)
-    marks = jnp.pad(marks, ((0, 1), (0, 4096 - NG * W - W)))
-    own = jnp.concatenate([green_occ[0], green_virt[0], marks], axis=0)
-    every = jnp.broadcast_to(own[None], (NOB,) + own.shape)
+    every = pack(tensor_pattern.transpose(2, 1, 0), green_pattern, green_occ, green_virt)
     every = lax.all_to_all(every, "orb", split_axis=0, concat_axis=0, tiled=True)
 
     *tb, x = lax.optimization_barrier((*block_pairs(pos, perm, x), x))
@@ -394,11 +417,13 @@
     part = lax.all_to_all(part, "orb", split_axis=0, concat_axis=0, tiled=True)
     part = jnp.sum(part.astype(F32), axis=0).reshape(4, NPD, 1280)
     x = a // 2
-    total = lax.dynamic_index_in_dim(part, x, 0, keepdims=False)
-    for dx in range(1, 4):
-        piece = lax.dynamic_index_in_dim(part, lax.rem(x + dx, 4), 0, keepdims=False)
-        total = total + lax.ppermute(piece, "aux", pairs_of(2 * dx))
-    return total
+    high, low = (x // 2) * 2, lax.rem(x, 2)
+    kept = lax.dynamic_slice_in_dim(part, high, 2, axis=0)
+    sent = lax.dynamic_slice_in_dim(part, 2 - high, 2, axis=0)
+    kept = kept + lax.ppermute(sent, "aux", pairs_of(4))
+    sent = lax.dynamic_index_in_dim(kept, 1 - low, 0, keepdims=False)
+    kept = lax.dynamic_index_in_dim(kept, low, 0, keepdims=False)
+    return kept + lax.ppermute(sent, "aux", [(i, i ^ 2) for i in range(8)])
 
 
 def solution(mesh):

time: 223 us -> 226 us (1.013)
  waiting for transfers between devices: 92.1 us -> 97.5 us
  starting transfers between devices: 55.9 us -> 52.7 us
  other arithmetic: 8.19 us -> 5.11 us
  local copies, waits for them, and re-layouts: 13.2 us -> 15.5 us
    ppermute x3 -> x2, waiting for transfers between devices: 5.58 us -> 11.1 us  [the longest x1 6.8 us: body(): kept = kept + lax.ppermute(sent, 'aux', pairs_of(4))]
    ppermute x3 -> x2, starting transfers between devices: 3.81 us -> 0.36 us  [the longest x1 0.27 us: body(): return kept + lax.ppermute(sent, 'aux', [(i, i ^ 2) for i in range(8)])]
    unnamed x33 -> x39, local copies, waits for them, and re-layouts: 6.05 us -> 8.91 us
  transfers between devices with their start and end apart: 23 -> 22, of which waited for: 14 -> 14; matrix products, arithmetic and copies ran while one was open for 3% -> 3% of each run, Pallas kernels for 19% -> 19%
where the time goes in v9:
time: 226 us; the launch traced here: 225 us
  waiting for transfers between devices  97.5 us (43%)
  Pallas kernels  54.2 us (24%)
  starting transfers between devices  52.7 us (23%)
  local copies, waits for them, and re-layouts  15.5 us (7%)
  other arithmetic  5.11 us (2%)
    all_to_all x1, waiting for transfers between devices, body(): part = lax.all_to_all(part, 'orb', split_axis=0, concat_axis=0, tiled=True)  25.6 us
    ppermute x7, waiting for transfers between devices, body(): us[k] = lax.ppermute(u, 'aux', pairs_of(k))  25 us
    ppermute x7, waiting for transfers between devices, body(): tb[k] = lax.ppermute(tb[k], 'aux', pairs_of(k))  19.6 us
    pallas_call x2, Pallas kernels, second_products(): pl.pallas_call(functools.partial(second_kernel, steps), in_specs=[sspec()...  17.6 us
    pallas_call x1, Pallas kernels, first_products(): pl.pallas_call(first_kernel, in_specs=[sspec(), sspec(), vspec(), vspec()...  12.7 us
    pallas_call x1, Pallas kernels, chi_share(): pl.pallas_call(chi_kernel, grid=(5,), in_specs=[sspec(), vspec()] + [vspe...  10.8 us
    all_to_all x1, starting transfers between devices, body(): lax.all_to_all(first, 'orb', split_axis=0, concat_axis=0, tiled=True)  10.7 us
    ppermute x7, starting transfers between devices, body(): us[k] = lax.ppermute(u, 'aux', pairs_of(k))  9.64 us
  transfers between devices with their start and end apart: 22, of which 14 were waited for; matrix products, arithmetic and copies ran while one was open for 3% of the time, Pallas kernels for 19%

profile of v9, /device:TPU:0, one launch (start us, length us, event | category | flops | bytes accessed | tf_op | source)
XLA Modules:
  0.0 225.3 jit_solution(538312109540211205)
XLA Ops:
  2.9 1.7 pack.1
  4.6 8.2 %all-to-all-start = ((bf16[16,8,4096]{2,1,0:T(8,128)(2,1)}), bf16[16,8,4096]{2,1,0:T(8,128)(2,1)}, u32[]{:S(2)}, u32[]{:S(2)}) async-start(bf16[16,8,4096]{2,1,0:T(8,128)(2,1)} %pack.1), calls=%async_computation | async-start | bytes 2097152 | tf_op jit(solution)/shard_map/all_to_all | solution.py:382
  12.8 2.1 copy-done
  15.0 3.8 %block_pairs.1 = (bf16[2,3,10,32,128]{4,3,2,1,0:T(8,128)(2,1)S(1)}, bf16[2,3,10,32,128]{4,3,2,1,0:T(8,128)(2,1)}, bf16[2,3,10,32,128]{4,3,2,1,0:T(8,128)(2,1)S(1...) custom-call(s32[2]{0:T(128)S(1)} %pad_add_fusion.pos, ...), custom_call_target="tpu_custom_call" | custom-call | flops 1000000000 | bytes 8000000 | tf_op jit(solution)/shard_map/block_pairs/pallas_call | solution.py:102
  21.0 1.7 collective-permute-start.3
  23.4 1.9 copy-done.2
  25.3 5.2 %all-to-all-done = bf16[16,8,4096]{2,1,0:T(8,128)(2,1)} async-done(((bf16[16,8,4096]{2,1,0:T(8,128)(2,1)}), bf16[16,8,4096]{2,1,0:T(8,128)(2,1)}, u32[]{:S(2)}, u32[]{:S(2)}) %all-to-all-start) | async-done | bytes 1048608 | tf_op jit(solution)/shard_map/all_to_all | solution.py:382
  32.5 2.0 collective-permute-done.2.rest_2_
  34.5 7.2 %all-to-all-start.2 = ((bf16[16,30,16,256]{3,2,1,0:T(8,128)(2,1)}), bf16[16,30,16,256]{3,2,1,0:T(8,128)(2,1)}, u32[]{:S(2)}, u32[]{:S(2)}) async-start(bf16[16,30,16,256]{3,2,1,0:T(8,128)(2,1)} %copy-done.2), calls=%async_computation.2 | async-start | bytes 7864320 | tf_op jit(solution)/shard_map/all_to_all | solution.py:391
  42.1 2.9 %collective-permute-start.5 = (bf16[1952,128]{1,0:T(8,128)(2,1)S(1)}, bf16[1952,128]{1,0:T(8,128)(2,1)S(1)}, u32[]{:S(2)}, u32[]{:S(2)}) collective-permute-start(bf16[1952,128]{1,0:T(8,128)(2,1)S(1)} %get-tuple-element.92), channel_id=1, source_target_pairs={{0,64},{16,80},{32,96},{48,112},{64,0},{80,16},{96,32},{112,48},{1... | collective-permute-start | bytes 1499144 | tf_op jit(solution)/shard_map/ppermute | solution.py:395
  45.1 1.6 collective-permute-start.6
  48.2 3.6 %reshape.58.g_ref = bf16[16,6,64,64]{3,2,1,0:T(8,128)(2,1)} reshape(bf16[16,6,4096]{2,1,0:T(8,128)(2,1)} %bitcast.24) | data formatting | bytes 1572864 | tf_op jit(solution)/shard_map/reshape | solution.py:400
  51.8 7.0 %greens.1 = (bf16[16,3,64,128]{3,2,1,0:T(8,128)(2,1)}, bf16[2,192,192]{2,1,0:T(8,128)(2,1)}) custom-call(s32[2]{0:T(128)} %copy-done.6, s32[16]{0:T(128)} %size.1, s32[2048]{0:T(1024)} %bitcast_convert_fusion.meta.pat, bf16[16,6,64,64]{3,2,1,0:T(8,128)(2,1)} %reshape.58.g_ref, bf16[2,32,64]{2,1,0:T(8,128)(2,1)} %constant.54.clone.rows_ref, ...), custom_call_target="tpu_custom_call" | custom-call | flops 1000000 | bytes 8000000 | tf_op jit(solution)/shard_map/greens/pallas_call | solution.py:189
  59.1 8.2 %collective-permute-done.5.rest_4_ = bf16[1952,128]{1,0:T(8,128)(2,1)S(1)} collective-permute-done((bf16[1952,128]{1,0:T(8,128)(2,1)S(1)}, bf16[1952,128]{1,0:T(8,128)(2,1)S(1)}, u32[]{:S(2)}, u32[]{:S(2)}) %collective-permute-start.5) | collective-permute-done | bytes 499744 | tf_op jit(solution)/shard_map/ppermute | solution.py:395
  69.4 9.2 %collective-permute-done.7.rest_5_ = bf16[1920,128]{1,0:T(8,128)(2,1)} collective-permute-done((bf16[1920,128]{1,0:T(8,128)(2,1)S(1)}, bf16[1920,128]{1,0:T(8,128)(2,1)}, u32[]{:S(2)}, u32[]{:S(2)}) %collective-permute-start.7) | collective-permute-done | bytes 491552 | tf_op jit(solution)/shard_map/ppermute | solution.py:395
  78.6 12.7 %first.1 = bf16[16,6,80,256]{3,2,1,0:T(8,128)(2,1)} custom-call(s32[2]{0:T(128)} %copy-done.6, s32[4096]{0:T(1024)} %reshape.55.pat, bf16[256,256]{1,0:T(8,128)(2,1)} %constant.53.clone.perm, bf16[2,192,192]{2,1,0:T(8,128)(2,1)} %get-tuple-element.64.w_ref, bf16[1920,128]{1,0:T(8,128)(2,1)} %bitcast.31, bf16[1920,128]{1,0:T(8,128)(2,1)} %collective-permute-done.1.rest_1_, ...), custom_call_target="tpu_custom_call" | custom-call | flops 3000000000 | bytes 8000000 | tf_op jit(solution)/shard_map/first/pallas_call | solution.py:310
  91.3 6.5 %all-to-all-done.2 = bf16[16,30,16,256]{3,2,1,0:T(8,128)(2,1)} async-done(((bf16[16,30,16,256]{3,2,1,0:T(8,128)(2,1)}), bf16[16,30,16,256]{3,2,1,0:T(8,128)(2,1)}, u32[]{:S(2)}, u32[]{:S(2)}) %all-to-all-start.2) | async-done | bytes 3932192 | tf_op jit(solution)/shard_map/all_to_all | solution.py:391
  97.8 10.7 %all-to-all-start.1 = ((bf16[16,6,80,256]{3,2,1,0:T(8,128)(2,1)}), bf16[16,6,80,256]{3,2,1,0:T(8,128)(2,1)}, u32[]{:S(2)}, u32[]{:S(2)}) async-start(bf16[16,6,80,256]{3,2,1,0:T(8,128)(2,1)} %first.1), calls=%async_computation.1 | async-start | bytes 7864320 | tf_op jit(solution)/shard_map/all_to_all | solution.py:404
  108.5 8.8 %second.3 = (bf16[6,160,256]{2,1,0:T(8,128)(2,1)}, bf16[6,160,256]{2,1,0:T(8,128)(2,1)}, bf16[6,160,256]{2,1,0:T(8,128)(2,1)}, bf16[6,160,256]{2,1,0:T(8,128)(2,1)}) custom-call(s32[2]{0:T(128)} %copy-done.6, s32[2048]{0:T(1024)} %bitcast_convert_fusion.meta.pat, bf16[256,256]{1,0:T(8,128)(2,1)} %constant.53.clone.perm, ...), custom_call_target="tpu_custom_call" | custom-call | flops 2000000000 | bytes 15000000 | tf_op jit(solution)/shard_map/second/pallas_call | solution.py:248
  117.3 3.2 %collective-permute-start.9 = (bf16[6,160,256]{2,1,0:T(8,128)(2,1)}, bf16[6,160,256]{2,1,0:T(8,128)(2,1)S(1)}, u32[]{:S(2)}, u32[]{:S(2)}) collective-permute-start(bf16[6,160,256]{2,1,0:T(8,128)(2,1)} %get-tuple-element.77), channel_id=1, source_target_pairs={{0,96},{16,112},{32,0},{48,16},{64,32},{80,48},{96,64},{112,80},{1... | collective-permute-start | bytes 1474568 | tf_op jit(solution)/shard_map/ppermute | solution.py:409
  120.6 3.0 %collective-permute-start.14 = (bf16[6,160,256]{2,1,0:T(8,128)(2,1)}, bf16[6,160,256]{2,1,0:T(8,128)(2,1)S(1)}, u32[]{:S(2)}, u32[]{:S(2)}) collective-permute-start(bf16[6,160,256]{2,1,0:T(8,128)(2,1)} %get-tuple-element.84), channel_id=1, source_target_pairs={{0,112},{16,96},{32,16},{48,0},{64,48},{80,32},{96,80},{112,64},{1... | collective-permute-start | bytes 1474568 | tf_op jit(solution)/shard_map/ppermute | solution.py:409
  123.5 8.8 %second.2 = (bf16[6,160,256]{2,1,0:T(8,128)(2,1)}, bf16[6,160,256]{2,1,0:T(8,128)(2,1)}, bf16[6,160,256]{2,1,0:T(8,128)(2,1)}, bf16[6,160,256]{2,1,0:T(8,128)(2,1)}) custom-call(s32[2]{0:T(128)} %copy-done.6, s32[2048]{0:T(1024)} %bitcast_convert_fusion.meta.pat, bf16[256,256]{1,0:T(8,128)(2,1)} %constant.53.clone.perm, ...), custom_call_target="tpu_custom_call" | custom-call | flops 2000000000 | bytes 15000000 | tf_op jit(solution)/shard_map/second/pallas_call | solution.py:248
  134.4 2.0 collective-permute-start.13
  136.4 2.4 %collective-permute-done.11.rest_3_ = bf16[6,160,256]{2,1,0:T(8,128)(2,1)S(1)} collective-permute-done((bf16[6,160,256]{2,1,0:T(8,128)(2,1)}, bf16[6,160,256]{2,1,0:T(8,128)(2,1)S(1)}, u32[]{:S(2)}, u32[]{:S(2)}) %collective-permute-start.11) | collective-permute-done | bytes 491552 | tf_op jit(solution)/shard_map/ppermute | solution.py:409
  138.8 22.0 %collective-permute-done.14.rest_7_ = bf16[6,160,256]{2,1,0:T(8,128)(2,1)S(1)} collective-permute-done((bf16[6,160,256]{2,1,0:T(8,128)(2,1)}, bf16[6,160,256]{2,1,0:T(8,128)(2,1)S(1)}, u32[]{:S(2)}, u32[]{:S(2)}) %collective-permute-start.14) | collective-permute-done | bytes 491552 | tf_op jit(solution)/shard_map/ppermute | solution.py:409
  162.2 10.8 %chi.1 = (bf16[16,40,1280]{2,1,0:T(8,128)(2,1)}, f32[16,40,1280]{2,1,0:T(8,128)}) custom-call(s32[2]{0:T(128)} %copy-done.6, bf16[16,6,80,256]{3,2,1,0:T(8,128)(2,1)} %all-to-all-done.1.first_ref, bf16[6,160,256]{2,1,0:T(8,128)(2,1)} %get-tuple-element.72.rest_0_, bf16[6,160,256]{2,1,0:T(8,128)(2,1)} %copy-done.16, bf16[6,160,256]{2,1,0:T(8,128)(2,1)} %copy-done.12, ...), custom_call_target="tpu_custom_call" | custom-call | flops 5000000000 | bytes 13000000 | tf_op jit(solution)/shard_map/chi/pallas_call | solution.py:349
  173.6 3.3 %collective-permute-done.15 = bf16[16,40,1280]{2,1,0:T(8,128)(2,1)S(1)} collective-permute-done((bf16[16,40,1280]{2,1,0:T(8,128)(2,1)}, bf16[16,40,1280]{2,1,0:T(8,128)(2,1)S(1)}, u32[]{:S(2)}, u32[]{:S(2)}) %collective-permute-start.15) | collective-permute-done | bytes 1638432 | tf_op jit(solution)/shard_map/ppermute | solution.py:416
  176.9 3.4 %add_convert_fusion = bf16[16,40,1280]{2,1,0:T(8,128)(2,1)} fusion(f32[16,40,1280]{2,1,0:T(8,128)} %get-tuple-element.85, bf16[16,40,1280]{2,1,0:T(8,128)(2,1)S(1)} %collective-permute-done.15), kind=kLoop, calls=%fused_computation.1 | loop fusion | flops 2457600 | bytes 6553600 | tf_op jit(solution)/shard_map/convert_element_type | solution.py:416
  180.4 6.9 %all-to-all-start.3 = ((bf16[16,40,1280]{2,1,0:T(8,128)(2,1)}), bf16[16,40,1280]{2,1,0:T(8,128)(2,1)S(1)}, u32[]{:S(2)}, u32[]{:S(2)}) async-start(bf16[16,40,1280]{2,1,0:T(8,128)(2,1)} %add_convert_fusion), calls=%async_computation.3 | async-start | bytes 3276800 | tf_op jit(solution)/shard_map/all_to_all | solution.py:417
  187.3 25.6 %all-to-all-done.3 = bf16[16,40,1280]{2,1,0:T(8,128)(2,1)S(1)} async-done(((bf16[16,40,1280]{2,1,0:T(8,128)(2,1)}), bf16[16,40,1280]{2,1,0:T(8,128)(2,1)S(1)}, u32[]{:S(2)}, u32[]{:S(2)}) %all-to-all-start.3) | async-done | bytes 1638432 | tf_op jit(solution)/shard_map/all_to_all | solution.py:417
  213.3 6.8 %collective-permute-done.16 = f32[2,10,1280]{2,1,0:T(8,128)S(1)} collective-permute-done((f32[2,10,1280]{2,1,0:T(8,128)S(1)}, f32[2,10,1280]{2,1,0:T(8,128)S(1)}, u32[]{:S(2)}, u32[]{:S(2)}) %collective-permute-start.16) | collective-permute-done | bytes 102432 | tf_op jit(solution)/shard_map/ppermute | solution.py:423
  220.4 4.2 %collective-permute-done.17 = f32[10,1280]{1,0:T(8,128)S(1)} collective-permute-done((f32[10,1280]{1,0:T(8,128)S(1)}, f32[10,1280]{1,0:T(8,128)S(1)}, u32[]{:S(2)}, u32[]{:S(2)}) %collective-permute-start.17) | collective-permute-done | bytes 51232 | tf_op jit(solution)/shard_map/ppermute | solution.py:426
  (85 shorter events, 17.2 us)
Async XLA Ops:
  0.0 12.8 %copy-start.3 = (bf16[256,256]{1,0:T(8,128)(2,1)S(1)}, bf16[256,256]{1,0:T(8,128)(2,1)}, u32[]{:S(2)}) copy-start(bf16[256,256]{1,0:T(8,128)(2,1)} %constant.53.clone.perm) | copy-start | bytes 393220
  4.6 25.9 %all-to-all-start = ((bf16[16,8,4096]{2,1,0:T(8,128)(2,1)}), bf16[16,8,4096]{2,1,0:T(8,128)(2,1)}, u32[]{:S(2)}, u32[]{:S(2)}) async-start(bf16[16,8,4096]{2,1,0:T(8,128)(2,1)} %pack.1), calls=%async_computation | async-start | bytes 2097152 | tf_op jit(solution)/shard_map/all_to_all | solution.py:382
  12.8 10.5 %copy-start.6 = (s32[2]{0:T(128)}, s32[2]{0:T(128)S(1)}, u32[]{:S(2)}) copy-start(s32[2]{0:T(128)S(1)} %pad_add_fusion.pos) | copy-start | bytes 28
  12.8 2.1 copy-start
  15.0 7.8 %copy-start.1 = (bf16[10,16,3,4096]{3,1,2,0:T(8,128)(2,1)S(1)}, bf16[10,16,3,4096]{3,1,2,0:T(8,128)(2,1)}, u32[]{:S(2)}) copy-start(bf16[10,16,3,4096]{3,1,2,0:T(8,128)(2,1)} %param.9) | copy-start | bytes 11796484
  19.6 13.0 %collective-permute-start.1 = (bf16[1920,128]{1,0:T(8,128)(2,1)}, bf16[1920,128]{1,0:T(8,128)(2,1)}, u32[]{:S(2)}, u32[]{:S(2)}) collective-permute-start(bf16[1920,128]{1,0:T(8,128)(2,1)} %bitcast.5), channel_id=1, source_target_pairs={{0,16},{16,0},{32,48},{48,32},{64,80},{80,64},{96,112},{112,96},{1... | collective-permute-start | bytes 1474568 | tf_op jit(solution)/shard_map/ppermute | solution.py:387
  19.6 14.9 %collective-permute-start.2 = (bf16[1920,128]{1,0:T(8,128)(2,1)S(1)}, bf16[1920,128]{1,0:T(8,128)(2,1)}, u32[]{:S(2)}, u32[]{:S(2)}) collective-permute-start(bf16[1920,128]{1,0:T(8,128)(2,1)S(1)} %bitcast.34), channel_id=1, source_target_pairs={{0,32},{16,48},{32,64},{48,80},{64,96},{80,112},{96,0},{112,16},{1... | collective-permute-start | bytes 1474568 | tf_op jit(solution)/shard_map/ppermute | solution.py:387
  21.0 13.5 %collective-permute-start.3 = (bf16[1920,128]{1,0:T(8,128)(2,1)S(1)}, bf16[1920,128]{1,0:T(8,128)(2,1)}, u32[]{:S(2)}, u32[]{:S(2)}) collective-permute-start(bf16[1920,128]{1,0:T(8,128)(2,1)S(1)} %bitcast.33), channel_id=1, source_target_pairs={{0,96},{16,112},{32,0},{48,16},{64,32},{80,48},{96,64},{112,80},{1... | collective-permute-start | bytes 1474568 | tf_op jit(solution)/shard_map/ppermute | solution.py:387
  23.4 1.9 copy-start.2
  31.3 1.2 collective-permute-start
  34.5 63.3 %all-to-all-start.2 = ((bf16[16,30,16,256]{3,2,1,0:T(8,128)(2,1)}), bf16[16,30,16,256]{3,2,1,0:T(8,128)(2,1)}, u32[]{:S(2)}, u32[]{:S(2)}) async-start(bf16[16,30,16,256]{3,2,1,0:T(8,128)(2,1)} %copy-done.2), calls=%async_computation.2 | async-start | bytes 7864320 | tf_op jit(solution)/shard_map/all_to_all | solution.py:391
  41.8 17.1 %collective-permute-start.4 = (bf16[1952,128]{1,0:T(8,128)(2,1)S(1)}, bf16[1952,128]{1,0:T(8,128)(2,1)S(1)}, u32[]{:S(2)}, u32[]{:S(2)}) collective-permute-start(bf16[1952,128]{1,0:T(8,128)(2,1)S(1)} %get-tuple-element.93), channel_id=1, source_target_pairs={{0,48},{16,32},{32,80},{48,64},{64,112},{80,96},{96,16},{112,0},{1... | collective-permute-start | bytes 1499144 | tf_op jit(solution)/shard_map/ppermute | solution.py:395
  42.1 25.2 %collective-permute-start.5 = (bf16[1952,128]{1,0:T(8,128)(2,1)S(1)}, bf16[1952,128]{1,0:T(8,128)(2,1)S(1)}, u32[]{:S(2)}, u32[]{:S(2)}) collective-permute-start(bf16[1952,128]{1,0:T(8,128)(2,1)S(1)} %get-tuple-element.92), channel_id=1, source_target_pairs={{0,64},{16,80},{32,96},{48,112},{64,0},{80,16},{96,32},{112,48},{1... | collective-permute-start | bytes 1499144 | tf_op jit(solution)/shard_map/ppermute | solution.py:395
  45.1 22.6 %collective-permute-start.6 = (bf16[1952,128]{1,0:T(8,128)(2,1)S(1)}, bf16[1952,128]{1,0:T(8,128)(2,1)}, u32[]{:S(2)}, u32[]{:S(2)}) collective-permute-start(bf16[1952,128]{1,0:T(8,128)(2,1)S(1)} %get-tuple-element.91), channel_id=1, source_target_pairs={{0,112},{16,96},{32,16},{48,0},{64,48},{80,32},{96,80},{112,64},{1... | collective-permute-start | bytes 1499144 | tf_op jit(solution)/shard_map/ppermute | solution.py:395
  46.7 32.0 %collective-permute-start.7 = (bf16[1920,128]{1,0:T(8,128)(2,1)S(1)}, bf16[1920,128]{1,0:T(8,128)(2,1)}, u32[]{:S(2)}, u32[]{:S(2)}) collective-permute-start(bf16[1920,128]{1,0:T(8,128)(2,1)S(1)} %bitcast.32), channel_id=1, source_target_pairs={{0,80},{16,64},{32,112},{48,96},{64,16},{80,0},{96,48},{112,32},{1... | collective-permute-start | bytes 1474568 | tf_op jit(solution)/shard_map/ppermute | solution.py:395
  58.9 19.7 %copy-start.10 = (bf16[1952,128]{1,0:T(8,128)(2,1)}, bf16[1952,128]{1,0:T(8,128)(2,1)S(1)}, u32[]{:S(2)}) copy-start(bf16[1952,128]{1,0:T(8,128)(2,1)S(1)} %collective-permute-done.4.rest_3_) | copy-start | bytes 1499140
  67.4 11.3 %copy-start.11 = (bf16[1952,128]{1,0:T(8,128)(2,1)}, bf16[1952,128]{1,0:T(8,128)(2,1)S(1)}, u32[]{:S(2)}) copy-start(bf16[1952,128]{1,0:T(8,128)(2,1)S(1)} %collective-permute-done.5.rest_4_) | copy-start | bytes 1499140
  97.8 63.0 %all-to-all-start.1 = ((bf16[16,6,80,256]{3,2,1,0:T(8,128)(2,1)}), bf16[16,6,80,256]{3,2,1,0:T(8,128)(2,1)}, u32[]{:S(2)}, u32[]{:S(2)}) async-start(bf16[16,6,80,256]{3,2,1,0:T(8,128)(2,1)} %first.1), calls=%async_computation.1 | async-start | bytes 7864320 | tf_op jit(solution)/shard_map/all_to_all | solution.py:404
  117.3 15.6 %collective-permute-start.8 = (bf16[6,160,256]{2,1,0:T(8,128)(2,1)}, bf16[6,160,256]{2,1,0:T(8,128)(2,1)S(1)}, u32[]{:S(2)}, u32[]{:S(2)}) collective-permute-start(bf16[6,160,256]{2,1,0:T(8,128)(2,1)} %get-tuple-element.76), channel_id=1, source_target_pairs={{0,32},{16,48},{32,64},{48,80},{64,96},{80,112},{96,0},{112,16},{1... | collective-permute-start | bytes 1474568 | tf_op jit(solution)/shard_map/ppermute | solution.py:409
  117.3 15.6 %collective-permute-start.9 = (bf16[6,160,256]{2,1,0:T(8,128)(2,1)}, bf16[6,160,256]{2,1,0:T(8,128)(2,1)S(1)}, u32[]{:S(2)}, u32[]{:S(2)}) collective-permute-start(bf16[6,160,256]{2,1,0:T(8,128)(2,1)} %get-tuple-element.77), channel_id=1, source_target_pairs={{0,96},{16,112},{32,0},{48,16},{64,32},{80,48},{96,64},{112,80},{1... | collective-permute-start | bytes 1474568 | tf_op jit(solution)/shard_map/ppermute | solution.py:409
  120.6 18.3 %collective-permute-start.11 = (bf16[6,160,256]{2,1,0:T(8,128)(2,1)}, bf16[6,160,256]{2,1,0:T(8,128)(2,1)S(1)}, u32[]{:S(2)}, u32[]{:S(2)}) collective-permute-start(bf16[6,160,256]{2,1,0:T(8,128)(2,1)} %get-tuple-element.80), channel_id=1, source_target_pairs={{0,48},{16,32},{32,80},{48,64},{64,112},{80,96},{96,16},{112,0},{1... | collective-permute-start | bytes 1474568 | tf_op jit(solution)/shard_map/ppermute | solution.py:409
  120.6 40.3 %collective-permute-start.14 = (bf16[6,160,256]{2,1,0:T(8,128)(2,1)}, bf16[6,160,256]{2,1,0:T(8,128)(2,1)S(1)}, u32[]{:S(2)}, u32[]{:S(2)}) collective-permute-start(bf16[6,160,256]{2,1,0:T(8,128)(2,1)} %get-tuple-element.84), channel_id=1, source_target_pairs={{0,112},{16,96},{32,16},{48,0},{64,48},{80,32},{96,80},{112,64},{1... | collective-permute-start | bytes 1474568 | tf_op jit(solution)/shard_map/ppermute | solution.py:409
  132.9 28.0 %copy-start.12 = (bf16[6,160,256]{2,1,0:T(8,128)(2,1)}, bf16[6,160,256]{2,1,0:T(8,128)(2,1)S(1)}, u32[]{:S(2)}) copy-start(bf16[6,160,256]{2,1,0:T(8,128)(2,1)S(1)} %collective-permute-done.8.rest_2_) | copy-start | bytes 1474564
  132.9 28.0 %copy-start.13 = (bf16[6,160,256]{2,1,0:T(8,128)(2,1)}, bf16[6,160,256]{2,1,0:T(8,128)(2,1)S(1)}, u32[]{:S(2)}) copy-start(bf16[6,160,256]{2,1,0:T(8,128)(2,1)S(1)} %collective-permute-done.9.rest_6_) | copy-start | bytes 1474564
  132.9 27.9 %collective-permute-start.10 = (bf16[6,160,256]{2,1,0:T(8,128)(2,1)}, bf16[6,160,256]{2,1,0:T(8,128)(2,1)S(1)}, u32[]{:S(2)}, u32[]{:S(2)}) collective-permute-start(bf16[6,160,256]{2,1,0:T(8,128)(2,1)} %get-tuple-element.78), channel_id=1, source_target_pairs={{0,16},{16,0},{32,48},{48,32},{64,80},{80,64},{96,112},{112,96},{1... | collective-permute-start | bytes 1474568 | tf_op jit(solution)/shard_map/ppermute | solution.py:413
  133.0 27.9 %collective-permute-start.12 = (bf16[6,160,256]{2,1,0:T(8,128)(2,1)}, bf16[6,160,256]{2,1,0:T(8,128)(2,1)S(1)}, u32[]{:S(2)}, u32[]{:S(2)}) collective-permute-start(bf16[6,160,256]{2,1,0:T(8,128)(2,1)} %get-tuple-element.81), channel_id=1, source_target_pairs={{0,64},{16,80},{32,96},{48,112},{64,0},{80,16},{96,32},{112,48},{1... | collective-permute-start | bytes 1474568 | tf_op jit(solution)/shard_map/ppermute | solution.py:413
  134.4 26.5 %collective-permute-start.13 = (bf16[6,160,256]{2,1,0:T(8,128)(2,1)}, bf16[6,160,256]{2,1,0:T(8,128)(2,1)S(1)}, u32[]{:S(2)}, u32[]{:S(2)}) collective-permute-start(bf16[6,160,256]{2,1,0:T(8,128)(2,1)} %get-tuple-element.82), channel_id=1, source_target_pairs={{0,80},{16,64},{32,112},{48,96},{64,16},{80,0},{96,48},{112,32},{1... | collective-permute-start | bytes 1474568 | tf_op jit(solution)/shard_map/ppermute | solution.py:413
  138.8 22.1 %copy-start.14 = (bf16[6,160,256]{2,1,0:T(8,128)(2,1)}, bf16[6,160,256]{2,1,0:T(8,128)(2,1)S(1)}, u32[]{:S(2)}) copy-start(bf16[6,160,256]{2,1,0:T(8,128)(2,1)S(1)} %collective-permute-done.11.rest_3_) | copy-start | bytes 1474564
  173.0 3.9 %collective-permute-start.15 = (bf16[16,40,1280]{2,1,0:T(8,128)(2,1)}, bf16[16,40,1280]{2,1,0:T(8,128)(2,1)S(1)}, u32[]{:S(2)}, u32[]{:S(2)}) collective-permute-start(bf16[16,40,1280]{2,1,0:T(8,128)(2,1)} %get-tuple-element.86), channel_id=1, source_target_pairs={{0,16},{16,0},{32,48},{48,32},{64,80},{80,64},{96,112},{112,96},{1... | collective-permute-start | bytes 4915208 | tf_op jit(solution)/shard_map/ppermute | solution.py:416
  180.4 32.5 %all-to-all-start.3 = ((bf16[16,40,1280]{2,1,0:T(8,128)(2,1)}), bf16[16,40,1280]{2,1,0:T(8,128)(2,1)S(1)}, u32[]{:S(2)}, u32[]{:S(2)}) async-start(bf16[16,40,1280]{2,1,0:T(8,128)(2,1)} %add_convert_fusion), calls=%async_computation.3 | async-start | bytes 3276800 | tf_op jit(solution)/shard_map/all_to_all | solution.py:417
  213.2 6.9 %collective-permute-start.16 = (f32[2,10,1280]{2,1,0:T(8,128)S(1)}, f32[2,10,1280]{2,1,0:T(8,128)S(1)}, u32[]{:S(2)}, u32[]{:S(2)}) collective-permute-start(f32[2,10,1280]{2,1,0:T(8,128)S(1)} %constant_dynamic-slice_fusion), channel_id=1, source_target_pairs={{0,64},{16,80},{32,96},{48,112},{64,0},{80,16},{96,32},{112,48},{1... | collective-permute-start | bytes 307208 | tf_op jit(solution)/shard_map/ppermute | solution.py:423
  220.2 4.5 %collective-permute-start.17 = (f32[10,1280]{1,0:T(8,128)S(1)}, f32[10,1280]{1,0:T(8,128)S(1)}, u32[]{:S(2)}, u32[]{:S(2)}) collective-permute-start(f32[10,1280]{1,0:T(8,128)S(1)} %dynamic-slice_bitcast_fusion), channel_id=1, source_target_pairs={{0,32},{16,48},{32,0},{48,16},{64,96},{80,112},{96,64},{112,80},{1... | collective-permute-start | bytes 153608 | tf_op jit(solution)/shard_map/ppermute | solution.py:426
  (9 other events, 7.8 us)

commit v10 on v8

--- a/solution.py
+++ b/solution.py
@@ -225,7 +225,7 @@
         out_specs=[vspec()] * 4,
         out_shape=[jax.ShapeDtypeStruct((2 * W, 160, 256), BF)] * 4,
         scratch_shapes=[pltpu.VMEM((NOB + 2, W, 160, 256), BF), pltpu.VMEM((256 * W, 256), BF)],
-        compiler_params=pltpu.CompilerParams(vmem_limit_bytes=VLIM),
+        compiler_params=pltpu.CompilerParams(vmem_limit_bytes=VSMALL),
         cost_estimate=pl.CostEstimate(flops=2 * 10**9, bytes_accessed=15 * 10**6, transcendentals=0),
         name="second",
     )(pos, pat, perm, ta, v)
@@ -327,7 +327,7 @@
         out_specs=[pl.BlockSpec((16, 40, 256), lambda t: (0, 0, t))] * 2,
         out_shape=[jax.ShapeDtypeStruct((16, 40, 1280), BF), jax.ShapeDtypeStruct((16, 40, 1280), F32)],
         scratch_shapes=[pltpu.VMEM((1280, 1536), BF)],
-        compiler_params=pltpu.CompilerParams(vmem_limit_bytes=VLIM),
+        compiler_params=pltpu.CompilerParams(vmem_limit_bytes=VSMALL),
         cost_estimate=pl.CostEstimate(flops=5 * 10**9, bytes_accessed=13 * 10**6, transcendentals=0),
         name="chi",
     )(pos, first, *us)

time: 223 us -> 218 us (0.978)
  Pallas kernels: 52.6 us -> 49.2 us
    unnamed x33 -> x31, local copies, waits for them, and re-layouts: 6.05 us -> 6.65 us
  transfers between devices with their start and end apart: 23 -> 23, of which waited for: 14 -> 14; matrix products, arithmetic and copies ran while one was open for 3% -> 3% of each run, Pallas kernels for 19% -> 18%
where the time goes in v10:
time: 218 us; the launch traced here: 217 us
  waiting for transfers between devices  91.3 us (42%)
  starting transfers between devices  56.1 us (26%)
  Pallas kernels  49.2 us (23%)
  local copies, waits for them, and re-layouts  13.9 us (6%)
  other arithmetic  6.29 us (3%)
    all_to_all x1, waiting for transfers between devices, body(): part = lax.all_to_all(part, 'orb', split_axis=0, concat_axis=0, tiled=True)  25.6 us
    ppermute x7, waiting for transfers between devices, body(): us[k] = lax.ppermute(u, 'aux', pairs_of(k))  24.5 us
    ppermute x7, waiting for transfers between devices, body(): tb[k] = lax.ppermute(tb[k], 'aux', pairs_of(k))  20.6 us
    pallas_call x2, Pallas kernels, second_products(): pl.pallas_call(functools.partial(second_kernel, steps), in_specs=[sspec()...  15.9 us
    pallas_call x1, Pallas kernels, first_products(): pl.pallas_call(first_kernel, in_specs=[sspec(), sspec(), vspec(), vspec()...  12.6 us
    all_to_all x1, starting transfers between devices, body(): lax.all_to_all(first, 'orb', split_axis=0, concat_axis=0, tiled=True)  10.7 us
    ppermute x7, starting transfers between devices, body(): us[k] = lax.ppermute(u, 'aux', pairs_of(k))  9.62 us
    pallas_call x1, Pallas kernels, chi_share(): pl.pallas_call(chi_kernel, grid=(5,), in_specs=[sspec(), vspec()] + [vspe...  9.21 us
  transfers between devices with their start and end apart: 23, of which 14 were waited for; matrix products, arithmetic and copies ran while one was open for 3% of the time, Pallas kernels for 18%

profile of v10, /device:TPU:0, one launch (start us, length us, event | category | flops | bytes accessed | tf_op | source)
XLA Modules:
  0.0 217.2 jit_solution(3285013167685033061)
XLA Ops:
  3.7 8.2 %all-to-all-start = ((bf16[16,8,4096]{2,1,0:T(8,128)(2,1)}), bf16[16,8,4096]{2,1,0:T(8,128)(2,1)}, u32[]{:S(2)}, u32[]{:S(2)}) async-start(bf16[16,8,4096]{2,1,0:T(8,128)(2,1)} %broadcast_in_dim.2), calls=%async_computation | async-start | bytes 2097152 | tf_op jit(solution)/shard_map/all_to_all | solution.py:359
  11.9 2.1 copy-done
  14.1 3.8 %block_pairs.1 = (bf16[2,3,10,32,128]{4,3,2,1,0:T(8,128)(2,1)S(1)}, bf16[2,3,10,32,128]{4,3,2,1,0:T(8,128)(2,1)}, bf16[2,3,10,32,128]{4,3,2,1,0:T(8,128)(2,1)S(1...) custom-call(s32[2]{0:T(128)S(1)} %pad_add_fusion.pos, ...), custom_call_target="tpu_custom_call" | custom-call | flops 1000000000 | bytes 8000000 | tf_op jit(solution)/shard_map/block_pairs/pallas_call | solution.py:102
  20.2 1.8 collective-permute-start.3
  22.5 1.9 copy-done.2
  24.4 5.2 %all-to-all-done = bf16[16,8,4096]{2,1,0:T(8,128)(2,1)} async-done(((bf16[16,8,4096]{2,1,0:T(8,128)(2,1)}), bf16[16,8,4096]{2,1,0:T(8,128)(2,1)}, u32[]{:S(2)}, u32[]{:S(2)}) %all-to-all-start) | async-done | bytes 1048608 | tf_op jit(solution)/shard_map/all_to_all | solution.py:359
  31.6 2.0 collective-permute-done.2.rest_2_
  33.6 7.2 %all-to-all-start.2 = ((bf16[16,30,16,256]{3,2,1,0:T(8,128)(2,1)}), bf16[16,30,16,256]{3,2,1,0:T(8,128)(2,1)}, u32[]{:S(2)}, u32[]{:S(2)}) async-start(bf16[16,30,16,256]{3,2,1,0:T(8,128)(2,1)} %copy-done.2), calls=%async_computation.2 | async-start | bytes 7864320 | tf_op jit(solution)/shard_map/all_to_all | solution.py:368
  42.0 2.9 %collective-permute-start.5 = (bf16[1952,128]{1,0:T(8,128)(2,1)S(1)}, bf16[1952,128]{1,0:T(8,128)(2,1)S(1)}, u32[]{:S(2)}, u32[]{:S(2)}) collective-permute-start(bf16[1952,128]{1,0:T(8,128)(2,1)S(1)} %get-tuple-element.95), channel_id=1, source_target_pairs={{0,64},{16,80},{32,96},{48,112},{64,0},{80,16},{96,32},{112,48},{1... | collective-permute-start | bytes 1499144 | tf_op jit(solution)/shard_map/ppermute | solution.py:372
  44.9 1.7 collective-permute-start.6
  47.9 3.6 %reshape.93.g_ref = bf16[16,6,64,64]{3,2,1,0:T(8,128)(2,1)} reshape(bf16[16,6,4096]{2,1,0:T(8,128)(2,1)} %bitcast.35) | data formatting | bytes 1572864 | tf_op jit(solution)/shard_map/reshape | solution.py:377
  51.6 7.1 %greens.1 = (bf16[16,3,64,128]{3,2,1,0:T(8,128)(2,1)}, bf16[2,192,192]{2,1,0:T(8,128)(2,1)}) custom-call(s32[2]{0:T(128)} %copy-done.6, s32[16]{0:T(128)} %size.1, s32[2048]{0:T(1024)} %bitcast_convert_fusion.meta.pat, bf16[16,6,64,64]{3,2,1,0:T(8,128)(2,1)} %reshape.93.g_ref, bf16[2,32,64]{2,1,0:T(8,128)(2,1)} %constant.57.clone.rows_ref, ...), custom_call_target="tpu_custom_call" | custom-call | flops 1000000 | bytes 8000000 | tf_op jit(solution)/shard_map/greens/pallas_call | solution.py:163
  58.9 8.5 %collective-permute-done.5.rest_4_ = bf16[1952,128]{1,0:T(8,128)(2,1)S(1)} collective-permute-done((bf16[1952,128]{1,0:T(8,128)(2,1)S(1)}, bf16[1952,128]{1,0:T(8,128)(2,1)S(1)}, u32[]{:S(2)}, u32[]{:S(2)}) %collective-permute-start.5) | collective-permute-done | bytes 499744 | tf_op jit(solution)/shard_map/ppermute | solution.py:372
  68.6 10.1 %collective-permute-done.7.rest_5_ = bf16[1920,128]{1,0:T(8,128)(2,1)} collective-permute-done((bf16[1920,128]{1,0:T(8,128)(2,1)S(1)}, bf16[1920,128]{1,0:T(8,128)(2,1)}, u32[]{:S(2)}, u32[]{:S(2)}) %collective-permute-start.7) | collective-permute-done | bytes 491552 | tf_op jit(solution)/shard_map/ppermute | solution.py:372
  78.7 12.6 %first.1 = bf16[16,6,80,256]{3,2,1,0:T(8,128)(2,1)} custom-call(s32[2]{0:T(128)} %copy-done.6, s32[4096]{0:T(1024)} %reshape.90.pat, bf16[256,256]{1,0:T(8,128)(2,1)} %constant.56.clone.perm, bf16[2,192,192]{2,1,0:T(8,128)(2,1)} %get-tuple-element.64.w_ref, bf16[1920,128]{1,0:T(8,128)(2,1)} %bitcast.41, bf16[1920,128]{1,0:T(8,128)(2,1)} %collective-permute-done.1.rest_1_, ...), custom_call_target="tpu_custom_call" | custom-call | flops 3000000000 | bytes 8000000 | tf_op jit(solution)/shard_map/first/pallas_call | solution.py:284
  91.4 5.5 %all-to-all-done.2 = bf16[16,30,16,256]{3,2,1,0:T(8,128)(2,1)} async-done(((bf16[16,30,16,256]{3,2,1,0:T(8,128)(2,1)}), bf16[16,30,16,256]{3,2,1,0:T(8,128)(2,1)}, u32[]{:S(2)}, u32[]{:S(2)}) %all-to-all-start.2) | async-done | bytes 3932192 | tf_op jit(solution)/shard_map/all_to_all | solution.py:368
  96.9 10.7 %all-to-all-start.1 = ((bf16[16,6,80,256]{3,2,1,0:T(8,128)(2,1)}), bf16[16,6,80,256]{3,2,1,0:T(8,128)(2,1)}, u32[]{:S(2)}, u32[]{:S(2)}) async-start(bf16[16,6,80,256]{3,2,1,0:T(8,128)(2,1)} %first.1), calls=%async_computation.1 | async-start | bytes 7864320 | tf_op jit(solution)/shard_map/all_to_all | solution.py:381
  107.6 7.6 %second.3 = (bf16[6,160,256]{2,1,0:T(8,128)(2,1)S(1)}, bf16[6,160,256]{2,1,0:T(8,128)(2,1)S(1)}, bf16[6,160,256]{2,1,0:T(8,128)(2,1)S(1)}, bf16[6,160,256]{2,1,0:T(8,128)(2,1)S(1)}) custom-call(s32[2]{0:T(128)S(1)} %copy-done.7, s32[2048]{0:T(1024)S(1)} %copy-done.5, bf16[256,256]{1,0:T(8,128)(2,1)S(1)} %copy-done.4, ...), custom_call_target="tpu_custom_call" | custom-call | flops 2000000000 | bytes 15000000 | tf_op jit(solution)/shard_map/second/pallas_call | solution.py:222
  115.3 3.2 %collective-permute-start.9 = (bf16[6,160,256]{2,1,0:T(8,128)(2,1)S(1)}, bf16[6,160,256]{2,1,0:T(8,128)(2,1)S(1)}, u32[]{:S(2)}, u32[]{:S(2)}) collective-permute-start(bf16[6,160,256]{2,1,0:T(8,128)(2,1)S(1)} %get-tuple-element.77), channel_id=1, source_target_pairs={{0,96},{16,112},{32,0},{48,16},{64,32},{80,48},{96,64},{112,80},{1... | collective-permute-start | bytes 1474568 | tf_op jit(solution)/shard_map/ppermute | solution.py:386
  118.6 3.0 %collective-permute-start.14 = (bf16[6,160,256]{2,1,0:T(8,128)(2,1)S(1)}, bf16[6,160,256]{2,1,0:T(8,128)(2,1)S(1)}, u32[]{:S(2)}, u32[]{:S(2)}) collective-permute-start(bf16[6,160,256]{2,1,0:T(8,128)(2,1)S(1)} %get-tuple-element.84), channel_id=1, source_target_pairs={{0,112},{16,96},{32,16},{48,0},{64,48},{80,32},{96,80},{112,64},{1... | collective-permute-start | bytes 1474568 | tf_op jit(solution)/shard_map/ppermute | solution.py:386
  121.5 8.3 %second.2 = (bf16[6,160,256]{2,1,0:T(8,128)(2,1)}, bf16[6,160,256]{2,1,0:T(8,128)(2,1)S(1)}, bf16[6,160,256]{2,1,0:T(8,128)(2,1)}, bf16[6,160,256]{2,1,0:T(8,128)(2,1)S(1)}) custom-call(s32[2]{0:T(128)S(1)} %copy-done.7, s32[2048]{0:T(1024)S(1)} %copy-done.5, bf16[256,256]{1,0:T(8,128)(2,1)S(1)} %copy-done.4, bf16[160,3,16,256]{3,2,1,0:T(8,128)(2,1)} %bitcast.16.ta_ref, ...), custom_call_target="tpu_custom_call" | custom-call | flops 2000000000 | bytes 15000000 | tf_op jit(solution)/shard_map/second/pallas_call | solution.py:222
  132.2 1.9 collective-permute-start.13
  134.1 2.4 %collective-permute-done.11.rest_3_ = bf16[6,160,256]{2,1,0:T(8,128)(2,1)S(1)} collective-permute-done((bf16[6,160,256]{2,1,0:T(8,128)(2,1)S(1)}, bf16[6,160,256]{2,1,0:T(8,128)(2,1)S(1)}, u32[]{:S(2)}, u32[]{:S(2)}) %collective-permute-start.11) | collective-permute-done | bytes 491552 | tf_op jit(solution)/shard_map/ppermute | solution.py:386
  136.5 22.0 %collective-permute-done.14.rest_7_ = bf16[6,160,256]{2,1,0:T(8,128)(2,1)S(1)} collective-permute-done((bf16[6,160,256]{2,1,0:T(8,128)(2,1)S(1)}, bf16[6,160,256]{2,1,0:T(8,128)(2,1)S(1)}, u32[]{:S(2)}, u32[]{:S(2)}) %collective-permute-start.14) | collective-permute-done | bytes 491552 | tf_op jit(solution)/shard_map/ppermute | solution.py:386
  159.6 9.2 %chi.1 = (bf16[16,40,1280]{2,1,0:T(8,128)(2,1)S(1)}, f32[16,40,1280]{2,1,0:T(8,128)S(1)}) custom-call(s32[2]{0:T(128)S(1)} %copy-done.7, bf16[16,6,80,256]{3,2,1,0:T(8,128)(2,1)} %all-to-all-done.1.first_ref, bf16[6,160,256]{2,1,0:T(8,128)(2,1)S(1)} %copy-done.11, bf16[6,160,256]{2,1,0:T(8,128)(2,1)S(1)} %collective-permute-done.10.rest_1_, ...), custom_call_target="tpu_custom_call" | custom-call | flops 5000000000 | bytes 13000000 | tf_op jit(solution)/shard_map/chi/pallas_call | solution.py:323
  169.4 3.1 %collective-permute-done.15 = bf16[16,40,1280]{2,1,0:T(8,128)(2,1)S(1)} collective-permute-done((bf16[16,40,1280]{2,1,0:T(8,128)(2,1)S(1)}, bf16[16,40,1280]{2,1,0:T(8,128)(2,1)S(1)}, u32[]{:S(2)}, u32[]{:S(2)}) %collective-permute-start.15) | collective-permute-done | bytes 1638432 | tf_op jit(solution)/shard_map/ppermute | solution.py:393
  172.6 1.5 add_convert_fusion
  174.1 6.9 %all-to-all-start.3 = ((bf16[16,40,1280]{2,1,0:T(8,128)(2,1)}), bf16[16,40,1280]{2,1,0:T(8,128)(2,1)S(1)}, u32[]{:S(2)}, u32[]{:S(2)}) async-start(bf16[16,40,1280]{2,1,0:T(8,128)(2,1)} %add_convert_fusion), calls=%async_computation.3 | async-start | bytes 3276800 | tf_op jit(solution)/shard_map/all_to_all | solution.py:394
  181.0 25.6 %all-to-all-done.3 = bf16[16,40,1280]{2,1,0:T(8,128)(2,1)S(1)} async-done(((bf16[16,40,1280]{2,1,0:T(8,128)(2,1)}), bf16[16,40,1280]{2,1,0:T(8,128)(2,1)S(1)}, u32[]{:S(2)}, u32[]{:S(2)}) %all-to-all-start.3) | async-done | bytes 1638432 | tf_op jit(solution)/shard_map/all_to_all | solution.py:394
  206.9 3.0 %collective-permute-start.18 = (f32[10,1280]{1,0:T(8,128)S(1)}, f32[10,1280]{1,0:T(8,128)S(1)}, u32[]{:S(2)}, u32[]{:S(2)}) collective-permute-start(f32[10,1280]{1,0:T(8,128)S(1)} %get-tuple-element.92), channel_id=1, source_target_pairs={{0,96},{16,112},{32,0},{48,16},{64,32},{80,48},{96,64},{112,80},{1... | collective-permute-start | bytes 153608 | tf_op jit(solution)/shard_map/ppermute | solution.py:400
  210.9 1.9 collective-permute-done.18
  212.8 3.2 %collective-permute-done.17 = f32[10,1280]{1,0:T(8,128)S(1)} collective-permute-done((f32[10,1280]{1,0:T(8,128)S(1)}, f32[10,1280]{1,0:T(8,128)S(1)}, u32[]{:S(2)}, u32[]{:S(2)}) %collective-permute-start.17) | collective-permute-done | bytes 51232 | tf_op jit(solution)/shard_map/ppermute | solution.py:400
  (83 shorter events, 19.1 us)
Async XLA Ops:
  0.0 11.9 %copy-start.3 = (bf16[256,256]{1,0:T(8,128)(2,1)S(1)}, bf16[256,256]{1,0:T(8,128)(2,1)}, u32[]{:S(2)}) copy-start(bf16[256,256]{1,0:T(8,128)(2,1)} %constant.56.clone.perm) | copy-start | bytes 393220
  3.7 25.9 %all-to-all-start = ((bf16[16,8,4096]{2,1,0:T(8,128)(2,1)}), bf16[16,8,4096]{2,1,0:T(8,128)(2,1)}, u32[]{:S(2)}, u32[]{:S(2)}) async-start(bf16[16,8,4096]{2,1,0:T(8,128)(2,1)} %broadcast_in_dim.2), calls=%async_computation | async-start | bytes 2097152 | tf_op jit(solution)/shard_map/all_to_all | solution.py:359
  11.9 10.6 %copy-start.6 = (s32[2]{0:T(128)}, s32[2]{0:T(128)S(1)}, u32[]{:S(2)}) copy-start(s32[2]{0:T(128)S(1)} %pad_add_fusion.pos) | copy-start | bytes 28
  18.7 13.0 %collective-permute-start.1 = (bf16[1920,128]{1,0:T(8,128)(2,1)}, bf16[1920,128]{1,0:T(8,128)(2,1)}, u32[]{:S(2)}, u32[]{:S(2)}) collective-permute-start(bf16[1920,128]{1,0:T(8,128)(2,1)} %bitcast.6), channel_id=1, source_target_pairs={{0,16},{16,0},{32,48},{48,32},{64,80},{80,64},{96,112},{112,96},{1... | collective-permute-start | bytes 1474568 | tf_op jit(solution)/shard_map/ppermute | solution.py:364
  18.7 14.9 %collective-permute-start.2 = (bf16[1920,128]{1,0:T(8,128)(2,1)S(1)}, bf16[1920,128]{1,0:T(8,128)(2,1)}, u32[]{:S(2)}, u32[]{:S(2)}) collective-permute-start(bf16[1920,128]{1,0:T(8,128)(2,1)S(1)} %bitcast.44), channel_id=1, source_target_pairs={{0,32},{16,48},{32,64},{48,80},{64,96},{80,112},{96,0},{112,16},{1... | collective-permute-start | bytes 1474568 | tf_op jit(solution)/shard_map/ppermute | solution.py:364
  20.2 13.5 %collective-permute-start.3 = (bf16[1920,128]{1,0:T(8,128)(2,1)S(1)}, bf16[1920,128]{1,0:T(8,128)(2,1)}, u32[]{:S(2)}, u32[]{:S(2)}) collective-permute-start(bf16[1920,128]{1,0:T(8,128)(2,1)S(1)} %bitcast.43), channel_id=1, source_target_pairs={{0,96},{16,112},{32,0},{48,16},{64,32},{80,48},{96,64},{112,80},{1... | collective-permute-start | bytes 1474568 | tf_op jit(solution)/shard_map/ppermute | solution.py:364
  30.4 1.2 collective-permute-start
  33.6 63.2 %all-to-all-start.2 = ((bf16[16,30,16,256]{3,2,1,0:T(8,128)(2,1)}), bf16[16,30,16,256]{3,2,1,0:T(8,128)(2,1)}, u32[]{:S(2)}, u32[]{:S(2)}) async-start(bf16[16,30,16,256]{3,2,1,0:T(8,128)(2,1)} %copy-done.2), calls=%async_computation.2 | async-start | bytes 7864320 | tf_op jit(solution)/shard_map/all_to_all | solution.py:368
  41.8 17.0 %collective-permute-start.4 = (bf16[1952,128]{1,0:T(8,128)(2,1)}, bf16[1952,128]{1,0:T(8,128)(2,1)S(1)}, u32[]{:S(2)}, u32[]{:S(2)}) collective-permute-start(bf16[1952,128]{1,0:T(8,128)(2,1)} %get-tuple-element.96), channel_id=1, source_target_pairs={{0,48},{16,32},{32,80},{48,64},{64,112},{80,96},{96,16},{112,0},{1... | collective-permute-start | bytes 1499144 | tf_op jit(solution)/shard_map/ppermute | solution.py:372
  42.0 25.4 %collective-permute-start.5 = (bf16[1952,128]{1,0:T(8,128)(2,1)S(1)}, bf16[1952,128]{1,0:T(8,128)(2,1)S(1)}, u32[]{:S(2)}, u32[]{:S(2)}) collective-permute-start(bf16[1952,128]{1,0:T(8,128)(2,1)S(1)} %get-tuple-element.95), channel_id=1, source_target_pairs={{0,64},{16,80},{32,96},{48,112},{64,0},{80,16},{96,32},{112,48},{1... | collective-permute-start | bytes 1499144 | tf_op jit(solution)/shard_map/ppermute | solution.py:372
  44.9 22.6 %collective-permute-start.6 = (bf16[1952,128]{1,0:T(8,128)(2,1)S(1)}, bf16[1952,128]{1,0:T(8,128)(2,1)S(1)}, u32[]{:S(2)}, u32[]{:S(2)}) collective-permute-start(bf16[1952,128]{1,0:T(8,128)(2,1)S(1)} %get-tuple-element.94), channel_id=1, source_target_pairs={{0,112},{16,96},{32,16},{48,0},{64,48},{80,32},{96,80},{112,64},{1... | collective-permute-start | bytes 1499144 | tf_op jit(solution)/shard_map/ppermute | solution.py:372
  46.5 32.2 %collective-permute-start.7 = (bf16[1920,128]{1,0:T(8,128)(2,1)S(1)}, bf16[1920,128]{1,0:T(8,128)(2,1)}, u32[]{:S(2)}, u32[]{:S(2)}) collective-permute-start(bf16[1920,128]{1,0:T(8,128)(2,1)S(1)} %bitcast.42), channel_id=1, source_target_pairs={{0,80},{16,64},{32,112},{48,96},{64,16},{80,0},{96,48},{112,32},{1... | collective-permute-start | bytes 1474568 | tf_op jit(solution)/shard_map/ppermute | solution.py:372
  58.7 20.0 %copy-start.12 = (bf16[1952,128]{1,0:T(8,128)(2,1)}, bf16[1952,128]{1,0:T(8,128)(2,1)S(1)}, u32[]{:S(2)}) copy-start(bf16[1952,128]{1,0:T(8,128)(2,1)S(1)} %collective-permute-done.4.rest_3_) | copy-start | bytes 1499140
  67.4 11.3 %copy-start.13 = (bf16[1952,128]{1,0:T(8,128)(2,1)}, bf16[1952,128]{1,0:T(8,128)(2,1)S(1)}, u32[]{:S(2)}) copy-start(bf16[1952,128]{1,0:T(8,128)(2,1)S(1)} %collective-permute-done.5.rest_4_) | copy-start | bytes 1499140
  67.5 11.2 %copy-start.14 = (bf16[1952,128]{1,0:T(8,128)(2,1)}, bf16[1952,128]{1,0:T(8,128)(2,1)S(1)}, u32[]{:S(2)}) copy-start(bf16[1952,128]{1,0:T(8,128)(2,1)S(1)} %collective-permute-done.6.rest_7_) | copy-start | bytes 1499140
  91.3 16.3 %copy-start.4 = (bf16[256,256]{1,0:T(8,128)(2,1)S(1)}, bf16[256,256]{1,0:T(8,128)(2,1)}, u32[]{:S(2)}) copy-start(bf16[256,256]{1,0:T(8,128)(2,1)} %constant.56.clone.perm) | copy-start | bytes 393220
  91.3 16.3 %copy-start.5 = (s32[2048]{0:T(1024)S(1)}, s32[2048]{0:T(1024)}, u32[]{:S(2)}) copy-start(s32[2048]{0:T(1024)} %bitcast_convert_fusion.meta.pat) | copy-start | bytes 24580
  91.3 16.3 %copy-start.7 = (s32[2]{0:T(128)S(1)}, s32[2]{0:T(128)}, u32[]{:S(2)}) copy-start(s32[2]{0:T(128)} %copy-done.6) | copy-start | bytes 28
  91.3 16.3 %copy-start.8 = (bf16[16,3,64,128]{3,2,1,0:T(8,128)(2,1)S(1)}, bf16[16,3,64,128]{3,2,1,0:T(8,128)(2,1)}, u32[]{:S(2)}) copy-start(bf16[16,3,64,128]{3,2,1,0:T(8,128)(2,1)} %get-tuple-element.71.v_ref) | copy-start | bytes 2359300
  96.9 61.6 %all-to-all-start.1 = ((bf16[16,6,80,256]{3,2,1,0:T(8,128)(2,1)}), bf16[16,6,80,256]{3,2,1,0:T(8,128)(2,1)}, u32[]{:S(2)}, u32[]{:S(2)}) async-start(bf16[16,6,80,256]{3,2,1,0:T(8,128)(2,1)} %first.1), calls=%async_computation.1 | async-start | bytes 7864320 | tf_op jit(solution)/shard_map/all_to_all | solution.py:381
  115.3 15.4 %collective-permute-start.8 = (bf16[6,160,256]{2,1,0:T(8,128)(2,1)S(1)}, bf16[6,160,256]{2,1,0:T(8,128)(2,1)S(1)}, u32[]{:S(2)}, u32[]{:S(2)}) collective-permute-start(bf16[6,160,256]{2,1,0:T(8,128)(2,1)S(1)} %get-tuple-element.76), channel_id=1, source_target_pairs={{0,32},{16,48},{32,64},{48,80},{64,96},{80,112},{96,0},{112,16},{1... | collective-permute-start | bytes 1474568 | tf_op jit(solution)/shard_map/ppermute | solution.py:386
  115.3 15.4 %collective-permute-start.9 = (bf16[6,160,256]{2,1,0:T(8,128)(2,1)S(1)}, bf16[6,160,256]{2,1,0:T(8,128)(2,1)S(1)}, u32[]{:S(2)}, u32[]{:S(2)}) collective-permute-start(bf16[6,160,256]{2,1,0:T(8,128)(2,1)S(1)} %get-tuple-element.77), channel_id=1, source_target_pairs={{0,96},{16,112},{32,0},{48,16},{64,32},{80,48},{96,64},{112,80},{1... | collective-permute-start | bytes 1474568 | tf_op jit(solution)/shard_map/ppermute | solution.py:386
  118.6 17.9 %collective-permute-start.11 = (bf16[6,160,256]{2,1,0:T(8,128)(2,1)S(1)}, bf16[6,160,256]{2,1,0:T(8,128)(2,1)S(1)}, u32[]{:S(2)}, u32[]{:S(2)}) collective-permute-start(bf16[6,160,256]{2,1,0:T(8,128)(2,1)S(1)} %get-tuple-element.80), channel_id=1, source_target_pairs={{0,48},{16,32},{32,80},{48,64},{64,112},{80,96},{96,16},{112,0},{1... | collective-permute-start | bytes 1474568 | tf_op jit(solution)/shard_map/ppermute | solution.py:386
  118.6 39.9 %collective-permute-start.14 = (bf16[6,160,256]{2,1,0:T(8,128)(2,1)S(1)}, bf16[6,160,256]{2,1,0:T(8,128)(2,1)S(1)}, u32[]{:S(2)}, u32[]{:S(2)}) collective-permute-start(bf16[6,160,256]{2,1,0:T(8,128)(2,1)S(1)} %get-tuple-element.84), channel_id=1, source_target_pairs={{0,112},{16,96},{32,16},{48,0},{64,48},{80,32},{96,80},{112,64},{1... | collective-permute-start | bytes 1474568 | tf_op jit(solution)/shard_map/ppermute | solution.py:386
  130.7 27.8 %collective-permute-start.10 = (bf16[6,160,256]{2,1,0:T(8,128)(2,1)}, bf16[6,160,256]{2,1,0:T(8,128)(2,1)S(1)}, u32[]{:S(2)}, u32[]{:S(2)}) collective-permute-start(bf16[6,160,256]{2,1,0:T(8,128)(2,1)} %get-tuple-element.78), channel_id=1, source_target_pairs={{0,16},{16,0},{32,48},{48,32},{64,80},{80,64},{96,112},{112,96},{1... | collective-permute-start | bytes 1474568 | tf_op jit(solution)/shard_map/ppermute | solution.py:390
  130.7 27.8 %collective-permute-start.12 = (bf16[6,160,256]{2,1,0:T(8,128)(2,1)}, bf16[6,160,256]{2,1,0:T(8,128)(2,1)}, u32[]{:S(2)}, u32[]{:S(2)}) collective-permute-start(bf16[6,160,256]{2,1,0:T(8,128)(2,1)} %get-tuple-element.81), channel_id=1, source_target_pairs={{0,64},{16,80},{32,96},{48,112},{64,0},{80,16},{96,32},{112,48},{1... | collective-permute-start | bytes 1474568 | tf_op jit(solution)/shard_map/ppermute | solution.py:390
  132.2 26.4 %collective-permute-start.13 = (bf16[6,160,256]{2,1,0:T(8,128)(2,1)S(1)}, bf16[6,160,256]{2,1,0:T(8,128)(2,1)}, u32[]{:S(2)}, u32[]{:S(2)}) collective-permute-start(bf16[6,160,256]{2,1,0:T(8,128)(2,1)S(1)} %get-tuple-element.82), channel_id=1, source_target_pairs={{0,80},{16,64},{32,112},{48,96},{64,16},{80,0},{96,48},{112,32},{1... | collective-permute-start | bytes 1474568 | tf_op jit(solution)/shard_map/ppermute | solution.py:390
  168.8 3.8 %collective-permute-start.15 = (bf16[16,40,1280]{2,1,0:T(8,128)(2,1)S(1)}, bf16[16,40,1280]{2,1,0:T(8,128)(2,1)S(1)}, u32[]{:S(2)}, u32[]{:S(2)}) collective-permute-start(bf16[16,40,1280]{2,1,0:T(8,128)(2,1)S(1)} %get-tuple-element.86), channel_id=1, source_target_pairs={{0,16},{16,0},{32,48},{48,32},{64,80},{80,64},{96,112},{112,96},{1... | collective-permute-start | bytes 4915208 | tf_op jit(solution)/shard_map/ppermute | solution.py:393
  174.1 32.5 %all-to-all-start.3 = ((bf16[16,40,1280]{2,1,0:T(8,128)(2,1)}), bf16[16,40,1280]{2,1,0:T(8,128)(2,1)S(1)}, u32[]{:S(2)}, u32[]{:S(2)}) async-start(bf16[16,40,1280]{2,1,0:T(8,128)(2,1)} %add_convert_fusion), calls=%async_computation.3 | async-start | bytes 3276800 | tf_op jit(solution)/shard_map/all_to_all | solution.py:394
  206.9 5.9 %collective-permute-start.18 = (f32[10,1280]{1,0:T(8,128)S(1)}, f32[10,1280]{1,0:T(8,128)S(1)}, u32[]{:S(2)}, u32[]{:S(2)}) collective-permute-start(f32[10,1280]{1,0:T(8,128)S(1)} %get-tuple-element.92), channel_id=1, source_target_pairs={{0,96},{16,112},{32,0},{48,16},{64,32},{80,48},{96,64},{112,80},{1... | collective-permute-start | bytes 153608 | tf_op jit(solution)/shard_map/ppermute | solution.py:400
  209.9 6.1 %collective-permute-start.17 = (f32[10,1280]{1,0:T(8,128)S(1)}, f32[10,1280]{1,0:T(8,128)S(1)}, u32[]{:S(2)}, u32[]{:S(2)}) collective-permute-start(f32[10,1280]{1,0:T(8,128)S(1)} %get-tuple-element.93), channel_id=1, source_target_pairs={{0,64},{16,80},{32,96},{48,112},{64,0},{80,16},{96,32},{112,48},{1... | collective-permute-start | bytes 153608 | tf_op jit(solution)/shard_map/ppermute | solution.py:400
  210.0 6.5 %collective-permute-start.16 = (f32[10,1280]{1,0:T(8,128)S(1)}, f32[10,1280]{1,0:T(8,128)S(1)}, u32[]{:S(2)}, u32[]{:S(2)}) collective-permute-start(f32[10,1280]{1,0:T(8,128)S(1)} %get-tuple-element.91), channel_id=1, source_target_pairs={{0,32},{16,48},{32,64},{48,80},{64,96},{80,112},{96,0},{112,16},{1... | collective-permute-start | bytes 153608 | tf_op jit(solution)/shard_map/ppermute | solution.py:400
  (6 other events, 14.5 us)

commit v11 on v9

--- a/solution.py
+++ b/solution.py
@@ -136,7 +136,7 @@
         in_specs=[sspec(), sspec(), vspec(), vspec()],
         out_specs=vspec(),
         out_shape=jax.ShapeDtypeStruct((NOB, 8, 4096), BF),
-        compiler_params=pltpu.CompilerParams(vmem_limit_bytes=VSMALL),
+        compiler_params=pltpu.CompilerParams(vmem_limit_bytes=VLIM),
         cost_estimate=pl.CostEstimate(flops=0, bytes_accessed=11 * 10**5, transcendentals=0),
         name="pack",
     )(tpat, gpat, occ, virt)
@@ -251,7 +251,7 @@
         out_specs=[vspec()] * 4,
         out_shape=[jax.ShapeDtypeStruct((2 * W, 160, 256), BF)] * 4,
         scratch_shapes=[pltpu.VMEM((NOB + 2, W, 160, 256), BF), pltpu.VMEM((256 * W, 256), BF)],
-        compiler_params=pltpu.CompilerParams(vmem_limit_bytes=VLIM),
+        compiler_params=pltpu.CompilerParams(vmem_limit_bytes=VSMALL),
         cost_estimate=pl.CostEstimate(flops=2 * 10**9, bytes_accessed=15 * 10**6, transcendentals=0),
         name="second",
     )(pos, pat, perm, ta, v)
@@ -353,7 +353,7 @@
         out_specs=[pl.BlockSpec((16, 40, 256), lambda t: (0, 0, t))] * 2,
         out_shape=[jax.ShapeDtypeStruct((16, 40, 1280), BF), jax.ShapeDtypeStruct((16, 40, 1280), F32)],
         scratch_shapes=[pltpu.VMEM((1280, 1536), BF)],
-        compiler_params=pltpu.CompilerParams(vmem_limit_bytes=VLIM),
+        compiler_params=pltpu.CompilerParams(vmem_limit_bytes=VSMALL),
         cost_estimate=pl.CostEstimate(flops=5 * 10**9, bytes_accessed=13 * 10**6, transcendentals=0),
         name="chi",
     )(pos, first, *us)
@@ -417,13 +417,11 @@
     part = lax.all_to_all(part, "orb", split_axis=0, concat_axis=0, tiled=True)
     part = jnp.sum(part.astype(F32), axis=0).reshape(4, NPD, 1280)
     x = a // 2
-    high, low = (x // 2) * 2, lax.rem(x, 2)
-    kept = lax.dynamic_slice_in_dim(part, high, 2, axis=0)
-    sent = lax.dynamic_slice_in_dim(part, 2 - high, 2, axis=0)
-    kept = kept + lax.ppermute(sent, "aux", pairs_of(4))
-    sent = lax.dynamic_index_in_dim(kept, 1 - low, 0, keepdims=False)
-    kept = lax.dynamic_index_in_dim(kept, low, 0, keepdims=False)
-    return kept + lax.ppermute(sent, "aux", [(i, i ^ 2) for i in range(8)])
+    total = lax.dynamic_index_in_dim(part, x, 0, keepdims=False)
+    for dx in range(1, 4):
+        piece = lax.dynamic_index_in_dim(part, lax.rem(x + dx, 4), 0, keepdims=False)
+        total = total + lax.ppermute(piece, "aux", pairs_of(2 * dx))
+    return total
 
 
 def solution(mesh):

time: 226 us -> 216 us (0.956)
  waiting for transfers between devices: 97.5 us -> 91.4 us
  starting transfers between devices: 52.7 us -> 56.2 us
  Pallas kernels: 54.2 us -> 51.3 us
  local copies, waits for them, and re-layouts: 15.5 us -> 13.2 us
    ppermute x2 -> x3, waiting for transfers between devices: 11.1 us -> 5.63 us  [body(): total = total + lax.ppermute(piece, 'aux', pairs_of(2 * dx))]
    ppermute x2 -> x3, starting transfers between devices: 0.36 us -> 3.96 us  [body(): total = total + lax.ppermute(piece, 'aux', pairs_of(2 * dx))]
    unnamed x39 -> x29, local copies, waits for them, and re-layouts: 8.91 us -> 6.61 us
  transfers between devices with their start and end apart: 22 -> 23, of which waited for: 14 -> 15; matrix products, arithmetic and copies ran while one was open for 3% -> 3% of each run, Pallas kernels for 19% -> 19%
where the time goes in v11:
time: 216 us
  waiting for transfers between devices  91.4 us (42%)
  starting transfers between devices  56.2 us (26%)
  Pallas kernels  51.3 us (24%)
  local copies, waits for them, and re-layouts  13.2 us (6%)
  other arithmetic  3.18 us (1%)
    all_to_all x1, waiting for transfers between devices, body(): part = lax.all_to_all(part, 'orb', split_axis=0, concat_axis=0, tiled=True)  25.6 us
    ppermute x7, waiting for transfers between devices, body(): us[k] = lax.ppermute(u, 'aux', pairs_of(k))  24.4 us
    ppermute x7, waiting for transfers between devices, body(): tb[k] = lax.ppermute(tb[k], 'aux', pairs_of(k))  19.7 us
    pallas_call x2, Pallas kernels, second_products(): pl.pallas_call(functools.partial(second_kernel, steps), in_specs=[sspec()...  15.9 us
    pallas_call x1, Pallas kernels, first_products(): pl.pallas_call(first_kernel, in_specs=[sspec(), sspec(), vspec(), vspec()...  12.6 us
    all_to_all x1, starting transfers between devices, body(): lax.all_to_all(first, 'orb', split_axis=0, concat_axis=0, tiled=True)  10.6 us
    ppermute x7, starting transfers between devices, body(): us[k] = lax.ppermute(u, 'aux', pairs_of(k))  9.62 us
    pallas_call x1, Pallas kernels, chi_share(): pl.pallas_call(chi_kernel, grid=(5,), in_specs=[sspec(), vspec()] + [vspe...  9.2 us
  transfers between devices with their start and end apart: 23, of which 15 were waited for; matrix products, arithmetic and copies ran while one was open for 3% of the time, Pallas kernels for 19%

profile of v11, /device:TPU:0, one launch (start us, length us, event | category | flops | bytes accessed | tf_op | source)
XLA Modules:
  0.0 215.5 jit_solution(4238606997247898329)
XLA Ops:
  0.0 2.0 pack.1
  2.0 8.2 %all-to-all-start = ((bf16[16,8,4096]{2,1,0:T(8,128)(2,1)}), bf16[16,8,4096]{2,1,0:T(8,128)(2,1)}, u32[]{:S(2)}, u32[]{:S(2)}) async-start(bf16[16,8,4096]{2,1,0:T(8,128)(2,1)} %pack.1), calls=%async_computation | async-start | bytes 2097152 | tf_op jit(solution)/shard_map/all_to_all | solution.py:382
  10.3 2.1 copy-done
  12.4 3.9 %block_pairs.1 = (bf16[2,3,10,32,128]{4,3,2,1,0:T(8,128)(2,1)S(1)}, bf16[2,3,10,32,128]{4,3,2,1,0:T(8,128)(2,1)}, bf16[2,3,10,32,128]{4,3,2,1,0:T(8,128)(2,1)S(1...) custom-call(s32[2]{0:T(128)S(1)} %pad_add_fusion.pos, ...), custom_call_target="tpu_custom_call" | custom-call | flops 1000000000 | bytes 8000000 | tf_op jit(solution)/shard_map/block_pairs/pallas_call | solution.py:102
  18.6 1.7 collective-permute-start.3
  20.9 1.9 copy-done.2
  22.8 5.2 %all-to-all-done = bf16[16,8,4096]{2,1,0:T(8,128)(2,1)} async-done(((bf16[16,8,4096]{2,1,0:T(8,128)(2,1)}), bf16[16,8,4096]{2,1,0:T(8,128)(2,1)}, u32[]{:S(2)}, u32[]{:S(2)}) %all-to-all-start) | async-done | bytes 1048608 | tf_op jit(solution)/shard_map/all_to_all | solution.py:382
  30.0 2.0 collective-permute-done.2.rest_2_
  32.0 7.2 %all-to-all-start.2 = ((bf16[16,30,16,256]{3,2,1,0:T(8,128)(2,1)}), bf16[16,30,16,256]{3,2,1,0:T(8,128)(2,1)}, u32[]{:S(2)}, u32[]{:S(2)}) async-start(bf16[16,30,16,256]{3,2,1,0:T(8,128)(2,1)} %copy-done.2), calls=%async_computation.2 | async-start | bytes 7864320 | tf_op jit(solution)/shard_map/all_to_all | solution.py:391
  39.6 2.9 %collective-permute-start.5 = (bf16[1952,128]{1,0:T(8,128)(2,1)S(1)}, bf16[1952,128]{1,0:T(8,128)(2,1)S(1)}, u32[]{:S(2)}, u32[]{:S(2)}) collective-permute-start(bf16[1952,128]{1,0:T(8,128)(2,1)S(1)} %get-tuple-element.95), channel_id=1, source_target_pairs={{0,64},{16,80},{32,96},{48,112},{64,0},{80,16},{96,32},{112,48},{1... | collective-permute-start | bytes 1499144 | tf_op jit(solution)/shard_map/ppermute | solution.py:395
  42.6 1.7 collective-permute-start.6
  45.7 3.6 %reshape.58.g_ref = bf16[16,6,64,64]{3,2,1,0:T(8,128)(2,1)} reshape(bf16[16,6,4096]{2,1,0:T(8,128)(2,1)} %bitcast.32) | data formatting | bytes 1572864 | tf_op jit(solution)/shard_map/reshape | solution.py:400
  49.3 7.1 %greens.1 = (bf16[16,3,64,128]{3,2,1,0:T(8,128)(2,1)}, bf16[2,192,192]{2,1,0:T(8,128)(2,1)}) custom-call(s32[2]{0:T(128)} %copy-done.6, s32[16]{0:T(128)} %size.1, s32[2048]{0:T(1024)} %bitcast_convert_fusion.meta.pat, bf16[16,6,64,64]{3,2,1,0:T(8,128)(2,1)} %reshape.58.g_ref, bf16[2,32,64]{2,1,0:T(8,128)(2,1)} %constant.54.clone.rows_ref, ...), custom_call_target="tpu_custom_call" | custom-call | flops 1000000 | bytes 8000000 | tf_op jit(solution)/shard_map/greens/pallas_call | solution.py:189
  56.6 8.2 %collective-permute-done.5.rest_4_ = bf16[1952,128]{1,0:T(8,128)(2,1)S(1)} collective-permute-done((bf16[1952,128]{1,0:T(8,128)(2,1)S(1)}, bf16[1952,128]{1,0:T(8,128)(2,1)S(1)}, u32[]{:S(2)}, u32[]{:S(2)}) %collective-permute-start.5) | collective-permute-done | bytes 499744 | tf_op jit(solution)/shard_map/ppermute | solution.py:395
  66.9 9.2 %collective-permute-done.7.rest_5_ = bf16[1920,128]{1,0:T(8,128)(2,1)} collective-permute-done((bf16[1920,128]{1,0:T(8,128)(2,1)S(1)}, bf16[1920,128]{1,0:T(8,128)(2,1)}, u32[]{:S(2)}, u32[]{:S(2)}) %collective-permute-start.7) | collective-permute-done | bytes 491552 | tf_op jit(solution)/shard_map/ppermute | solution.py:395
  76.2 12.6 %first.1 = bf16[16,6,80,256]{3,2,1,0:T(8,128)(2,1)} custom-call(s32[2]{0:T(128)} %copy-done.6, s32[4096]{0:T(1024)} %reshape.55.pat, bf16[256,256]{1,0:T(8,128)(2,1)} %constant.53.clone.perm, bf16[2,192,192]{2,1,0:T(8,128)(2,1)} %get-tuple-element.64.w_ref, bf16[1920,128]{1,0:T(8,128)(2,1)} %bitcast.38, bf16[1920,128]{1,0:T(8,128)(2,1)} %collective-permute-done.1.rest_1_, ...), custom_call_target="tpu_custom_call" | custom-call | flops 3000000000 | bytes 8000000 | tf_op jit(solution)/shard_map/first/pallas_call | solution.py:310
  88.8 6.6 %all-to-all-done.2 = bf16[16,30,16,256]{3,2,1,0:T(8,128)(2,1)} async-done(((bf16[16,30,16,256]{3,2,1,0:T(8,128)(2,1)}), bf16[16,30,16,256]{3,2,1,0:T(8,128)(2,1)}, u32[]{:S(2)}, u32[]{:S(2)}) %all-to-all-start.2) | async-done | bytes 3932192 | tf_op jit(solution)/shard_map/all_to_all | solution.py:391
  95.4 10.6 %all-to-all-start.1 = ((bf16[16,6,80,256]{3,2,1,0:T(8,128)(2,1)}), bf16[16,6,80,256]{3,2,1,0:T(8,128)(2,1)}, u32[]{:S(2)}, u32[]{:S(2)}) async-start(bf16[16,6,80,256]{3,2,1,0:T(8,128)(2,1)} %first.1), calls=%async_computation.1 | async-start | bytes 7864320 | tf_op jit(solution)/shard_map/all_to_all | solution.py:404
  106.1 7.6 %second.3 = (bf16[6,160,256]{2,1,0:T(8,128)(2,1)S(1)}, bf16[6,160,256]{2,1,0:T(8,128)(2,1)S(1)}, bf16[6,160,256]{2,1,0:T(8,128)(2,1)S(1)}, bf16[6,160,256]{2,1,0:T(8,128)(2,1)S(1)}) custom-call(s32[2]{0:T(128)S(1)} %copy-done.7, s32[2048]{0:T(1024)S(1)} %copy-done.5, bf16[256,256]{1,0:T(8,128)(2,1)S(1)} %copy-done.4, ...), custom_call_target="tpu_custom_call" | custom-call | flops 2000000000 | bytes 15000000 | tf_op jit(solution)/shard_map/second/pallas_call | solution.py:248
  113.8 3.2 %collective-permute-start.9 = (bf16[6,160,256]{2,1,0:T(8,128)(2,1)S(1)}, bf16[6,160,256]{2,1,0:T(8,128)(2,1)S(1)}, u32[]{:S(2)}, u32[]{:S(2)}) collective-permute-start(bf16[6,160,256]{2,1,0:T(8,128)(2,1)S(1)} %get-tuple-element.77), channel_id=1, source_target_pairs={{0,96},{16,112},{32,0},{48,16},{64,32},{80,48},{96,64},{112,80},{1... | collective-permute-start | bytes 1474568 | tf_op jit(solution)/shard_map/ppermute | solution.py:409
  117.0 3.0 %collective-permute-start.14 = (bf16[6,160,256]{2,1,0:T(8,128)(2,1)S(1)}, bf16[6,160,256]{2,1,0:T(8,128)(2,1)S(1)}, u32[]{:S(2)}, u32[]{:S(2)}) collective-permute-start(bf16[6,160,256]{2,1,0:T(8,128)(2,1)S(1)} %get-tuple-element.84), channel_id=1, source_target_pairs={{0,112},{16,96},{32,16},{48,0},{64,48},{80,32},{96,80},{112,64},{1... | collective-permute-start | bytes 1474568 | tf_op jit(solution)/shard_map/ppermute | solution.py:409
  120.0 8.3 %second.2 = (bf16[6,160,256]{2,1,0:T(8,128)(2,1)}, bf16[6,160,256]{2,1,0:T(8,128)(2,1)S(1)}, bf16[6,160,256]{2,1,0:T(8,128)(2,1)}, bf16[6,160,256]{2,1,0:T(8,128)(2,1)S(1)}) custom-call(s32[2]{0:T(128)S(1)} %copy-done.7, s32[2048]{0:T(1024)S(1)} %copy-done.5, bf16[256,256]{1,0:T(8,128)(2,1)S(1)} %copy-done.4, bf16[160,3,16,256]{3,2,1,0:T(8,128)(2,1)} %bitcast.15.ta_ref, ...), custom_call_target="tpu_custom_call" | custom-call | flops 2000000000 | bytes 15000000 | tf_op jit(solution)/shard_map/second/pallas_call | solution.py:248
  130.6 1.9 collective-permute-start.13
  132.5 2.2 %collective-permute-done.11.rest_3_ = bf16[6,160,256]{2,1,0:T(8,128)(2,1)S(1)} collective-permute-done((bf16[6,160,256]{2,1,0:T(8,128)(2,1)S(1)}, bf16[6,160,256]{2,1,0:T(8,128)(2,1)S(1)}, u32[]{:S(2)}, u32[]{:S(2)}) %collective-permute-start.11) | collective-permute-done | bytes 491552 | tf_op jit(solution)/shard_map/ppermute | solution.py:409
  134.7 22.1 %collective-permute-done.14.rest_7_ = bf16[6,160,256]{2,1,0:T(8,128)(2,1)S(1)} collective-permute-done((bf16[6,160,256]{2,1,0:T(8,128)(2,1)S(1)}, bf16[6,160,256]{2,1,0:T(8,128)(2,1)S(1)}, u32[]{:S(2)}, u32[]{:S(2)}) %collective-permute-start.14) | collective-permute-done | bytes 491552 | tf_op jit(solution)/shard_map/ppermute | solution.py:409
  157.9 9.2 %chi.1 = (bf16[16,40,1280]{2,1,0:T(8,128)(2,1)S(1)}, f32[16,40,1280]{2,1,0:T(8,128)S(1)}) custom-call(s32[2]{0:T(128)S(1)} %copy-done.7, bf16[16,6,80,256]{3,2,1,0:T(8,128)(2,1)} %all-to-all-done.1.first_ref, bf16[6,160,256]{2,1,0:T(8,128)(2,1)S(1)} %copy-done.11, bf16[6,160,256]{2,1,0:T(8,128)(2,1)S(1)} %collective-permute-done.10.rest_1_, ...), custom_call_target="tpu_custom_call" | custom-call | flops 5000000000 | bytes 13000000 | tf_op jit(solution)/shard_map/chi/pallas_call | solution.py:349
  167.8 3.1 %collective-permute-done.15 = bf16[16,40,1280]{2,1,0:T(8,128)(2,1)S(1)} collective-permute-done((bf16[16,40,1280]{2,1,0:T(8,128)(2,1)S(1)}, bf16[16,40,1280]{2,1,0:T(8,128)(2,1)S(1)}, u32[]{:S(2)}, u32[]{:S(2)}) %collective-permute-start.15) | collective-permute-done | bytes 1638432 | tf_op jit(solution)/shard_map/ppermute | solution.py:416
  172.4 6.9 %all-to-all-start.3 = ((bf16[16,40,1280]{2,1,0:T(8,128)(2,1)}), bf16[16,40,1280]{2,1,0:T(8,128)(2,1)S(1)}, u32[]{:S(2)}, u32[]{:S(2)}) async-start(bf16[16,40,1280]{2,1,0:T(8,128)(2,1)} %add_convert_fusion), calls=%async_computation.3 | async-start | bytes 3276800 | tf_op jit(solution)/shard_map/all_to_all | solution.py:417
  179.4 25.6 %all-to-all-done.3 = bf16[16,40,1280]{2,1,0:T(8,128)(2,1)S(1)} async-done(((bf16[16,40,1280]{2,1,0:T(8,128)(2,1)}), bf16[16,40,1280]{2,1,0:T(8,128)(2,1)S(1)}, u32[]{:S(2)}, u32[]{:S(2)}) %all-to-all-start.3) | async-done | bytes 1638432 | tf_op jit(solution)/shard_map/all_to_all | solution.py:417
  205.3 3.0 %collective-permute-start.18 = (f32[10,1280]{1,0:T(8,128)S(1)}, f32[10,1280]{1,0:T(8,128)S(1)}, u32[]{:S(2)}, u32[]{:S(2)}) collective-permute-start(f32[10,1280]{1,0:T(8,128)S(1)} %get-tuple-element.92), channel_id=1, source_target_pairs={{0,96},{16,112},{32,0},{48,16},{64,32},{80,48},{96,64},{112,80},{1... | collective-permute-start | bytes 153608 | tf_op jit(solution)/shard_map/ppermute | solution.py:423
  209.3 1.9 collective-permute-done.18
  211.2 3.2 %collective-permute-done.17 = f32[10,1280]{1,0:T(8,128)S(1)} collective-permute-done((f32[10,1280]{1,0:T(8,128)S(1)}, f32[10,1280]{1,0:T(8,128)S(1)}, u32[]{:S(2)}, u32[]{:S(2)}) %collective-permute-start.17) | collective-permute-done | bytes 51232 | tf_op jit(solution)/shard_map/ppermute | solution.py:423
  (75 shorter events, 17.2 us)
Async XLA Ops:
  0.0 10.3 %copy-start.3 = (bf16[256,256]{1,0:T(8,128)(2,1)S(1)}, bf16[256,256]{1,0:T(8,128)(2,1)}, u32[]{:S(2)}) copy-start(bf16[256,256]{1,0:T(8,128)(2,1)} %constant.53.clone.perm) | copy-start | bytes 393220
  2.0 25.9 %all-to-all-start = ((bf16[16,8,4096]{2,1,0:T(8,128)(2,1)}), bf16[16,8,4096]{2,1,0:T(8,128)(2,1)}, u32[]{:S(2)}, u32[]{:S(2)}) async-start(bf16[16,8,4096]{2,1,0:T(8,128)(2,1)} %pack.1), calls=%async_computation | async-start | bytes 2097152 | tf_op jit(solution)/shard_map/all_to_all | solution.py:382
  10.3 10.6 %copy-start.6 = (s32[2]{0:T(128)}, s32[2]{0:T(128)S(1)}, u32[]{:S(2)}) copy-start(s32[2]{0:T(128)S(1)} %pad_add_fusion.pos) | copy-start | bytes 28
  12.4 7.9 %copy-start.1 = (bf16[10,16,3,4096]{3,1,2,0:T(8,128)(2,1)S(1)}, bf16[10,16,3,4096]{3,1,2,0:T(8,128)(2,1)}, u32[]{:S(2)}) copy-start(bf16[10,16,3,4096]{3,1,2,0:T(8,128)(2,1)} %param.9) | copy-start | bytes 11796484
  17.1 12.9 %collective-permute-start.1 = (bf16[1920,128]{1,0:T(8,128)(2,1)}, bf16[1920,128]{1,0:T(8,128)(2,1)}, u32[]{:S(2)}, u32[]{:S(2)}) collective-permute-start(bf16[1920,128]{1,0:T(8,128)(2,1)} %bitcast.5), channel_id=1, source_target_pairs={{0,16},{16,0},{32,48},{48,32},{64,80},{80,64},{96,112},{112,96},{1... | collective-permute-start | bytes 1474568 | tf_op jit(solution)/shard_map/ppermute | solution.py:387
  17.1 14.9 %collective-permute-start.2 = (bf16[1920,128]{1,0:T(8,128)(2,1)S(1)}, bf16[1920,128]{1,0:T(8,128)(2,1)}, u32[]{:S(2)}, u32[]{:S(2)}) collective-permute-start(bf16[1920,128]{1,0:T(8,128)(2,1)S(1)} %bitcast.41), channel_id=1, source_target_pairs={{0,32},{16,48},{32,64},{48,80},{64,96},{80,112},{96,0},{112,16},{1... | collective-permute-start | bytes 1474568 | tf_op jit(solution)/shard_map/ppermute | solution.py:387
  18.6 13.5 %collective-permute-start.3 = (bf16[1920,128]{1,0:T(8,128)(2,1)S(1)}, bf16[1920,128]{1,0:T(8,128)(2,1)}, u32[]{:S(2)}, u32[]{:S(2)}) collective-permute-start(bf16[1920,128]{1,0:T(8,128)(2,1)S(1)} %bitcast.40), channel_id=1, source_target_pairs={{0,96},{16,112},{32,0},{48,16},{64,32},{80,48},{96,64},{112,80},{1... | collective-permute-start | bytes 1474568 | tf_op jit(solution)/shard_map/ppermute | solution.py:387
  28.7 1.2 collective-permute-start
  32.0 63.4 %all-to-all-start.2 = ((bf16[16,30,16,256]{3,2,1,0:T(8,128)(2,1)}), bf16[16,30,16,256]{3,2,1,0:T(8,128)(2,1)}, u32[]{:S(2)}, u32[]{:S(2)}) async-start(bf16[16,30,16,256]{3,2,1,0:T(8,128)(2,1)} %copy-done.2), calls=%async_computation.2 | async-start | bytes 7864320 | tf_op jit(solution)/shard_map/all_to_all | solution.py:391
  39.3 17.1 %collective-permute-start.4 = (bf16[1952,128]{1,0:T(8,128)(2,1)S(1)}, bf16[1952,128]{1,0:T(8,128)(2,1)S(1)}, u32[]{:S(2)}, u32[]{:S(2)}) collective-permute-start(bf16[1952,128]{1,0:T(8,128)(2,1)S(1)} %get-tuple-element.96), channel_id=1, source_target_pairs={{0,48},{16,32},{32,80},{48,64},{64,112},{80,96},{96,16},{112,0},{1... | collective-permute-start | bytes 1499144 | tf_op jit(solution)/shard_map/ppermute | solution.py:395
  39.6 25.2 %collective-permute-start.5 = (bf16[1952,128]{1,0:T(8,128)(2,1)S(1)}, bf16[1952,128]{1,0:T(8,128)(2,1)S(1)}, u32[]{:S(2)}, u32[]{:S(2)}) collective-permute-start(bf16[1952,128]{1,0:T(8,128)(2,1)S(1)} %get-tuple-element.95), channel_id=1, source_target_pairs={{0,64},{16,80},{32,96},{48,112},{64,0},{80,16},{96,32},{112,48},{1... | collective-permute-start | bytes 1499144 | tf_op jit(solution)/shard_map/ppermute | solution.py:395
  42.6 22.6 %collective-permute-start.6 = (bf16[1952,128]{1,0:T(8,128)(2,1)S(1)}, bf16[1952,128]{1,0:T(8,128)(2,1)}, u32[]{:S(2)}, u32[]{:S(2)}) collective-permute-start(bf16[1952,128]{1,0:T(8,128)(2,1)S(1)} %get-tuple-element.94), channel_id=1, source_target_pairs={{0,112},{16,96},{32,16},{48,0},{64,48},{80,32},{96,80},{112,64},{1... | collective-permute-start | bytes 1499144 | tf_op jit(solution)/shard_map/ppermute | solution.py:395
  44.2 31.9 %collective-permute-start.7 = (bf16[1920,128]{1,0:T(8,128)(2,1)S(1)}, bf16[1920,128]{1,0:T(8,128)(2,1)}, u32[]{:S(2)}, u32[]{:S(2)}) collective-permute-start(bf16[1920,128]{1,0:T(8,128)(2,1)S(1)} %bitcast.39), channel_id=1, source_target_pairs={{0,80},{16,64},{32,112},{48,96},{64,16},{80,0},{96,48},{112,32},{1... | collective-permute-start | bytes 1474568 | tf_op jit(solution)/shard_map/ppermute | solution.py:395
  56.5 19.7 %copy-start.12 = (bf16[1952,128]{1,0:T(8,128)(2,1)}, bf16[1952,128]{1,0:T(8,128)(2,1)S(1)}, u32[]{:S(2)}) copy-start(bf16[1952,128]{1,0:T(8,128)(2,1)S(1)} %collective-permute-done.4.rest_3_) | copy-start | bytes 1499140
  64.9 11.3 %copy-start.13 = (bf16[1952,128]{1,0:T(8,128)(2,1)}, bf16[1952,128]{1,0:T(8,128)(2,1)S(1)}, u32[]{:S(2)}) copy-start(bf16[1952,128]{1,0:T(8,128)(2,1)S(1)} %collective-permute-done.5.rest_4_) | copy-start | bytes 1499140
  88.8 17.3 %copy-start.4 = (bf16[256,256]{1,0:T(8,128)(2,1)S(1)}, bf16[256,256]{1,0:T(8,128)(2,1)}, u32[]{:S(2)}) copy-start(bf16[256,256]{1,0:T(8,128)(2,1)} %constant.53.clone.perm) | copy-start | bytes 393220
  88.8 17.3 %copy-start.5 = (s32[2048]{0:T(1024)S(1)}, s32[2048]{0:T(1024)}, u32[]{:S(2)}) copy-start(s32[2048]{0:T(1024)} %bitcast_convert_fusion.meta.pat) | copy-start | bytes 24580
  88.8 17.3 %copy-start.7 = (s32[2]{0:T(128)S(1)}, s32[2]{0:T(128)}, u32[]{:S(2)}) copy-start(s32[2]{0:T(128)} %copy-done.6) | copy-start | bytes 28
  88.8 17.3 %copy-start.8 = (bf16[16,3,64,128]{3,2,1,0:T(8,128)(2,1)S(1)}, bf16[16,3,64,128]{3,2,1,0:T(8,128)(2,1)}, u32[]{:S(2)}) copy-start(bf16[16,3,64,128]{3,2,1,0:T(8,128)(2,1)} %get-tuple-element.71.v_ref) | copy-start | bytes 2359300
  95.4 61.4 %all-to-all-start.1 = ((bf16[16,6,80,256]{3,2,1,0:T(8,128)(2,1)}), bf16[16,6,80,256]{3,2,1,0:T(8,128)(2,1)}, u32[]{:S(2)}, u32[]{:S(2)}) async-start(bf16[16,6,80,256]{3,2,1,0:T(8,128)(2,1)} %first.1), calls=%async_computation.1 | async-start | bytes 7864320 | tf_op jit(solution)/shard_map/all_to_all | solution.py:404
  113.7 15.4 %collective-permute-start.8 = (bf16[6,160,256]{2,1,0:T(8,128)(2,1)S(1)}, bf16[6,160,256]{2,1,0:T(8,128)(2,1)S(1)}, u32[]{:S(2)}, u32[]{:S(2)}) collective-permute-start(bf16[6,160,256]{2,1,0:T(8,128)(2,1)S(1)} %get-tuple-element.76), channel_id=1, source_target_pairs={{0,32},{16,48},{32,64},{48,80},{64,96},{80,112},{96,0},{112,16},{1... | collective-permute-start | bytes 1474568 | tf_op jit(solution)/shard_map/ppermute | solution.py:409
  113.8 15.4 %collective-permute-start.9 = (bf16[6,160,256]{2,1,0:T(8,128)(2,1)S(1)}, bf16[6,160,256]{2,1,0:T(8,128)(2,1)S(1)}, u32[]{:S(2)}, u32[]{:S(2)}) collective-permute-start(bf16[6,160,256]{2,1,0:T(8,128)(2,1)S(1)} %get-tuple-element.77), channel_id=1, source_target_pairs={{0,96},{16,112},{32,0},{48,16},{64,32},{80,48},{96,64},{112,80},{1... | collective-permute-start | bytes 1474568 | tf_op jit(solution)/shard_map/ppermute | solution.py:409
  117.0 17.7 %collective-permute-start.11 = (bf16[6,160,256]{2,1,0:T(8,128)(2,1)S(1)}, bf16[6,160,256]{2,1,0:T(8,128)(2,1)S(1)}, u32[]{:S(2)}, u32[]{:S(2)}) collective-permute-start(bf16[6,160,256]{2,1,0:T(8,128)(2,1)S(1)} %get-tuple-element.80), channel_id=1, source_target_pairs={{0,48},{16,32},{32,80},{48,64},{64,112},{80,96},{96,16},{112,0},{1... | collective-permute-start | bytes 1474568 | tf_op jit(solution)/shard_map/ppermute | solution.py:409
  117.0 39.8 %collective-permute-start.14 = (bf16[6,160,256]{2,1,0:T(8,128)(2,1)S(1)}, bf16[6,160,256]{2,1,0:T(8,128)(2,1)S(1)}, u32[]{:S(2)}, u32[]{:S(2)}) collective-permute-start(bf16[6,160,256]{2,1,0:T(8,128)(2,1)S(1)} %get-tuple-element.84), channel_id=1, source_target_pairs={{0,112},{16,96},{32,16},{48,0},{64,48},{80,32},{96,80},{112,64},{1... | collective-permute-start | bytes 1474568 | tf_op jit(solution)/shard_map/ppermute | solution.py:409
  129.2 27.7 %collective-permute-start.10 = (bf16[6,160,256]{2,1,0:T(8,128)(2,1)}, bf16[6,160,256]{2,1,0:T(8,128)(2,1)S(1)}, u32[]{:S(2)}, u32[]{:S(2)}) collective-permute-start(bf16[6,160,256]{2,1,0:T(8,128)(2,1)} %get-tuple-element.78), channel_id=1, source_target_pairs={{0,16},{16,0},{32,48},{48,32},{64,80},{80,64},{96,112},{112,96},{1... | collective-permute-start | bytes 1474568 | tf_op jit(solution)/shard_map/ppermute | solution.py:413
  129.2 27.7 %collective-permute-start.12 = (bf16[6,160,256]{2,1,0:T(8,128)(2,1)}, bf16[6,160,256]{2,1,0:T(8,128)(2,1)}, u32[]{:S(2)}, u32[]{:S(2)}) collective-permute-start(bf16[6,160,256]{2,1,0:T(8,128)(2,1)} %get-tuple-element.81), channel_id=1, source_target_pairs={{0,64},{16,80},{32,96},{48,112},{64,0},{80,16},{96,32},{112,48},{1... | collective-permute-start | bytes 1474568 | tf_op jit(solution)/shard_map/ppermute | solution.py:413
  130.6 26.3 %collective-permute-start.13 = (bf16[6,160,256]{2,1,0:T(8,128)(2,1)S(1)}, bf16[6,160,256]{2,1,0:T(8,128)(2,1)}, u32[]{:S(2)}, u32[]{:S(2)}) collective-permute-start(bf16[6,160,256]{2,1,0:T(8,128)(2,1)S(1)} %get-tuple-element.82), channel_id=1, source_target_pairs={{0,80},{16,64},{32,112},{48,96},{64,16},{80,0},{96,48},{112,32},{1... | collective-permute-start | bytes 1474568 | tf_op jit(solution)/shard_map/ppermute | solution.py:413
  167.1 3.8 %collective-permute-start.15 = (bf16[16,40,1280]{2,1,0:T(8,128)(2,1)S(1)}, bf16[16,40,1280]{2,1,0:T(8,128)(2,1)S(1)}, u32[]{:S(2)}, u32[]{:S(2)}) collective-permute-start(bf16[16,40,1280]{2,1,0:T(8,128)(2,1)S(1)} %get-tuple-element.86), channel_id=1, source_target_pairs={{0,16},{16,0},{32,48},{48,32},{64,80},{80,64},{96,112},{112,96},{1... | collective-permute-start | bytes 4915208 | tf_op jit(solution)/shard_map/ppermute | solution.py:416
  172.4 32.6 %all-to-all-start.3 = ((bf16[16,40,1280]{2,1,0:T(8,128)(2,1)}), bf16[16,40,1280]{2,1,0:T(8,128)(2,1)S(1)}, u32[]{:S(2)}, u32[]{:S(2)}) async-start(bf16[16,40,1280]{2,1,0:T(8,128)(2,1)} %add_convert_fusion), calls=%async_computation.3 | async-start | bytes 3276800 | tf_op jit(solution)/shard_map/all_to_all | solution.py:417
  205.3 5.9 %collective-permute-start.18 = (f32[10,1280]{1,0:T(8,128)S(1)}, f32[10,1280]{1,0:T(8,128)S(1)}, u32[]{:S(2)}, u32[]{:S(2)}) collective-permute-start(f32[10,1280]{1,0:T(8,128)S(1)} %get-tuple-element.92), channel_id=1, source_target_pairs={{0,96},{16,112},{32,0},{48,16},{64,32},{80,48},{96,64},{112,80},{1... | collective-permute-start | bytes 153608 | tf_op jit(solution)/shard_map/ppermute | solution.py:423
  208.3 6.1 %collective-permute-start.17 = (f32[10,1280]{1,0:T(8,128)S(1)}, f32[10,1280]{1,0:T(8,128)S(1)}, u32[]{:S(2)}, u32[]{:S(2)}) collective-permute-start(f32[10,1280]{1,0:T(8,128)S(1)} %get-tuple-element.93), channel_id=1, source_target_pairs={{0,64},{16,80},{32,96},{48,112},{64,0},{80,16},{96,32},{112,48},{1... | collective-permute-start | bytes 153608 | tf_op jit(solution)/shard_map/ppermute | solution.py:423
  208.4 6.5 %collective-permute-start.16 = (f32[10,1280]{1,0:T(8,128)S(1)}, f32[10,1280]{1,0:T(8,128)S(1)}, u32[]{:S(2)}, u32[]{:S(2)}) collective-permute-start(f32[10,1280]{1,0:T(8,128)S(1)} %get-tuple-element.91), channel_id=1, source_target_pairs={{0,32},{16,48},{32,64},{48,80},{64,96},{80,112},{96,0},{112,16},{1... | collective-permute-start | bytes 153608 | tf_op jit(solution)/shard_map/ppermute | solution.py:423
  (5 other events, 6.6 us)
